TPU v7x, 32 devices: a whole 2x2x4 slice. The times are simulated.
32 devices in a mesh: dp: 4 (over x, core), seq: 8 (over z, y).
Axes of the slice: x: 2, y: 2, z: 4, core: 2. Of those that a mesh axis runs over, the one named last changes fastest.
Arguments:
- hidden_in: bfloat16 [16, 1024, 640], P('dp', 'seq'), may hold values from -6 to 6
- positions: int32 [16, 1024], P('dp', 'seq'), may hold values from 0 to 1023, as said below
- out_grad: bfloat16 [16, 1024, 640], P('dp', 'seq'), may hold values from -6 to 6
- w_attn_in: bfloat16 [2, 640, 1536], P(None, None, ('dp', 'seq')), may hold values from -0.25 to 0.25
- w_attn_out: bfloat16 [2, 1024, 640], P(None, ('dp', 'seq')), may hold values from -0.1875 to 0.1875
- w_ffn_in: bfloat16 [2, 640, 4096], P(None, None, ('dp', 'seq')), may hold values from -0.25 to 0.25
- w_ffn_out: bfloat16 [2, 2048, 640], P(None, ('dp', 'seq')), may hold values from -0.125 to 0.125
- gains: bfloat16 [2, 3072], P(None, ('dp', 'seq')), may hold values from 0.5 to 1.5
Outputs:
- hidden_out: bfloat16 [16, 1024, 640], P('dp', 'seq')
- input_grad: float32 [16, 1024, 640], P('dp', 'seq')
- grad_attn_in: float32 [2, 640, 1536], P(None, None, ('dp', 'seq'))
- grad_attn_out: float32 [2, 1024, 640], P(None, ('dp', 'seq'))
- grad_ffn_in: float32 [2, 640, 4096], P(None, None, ('dp', 'seq'))
- grad_ffn_out: float32 [2, 2048, 640], P(None, ('dp', 'seq'))
- grad_gains: float32 [2, 3072], P(None, ('dp', 'seq'))
Inputs may be any that keep to these rules, and one draw needn't show every extreme that they name: Within each sequence documents lie end to end and positions count up by one from 0 in each; in each group of 4 sequences along dp, one sequence is a single document.
All inputs are finite; a program needn't handle non-finite values.
Results may differ from a plain program's by a relative error of at most 0.02.
Values may be sent and summed in bfloat16 or wider, within the bound.
No kernel may reach another device: no remote copies, remote signals or barrier semaphores. Data moves between devices by JAX's collectives and lax.ppermute only.
A program may use at most 192 MiB of HBM per device.

v0:
```python
from functools import partial

import jax
import jax.numpy as jnp
from jax import lax
from jax.sharding import PartitionSpec as P

D = 640
HEADS = 4
HEAD_DIM = 256
WINDOW = 512


EPSILON = 1e-06
ROPE_BASE = 10000.0
SCORE_SCALE = 0.0625
MASKED_SCORE = -1e30


def from_behind(block, axis, distance):
    devices = range(lax.axis_size(axis))
    route = [(i - distance, i) for i in devices if i - distance in devices]
    return lax.ppermute(block, axis, route)


def as_sent(x):
    return jax.tree.map(lambda a: a.astype(jnp.bfloat16) if a.dtype == jnp.float32 else a, x)


def rms_norm(values, gain):
    return values * lax.rsqrt(jnp.mean(values * values, axis=-1, keepdims=True) + EPSILON) * gain


def angle_tables(places):
    half_dim = HEAD_DIM // 2
    inverse = ROPE_BASE ** (-(2.0 * jnp.arange(half_dim, dtype=jnp.float32)) / HEAD_DIM)
    phases = places.astype(jnp.float32)[..., None] * inverse
    return (jnp.cos(phases), jnp.sin(phases))


def rotate(values, cosine_tab, sine_tab):
    half_dim = values.shape[-1] // 2
    first_half = values[..., :half_dim]
    second_half = values[..., half_dim:]
    return jnp.concatenate(
        [
            first_half * cosine_tab - second_half * sine_tab,
            second_half * cosine_tab + first_half * sine_tab,
        ],
        axis=-1,
    )


def prepare(raw_part, gain_part, cosine_tab, sine_tab):
    return rotate(rms_norm(raw_part, gain_part), cosine_tab, sine_tab)


def gated_gelu(gate_and_up_rows):
    half_width = gate_and_up_rows.shape[-1] // 2
    return (
        jax.nn.gelu(gate_and_up_rows[..., :half_width], approximate=True)
        * gate_and_up_rows[..., half_width:]
    )


def split_gains(gain_row):
    gain_full = gain_row.astype(jnp.float32)
    return (
        gain_full[0:D],
        gain_full[D : 2 * D],
        gain_full[2 * D : 3 * D],
        gain_full[3 * D : 4 * D],
        gain_full[4 * D : 4 * D + HEAD_DIM],
        gain_full[4 * D + HEAD_DIM : 4 * D + 2 * HEAD_DIM],
    )


def allowed_keys(places, start):
    rows = places.shape[1]
    query_at = start + jnp.arange(rows, dtype=jnp.int32)
    key_at = start - WINDOW + jnp.arange(WINDOW + rows, dtype=jnp.int32)
    distance = query_at[:, None] - key_at[None, :]
    inside = (distance >= 0) & (distance < WINDOW)
    same_doc = key_at[None, None, :] >= (query_at[None, :] - places)[:, :, None]
    return inside[None] & same_doc


def score_block(queries, keys_ext, allowed):
    scores = (
        jnp.einsum("sqhd,skd->shqk", queries, keys_ext, preferred_element_type=jnp.float32)
        * SCORE_SCALE
    )
    return jnp.where(allowed[:, None], scores, MASKED_SCORE)


def gather_window(keys_rot, values, hops):
    received = []
    carried = (keys_rot, values)
    for offset in range(hops):
        carried = from_behind((carried[0], carried[1]), "seq", 1)
        received.insert(0, carried)
    keys_ext = jnp.concatenate([pair[0] for pair in received] + [keys_rot], axis=1)
    values_ext = jnp.concatenate([pair[1] for pair in received] + [values], axis=1)
    return (keys_ext, values_ext)


def return_window(key_grads, value_grads, hops, rows):

    def part_of(distance):
        lower = (hops - distance) * rows
        return (key_grads[:, lower : lower + rows], value_grads[:, lower : lower + rows])

    own_key, own_value = part_of(0)
    carried = part_of(hops)
    for distance in range(hops, 0, -1):
        if distance < hops:
            nearer = part_of(distance)
            carried = (carried[0] + nearer[0], carried[1] + nearer[1])
        carried = (
            from_behind(as_sent(carried[0]), "seq", -1),
            from_behind(carried[1].astype(jnp.bfloat16), "seq", -1).astype(jnp.float32),
        )
    own_key = own_key + carried[0]
    own_value = own_value + carried[1]
    return (own_key, own_value)


def forward_layer(stream, weights, cosine_tab, sine_tab, allowed, hops):
    attention_input_rows, attention_output_rows, feedforward_input, feedforward_output, gain_row = (
        weights
    )
    pre_attn, post_attn, pre_ffn, post_ffn, query_gain, key_gain = split_gains(gain_row)
    seq_count, rows = (stream.shape[0], stream.shape[1])
    query_cols = HEADS * HEAD_DIM
    normalized_rows = rms_norm(stream, pre_attn).astype(jnp.bfloat16)
    projected_rows = jnp.einsum(
        "sbd,de->sbe", normalized_rows, attention_input_rows, preferred_element_type=jnp.float32
    )
    query_raw = projected_rows[..., :query_cols].reshape(seq_count, rows, HEADS, HEAD_DIM)
    key_raw = projected_rows[..., query_cols : query_cols + HEAD_DIM]
    values = projected_rows[..., query_cols + HEAD_DIM :].astype(jnp.bfloat16)
    queries = prepare(
        query_raw, query_gain, cosine_tab[:, :, None, :], sine_tab[:, :, None, :]
    ).astype(jnp.bfloat16)
    keys_rot = prepare(key_raw, key_gain, cosine_tab, sine_tab).astype(jnp.bfloat16)
    keys_ext, values_ext = gather_window(keys_rot, values, hops)
    scores = score_block(queries, keys_ext, allowed)
    row_max = jnp.max(scores, axis=-1, keepdims=True)
    weights_exp = jnp.exp(scores - row_max)
    row_sum = jnp.sum(weights_exp, axis=-1, keepdims=True)
    probs = (weights_exp / row_sum).astype(jnp.bfloat16)
    logsum = row_max + jnp.log(row_sum)
    attended_values = jnp.einsum(
        "shqk,skd->sqhd", probs, values_ext, preferred_element_type=jnp.float32
    )
    attended_values = attended_values.astype(jnp.bfloat16).reshape(seq_count, rows, query_cols)
    residual_branch = jnp.einsum(
        "sbe,ed->sbd", attended_values, attention_output_rows, preferred_element_type=jnp.float32
    )
    middle = stream + rms_norm(residual_branch, post_attn)
    feedforward_normalized = rms_norm(middle, pre_ffn).astype(jnp.bfloat16)
    gate_and_up_rows = jnp.einsum(
        "sbd,df->sbf", feedforward_normalized, feedforward_input, preferred_element_type=jnp.float32
    )
    inner_activation = gated_gelu(gate_and_up_rows).astype(jnp.bfloat16)
    feedforward_branch = jnp.einsum(
        "sbf,fd->sbd", inner_activation, feedforward_output, preferred_element_type=jnp.float32
    )
    result = middle + rms_norm(feedforward_branch, post_ffn)
    record = (
        stream,
        normalized_rows,
        query_raw,
        key_raw,
        queries,
        keys_ext,
        values_ext,
        logsum,
        attended_values,
        residual_branch,
        middle,
        feedforward_normalized,
        gate_and_up_rows,
        inner_activation,
        feedforward_branch,
    )
    return (record, result)


def backward_layer(grad_out, weights, record, cosine_tab, sine_tab, allowed, hops):
    attention_input_rows, attention_output_rows, feedforward_input, feedforward_output, gain_row = (
        weights
    )
    pre_attn, post_attn, pre_ffn, post_ffn, query_gain, key_gain = split_gains(gain_row)
    (
        stream,
        normalized_rows,
        query_raw,
        key_raw,
        queries,
        keys_ext,
        values_ext,
        logsum,
        attended_values,
        residual_branch,
        middle,
        feedforward_normalized,
        gate_and_up_rows,
        inner_activation,
        feedforward_branch,
    ) = record
    seq_count, rows = (stream.shape[0], stream.shape[1])
    query_cols = HEADS * HEAD_DIM
    _, pull_post_ffn = jax.vjp(rms_norm, feedforward_branch, post_ffn)
    grad_ffn_branch, grad_post_ffn = pull_post_ffn(grad_out)
    grad_ffn_branch = grad_ffn_branch.astype(jnp.bfloat16)
    grad_ffn_out = jnp.einsum(
        "sbf,sbd->fd", inner_activation, grad_ffn_branch, preferred_element_type=jnp.float32
    )
    grad_inner = jnp.einsum(
        "sbd,fd->sbf", grad_ffn_branch, feedforward_output, preferred_element_type=jnp.float32
    )
    _, pull_act = jax.vjp(gated_gelu, gate_and_up_rows)
    grad_gate_up = pull_act(grad_inner)[0].astype(jnp.bfloat16)
    grad_ffn_in = jnp.einsum(
        "sbd,sbf->df", feedforward_normalized, grad_gate_up, preferred_element_type=jnp.float32
    )
    grad_ffn_normed = jnp.einsum(
        "sbf,df->sbd", grad_gate_up, feedforward_input, preferred_element_type=jnp.float32
    )
    _, pull_pre_ffn = jax.vjp(rms_norm, middle, pre_ffn)
    grad_middle_part, grad_pre_ffn = pull_pre_ffn(grad_ffn_normed)
    grad_middle = grad_out + grad_middle_part
    _, pull_post_attn = jax.vjp(rms_norm, residual_branch, post_attn)
    grad_branch, grad_post_attn = pull_post_attn(grad_middle)
    grad_branch = grad_branch.astype(jnp.bfloat16)
    grad_attn_out = jnp.einsum(
        "sbe,sbd->ed", attended_values, grad_branch, preferred_element_type=jnp.float32
    )
    grad_context = jnp.einsum(
        "sbd,ed->sbe", grad_branch, attention_output_rows, preferred_element_type=jnp.float32
    )
    grad_context = grad_context.astype(jnp.bfloat16).reshape(seq_count, rows, HEADS, HEAD_DIM)
    scores = score_block(queries, keys_ext, allowed)
    probs = jnp.exp(scores - logsum)
    grad_probs = jnp.einsum(
        "sqhd,skd->shqk", grad_context, values_ext, preferred_element_type=jnp.float32
    )
    grad_values_ext = jnp.einsum(
        "shqk,sqhd->skd",
        probs.astype(jnp.bfloat16),
        grad_context,
        preferred_element_type=jnp.float32,
    )
    inner_sum = jnp.sum(probs * grad_probs, axis=-1, keepdims=True)
    grad_scores = (probs * (grad_probs - inner_sum)).astype(jnp.bfloat16)
    grad_queries = (
        jnp.einsum("shqk,skd->sqhd", grad_scores, keys_ext, preferred_element_type=jnp.float32)
        * SCORE_SCALE
    )
    grad_keys_ext = (
        jnp.einsum("shqk,sqhd->skd", grad_scores, queries, preferred_element_type=jnp.float32)
        * SCORE_SCALE
    )
    grad_keys, grad_values = return_window(grad_keys_ext, grad_values_ext, hops, rows)
    _, pull_query = jax.vjp(
        partial(prepare, cosine_tab=cosine_tab[:, :, None, :], sine_tab=sine_tab[:, :, None, :]),
        query_raw,
        query_gain,
    )
    grad_query_raw, grad_query_gain = pull_query(grad_queries)
    _, pull_key = jax.vjp(
        partial(prepare, cosine_tab=cosine_tab, sine_tab=sine_tab), key_raw, key_gain
    )
    grad_key_raw, grad_key_gain = pull_key(grad_keys)
    grad_projected = jnp.concatenate(
        [grad_query_raw.reshape(seq_count, rows, query_cols), grad_key_raw, grad_values], axis=-1
    )
    grad_projected = grad_projected.astype(jnp.bfloat16)
    grad_attn_in = jnp.einsum(
        "sbd,sbe->de", normalized_rows, grad_projected, preferred_element_type=jnp.float32
    )
    grad_normed = jnp.einsum(
        "sbe,de->sbd", grad_projected, attention_input_rows, preferred_element_type=jnp.float32
    )
    _, pull_pre_attn = jax.vjp(rms_norm, stream, pre_attn)
    grad_stream_part, grad_pre_attn = pull_pre_attn(grad_normed)
    grad_in = grad_middle + grad_stream_part
    grad_gain_row = jnp.concatenate(
        [grad_pre_attn, grad_post_attn, grad_pre_ffn, grad_post_ffn, grad_query_gain, grad_key_gain]
    )
    return (grad_in, (grad_attn_in, grad_attn_out, grad_ffn_in, grad_ffn_out, grad_gain_row))


def body(hidden_in, positions, out_grad, w_attn_in, w_attn_out, w_ffn_in, w_ffn_out, gains):
    rows = hidden_in.shape[1]
    hops = WINDOW // rows
    layer_count = w_attn_in.shape[0]
    start = lax.axis_index("seq") * rows
    cosine_tab, sine_tab = angle_tables(positions)
    allowed = allowed_keys(positions, start)
    stream = hidden_in.astype(jnp.float32)
    records = []
    for layer_index in range(layer_count):
        weights = (
            lax.all_gather(w_attn_in[layer_index], ("dp", "seq"), axis=1, tiled=True),
            lax.all_gather(w_attn_out[layer_index], ("dp", "seq"), axis=0, tiled=True),
            lax.all_gather(w_ffn_in[layer_index], ("dp", "seq"), axis=1, tiled=True),
            lax.all_gather(w_ffn_out[layer_index], ("dp", "seq"), axis=0, tiled=True),
            lax.all_gather(gains[layer_index], ("dp", "seq"), axis=0, tiled=True),
        )
        record, stream = forward_layer(stream, weights, cosine_tab, sine_tab, allowed, hops)
        records.append(record)
    hidden_out = stream.astype(jnp.bfloat16)
    grad_stream = out_grad.astype(jnp.float32)
    layer_grads = [None] * layer_count
    for layer_index in reversed(range(layer_count)):
        weights = (
            lax.all_gather(w_attn_in[layer_index], ("dp", "seq"), axis=1, tiled=True),
            lax.all_gather(w_attn_out[layer_index], ("dp", "seq"), axis=0, tiled=True),
            lax.all_gather(w_ffn_in[layer_index], ("dp", "seq"), axis=1, tiled=True),
            lax.all_gather(w_ffn_out[layer_index], ("dp", "seq"), axis=0, tiled=True),
            lax.all_gather(gains[layer_index], ("dp", "seq"), axis=0, tiled=True),
        )
        grad_stream, local_grads = backward_layer(
            grad_stream, weights, records[layer_index], cosine_tab, sine_tab, allowed, hops
        )
        layer_grads[layer_index] = (
            lax.psum_scatter(local_grads[0], ("dp", "seq"), scatter_dimension=1, tiled=True),
            lax.psum_scatter(local_grads[1], ("dp", "seq"), scatter_dimension=0, tiled=True),
            lax.psum_scatter(local_grads[2], ("dp", "seq"), scatter_dimension=1, tiled=True),
            lax.psum_scatter(local_grads[3], ("dp", "seq"), scatter_dimension=0, tiled=True),
            lax.psum_scatter(local_grads[4], ("dp", "seq"), scatter_dimension=0, tiled=True),
        )
    stacked = [jnp.stack([entry[member] for entry in layer_grads]) for member in range(5)]
    return (hidden_out, grad_stream, stacked[0], stacked[1], stacked[2], stacked[3], stacked[4])


def solution(mesh):
    return jax.shard_map(
        body,
        mesh=mesh,
        in_specs=(
            P("dp", "seq", None),
            P("dp", "seq"),
            P("dp", "seq", None),
            P(None, None, ("dp", "seq")),
            P(None, ("dp", "seq"), None),
            P(None, None, ("dp", "seq")),
            P(None, ("dp", "seq"), None),
            P(None, ("dp", "seq")),
        ),
        out_specs=(
            P("dp", "seq", None),
            P("dp", "seq", None),
            P(None, None, ("dp", "seq")),
            P(None, ("dp", "seq"), None),
            P(None, None, ("dp", "seq")),
            P(None, ("dp", "seq"), None),
            P(None, ("dp", "seq")),
        ),
        check_vma=False,
    )
```

profile of v0, /device:TPU:0, one launch (start us, length us, event | category | flops | bytes accessed | tf_op | source)
XLA Modules:
  0.0 1884.9 jit_solution(2823193784670276008)
XLA Ops:
  17.0 42.3 %all-reduce.17 = (bf16[3072]{0:T(1024)(128)(2,1)S(1)}, bf16[3072]{0:T(1024)(128)(2,1)S(1)}) all-reduce(bf16[3072]{0:T(1024)(128)(2,1)S(1)} %dynamic-update-slice, bf16[3072]{0:T(1024)(128)(2,1)S(1)} %dynamic-update-slice.1), channel_id=2, replica_groups=mesh['dp'=4,'seq'=8] {'dp','seq'}, use_global_device_ids=true, to_apply=%add.12 | all-reduce | flops 6144 | bytes 24576
  60.9 9.6 all-gather.19.cloned.1.call-done
  75.2 3.4 collective-permute-start.4
  83.2 3.3 collective-permute-start
  86.5 3.4 collective-permute-start.5
  92.7 4.4 collective-permute-start.1
  98.5 4.5 collective-permute-start.6
  104.6 5.0 collective-permute-start.2
  110.2 5.3 collective-permute-start.7
  118.6 5.7 collective-permute-start.3
  139.4 65.6 %all-gather.23.cloned.1.call-done = bf16[1,640,4096]{2,1,0:T(8,128)(2,1)} async-done(((bf16[1,640,128]{2,1,0:T(8,128)(2,1)}), bf16[1,640,4096]{2,1,0:T(8,128)(2,1)}) %all-gather.23.cloned.1.call-update) | async-done | bytes 5242896 | tf_op jit(solution)/shard_map/all_gather | solution.py:308
  205.0 5.5 fusion.12
  210.6 3.3 copy-done.4
  215.3 49.3 %all-gather.25.cloned.1.call-done = bf16[1,2048,640]{2,1,0:T(8,128)(2,1)} async-done(((bf16[1,64,640]{2,1,0:T(8,128)(2,1)}), bf16[1,2048,640]{2,1,0:T(8,128)(2,1)}) %all-gather.25.cloned.1.call-update) | async-done | bytes 2621456 | tf_op jit(solution)/shard_map/all_gather | solution.py:309
  264.6 3.6 multiply_reduce_fusion.21
  269.8 52.8 %all-gather.27.cloned.1.call-done = bf16[1,640,1536]{1,2,0:T(8,128)(2,1)} async-done(((bf16[1,640,48]{1,2,0:T(8,128)(2,1)}), bf16[1,640,1536]{1,2,0:T(8,128)(2,1)}) %all-gather.27.cloned.1.call-update) | async-done | bytes 1966096 | tf_op jit(solution)/shard_map/all_gather | solution.py:306
  330.1 4.1 collective-permute-start.12
  341.2 3.7 collective-permute-start.13
  349.9 3.2 collective-permute-start.9
  353.1 16.1 collective-permute-start.14
  370.3 5.4 collective-permute-start.10
  378.0 4.4 collective-permute-done.10
  382.5 4.4 collective-permute-start.11
  402.7 51.2 %all-gather.31.cloned.1.call-done = bf16[1,640,4096]{2,1,0:T(8,128)(2,1)} async-done(((bf16[1,640,128]{2,1,0:T(8,128)(2,1)}), bf16[1,640,4096]{2,1,0:T(8,128)(2,1)}) %all-gather.31.cloned.1.call-update) | async-done | bytes 5242896 | tf_op jit(solution)/shard_map/all_gather | solution.py:308
  453.9 5.8 fusion.8
  459.8 3.3 copy-done.5
  465.5 47.6 %all-gather.33.cloned.1.call-done = bf16[1,2048,640]{2,1,0:T(8,128)(2,1)} async-done(((bf16[1,64,640]{2,1,0:T(8,128)(2,1)}), bf16[1,2048,640]{2,1,0:T(8,128)(2,1)}) %all-gather.33.cloned.1.call-update) | async-done | bytes 2621456 | tf_op jit(solution)/shard_map/all_gather | solution.py:309
  513.1 4.4 multiply_reduce_fusion.17
  520.2 5.9 fusion.71
  526.1 8.1 multiply_reduce_fusion.5
  542.0 4.4 fusion.3
  556.1 7.2 collective-permute-done.16
  564.7 4.2 collective-permute-done.20
  570.2 4.5 collective-permute-done.17
  582.5 3.5 collective-permute-done.18
  599.7 4.2 collective-permute-done.23
  607.2 4.2 multiply_reduce_fusion.7
  614.6 8.4 fusion.70
  623.0 8.1 multiply_reduce_fusion.9
  637.4 3.3 convolution_convert_fusion
  643.1 4.6 convolution_bitcast_fusion.4
  647.7 4.4 fusion
  660.5 4.0 fusion.61
  667.7 6.3 collective-permute-done.24
  675.4 5.4 collective-permute-done.28
  683.3 3.6 collective-permute-done.25
  688.3 4.6 collective-permute-done.29
  694.3 4.5 collective-permute-done.26
  700.9 3.9 collective-permute-done.30
  709.8 6.1 collective-permute-done.31
  723.6 3.5 convolution_bitcast_fusion.5
  728.2 5.8 convolution_bitcast_fusion.2
  735.1 5.7 convolution_bitcast_fusion.3
  742.1 10.4 convolution_bitcast_fusion
  752.9 10.4 convolution_bitcast_fusion.1
  771.8 4.2 fusion.73
  783.7 42.3 %all-reduce.16 = (f32[3072]{0:T(1024)S(1)}, f32[3072]{0:T(1024)S(1)}) all-reduce(f32[3072]{0:T(1024)} %constant_dynamic-update-slice_fusion.23, f32[3072]{0:T(1024)} %constant_dynamic-update-slice_fusion.22), channel_id=21, replica_groups=mesh['dp'=4,'seq'=8] {'dp','seq'}, use_global_device_ids=true, to_apply=%region_51.52.clone | all-reduce | flops 6144 | bytes 49152
  829.4 78.6 %reduce-scatter.13.cloned.1.call-done = f32[32,640]{1,0:T(8,128)} async-done(((f32[1024,640]{1,0:T(8,128)}), f32[32,640]{1,0:T(8,128)}) %reduce-scatter.13.cloned.1.call-update) | async-done | bytes 81936 | tf_op jit(solution)/shard_map/reduce_scatter | solution.py:330
  909.7 104.8 %reduce-scatter.11.cloned.1.call-done = f32[640,48]{0,1:T(8,128)} async-done(((f32[640,1536]{0,1:T(8,128)}), f32[640,48]{0,1:T(8,128)}) %reduce-scatter.11.cloned.1.call-update) | async-done | bytes 122896 | tf_op jit(solution)/shard_map/reduce_scatter | solution.py:329
  1014.5 108.2 %reduce-scatter.9.cloned.1.call-done = f32[640,48]{0,1:T(8,128)} async-done(((f32[640,1536]{0,1:T(8,128)}), f32[640,48]{0,1:T(8,128)}) %reduce-scatter.9.cloned.1.call-update) | async-done | bytes 122896 | tf_op jit(solution)/shard_map/reduce_scatter | solution.py:329
  1124.3 146.8 %reduce-scatter.23.cloned.1.call-done = f32[64,640]{1,0:T(8,128)} async-done(((f32[2048,640]{1,0:T(8,128)}), f32[64,640]{1,0:T(8,128)}) %reduce-scatter.23.cloned.1.call-update) | async-done | bytes 163856 | tf_op jit(solution)/shard_map/reduce_scatter | solution.py:332
  1271.0 148.8 %reduce-scatter.21.cloned.1.call-done = f32[64,640]{1,0:T(8,128)} async-done(((f32[2048,640]{1,0:T(8,128)}), f32[64,640]{1,0:T(8,128)}) %reduce-scatter.21.cloned.1.call-update) | async-done | bytes 163856 | tf_op jit(solution)/shard_map/reduce_scatter | solution.py:332
  1421.5 225.4 %reduce-scatter.19.cloned.1.call-done = f32[640,128]{1,0:T(8,128)} async-done(((f32[640,4096]{1,0:T(8,128)}), f32[640,128]{1,0:T(8,128)}) %reduce-scatter.19.cloned.1.call-update) | async-done | bytes 327696 | tf_op jit(solution)/shard_map/reduce_scatter | solution.py:331
  1646.9 228.9 %reduce-scatter.17.cloned.1.call-done = f32[640,128]{1,0:T(8,128)} async-done(((f32[640,4096]{1,0:T(8,128)}), f32[640,128]{1,0:T(8,128)}) %reduce-scatter.17.cloned.1.call-update) | async-done | bytes 327696 | tf_op jit(solution)/shard_map/reduce_scatter | solution.py:331
  (589 shorter events, 210.2 us)
Async XLA Ops:
  7.2 52.2 %copy-start.43 = (bf16[4,128,640]{2,1,0:T(8,128)(2,1)S(1)}, bf16[4,128,640]{2,1,0:T(8,128)(2,1)}, u32[]{:S(2)}) copy-start(bf16[4,128,640]{2,1,0:T(8,128)(2,1)} %param.8) | copy-start | bytes 1966084
  7.2 53.0 %copy-start.154 = (s32[4,128]{1,0:T(4,128)S(1)}, s32[4,128]{1,0:T(4,128)}, u32[]{:S(2)}) copy-start(s32[4,128]{1,0:T(4,128)} %param.9) | copy-start | bytes 6148
  7.2 63.3 %all-gather.19.cloned.1.call-start = ((), (), s32[]{:S(2)}) async-start(), calls=%async_computation.16 | async-start | bytes 2027520 | tf_op jit(solution)/shard_map/all_gather | solution.py:306
  8.8 126.2 %all-gather.21.cloned.1.call-start = ((), (), s32[]{:S(2)}) async-start(), calls=%async_computation.17 | async-start | bytes 1351680 | tf_op jit(solution)/shard_map/all_gather | solution.py:307
  10.3 194.7 %all-gather.23.cloned.1.call-start = ((), (), s32[]{:S(2)}) async-start(), calls=%async_computation.18 | async-start | bytes 5406720 | tf_op jit(solution)/shard_map/all_gather | solution.py:308
  12.1 252.5 %all-gather.25.cloned.1.call-start = ((), (), s32[]{:S(2)}) async-start(), calls=%async_computation.19 | async-start | bytes 2703360 | tf_op jit(solution)/shard_map/all_gather | solution.py:309
  13.8 308.7 %all-gather.27.cloned.1.call-start = ((), (), s32[]{:S(2)}) async-start(), calls=%async_computation.20 | async-start | bytes 2027520 | tf_op jit(solution)/shard_map/all_gather | solution.py:306
  14.4 383.0 %all-gather.29.cloned.1.call-start = ((), (), s32[]{:S(2)}) async-start(), calls=%async_computation.21 | async-start | bytes 1351680 | tf_op jit(solution)/shard_map/all_gather | solution.py:307
  15.0 438.9 %all-gather.31.cloned.1.call-start = ((), (), s32[]{:S(2)}) async-start(), calls=%async_computation.22 | async-start | bytes 5406720 | tf_op jit(solution)/shard_map/all_gather | solution.py:308
  15.7 497.4 %all-gather.33.cloned.1.call-start = ((), (), s32[]{:S(2)}) async-start(), calls=%async_computation.23 | async-start | bytes 2703360 | tf_op jit(solution)/shard_map/all_gather | solution.py:309
  59.3 209.0 %copy-start.93 = (f32[640]{0:T(1024)}, f32[640]{0:T(1024)S(1)}, u32[]{:S(2)}) copy-start(f32[640]{0:T(1024)S(1)} %get-tuple-element.35) | copy-start | bytes 7684
  60.9 264.9 %copy-start.133 = (f32[1,256]{1,0:T(1,128)}, f32[1,256]{1,0:T(1,128)S(1)}, u32[]{:S(2)}) copy-start(f32[1,256]{1,0:T(1,128)S(1)} %get-tuple-element.83) | copy-start | bytes 3076
  75.2 11.3 collective-permute-start.4
  79.1 243.4 %copy-start.99 = (f32[640]{0:T(1024)}, f32[640]{0:T(1024)S(1)}, u32[]{:S(2)}) copy-start(f32[640]{0:T(1024)S(1)} %get-tuple-element.34) | copy-start | bytes 7684
  83.2 9.6 collective-permute-start
  86.5 12.1 collective-permute-start.5
  92.7 11.8 collective-permute-start.1
  98.5 11.7 collective-permute-start.6
  104.6 14.0 collective-permute-start.2
  110.2 14.1 collective-permute-start.7
  118.6 9.6 collective-permute-start.3
  137.8 72.7 %copy-start.119 = (f32[4,128]{1,0:T(4,128)}, f32[4,128]{1,0:T(4,128)S(1)}, u32[]{:S(2)}) copy-start(f32[4,128]{1,0:T(4,128)S(1)} %get-tuple-element.96) | copy-start | bytes 6148
  139.4 71.1 %copy-start.121 = (f32[4,128]{1,0:T(4,128)}, f32[4,128]{1,0:T(4,128)S(1)}, u32[]{:S(2)}) copy-start(f32[4,128]{1,0:T(4,128)S(1)} %get-tuple-element.50) | copy-start | bytes 6148
  215.3 52.9 %copy-start.51 = (bf16[4,128,2048]{2,1,0:T(8,128)(2,1)}, bf16[4,128,2048]{2,1,0:T(8,128)(2,1)S(1)}, u32[]{:S(2)}) copy-start(bf16[4,128,2048]{2,1,0:T(8,128)(2,1)S(1)} %multiply_convert_fusion.1) | copy-start | bytes 6291460
  268.3 57.3 %copy-start.142 = (f32[4,128]{1,0:T(4,128)}, f32[4,128]{1,0:T(4,128)S(1)}, u32[]{:S(2)}) copy-start(f32[4,128]{1,0:T(4,128)S(1)} %get-tuple-element.98) | copy-start | bytes 6148
  268.3 57.3 %copy-start.105 = (f32[4,128]{1,0:T(4,128)}, f32[4,128]{1,0:T(4,128)S(1)}, u32[]{:S(2)}) copy-start(f32[4,128]{1,0:T(4,128)S(1)} %fusion.154) | copy-start | bytes 6148
  269.7 55.9 %copy-start.14 = (f32[4,128,640]{2,1,0:T(8,128)}, f32[4,128,640]{2,1,0:T(8,128)S(1)}, u32[]{:S(2)}) copy-start(f32[4,128,640]{2,1,0:T(8,128)S(1)} %get-tuple-element.49) | copy-start | bytes 3932164
  269.7 55.9 %copy-start.123 = (f32[4,128]{1,0:T(4,128)}, f32[4,128]{1,0:T(4,128)S(1)}, u32[]{:S(2)}) copy-start(f32[4,128]{1,0:T(4,128)S(1)} %get-tuple-element.48) | copy-start | bytes 6148
  269.7 55.9 %copy-start.113 = (f32[4,128]{1,0:T(4,128)}, f32[4,128]{1,0:T(4,128)S(1)}, u32[]{:S(2)}) copy-start(f32[4,128]{1,0:T(4,128)S(1)} %fusion.155) | copy-start | bytes 6148
  330.1 11.1 collective-permute-start.12
  334.2 495.2 %reduce-scatter.15.cloned.1.call-start = ((), (), s32[]{:S(2)}) async-start(), calls=%async_computation.11 | async-start | bytes 2703360 | tf_op jit(solution)/shard_map/reduce_scatter | solution.py:330
  338.7 11.2 collective-permute-start.8
  341.2 11.9 collective-permute-start.13
  349.9 20.4 %collective-permute-start.9 = (bf16[4,128,256]{2,1,0:T(8,128)(2,1)}, bf16[4,128,256]{2,1,0:T(8,128)(2,1)S(1)}, u32[]{:S(2)}, u32[]{:S(2)}) collective-permute-start(bf16[4,128,256]{2,1,0:T(8,128)(2,1)} %collective-permute-done.8), channel_id=1, source_target_pairs={{0,1},{1,2},{2,3},{3,4},{4,5},{5,6},{6,7},{8,9},{9,10},{10,11},{11... | collective-permute-start | bytes 786440 | tf_op jit(solution)/shard_map/ppermute | solution.py:23
  353.1 22.6 %collective-permute-start.14 = (bf16[4,128,256]{2,1,0:T(8,128)(2,1)}, bf16[4,128,256]{2,1,0:T(8,128)(2,1)S(1)}, u32[]{:S(2)}, u32[]{:S(2)}) collective-permute-start(bf16[4,128,256]{2,1,0:T(8,128)(2,1)} %collective-permute-done.13), channel_id=1, source_target_pairs={{0,1},{1,2},{2,3},{3,4},{4,5},{5,6},{6,7},{8,9},{9,10},{10,11},{11... | collective-permute-start | bytes 786440 | tf_op jit(solution)/shard_map/ppermute | solution.py:23
  370.3 12.2 collective-permute-start.10
  375.8 11.8 collective-permute-start.15
  382.5 8.3 collective-permute-start.11
  465.5 52.0 %copy-start.98 = (f32[640]{0:T(1024)S(1)}, f32[640]{0:T(1024)}, u32[]{:S(2)}) copy-start(f32[640]{0:T(1024)} %get-tuple-element.31) | copy-start | bytes 7684
  552.2 11.0 collective-permute-start.16
  553.6 15.3 collective-permute-start.20
  563.3 11.4 collective-permute-start.17
  568.9 11.5 collective-permute-start.21
  574.8 11.2 collective-permute-start.18
  581.2 11.5 collective-permute-start.22
  586.7 9.7 collective-permute-start.19
  592.6 315.4 %reduce-scatter.13.cloned.1.call-start = ((), (), s32[]{:S(2)}) async-start(), calls=%async_computation.10 | async-start | bytes 2703360 | tf_op jit(solution)/shard_map/reduce_scatter | solution.py:330
  594.0 9.9 collective-permute-start.23
  636.7 377.8 %reduce-scatter.11.cloned.1.call-start = ((), (), s32[]{:S(2)}) async-start(), calls=%async_computation.9 | async-start | bytes 4055040 | tf_op jit(solution)/shard_map/reduce_scatter | solution.py:329
  655.1 467.5 %reduce-scatter.9.cloned.1.call-start = ((), (), s32[]{:S(2)}) async-start(), calls=%async_computation.8 | async-start | bytes 4055040 | tf_op jit(solution)/shard_map/reduce_scatter | solution.py:329
  659.0 15.1 collective-permute-start.24
  664.7 16.2 collective-permute-start.28
  674.1 12.8 collective-permute-start.25
  680.9 11.9 collective-permute-start.29
  687.0 11.8 collective-permute-start.26
  692.9 11.8 collective-permute-start.30
  699.6 17.7 collective-permute-start.27
  705.5 10.4 collective-permute-start.31
  727.1 543.9 %reduce-scatter.23.cloned.1.call-start = ((), (), s32[]{:S(2)}) async-start(), calls=%async_computation.15 | async-start | bytes 5406720 | tf_op jit(solution)/shard_map/reduce_scatter | solution.py:332
  734.0 685.8 %reduce-scatter.21.cloned.1.call-start = ((), (), s32[]{:S(2)}) async-start(), calls=%async_computation.14 | async-start | bytes 5406720 | tf_op jit(solution)/shard_map/reduce_scatter | solution.py:332
  740.8 906.1 %reduce-scatter.19.cloned.1.call-start = ((), (), s32[]{:S(2)}) async-start(), calls=%async_computation.13 | async-start | bytes 10813440 | tf_op jit(solution)/shard_map/reduce_scatter | solution.py:331
  752.6 1123.3 %reduce-scatter.17.cloned.1.call-start = ((), (), s32[]{:S(2)}) async-start(), calls=%async_computation.12 | async-start | bytes 10813440 | tf_op jit(solution)/shard_map/reduce_scatter | solution.py:331
  771.8 54.9 %copy-start.116 = (f32[4,128]{1,0:T(4,128)S(1)}, f32[4,128]{1,0:T(4,128)}, u32[]{:S(2)}) copy-start(f32[4,128]{1,0:T(4,128)} %copy-done.115) | copy-start | bytes 6148
  771.8 55.6 %copy-start.28 = (f32[4,128,640]{2,1,0:T(8,128)S(1)}, f32[4,128,640]{2,1,0:T(8,128)}, u32[]{:S(2)}) copy-start(f32[4,128,640]{2,1,0:T(8,128)} %copy-done.27) | copy-start | bytes 3932164
  (150 other events, 1097.0 us)
Sparse Core Ops, SparseCore 0:
  11.5 58.9 all-gather.18
  73.9 56.3 all-gather.20
  133.8 71.1 all-gather.22
  208.4 56.2 all-gather.24
  267.4 55.1 all-gather.26
  325.3 53.7 all-gather.28
  382.5 71.3 all-gather.30
  456.9 56.2 all-gather.32
  592.7 173.1 reduce-scatter.14
  768.1 139.9 reduce-scatter.12
  913.5 100.9 reduce-scatter.10
  1019.7 102.8 reduce-scatter.8
  1124.9 146.0 reduce-scatter.22
  1273.2 146.5 reduce-scatter.20
  1421.9 224.9 reduce-scatter.18
  1649.1 226.7 reduce-scatter.16
where the time goes:
time: 1890 us; the launch traced here: 1880 us
  waiting for transfers between devices  1400 us (74%)
  matrix products  145 us (8%)
  starting transfers between devices  98.3 us (5%)
  blocking collectives  84.6 us (4%)
  local copies, waits for them, and re-layouts  78.8 us (4%)
  other arithmetic  64 us (3%)
    reduce_scatter x2, waiting for transfers between devices, body(): lax.psum_scatter(local_grads[2], ('dp', 'seq'), scatter_dimension=1, tile...  454 us
    reduce_scatter x2, waiting for transfers between devices, body(): lax.psum_scatter(local_grads[3], ('dp', 'seq'), scatter_dimension=0, tile...  296 us
    reduce_scatter x2, waiting for transfers between devices, body(): lax.psum_scatter(local_grads[0], ('dp', 'seq'), scatter_dimension=1, tile...  213 us
    all_gather x2, waiting for transfers between devices, body(): lax.all_gather(w_ffn_in[layer_index], ('dp', 'seq'), axis=1, tiled=True)  117 us
    ppermute x32, starting transfers between devices, from_behind(): return lax.ppermute(block, axis, route)  97.3 us
    all_gather x2, waiting for transfers between devices, body(): lax.all_gather(w_ffn_out[layer_index], ('dp', 'seq'), axis=0, tiled=True)  96.9 us
    unnamed x2, blocking collectives  84.6 us
    reduce_scatter x2, waiting for transfers between devices, body(): lax.psum_scatter(local_grads[1], ('dp', 'seq'), scatter_dimension=0, tile...  78.6 us
  transfers between devices with their start and end apart: 48, of which 36 were waited for; matrix products, arithmetic and copies ran while one was open for 12% of the time, Pallas kernels for 0%

commit v1 on v0

v1 whole, which is shorter than its diff:
```python
import jax
import jax.numpy as jnp
from jax import lax
from jax.experimental import pallas as pl
from jax.experimental.pallas import tpu as pltpu
from jax.sharding import PartitionSpec as P

D = 640
HEADS = 4
HEAD_DIM = 256
WINDOW = 512
QUERY_BLOCK = 256

EPSILON = 1e-06
ROPE_BASE = 10000.0
SCORE_SCALE = 0.0625
MASKED_SCORE = -1e30
BF16 = jnp.bfloat16
F32 = jnp.float32
ALL = ("dp", "seq")


def dot(a, b, a_dim, b_dim):
    return lax.dot_general(a, b, (((a_dim,), (b_dim,)), ((), ())), preferred_element_type=F32)


def rms_norm(values, gain):
    return values * lax.rsqrt(jnp.mean(values * values, axis=-1, keepdims=True) + EPSILON) * gain


def angle_tables(places):
    half_dim = HEAD_DIM // 2
    inverse = ROPE_BASE ** (-(2.0 * jnp.arange(half_dim, dtype=F32)) / HEAD_DIM)
    phases = places.astype(F32)[..., None] * inverse
    return (jnp.cos(phases), jnp.sin(phases))


def rotate(values, cosine_tab, sine_tab):
    half_dim = values.shape[-1] // 2
    first_half = values[..., :half_dim]
    second_half = values[..., half_dim:]
    return jnp.concatenate(
        [
            first_half * cosine_tab - second_half * sine_tab,
            second_half * cosine_tab + first_half * sine_tab,
        ],
        axis=-1,
    )


def prepare(raw_part, gain_part, cosine_tab, sine_tab):
    return rotate(rms_norm(raw_part, gain_part), cosine_tab, sine_tab)


def gated_gelu(gate_and_up_rows):
    half_width = gate_and_up_rows.shape[-1] // 2
    return (
        jax.nn.gelu(gate_and_up_rows[..., :half_width], approximate=True)
        * gate_and_up_rows[..., half_width:]
    )


def split_gains(gain_full):
    return (
        gain_full[0:D],
        gain_full[D : 2 * D],
        gain_full[2 * D : 3 * D],
        gain_full[3 * D : 4 * D],
        gain_full[4 * D : 4 * D + HEAD_DIM],
        gain_full[4 * D + HEAD_DIM : 4 * D + 2 * HEAD_DIM],
    )


def to_long(block):
    count, size = block.shape[0], lax.axis_size("seq")
    per = size // count
    me = lax.axis_index("seq")
    received = []
    for k in range(count):
        route = [(i, ((i + k) % count) * per + i // count) for i in range(size)]
        piece = lax.dynamic_index_in_dim(block, (me + k) % count, 0, keepdims=False)
        received.append(lax.ppermute(piece, "seq", route))
    own = me // per
    twice = jnp.stack((received[::-1] * 2)[: 2 * count - 1])
    long = lax.dynamic_slice_in_dim(twice, count - 1 - own, count, 0)
    return long.reshape((count * block.shape[1],) + block.shape[2:])


def to_short(long, count):
    size = lax.axis_size("seq")
    per = size // count
    me = lax.axis_index("seq")
    own = me // per
    parts = long.reshape((count, long.shape[0] // count) + long.shape[1:])
    received = []
    for k in range(count):
        route = [(((i + k) % count) * per + i // count, i) for i in range(size)]
        piece = lax.dynamic_index_in_dim(parts, (own - k) % count, 0, keepdims=False)
        received.append(lax.ppermute(piece, "seq", route))
    twice = jnp.stack((received * 2)[: 2 * count - 1])
    return lax.dynamic_slice_in_dim(twice, (count - me % count) % count, count, 0)


def neighbour(block, back):
    size = lax.axis_size("seq")
    per = size // SEQ_PER_DP
    pairs = [(i, i + 1) for i in range(size) if (i + 1) % per]
    if back:
        pairs = [(j, i) for i, j in pairs]
    return lax.ppermute(block, "seq", pairs)


SEQ_PER_DP = 4


def halving(array):
    n_dp, n_seq = lax.axis_size("dp"), lax.axis_size("seq")
    rest = array.shape[1:]
    steps = []
    bit = 1
    while bit < n_dp:
        steps.append(("dp", bit))
        bit *= 2
    bit = 1
    while bit < n_seq:
        steps.append(("seq", bit))
        bit *= 2
    dtype = array.dtype
    left = {"dp": n_dp, "seq": n_seq}
    for axis, bit in steps:
        size = lax.axis_size(axis)
        mine = (lax.axis_index(axis) // bit) % 2
        inner = left["seq"] if axis == "dp" else 1
        view = array.reshape((-1, 2, inner) + rest)
        send = lax.dynamic_index_in_dim(view, 1 - mine, 1, keepdims=False)
        keep = lax.dynamic_index_in_dim(view, mine, 1, keepdims=False)
        got = lax.ppermute(send, axis, [(i, i ^ bit) for i in range(size)])
        array = (keep.astype(F32) + got.astype(F32)).astype(dtype)
        left[axis] //= 2
    return array.reshape(rest)


def allowed_pairs(start, key_count, reach, lanes):
    key_at = lax.broadcasted_iota(jnp.int32, (key_count, lanes), 0)
    query_at = lax.broadcasted_iota(jnp.int32, (key_count, lanes), 1) % QUERY_BLOCK
    distance = query_at + WINDOW - key_at
    return (distance >= 0) & (distance <= reach)


def stacked_heads(ref, start):
    return jnp.concatenate(
        [
            ref[start : start + QUERY_BLOCK, h * HEAD_DIM : (h + 1) * HEAD_DIM]
            for h in range(HEADS)
        ],
        axis=0,
    )


def window_rows(before_ref, own_ref, start, count):
    return jnp.concatenate([before_ref[start:, :], own_ref[: count - (WINDOW - start), :]], axis=0)


def attention_forward_kernel(q_ref, kb_ref, vb_ref, k_ref, v_ref, reach_ref, ctx_ref, lse_ref):
    key_count = QUERY_BLOCK + WINDOW
    for block in range(q_ref.shape[0] // QUERY_BLOCK):
        start = block * QUERY_BLOCK
        queries = stacked_heads(q_ref, start)
        keys = window_rows(kb_ref, k_ref, start, key_count)
        values = window_rows(vb_ref, v_ref, start, key_count)
        allowed = allowed_pairs(start, key_count, reach_ref[block : block + 1, :], HEADS * QUERY_BLOCK)
        scores = jnp.where(allowed, dot(keys, queries, 1, 1), MASKED_SCORE)
        row_max = jnp.max(scores, axis=0, keepdims=True)
        weights = jnp.exp(scores - row_max)
        row_sum = jnp.sum(weights, axis=0, keepdims=True)
        probs = (weights * (1.0 / row_sum)).astype(BF16)
        lse_ref[block : block + 1, :] = row_max + jnp.log(row_sum)
        context = dot(probs, values, 0, 0).astype(BF16)
        for h in range(HEADS):
            ctx_ref[start : start + QUERY_BLOCK, h * HEAD_DIM : (h + 1) * HEAD_DIM] = context[
                h * QUERY_BLOCK : (h + 1) * QUERY_BLOCK
            ]


def attention_backward_kernel(
    q_ref, kb_ref, vb_ref, k_ref, v_ref, reach_ref, lse_ref, g_ref, dq_ref, before_ref, own_ref, acc
):
    key_count = QUERY_BLOCK + WINDOW
    acc[...] = jnp.zeros_like(acc)
    for block in range(q_ref.shape[0] // QUERY_BLOCK):
        start = block * QUERY_BLOCK
        queries = stacked_heads(q_ref, start)
        grads = stacked_heads(g_ref, start)
        keys = window_rows(kb_ref, k_ref, start, key_count)
        values = window_rows(vb_ref, v_ref, start, key_count)
        allowed = allowed_pairs(start, key_count, reach_ref[block : block + 1, :], HEADS * QUERY_BLOCK)
        scores = jnp.where(allowed, dot(keys, queries, 1, 1), MASKED_SCORE)
        probs = jnp.exp(scores - lse_ref[block : block + 1, :])
        grad_probs = dot(values, grads, 1, 1)
        inner = jnp.sum(probs * grad_probs, axis=0, keepdims=True)
        grad_scores = (probs * (grad_probs - inner)).astype(BF16)
        acc[start : start + key_count, HEAD_DIM:] += dot(probs.astype(BF16), grads, 1, 0)
        acc[start : start + key_count, :HEAD_DIM] += dot(grad_scores, queries, 1, 0)
        grad_queries = dot(grad_scores, keys, 0, 0) * SCORE_SCALE
        for h in range(HEADS):
            dq_ref[start : start + QUERY_BLOCK, h * HEAD_DIM : (h + 1) * HEAD_DIM] = grad_queries[
                h * QUERY_BLOCK : (h + 1) * QUERY_BLOCK
            ]
    before_ref[...] = acc[:WINDOW, :].astype(BF16)
    own_ref[...] = acc[WINDOW:, :]


def vmem(count):
    return [pl.BlockSpec(memory_space=pltpu.VMEM)] * count


def attention_forward(queries, before, own, reach):
    tokens = queries.shape[0]
    kb, vb = before[:, :HEAD_DIM], before[:, HEAD_DIM:]
    k, v = own[:, :HEAD_DIM], own[:, HEAD_DIM:]
    return pl.pallas_call(
        attention_forward_kernel,
        out_shape=(
            jax.ShapeDtypeStruct((tokens, HEADS * HEAD_DIM), BF16),
            jax.ShapeDtypeStruct(reach.shape, F32),
        ),
        in_specs=vmem(6),
        out_specs=tuple(vmem(2)),
        compiler_params=pltpu.CompilerParams(vmem_limit_bytes=40 * 2**20),
        cost_estimate=pl.CostEstimate(
            flops=4 * tokens * HEADS * HEAD_DIM * (QUERY_BLOCK + WINDOW),
            bytes_accessed=6 * 2**20,
            transcendentals=tokens * HEADS * (QUERY_BLOCK + WINDOW),
        ),
        name="attention_forward",
    )(queries, kb, vb, k, v, reach)


def attention_backward(queries, before, own, reach, lse, grads):
    tokens = queries.shape[0]
    kb, vb = before[:, :HEAD_DIM], before[:, HEAD_DIM:]
    k, v = own[:, :HEAD_DIM], own[:, HEAD_DIM:]
    return pl.pallas_call(
        attention_backward_kernel,
        out_shape=(
            jax.ShapeDtypeStruct((tokens, HEADS * HEAD_DIM), F32),
            jax.ShapeDtypeStruct((WINDOW, 2 * HEAD_DIM), BF16),
            jax.ShapeDtypeStruct((tokens, 2 * HEAD_DIM), F32),
        ),
        in_specs=vmem(8),
        out_specs=tuple(vmem(3)),
        scratch_shapes=[pltpu.VMEM((WINDOW + tokens, 2 * HEAD_DIM), F32)],
        compiler_params=pltpu.CompilerParams(vmem_limit_bytes=40 * 2**20),
        cost_estimate=pl.CostEstimate(
            flops=10 * tokens * HEADS * HEAD_DIM * (QUERY_BLOCK + WINDOW),
            bytes_accessed=10 * 2**20,
            transcendentals=tokens * HEADS * (QUERY_BLOCK + WINDOW),
        ),
        name="attention_backward",
    )(queries, kb, vb, k, v, reach, lse, grads)


def forward_layer(stream, weights, tables, reach):
    attn_in, attn_out, ffn_in, ffn_out, gain_row = weights
    pre_attn, post_attn, pre_ffn, post_ffn, query_gain, key_gain = split_gains(gain_row)
    cosine_tab, sine_tab = tables
    tokens = stream.shape[0]
    query_cols = HEADS * HEAD_DIM
    normed = rms_norm(stream, pre_attn).astype(BF16)
    key_value_raw = dot(normed, attn_in[query_cols:], 1, 1)
    key_raw = key_value_raw[:, :HEAD_DIM]
    keys = prepare(key_raw, key_gain, cosine_tab, sine_tab).astype(BF16)
    own = jnp.concatenate([keys, key_value_raw[:, HEAD_DIM:].astype(BF16)], axis=1)
    before = neighbour(own, False)
    query_raw = dot(normed, attn_in[:query_cols], 1, 1).reshape(tokens, HEADS, HEAD_DIM)
    queries = prepare(query_raw, query_gain, cosine_tab[:, None, :], sine_tab[:, None, :])
    queries = (queries.astype(BF16) * SCORE_SCALE).reshape(tokens, query_cols)
    context, lse = attention_forward(queries, before, own, reach)
    branch = dot(context, attn_out, 1, 0)
    middle = stream + rms_norm(branch, post_attn)
    ffn_normed = rms_norm(middle, pre_ffn).astype(BF16)
    gate_up = dot(ffn_normed, ffn_in, 1, 1)
    inner = gated_gelu(gate_up).astype(BF16)
    ffn_branch = dot(inner, ffn_out, 1, 0)
    result = middle + rms_norm(ffn_branch, post_ffn)
    record = (
        stream, normed, query_raw, key_raw, queries, before, own, lse, context,
        branch, middle, ffn_normed, gate_up, inner, ffn_branch,
    )
    return record, result


def pieces(array):
    devices = lax.axis_size("dp") * lax.axis_size("seq")
    return array.astype(BF16).reshape(devices, array.shape[0] // devices, array.shape[1])


def backward_layer(grad_out, weights, record, tables, reach):
    attn_in, attn_out, ffn_in, ffn_out, gain_row = weights
    pre_attn, post_attn, pre_ffn, post_ffn, query_gain, key_gain = split_gains(gain_row)
    cosine_tab, sine_tab = tables
    (
        stream, normed, query_raw, key_raw, queries, before, own, lse, context,
        branch, middle, ffn_normed, gate_up, inner, ffn_branch,
    ) = record
    tokens = stream.shape[0]
    query_cols = HEADS * HEAD_DIM
    _, pull_post_ffn = jax.vjp(rms_norm, ffn_branch, post_ffn)
    grad_ffn_branch, grad_post_ffn = pull_post_ffn(grad_out)
    grad_ffn_branch = grad_ffn_branch.astype(BF16)
    grad_ffn_out = halving(pieces(dot(inner, grad_ffn_branch, 0, 0)))
    grad_inner = dot(grad_ffn_branch, ffn_out, 1, 1)
    _, pull_act = jax.vjp(gated_gelu, gate_up)
    grad_gate_up = pull_act(grad_inner)[0].astype(BF16)
    grad_ffn_in = halving(pieces(dot(grad_gate_up, ffn_normed, 0, 0)))
    grad_ffn_normed = dot(grad_gate_up, ffn_in, 1, 0)
    _, pull_pre_ffn = jax.vjp(rms_norm, middle, pre_ffn)
    grad_middle_part, grad_pre_ffn = pull_pre_ffn(grad_ffn_normed)
    grad_middle = grad_out + grad_middle_part
    _, pull_post_attn = jax.vjp(rms_norm, branch, post_attn)
    grad_branch, grad_post_attn = pull_post_attn(grad_middle)
    grad_branch = grad_branch.astype(BF16)
    grad_attn_out = halving(pieces(dot(context, grad_branch, 0, 0)))
    grad_context = dot(grad_branch, attn_out, 1, 1).astype(BF16)
    grad_queries, grad_before, grad_own = attention_backward(
        queries, before, own, reach, lse, grad_context
    )
    grad_own = grad_own + neighbour(grad_before, True).astype(F32)
    _, pull_query = jax.vjp(
        lambda raw, gain: prepare(raw, gain, cosine_tab[:, None, :], sine_tab[:, None, :]),
        query_raw,
        query_gain,
    )
    grad_query_raw, grad_query_gain = pull_query(grad_queries.reshape(tokens, HEADS, HEAD_DIM))
    _, pull_key = jax.vjp(
        lambda raw, gain: prepare(raw, gain, cosine_tab, sine_tab), key_raw, key_gain
    )
    grad_key_raw, grad_key_gain = pull_key(grad_own[:, :HEAD_DIM])
    grad_projected = jnp.concatenate(
        [grad_query_raw.reshape(tokens, query_cols), grad_key_raw, grad_own[:, HEAD_DIM:]], axis=-1
    ).astype(BF16)
    grad_attn_in = halving(pieces(dot(grad_projected, normed, 0, 0)))
    grad_normed = dot(grad_projected, attn_in, 1, 0)
    _, pull_pre_attn = jax.vjp(rms_norm, stream, pre_attn)
    grad_stream_part, grad_pre_attn = pull_pre_attn(grad_normed)
    grad_in = grad_middle + grad_stream_part
    grad_gain_row = jnp.concatenate(
        [grad_pre_attn, grad_post_attn, grad_pre_ffn, grad_post_ffn, grad_query_gain, grad_key_gain]
    )
    return grad_in, (grad_attn_in, grad_attn_out, grad_ffn_in, grad_ffn_out, grad_gain_row)


def gather_weights(w_attn_in, w_attn_out, w_ffn_in, w_ffn_out, gains):
    parts = [w_attn_in.T, w_attn_out, w_ffn_in.T, w_ffn_out]
    sizes = [part.shape[0] for part in parts]
    gain_rows = jnp.pad(gains[None, :], ((0, 15), (0, D - gains.shape[0])))
    packed = jnp.concatenate(parts + [gain_rows], axis=0)
    whole = lax.all_gather(packed, ALL, axis=0, tiled=False)
    out, at = [], 0
    for size in sizes:
        out.append(whole[:, at : at + size].reshape(-1, D))
        at += size
    gain_full = whole[:, at, : gains.shape[0]].reshape(-1).astype(F32)
    return tuple(out) + (gain_full,)


def body(hidden_in, positions, out_grad, w_attn_in, w_attn_out, w_ffn_in, w_ffn_out, gains):
    count = hidden_in.shape[0]
    layer_count = w_attn_in.shape[0]
    weights = [
        gather_weights(w_attn_in[l], w_attn_out[l], w_ffn_in[l], w_ffn_out[l], gains[l])
        for l in range(layer_count)
    ]
    places = to_long(positions)
    stream = to_long(hidden_in).astype(F32)
    tables = angle_tables(places)
    tokens = places.shape[0]
    blocks = tokens // QUERY_BLOCK
    reach = jnp.minimum(places, WINDOW - 1).reshape(blocks, QUERY_BLOCK)
    reach = jnp.tile(reach, (1, HEADS))
    records = []
    for layer_index in range(layer_count):
        record, stream = forward_layer(stream, weights[layer_index], tables, reach)
        records.append(record)
    hidden_out = to_short(stream.astype(BF16), count)
    grad_stream = to_long(out_grad).astype(F32)
    layer_grads = [None] * layer_count
    for layer_index in reversed(range(layer_count)):
        grad_stream, layer_grads[layer_index] = backward_layer(
            grad_stream, weights[layer_index], records[layer_index], tables, reach
        )
    input_grad = to_short(grad_stream.astype(BF16), count).astype(F32)
    devices = lax.axis_size("dp") * lax.axis_size("seq")
    gain_grads = jnp.stack([entry[4].reshape(devices, -1) for entry in layer_grads], axis=1)
    gain_grads = halving(gain_grads)
    members = [jnp.stack([entry[m].astype(F32) for entry in layer_grads]) for m in range(4)]
    return (
        hidden_out,
        input_grad,
        members[0].transpose(0, 2, 1),
        members[1],
        members[2].transpose(0, 2, 1),
        members[3],
        gain_grads,
    )


def solution(mesh):
    return jax.shard_map(
        body,
        mesh=mesh,
        in_specs=(
            P("dp", "seq", None),
            P("dp", "seq"),
            P("dp", "seq", None),
            P(None, None, ("dp", "seq")),
            P(None, ("dp", "seq"), None),
            P(None, None, ("dp", "seq")),
            P(None, ("dp", "seq"), None),
            P(None, ("dp", "seq")),
        ),
        out_specs=(
            P("dp", "seq", None),
            P("dp", "seq", None),
            P(None, None, ("dp", "seq")),
            P(None, ("dp", "seq"), None),
            P(None, None, ("dp", "seq")),
            P(None, ("dp", "seq"), None),
            P(None, ("dp", "seq")),
        ),
        check_vma=False,
    )
```

time: 1890 us -> 723 us (0.38)
  waiting for transfers between devices: 1400 us -> 325 us
  blocking collectives: 84.6 us -> 0 us
  matrix products: 145 us -> 82.3 us
  starting transfers between devices: 98.3 us -> 121 us
    reduce_scatter x8 -> x0, waiting for transfers between devices: 1040 us -> none  [the longest x2 454 us: body(): lax.psum_scatter(local_grads[2], ('dp', 'seq'), scatter_dimension=1, tile...]
    all_gather x8 -> x2, waiting for transfers between devices: 276 us -> 133 us  [gather_weights(): whole = lax.all_gather(packed, ALL, axis=0, tiled=False)]
    ppermute x32 -> x69, waiting for transfers between devices: 77.2 us -> 192 us  [the longest x45 148 us: halving(): got = lax.ppermute(send, axis, [(i, i ^ bit) for i in range(size)])]
    unnamed x2 -> x0, blocking collectives: 84.6 us -> none
    dot_general x36 -> x26, matrix products: 145 us -> 82.3 us  [dot(): lax.dot_general(a, b, (((a_dim,), (b_dim,)), ((), ())), preferred_element...]
    ppermute x32 -> x69, starting transfers between devices: 97.3 us -> 121 us  [the longest x12 43.3 us: to_long(): received.append(lax.ppermute(piece, 'seq', route))]
    slice x16 -> x22, local copies, waits for them, and re-layouts: 10.6 us -> 32.8 us  [the longest x8 24.7 us: gather_weights(): out.append(whole[:, at:at + size].reshape(-1, D))]
    unnamed x361 -> x392, local copies, waits for them, and re-layouts: 49.8 us -> 34.4 us
  transfers between devices with their start and end apart: 48 -> 71, of which waited for: 36 -> 38; matrix products, arithmetic and copies ran while one was open for 12% -> 17% of each run, Pallas kernels for 0% -> 2%
where the time goes in v1:
time: 723 us; the launch traced here: 714 us
  waiting for transfers between devices  325 us (45%)
  starting transfers between devices  121 us (17%)
  local copies, waits for them, and re-layouts  93.3 us (13%)
  matrix products  82.3 us (11%)
  other arithmetic  56.3 us (8%)
  Pallas kernels  18.7 us (3%)
  between operations  17.8 us (2%)
    ppermute x45, waiting for transfers between devices, halving(): got = lax.ppermute(send, axis, [(i, i ^ bit) for i in range(size)])  148 us
    all_gather x2, waiting for transfers between devices, gather_weights(): whole = lax.all_gather(packed, ALL, axis=0, tiled=False)  133 us
    dot_general x26, matrix products, dot(): lax.dot_general(a, b, (((a_dim,), (b_dim,)), ((), ())), preferred_element...  82.3 us
    ppermute x12, starting transfers between devices, to_long(): received.append(lax.ppermute(piece, 'seq', route))  43.3 us
    unnamed x392, local copies, waits for them, and re-layouts  34.4 us
    ppermute x45, starting transfers between devices, halving(): got = lax.ppermute(send, axis, [(i, i ^ bit) for i in range(size)])  34.3 us
    ppermute x8, starting transfers between devices, to_short(): received.append(lax.ppermute(piece, 'seq', route))  30.3 us
    slice x8, local copies, waits for them, and re-layouts, gather_weights(): out.append(whole[:, at:at + size].reshape(-1, D))  24.7 us
  transfers between devices with their start and end apart: 71, of which 38 were waited for; matrix products, arithmetic and copies ran while one was open for 17% of the time, Pallas kernels for 2%

profile of v1, /device:TPU:0, one launch (start us, length us, event | category | flops | bytes accessed | tf_op | source)
XLA Modules:
  0.0 714.4 jit_solution(8937304779708294966)
XLA Ops:
  11.9 6.6 collective-permute-start.5
  18.6 4.3 collective-permute-start.4
  27.1 6.4 collective-permute-start.1
  33.5 2.8 collective-permute-start
  39.9 2.8 collective-permute-done
  42.8 8.2 %collective-permute-start.15 = (bf16[128,640]{1,0:T(8,128)(2,1)}, bf16[128,640]{1,0:T(8,128)(2,1)S(1)}, u32[]{:S(2)}, u32[]{:S(2)}) collective-permute-start(bf16[128,640]{1,0:T(8,128)(2,1)} %get-tuple-element.111), channel_id=1, source_target_pairs={{0,4},{1,6},{2,0},{3,2},{4,5},{5,7},{6,1},{7,3},{8,12},{9,14},{10,... | collective-permute-start | bytes 491528 | tf_op jit(solution)/shard_map/ppermute | solution.py:82
  51.0 5.6 collective-permute-start.14
  59.9 6.4 collective-permute-done.14
  66.4 14.2 %collective-permute-done.16 = bf16[128,640]{1,0:T(8,128)(2,1)S(1)} collective-permute-done((bf16[128,640]{1,0:T(8,128)(2,1)}, bf16[128,640]{1,0:T(8,128)(2,1)S(1)}, u32[]{:S(2)}, u32[]{:S(2)}) %collective-permute-start.16) | collective-permute-done | bytes 163872 | tf_op jit(solution)/shard_map/ppermute | solution.py:82
  80.9 43.0 %all-gather.5.cloned.1.call-done = bf16[9216,640]{1,0:T(8,128)(2,1)} async-done(((bf16[288,640]{1,0:T(8,128)(2,1)}), bf16[9216,640]{1,0:T(8,128)(2,1)}) %all-gather.5.cloned.1.call-update) | async-done | bytes 11796496 | tf_op jit(solution)/shard_map/all_gather | solution.py:358
  128.5 89.6 %all-gather.7.cloned.1.call-done = bf16[9216,640]{1,0:T(8,128)(2,1)} async-done(((bf16[288,640]{1,0:T(8,128)(2,1)}), bf16[9216,640]{1,0:T(8,128)(2,1)}) %all-gather.7.cloned.1.call-update) | async-done | bytes 11796496 | tf_op jit(solution)/shard_map/all_gather | solution.py:358
  226.3 3.8 slice.287
  231.9 3.1 slice.280
  235.0 3.5 slice.306
  238.5 5.6 slice.303
  249.6 4.2 collective-permute-start.8
  266.0 3.9 attention_forward.2
  272.3 3.5 fusion.141
  289.5 5.2 collective-permute-start.9
  299.8 5.1 collective-permute-done.9
  306.1 4.0 attention_forward.3
  312.1 3.5 fusion.142
  320.4 5.9 fusion.23
  328.4 6.0 multiply_reduce_fusion.6
  334.4 8.1 %convolution_convert_fusion = bf16[4096,640]{1,0:T(8,128)(2,1)} fusion(f32[512,2048]{1,0:T(8,128)S(1)} %copy-done.159, f32[512,2048]{1,0:T(8,128)} %copy-done.158, f32[512,640]{1,0:T(8,128)S(1)} %get-tuple-element.83, f32[640]{0:T(1024)S(1)} %copy-done.130, f32[512]{0:T(512)S(1)} %fusion.123), kind=kOutput, calls=%fused_computation.2 | convolution fusion | flops 2692153344 | bytes 14946816 | tf_op jit(solution)/shard_map/dot_general | solution.py:24
  348.3 3.3 convolution_convert_fusion.2
  352.4 4.4 collective-permute-start.13
  356.9 4.0 collective-permute-start.11
  360.9 3.1 collective-permute-start.10
  364.0 5.3 attention_backward.2
  397.9 3.7 multiply_reduce_fusion.8
  407.3 5.9 fusion.22
  413.3 3.4 convolution_convert_fusion.3
  418.2 4.1 multiply_reduce_fusion.10
  428.2 5.5 attention_backward.3
  445.9 8.2 %convolution_convert_fusion.1 = bf16[4096,640]{1,0:T(8,128)(2,1)} fusion(f32[512,2048]{1,0:T(8,128)} %get-tuple-element.89, f32[512,2048]{1,0:T(8,128)S(1)} %copy-done.156, f32[512,640]{1,0:T(8,128)S(1)} %copy-done.37, f32[640]{0:T(1024)S(1)} %copy-done.136, f32[512]{0:T(512)S(1)} %copy-done.144), kind=kOutput, calls=%fused_computation.3 | convolution fusion | flops 2692153344 | bytes 14946816 | tf_op jit(solution)/shard_map/dot_general | solution.py:24
  458.9 3.7 dynamic-slice_bitcast_fusion.1
  462.7 4.3 collective-permute-done.40
  471.7 4.6 fusion.43
  480.6 3.1 collective-permute-done.65
  483.7 4.4 collective-permute-start.66
  500.4 3.3 collective-permute-done.41
  503.7 4.4 collective-permute-start.23
  510.2 12.1 %collective-permute-start.21 = (bf16[128,640]{1,0:T(8,128)(2,1)S(1)}, bf16[128,640]{1,0:T(8,128)(2,1)S(1)}, u32[]{:S(2)}, u32[]{:S(2)}) collective-permute-start(bf16[128,640]{1,0:T(8,128)(2,1)S(1)} %get-tuple-element.108), channel_id=1, source_target_pairs={{2,0},{4,1},{6,2},{0,3},{3,4},{5,5},{7,6},{1,7},{10,8},{12,9},{14,... | collective-permute-start | bytes 491528 | tf_op jit(solution)/shard_map/ppermute | solution.py:99
  522.3 7.5 %collective-permute-done.21 = bf16[128,640]{1,0:T(8,128)(2,1)S(1)} collective-permute-done((bf16[128,640]{1,0:T(8,128)(2,1)S(1)}, bf16[128,640]{1,0:T(8,128)(2,1)S(1)}, u32[]{:S(2)}, u32[]{:S(2)}) %collective-permute-start.21) | collective-permute-done | bytes 163872 | tf_op jit(solution)/shard_map/ppermute | solution.py:99
  531.6 4.9 collective-permute-done.22
  537.7 3.6 collective-permute-done.42
  543.0 3.3 collective-permute-done.43
  549.0 4.3 collective-permute-done.36
  555.1 3.1 collective-permute-done.37
  559.0 4.4 collective-permute-done.38
  566.7 14.4 %collective-permute-done.60 = bf16[1,8,64,640]{3,2,1,0:T(8,128)(2,1)S(1)} collective-permute-done((bf16[1,8,64,640]{3,2,1,0:T(8,128)(2,1)S(1)}, bf16[1,8,64,640]{3,2,1,0:T(8,128)(2,1)S(1)}, u32[]{:S(2)}, u32[]{:S(2)}) %collective-permute-start.60) | collective-permute-done | bytes 655392 | tf_op jit(solution)/shard_map/ppermute | solution.py:137
  582.0 9.6 %collective-permute-done.30 = bf16[1,8,48,640]{3,2,1,0:T(8,128)(2,1)S(1)} collective-permute-done((bf16[1,8,48,640]{3,2,1,0:T(8,128)(2,1)S(1)}, bf16[1,8,48,640]{3,2,1,0:T(8,128)(2,1)S(1)}, u32[]{:S(2)}, u32[]{:S(2)}) %collective-permute-start.30) | collective-permute-done | bytes 491552 | tf_op jit(solution)/shard_map/ppermute | solution.py:137
  594.3 7.7 %collective-permute-done.31 = bf16[4,1,48,640]{3,2,0,1:T(8,128)(2,1)S(1)} collective-permute-done((bf16[4,1,48,640]{3,2,0,1:T(8,128)(2,1)S(1)}, bf16[4,1,48,640]{3,2,0,1:T(8,128)(2,1)S(1)}, u32[]{:S(2)}, u32[]{:S(2)}) %collective-permute-start.31) | collective-permute-done | bytes 245792 | tf_op jit(solution)/shard_map/ppermute | solution.py:137
  603.3 4.6 collective-permute-done.32
  608.1 5.3 collective-permute-done.33
  613.4 5.3 collective-permute-done.62
  621.5 3.1 collective-permute-done.63
  631.0 2.9 collective-permute-done.27
  645.9 13.4 %collective-permute-done.50 = bf16[1,8,128,640]{3,2,1,0:T(8,128)(2,1)S(1)} collective-permute-done((bf16[1,8,128,640]{3,2,1,0:T(8,128)(2,1)S(1)}, bf16[1,8,128,640]{3,2,1,0:T(8,128)(2,1)S(1)}, u32[]{:S(2)}, u32[]{:S(2)}) %collective-permute-start.50) | collective-permute-done | bytes 1310752 | tf_op jit(solution)/shard_map/ppermute | solution.py:137
  660.0 17.0 %collective-permute-done.45 = bf16[1,8,128,640]{3,2,1,0:T(8,128)(2,1)S(1)} collective-permute-done((bf16[1,8,128,640]{3,2,1,0:T(8,128)(2,1)S(1)}, bf16[1,8,128,640]{3,2,1,0:T(8,128)(2,1)S(1)}, u32[]{:S(2)}, u32[]{:S(2)}) %collective-permute-start.45) | collective-permute-done | bytes 1310752 | tf_op jit(solution)/shard_map/ppermute | solution.py:137
  678.9 9.2 %collective-permute-done.46 = bf16[4,1,128,640]{3,2,0,1:T(8,128)(2,1)S(1)} collective-permute-done((bf16[4,1,128,640]{3,2,0,1:T(8,128)(2,1)S(1)}, bf16[4,1,128,640]{3,2,0,1:T(8,128)(2,1)S(1)}, u32[]{:S(2)}, u32[]{:S(2)}) %collective-permute-start.46) | collective-permute-done | bytes 655392 | tf_op jit(solution)/shard_map/ppermute | solution.py:137
  690.7 8.1 %collective-permute-done.47 = bf16[2,1,128,640]{3,2,0,1:T(8,128)(2,1)S(1)} collective-permute-done((bf16[2,1,128,640]{3,2,0,1:T(8,128)(2,1)S(1)}, bf16[2,1,128,640]{3,2,0,1:T(8,128)(2,1)S(1)}, u32[]{:S(2)}, u32[]{:S(2)}) %collective-permute-start.47) | collective-permute-done | bytes 327712 | tf_op jit(solution)/shard_map/ppermute | solution.py:137
  699.0 6.9 collective-permute-done.48
  (738 shorter events, 211.7 us)
Async XLA Ops:
  7.2 116.7 %all-gather.5.cloned.1.call-start = ((), (), s32[]{:S(2)}) async-start(), calls=%async_computation | async-start | bytes 12165120 | tf_op jit(solution)/shard_map/all_gather | solution.py:358
  10.3 207.8 %all-gather.7.cloned.1.call-start = ((), (), s32[]{:S(2)}) async-start(), calls=%async_computation.1 | async-start | bytes 12165120 | tf_op jit(solution)/shard_map/all_gather | solution.py:358
  11.3 15.8 %collective-permute-start.7 = (s32[128]{0:T(128)S(1)}, s32[128]{0:T(128)S(1)}, u32[]{:S(2)}, u32[]{:S(2)}) collective-permute-start(s32[128]{0:T(128)S(1)} %get-tuple-element.158), channel_id=1, source_target_pairs={{0,0},{1,2},{2,4},{3,6},{4,1},{5,3},{6,5},{7,7},{8,8},{9,10},{10,1... | collective-permute-start | bytes 1544 | tf_op jit(solution)/shard_map/ppermute | solution.py:82
  11.9 21.6 %collective-permute-start.5 = (s32[128]{0:T(128)S(1)}, s32[128]{0:T(128)S(1)}, u32[]{:S(2)}, u32[]{:S(2)}) collective-permute-start(s32[128]{0:T(128)S(1)} %get-tuple-element.159), channel_id=1, source_target_pairs={{0,4},{1,6},{2,0},{3,2},{4,5},{5,7},{6,1},{7,3},{8,12},{9,14},{10,... | collective-permute-start | bytes 1544 | tf_op jit(solution)/shard_map/ppermute | solution.py:82
  18.6 17.8 %collective-permute-start.4 = (s32[128]{0:T(128)S(1)}, s32[128]{0:T(128)S(1)}, u32[]{:S(2)}, u32[]{:S(2)}) collective-permute-start(s32[128]{0:T(128)S(1)} %get-tuple-element.160), channel_id=1, source_target_pairs={{0,6},{1,0},{2,2},{3,4},{4,7},{5,1},{6,3},{7,5},{8,14},{9,8},{10,1... | collective-permute-start | bytes 1544 | tf_op jit(solution)/shard_map/ppermute | solution.py:82
  22.9 15.4 %collective-permute-start.6 = (s32[128]{0:T(128)S(1)}, s32[128]{0:T(128)S(1)}, u32[]{:S(2)}, u32[]{:S(2)}) collective-permute-start(s32[128]{0:T(128)S(1)} %get-tuple-element.161), channel_id=1, source_target_pairs={{0,2},{1,4},{2,6},{3,0},{4,3},{5,5},{6,7},{7,1},{8,10},{9,12},{10,... | collective-permute-start | bytes 1544 | tf_op jit(solution)/shard_map/ppermute | solution.py:82
  24.9 33.8 %collective-permute-start.3 = (bf16[128,640]{1,0:T(8,128)(2,1)S(1)}, bf16[128,640]{1,0:T(8,128)(2,1)}, u32[]{:S(2)}, u32[]{:S(2)}) collective-permute-start(bf16[128,640]{1,0:T(8,128)(2,1)S(1)} %get-tuple-element.118), channel_id=1, source_target_pairs={{0,0},{1,2},{2,4},{3,6},{4,1},{5,3},{6,5},{7,7},{8,8},{9,10},{10,1... | collective-permute-start | bytes 491528 | tf_op jit(solution)/shard_map/ppermute | solution.py:82
  27.1 23.9 %collective-permute-start.1 = (bf16[128,640]{1,0:T(8,128)(2,1)S(1)}, bf16[128,640]{1,0:T(8,128)(2,1)S(1)}, u32[]{:S(2)}, u32[]{:S(2)}) collective-permute-start(bf16[128,640]{1,0:T(8,128)(2,1)S(1)} %get-tuple-element.119), channel_id=1, source_target_pairs={{0,4},{1,6},{2,0},{3,2},{4,5},{5,7},{6,1},{7,3},{8,12},{9,14},{10,... | collective-permute-start | bytes 491528 | tf_op jit(solution)/shard_map/ppermute | solution.py:82
  33.5 9.2 %collective-permute-start = (bf16[128,640]{1,0:T(8,128)(2,1)S(1)}, bf16[128,640]{1,0:T(8,128)(2,1)S(1)}, u32[]{:S(2)}, u32[]{:S(2)}) collective-permute-start(bf16[128,640]{1,0:T(8,128)(2,1)S(1)} %get-tuple-element.120), channel_id=1, source_target_pairs={{0,6},{1,0},{2,2},{3,4},{4,7},{5,1},{6,3},{7,5},{8,14},{9,8},{10,1... | collective-permute-start | bytes 491528 | tf_op jit(solution)/shard_map/ppermute | solution.py:82
  36.3 20.3 %collective-permute-start.2 = (bf16[128,640]{1,0:T(8,128)(2,1)S(1)}, bf16[128,640]{1,0:T(8,128)(2,1)S(1)}, u32[]{:S(2)}, u32[]{:S(2)}) collective-permute-start(bf16[128,640]{1,0:T(8,128)(2,1)S(1)} %get-tuple-element.121), channel_id=1, source_target_pairs={{0,2},{1,4},{2,6},{3,0},{4,3},{5,5},{6,7},{7,1},{8,10},{9,12},{10,... | collective-permute-start | bytes 491528 | tf_op jit(solution)/shard_map/ppermute | solution.py:82
  38.3 42.4 %collective-permute-start.17 = (bf16[128,640]{1,0:T(8,128)(2,1)}, bf16[128,640]{1,0:T(8,128)(2,1)S(1)}, u32[]{:S(2)}, u32[]{:S(2)}) collective-permute-start(bf16[128,640]{1,0:T(8,128)(2,1)} %get-tuple-element.110), channel_id=1, source_target_pairs={{0,0},{1,2},{2,4},{3,6},{4,1},{5,3},{6,5},{7,7},{8,8},{9,10},{10,1... | collective-permute-start | bytes 491528 | tf_op jit(solution)/shard_map/ppermute | solution.py:82
  42.8 23.6 %collective-permute-start.15 = (bf16[128,640]{1,0:T(8,128)(2,1)}, bf16[128,640]{1,0:T(8,128)(2,1)S(1)}, u32[]{:S(2)}, u32[]{:S(2)}) collective-permute-start(bf16[128,640]{1,0:T(8,128)(2,1)} %get-tuple-element.111), channel_id=1, source_target_pairs={{0,4},{1,6},{2,0},{3,2},{4,5},{5,7},{6,1},{7,3},{8,12},{9,14},{10,... | collective-permute-start | bytes 491528 | tf_op jit(solution)/shard_map/ppermute | solution.py:82
  51.0 15.4 %collective-permute-start.14 = (bf16[128,640]{1,0:T(8,128)(2,1)}, bf16[128,640]{1,0:T(8,128)(2,1)S(1)}, u32[]{:S(2)}, u32[]{:S(2)}) collective-permute-start(bf16[128,640]{1,0:T(8,128)(2,1)} %get-tuple-element.112), channel_id=1, source_target_pairs={{0,6},{1,0},{2,2},{3,4},{4,7},{5,1},{6,3},{7,5},{8,14},{9,8},{10,1... | collective-permute-start | bytes 491528 | tf_op jit(solution)/shard_map/ppermute | solution.py:82
  56.7 24.0 %collective-permute-start.16 = (bf16[128,640]{1,0:T(8,128)(2,1)}, bf16[128,640]{1,0:T(8,128)(2,1)S(1)}, u32[]{:S(2)}, u32[]{:S(2)}) collective-permute-start(bf16[128,640]{1,0:T(8,128)(2,1)} %get-tuple-element.113), channel_id=1, source_target_pairs={{0,2},{1,4},{2,6},{3,0},{4,3},{5,5},{6,7},{7,1},{8,10},{9,12},{10,... | collective-permute-start | bytes 491528 | tf_op jit(solution)/shard_map/ppermute | solution.py:82
  249.6 15.3 %collective-permute-start.8 = (bf16[512,512]{1,0:T(8,128)(2,1)}, bf16[512,512]{1,0:T(8,128)(2,1)}, u32[]{:S(2)}, u32[]{:S(2)}) collective-permute-start(bf16[512,512]{1,0:T(8,128)(2,1)} %pad_maximum_fusion.6), channel_id=1, source_target_pairs={{0,1},{2,3},{4,5},{6,7},{8,9},{10,11},{12,13},{14,15},{16,17},{18,... | collective-permute-start | bytes 1572872 | tf_op jit(solution)/shard_map/ppermute | solution.py:110
  289.5 15.5 %collective-permute-start.9 = (bf16[512,512]{1,0:T(8,128)(2,1)}, bf16[512,512]{1,0:T(8,128)(2,1)}, u32[]{:S(2)}, u32[]{:S(2)}) collective-permute-start(bf16[512,512]{1,0:T(8,128)(2,1)} %pad_maximum_fusion.7), channel_id=1, source_target_pairs={{0,1},{2,3},{4,5},{6,7},{8,9},{10,11},{12,13},{14,15},{16,17},{18,... | collective-permute-start | bytes 1572872 | tf_op jit(solution)/shard_map/ppermute | solution.py:110
  352.4 34.5 %collective-permute-start.13 = (bf16[128,640]{1,0:T(8,128)(2,1)}, bf16[128,640]{1,0:T(8,128)(2,1)}, u32[]{:S(2)}, u32[]{:S(2)}) collective-permute-start(bf16[128,640]{1,0:T(8,128)(2,1)} %get-tuple-element.114), channel_id=1, source_target_pairs={{6,0},{0,1},{2,2},{4,3},{7,4},{1,5},{3,6},{5,7},{14,8},{8,9},{10,1... | collective-permute-start | bytes 491528 | tf_op jit(solution)/shard_map/ppermute | solution.py:99
  356.8 29.1 %collective-permute-start.12 = (bf16[128,640]{1,0:T(8,128)(2,1)}, bf16[128,640]{1,0:T(8,128)(2,1)}, u32[]{:S(2)}, u32[]{:S(2)}) collective-permute-start(bf16[128,640]{1,0:T(8,128)(2,1)} %get-tuple-element.115), channel_id=1, source_target_pairs={{4,0},{6,1},{0,2},{2,3},{5,4},{7,5},{1,6},{3,7},{12,8},{14,9},{8,1... | collective-permute-start | bytes 491528 | tf_op jit(solution)/shard_map/ppermute | solution.py:99
  356.9 27.5 %collective-permute-start.11 = (bf16[128,640]{1,0:T(8,128)(2,1)}, bf16[128,640]{1,0:T(8,128)(2,1)}, u32[]{:S(2)}, u32[]{:S(2)}) collective-permute-start(bf16[128,640]{1,0:T(8,128)(2,1)} %get-tuple-element.116), channel_id=1, source_target_pairs={{2,0},{4,1},{6,2},{0,3},{3,4},{5,5},{7,6},{1,7},{10,8},{12,9},{14,... | collective-permute-start | bytes 491528 | tf_op jit(solution)/shard_map/ppermute | solution.py:99
  360.9 22.6 %collective-permute-start.10 = (bf16[128,640]{1,0:T(8,128)(2,1)}, bf16[128,640]{1,0:T(8,128)(2,1)}, u32[]{:S(2)}, u32[]{:S(2)}) collective-permute-start(bf16[128,640]{1,0:T(8,128)(2,1)} %get-tuple-element.117), channel_id=1, source_target_pairs={{0,0},{2,1},{4,2},{6,3},{1,4},{3,5},{5,6},{7,7},{8,8},{10,9},{12,1... | collective-permute-start | bytes 491528 | tf_op jit(solution)/shard_map/ppermute | solution.py:99
  377.7 14.6 %collective-permute-start.18 = (bf16[512,512]{1,0:T(8,128)(2,1)S(1)}, bf16[512,512]{1,0:T(8,128)(2,1)S(1)}, u32[]{:S(2)}, u32[]{:S(2)}) collective-permute-start(bf16[512,512]{1,0:T(8,128)(2,1)S(1)} %copy-done.17), channel_id=1, source_target_pairs={{1,0},{3,2},{5,4},{7,6},{9,8},{11,10},{13,12},{15,14},{17,16},{19,... | collective-permute-start | bytes 1572872 | tf_op jit(solution)/shard_map/ppermute | solution.py:110
  383.5 70.6 %collective-permute-start.39 = (bf16[2,8,32,640]{3,2,1,0:T(8,128)(2,1)}, bf16[2,8,32,640]{3,2,1,0:T(8,128)(2,1)}, u32[]{:S(2)}, u32[]{:S(2)}) collective-permute-start(bf16[2,8,32,640]{3,2,1,0:T(8,128)(2,1)} %dynamic-slice_bitcast_fusion.8), channel_id=1, source_target_pairs={{0,8},{8,0},{16,24},{24,16},{1,9},{9,1},{17,25},{25,17},{2,10},{10... | collective-permute-start | bytes 1966088 | tf_op jit(solution)/shard_map/ppermute | solution.py:137
  384.4 162.7 %collective-permute-start.59 = (bf16[2,8,64,640]{3,2,1,0:T(8,128)(2,1)}, bf16[2,8,64,640]{3,2,1,0:T(8,128)(2,1)}, u32[]{:S(2)}, u32[]{:S(2)}) collective-permute-start(bf16[2,8,64,640]{3,2,1,0:T(8,128)(2,1)} %dynamic-slice_bitcast_fusion.2), channel_id=1, source_target_pairs={{0,8},{8,0},{16,24},{24,16},{1,9},{9,1},{17,25},{25,17},{2,10},{10... | collective-permute-start | bytes 3932168 | tf_op jit(solution)/shard_map/ppermute | solution.py:137
  385.9 238.6 %collective-permute-start.49 = (bf16[2,8,128,640]{3,2,1,0:T(8,128)(2,1)}, bf16[2,8,128,640]{3,2,1,0:T(8,128)(2,1)}, u32[]{:S(2)}, u32[]{:S(2)}) collective-permute-start(bf16[2,8,128,640]{3,2,1,0:T(8,128)(2,1)} %dynamic-slice_bitcast_fusion), channel_id=1, source_target_pairs={{0,8},{8,0},{16,24},{24,16},{1,9},{9,1},{17,25},{25,17},{2,10},{10... | collective-permute-start | bytes 7864328 | tf_op jit(solution)/shard_map/ppermute | solution.py:137
  441.8 25.2 %collective-permute-start.19 = (bf16[512,512]{1,0:T(8,128)(2,1)S(1)}, bf16[512,512]{1,0:T(8,128)(2,1)}, u32[]{:S(2)}, u32[]{:S(2)}) collective-permute-start(bf16[512,512]{1,0:T(8,128)(2,1)S(1)} %copy-done.15), channel_id=1, source_target_pairs={{1,0},{3,2},{5,4},{7,6},{9,8},{11,10},{13,12},{15,14},{17,16},{19,... | collective-permute-start | bytes 1572872 | tf_op jit(solution)/shard_map/ppermute | solution.py:110
  444.2 63.9 %collective-permute-start.34 = (bf16[2,8,32,640]{3,2,1,0:T(8,128)(2,1)}, bf16[2,8,32,640]{3,2,1,0:T(8,128)(2,1)}, u32[]{:S(2)}, u32[]{:S(2)}) collective-permute-start(bf16[2,8,32,640]{3,2,1,0:T(8,128)(2,1)} %dynamic-slice_bitcast_fusion.9), channel_id=1, source_target_pairs={{0,8},{8,0},{16,24},{24,16},{1,9},{9,1},{17,25},{25,17},{2,10},{10... | collective-permute-start | bytes 1966088 | tf_op jit(solution)/shard_map/ppermute | solution.py:137
  457.1 9.8 %collective-permute-start.40 = (bf16[1,8,32,640]{3,2,1,0:T(8,128)(2,1)}, bf16[1,8,32,640]{3,2,1,0:T(8,128)(2,1)S(1)}, u32[]{:S(2)}, u32[]{:S(2)}) collective-permute-start(bf16[1,8,32,640]{3,2,1,0:T(8,128)(2,1)} %constant_dynamic-slice_fusion.19), channel_id=1, source_target_pairs={{0,16},{8,24},{16,0},{24,8},{1,17},{9,25},{17,1},{25,9},{2,18},{10... | collective-permute-start | bytes 983048 | tf_op jit(solution)/shard_map/ppermute | solution.py:137
  466.9 86.4 %collective-permute-start.29 = (bf16[2,8,48,640]{3,2,1,0:T(8,128)(2,1)}, bf16[2,8,48,640]{3,2,1,0:T(8,128)(2,1)}, u32[]{:S(2)}, u32[]{:S(2)}) collective-permute-start(bf16[2,8,48,640]{3,2,1,0:T(8,128)(2,1)} %dynamic-slice_bitcast_fusion.4), channel_id=1, source_target_pairs={{0,8},{8,0},{16,24},{24,16},{1,9},{9,1},{17,25},{25,17},{2,10},{10... | collective-permute-start | bytes 2949128 | tf_op jit(solution)/shard_map/ppermute | solution.py:137
  483.7 6.0 collective-permute-start.66
  497.8 5.9 collective-permute-start.41
  503.7 33.3 %collective-permute-start.23 = (bf16[128,640]{1,0:T(8,128)(2,1)S(1)}, bf16[128,640]{1,0:T(8,128)(2,1)S(1)}, u32[]{:S(2)}, u32[]{:S(2)}) collective-permute-start(bf16[128,640]{1,0:T(8,128)(2,1)S(1)} %get-tuple-element.106), channel_id=1, source_target_pairs={{6,0},{0,1},{2,2},{4,3},{7,4},{1,5},{3,6},{5,7},{14,8},{8,9},{10,1... | collective-permute-start | bytes 491528 | tf_op jit(solution)/shard_map/ppermute | solution.py:99
  510.2 19.7 %collective-permute-start.21 = (bf16[128,640]{1,0:T(8,128)(2,1)S(1)}, bf16[128,640]{1,0:T(8,128)(2,1)S(1)}, u32[]{:S(2)}, u32[]{:S(2)}) collective-permute-start(bf16[128,640]{1,0:T(8,128)(2,1)S(1)} %get-tuple-element.108), channel_id=1, source_target_pairs={{2,0},{4,1},{6,2},{0,3},{3,4},{5,5},{7,6},{1,7},{10,8},{12,9},{14,... | collective-permute-start | bytes 491528 | tf_op jit(solution)/shard_map/ppermute | solution.py:99
  529.8 6.6 collective-permute-start.22
  537.0 9.4 %collective-permute-start.35 = (bf16[1,8,32,640]{3,2,1,0:T(8,128)(2,1)S(1)}, bf16[1,8,32,640]{3,2,1,0:T(8,128)(2,1)S(1)}, u32[]{:S(2)}, u32[]{:S(2)}) collective-permute-start(bf16[1,8,32,640]{3,2,1,0:T(8,128)(2,1)S(1)} %constant_dynamic-slice_fusion.21), channel_id=1, source_target_pairs={{0,16},{8,24},{16,0},{24,8},{1,17},{9,25},{17,1},{25,9},{2,18},{10... | collective-permute-start | bytes 983048 | tf_op jit(solution)/shard_map/ppermute | solution.py:137
  541.4 5.0 collective-permute-start.43
  546.3 18.5 %collective-permute-start.54 = (bf16[2,8,64,640]{3,2,1,0:T(8,128)(2,1)S(1)}, bf16[2,8,64,640]{3,2,1,0:T(8,128)(2,1)S(1)}, u32[]{:S(2)}, u32[]{:S(2)}) collective-permute-start(bf16[2,8,64,640]{3,2,1,0:T(8,128)(2,1)S(1)} %copy-done.82), channel_id=1, source_target_pairs={{0,8},{8,0},{16,24},{24,16},{1,9},{9,1},{17,25},{25,17},{2,10},{10... | collective-permute-start | bytes 3932168 | tf_op jit(solution)/shard_map/ppermute | solution.py:137
  546.4 87.6 %collective-permute-start.44 = (bf16[2,8,128,640]{3,2,1,0:T(8,128)(2,1)S(1)}, bf16[2,8,128,640]{3,2,1,0:T(8,128)(2,1)S(1)}, u32[]{:S(2)}, u32[]{:S(2)}) collective-permute-start(bf16[2,8,128,640]{3,2,1,0:T(8,128)(2,1)S(1)} %copy-done.66), channel_id=1, source_target_pairs={{0,8},{8,0},{16,24},{24,16},{1,9},{9,1},{17,25},{25,17},{2,10},{10... | collective-permute-start | bytes 7864328 | tf_op jit(solution)/shard_map/ppermute | solution.py:137
  547.1 6.2 collective-permute-start.36
  553.3 38.9 %collective-permute-start.24 = (bf16[2,8,48,640]{3,2,1,0:T(8,128)(2,1)S(1)}, bf16[2,8,48,640]{3,2,1,0:T(8,128)(2,1)S(1)}, u32[]{:S(2)}, u32[]{:S(2)}) collective-permute-start(bf16[2,8,48,640]{3,2,1,0:T(8,128)(2,1)S(1)} %dynamic-slice_bitcast_fusion.5), channel_id=1, source_target_pairs={{0,8},{8,0},{16,24},{24,16},{1,9},{9,1},{17,25},{25,17},{2,10},{10... | collective-permute-start | bytes 2949128 | tf_op jit(solution)/shard_map/ppermute | solution.py:137
  558.3 5.1 collective-permute-start.38
  563.5 17.7 %collective-permute-start.60 = (bf16[1,8,64,640]{3,2,1,0:T(8,128)(2,1)S(1)}, bf16[1,8,64,640]{3,2,1,0:T(8,128)(2,1)S(1)}, u32[]{:S(2)}, u32[]{:S(2)}) collective-permute-start(bf16[1,8,64,640]{3,2,1,0:T(8,128)(2,1)S(1)} %constant_dynamic-slice_fusion.11), channel_id=1, source_target_pairs={{0,16},{8,24},{16,0},{24,8},{1,17},{9,25},{17,1},{25,9},{2,18},{10... | collective-permute-start | bytes 1966088 | tf_op jit(solution)/shard_map/ppermute | solution.py:137
  564.8 26.8 %collective-permute-start.30 = (bf16[1,8,48,640]{3,2,1,0:T(8,128)(2,1)S(1)}, bf16[1,8,48,640]{3,2,1,0:T(8,128)(2,1)S(1)}, u32[]{:S(2)}, u32[]{:S(2)}) collective-permute-start(bf16[1,8,48,640]{3,2,1,0:T(8,128)(2,1)S(1)} %constant_dynamic-slice_fusion.23), channel_id=1, source_target_pairs={{0,16},{8,24},{16,0},{24,8},{1,17},{9,25},{17,1},{25,9},{2,18},{10... | collective-permute-start | bytes 1474568 | tf_op jit(solution)/shard_map/ppermute | solution.py:137
  581.1 37.8 %collective-permute-start.55 = (bf16[1,8,64,640]{3,2,1,0:T(8,128)(2,1)S(1)}, bf16[1,8,64,640]{3,2,1,0:T(8,128)(2,1)S(1)}, u32[]{:S(2)}, u32[]{:S(2)}) collective-permute-start(bf16[1,8,64,640]{3,2,1,0:T(8,128)(2,1)S(1)} %constant_dynamic-slice_fusion.13), channel_id=1, source_target_pairs={{0,16},{8,24},{16,0},{24,8},{1,17},{9,25},{17,1},{25,9},{2,18},{10... | collective-permute-start | bytes 1966088 | tf_op jit(solution)/shard_map/ppermute | solution.py:137
  591.7 11.3 %collective-permute-start.61 = (bf16[4,1,64,640]{3,2,0,1:T(8,128)(2,1)S(1)}, bf16[4,1,64,640]{3,2,0,1:T(8,128)(2,1)S(1)}, u32[]{:S(2)}, u32[]{:S(2)}) collective-permute-start(bf16[4,1,64,640]{3,2,0,1:T(8,128)(2,1)S(1)} %dynamic-slice_bitcast_fusion.10), channel_id=1, source_target_pairs={{0,1},{1,0},{2,3},{3,2},{4,5},{5,4},{6,7},{7,6},{8,9},{9,8},{10,11... | collective-permute-start | bytes 983048 | tf_op jit(solution)/shard_map/ppermute | solution.py:137
  592.1 9.8 %collective-permute-start.31 = (bf16[4,1,48,640]{3,2,0,1:T(8,128)(2,1)S(1)}, bf16[4,1,48,640]{3,2,0,1:T(8,128)(2,1)S(1)}, u32[]{:S(2)}, u32[]{:S(2)}) collective-permute-start(bf16[4,1,48,640]{3,2,0,1:T(8,128)(2,1)S(1)} %dynamic-slice_bitcast_fusion.14), channel_id=1, source_target_pairs={{0,1},{1,0},{2,3},{3,2},{4,5},{5,4},{6,7},{7,6},{8,9},{9,8},{10,11... | collective-permute-start | bytes 737288 | tf_op jit(solution)/shard_map/ppermute | solution.py:137
  602.0 17.5 %collective-permute-start.25 = (bf16[1,8,48,640]{3,2,1,0:T(8,128)(2,1)S(1)}, bf16[1,8,48,640]{3,2,1,0:T(8,128)(2,1)S(1)}, u32[]{:S(2)}, u32[]{:S(2)}) collective-permute-start(bf16[1,8,48,640]{3,2,1,0:T(8,128)(2,1)S(1)} %constant_dynamic-slice_fusion.25), channel_id=1, source_target_pairs={{0,16},{8,24},{16,0},{24,8},{1,17},{9,25},{17,1},{25,9},{2,18},{10... | collective-permute-start | bytes 1474568 | tf_op jit(solution)/shard_map/ppermute | solution.py:137
  602.9 4.9 collective-permute-start.32
  608.0 5.5 collective-permute-start.33
  613.4 5.3 collective-permute-start.62
  618.8 5.7 collective-permute-start.63
  619.1 11.8 %collective-permute-start.56 = (bf16[4,1,64,640]{3,2,0,1:T(8,128)(2,1)S(1)}, bf16[4,1,64,640]{3,2,0,1:T(8,128)(2,1)S(1)}, u32[]{:S(2)}, u32[]{:S(2)}) collective-permute-start(bf16[4,1,64,640]{3,2,0,1:T(8,128)(2,1)S(1)} %dynamic-slice_bitcast_fusion.11), channel_id=1, source_target_pairs={{0,1},{1,0},{2,3},{3,2},{4,5},{5,4},{6,7},{7,6},{8,9},{9,8},{10,11... | collective-permute-start | bytes 983048 | tf_op jit(solution)/shard_map/ppermute | solution.py:137
  619.7 9.2 %collective-permute-start.26 = (bf16[4,1,48,640]{3,2,0,1:T(8,128)(2,1)S(1)}, bf16[4,1,48,640]{3,2,0,1:T(8,128)(2,1)S(1)}, u32[]{:S(2)}, u32[]{:S(2)}) collective-permute-start(bf16[4,1,48,640]{3,2,0,1:T(8,128)(2,1)S(1)} %dynamic-slice_bitcast_fusion.15), channel_id=1, source_target_pairs={{0,1},{1,0},{2,3},{3,2},{4,5},{5,4},{6,7},{7,6},{8,9},{9,8},{10,11... | collective-permute-start | bytes 737288 | tf_op jit(solution)/shard_map/ppermute | solution.py:137
  627.5 31.8 %collective-permute-start.50 = (bf16[1,8,128,640]{3,2,1,0:T(8,128)(2,1)S(1)}, bf16[1,8,128,640]{3,2,1,0:T(8,128)(2,1)S(1)}, u32[]{:S(2)}, u32[]{:S(2)}) collective-permute-start(bf16[1,8,128,640]{3,2,1,0:T(8,128)(2,1)S(1)} %constant_dynamic-slice_fusion.15), channel_id=1, source_target_pairs={{0,16},{8,24},{16,0},{24,8},{1,17},{9,25},{17,1},{25,9},{2,18},{10... | collective-permute-start | bytes 3932168 | tf_op jit(solution)/shard_map/ppermute | solution.py:137
  629.0 4.9 collective-permute-start.27
  635.0 42.1 %collective-permute-start.45 = (bf16[1,8,128,640]{3,2,1,0:T(8,128)(2,1)S(1)}, bf16[1,8,128,640]{3,2,1,0:T(8,128)(2,1)S(1)}, u32[]{:S(2)}, u32[]{:S(2)}) collective-permute-start(bf16[1,8,128,640]{3,2,1,0:T(8,128)(2,1)S(1)} %constant_dynamic-slice_fusion.17), channel_id=1, source_target_pairs={{0,16},{8,24},{16,0},{24,8},{1,17},{9,25},{17,1},{25,9},{2,18},{10... | collective-permute-start | bytes 3932168 | tf_op jit(solution)/shard_map/ppermute | solution.py:137
  636.4 5.1 collective-permute-start.28
  639.1 5.4 collective-permute-start.57
  644.6 33.3 %collective-permute-start.58 = (bf16[1,1,64,640]{3,2,0,1:T(8,128)(2,1)S(1)}, bf16[1,1,64,640]{3,2,0,1:T(8,128)(2,1)S(1)}, u32[]{:S(2)}, u32[]{:S(2)}) collective-permute-start(bf16[1,1,64,640]{3,2,0,1:T(8,128)(2,1)S(1)} %constant_dynamic-slice_fusion.12), channel_id=1, source_target_pairs={{0,4},{1,5},{2,6},{3,7},{4,0},{5,1},{6,2},{7,3},{8,12},{9,13},{10,... | collective-permute-start | bytes 245768 | tf_op jit(solution)/shard_map/ppermute | solution.py:137
  659.7 19.0 %collective-permute-start.51 = (bf16[4,1,128,640]{3,2,0,1:T(8,128)(2,1)S(1)}, bf16[4,1,128,640]{3,2,0,1:T(8,128)(2,1)S(1)}, u32[]{:S(2)}, u32[]{:S(2)}) collective-permute-start(bf16[4,1,128,640]{3,2,0,1:T(8,128)(2,1)S(1)} %dynamic-slice_bitcast_fusion.6), channel_id=1, source_target_pairs={{0,1},{1,0},{2,3},{3,2},{4,5},{5,4},{6,7},{7,6},{8,9},{9,8},{10,11... | collective-permute-start | bytes 1966088 | tf_op jit(solution)/shard_map/ppermute | solution.py:137
  677.5 10.7 %collective-permute-start.46 = (bf16[4,1,128,640]{3,2,0,1:T(8,128)(2,1)S(1)}, bf16[4,1,128,640]{3,2,0,1:T(8,128)(2,1)S(1)}, u32[]{:S(2)}, u32[]{:S(2)}) collective-permute-start(bf16[4,1,128,640]{3,2,0,1:T(8,128)(2,1)S(1)} %dynamic-slice_bitcast_fusion.7), channel_id=1, source_target_pairs={{0,1},{1,0},{2,3},{3,2},{4,5},{5,4},{6,7},{7,6},{8,9},{9,8},{10,11... | collective-permute-start | bytes 1966088 | tf_op jit(solution)/shard_map/ppermute | solution.py:137
  678.9 10.0 %collective-permute-start.52 = (bf16[2,1,128,640]{3,2,1,0:T(8,128)(2,1)S(1)}, bf16[2,1,128,640]{3,2,1,0:T(8,128)(2,1)S(1)}, u32[]{:S(2)}, u32[]{:S(2)}) collective-permute-start(bf16[2,1,128,640]{3,2,1,0:T(8,128)(2,1)S(1)} %dynamic-slice_bitcast_fusion.12), channel_id=1, source_target_pairs={{0,2},{1,3},{2,0},{3,1},{4,6},{5,7},{6,4},{7,5},{8,10},{9,11},{10,... | collective-permute-start | bytes 983048 | tf_op jit(solution)/shard_map/ppermute | solution.py:137
  688.4 10.4 %collective-permute-start.47 = (bf16[2,1,128,640]{3,2,0,1:T(8,128)(2,1)S(1)}, bf16[2,1,128,640]{3,2,0,1:T(8,128)(2,1)S(1)}, u32[]{:S(2)}, u32[]{:S(2)}) collective-permute-start(bf16[2,1,128,640]{3,2,0,1:T(8,128)(2,1)S(1)} %dynamic-slice_bitcast_fusion.13), channel_id=1, source_target_pairs={{0,2},{1,3},{2,0},{3,1},{4,6},{5,7},{6,4},{7,5},{8,10},{9,11},{10,... | collective-permute-start | bytes 983048 | tf_op jit(solution)/shard_map/ppermute | solution.py:137
  689.0 10.0 %collective-permute-start.53 = (bf16[1,1,128,640]{3,2,1,0:T(8,128)(2,1)S(1)}, bf16[1,1,128,640]{3,2,1,0:T(8,128)(2,1)S(1)}, u32[]{:S(2)}, u32[]{:S(2)}) collective-permute-start(bf16[1,1,128,640]{3,2,1,0:T(8,128)(2,1)S(1)} %constant_dynamic-slice_fusion.14), channel_id=1, source_target_pairs={{0,4},{1,5},{2,6},{3,7},{4,0},{5,1},{6,2},{7,3},{8,12},{9,13},{10,... | collective-permute-start | bytes 491528 | tf_op jit(solution)/shard_map/ppermute | solution.py:137
  698.9 7.0 collective-permute-start.48
  (181 other events, 1979.3 us)
Sparse Core Ops, SparseCore 0:
  11.5 112.3 all-gather.4
  127.4 90.7 all-gather.6

commit v2 on v1

v2 whole, which is shorter than its diff:
```python
from functools import partial

import jax
import jax.numpy as jnp
from jax import lax
from jax.experimental import pallas as pl
from jax.experimental.pallas import tpu as pltpu
from jax.sharding import PartitionSpec as P

D = 640
HEADS = 4
HEAD_DIM = 256
WINDOW = 512
QUERY_BLOCK = 256

EPSILON = 1e-06
ROPE_BASE = 10000.0
SCORE_SCALE = 0.0625
MASKED_SCORE = -1e30
BF16 = jnp.bfloat16
F32 = jnp.float32
ALL = ("dp", "seq")
TILE = 16
QUERY_COLS = HEADS * HEAD_DIM
GELU_A = 0.7978845608028654
GELU_B = 0.044715
HIDDEN_BLOCK = 512


def dot(a, b, a_dim, b_dim):
    return lax.dot_general(a, b, (((a_dim,), (b_dim,)), ((), ())), preferred_element_type=F32)


def angle_tables(places):
    half_dim = HEAD_DIM // 2
    inverse = ROPE_BASE ** (-(2.0 * jnp.arange(half_dim, dtype=F32)) / HEAD_DIM)
    phases = places.astype(F32)[..., None] * inverse
    return (jnp.cos(phases), jnp.sin(phases))


def inverse_rms(values):
    return lax.rsqrt(jnp.mean(values * values, axis=-1, keepdims=True) + EPSILON)


def rms_norm(values, gain):
    return values * inverse_rms(values) * gain


def rms_backward(values, gain, grad):
    scale = inverse_rms(values)
    weighted = grad * gain
    shared = jnp.mean(weighted * values, axis=-1, keepdims=True) * (scale * scale * scale)
    grad_gain = jnp.sum(grad * (values * scale), axis=0, keepdims=True)
    return weighted * scale - values * shared, grad_gain


def rotate(values, cosine_tab, sine_tab):
    half_dim = HEAD_DIM // 2
    first, second = values[:, :half_dim], values[:, half_dim:]
    return jnp.concatenate(
        [first * cosine_tab - second * sine_tab, second * cosine_tab + first * sine_tab], axis=-1
    )


def rotate_back(values, cosine_tab, sine_tab):
    return rotate(values, cosine_tab, -sine_tab)


def gain_of(gains_ref, which):
    starts = (0, D, 2 * D, 3 * D, 4 * D, 4 * D + HEAD_DIM)
    return gains_ref[:, starts[which] : starts[which] + (D if which < 4 else HEAD_DIM)]


PRE_ATTN, POST_ATTN, PRE_FFN, POST_FFN, QUERY_GAIN, KEY_GAIN = range(6)


def weight_rows(ref, start, size):
    shards, rows, width = ref.shape
    if shards == 1:
        return ref[0, start : start + size, :]
    first, last = start // rows, -(-(start + size) // rows)
    value = ref[first:last].reshape((last - first) * rows, width)
    skip = start - first * rows
    return value[skip : skip + size]


def fetch(weight, ref, scratch, sem):
    _, start, rows = weight
    copy = pltpu.make_async_copy(ref.at[:, pl.ds(start, rows), :], scratch, sem)
    copy.start()
    return copy


def weight_scratch(weight):
    array, _, rows = weight
    return pltpu.VMEM((array.shape[0], rows, D), BF16)


def vmem(count):
    return [pl.BlockSpec(memory_space=pltpu.VMEM)] * count


def call(kernel, name, arrays, weights, outs, flops, scratch=()):
    outs = [jax.ShapeDtypeStruct(shape, dtype) for shape, dtype in outs]
    moved = sum(a.size * a.dtype.itemsize for a in list(arrays) + outs)
    return pl.pallas_call(
        kernel,
        out_shape=tuple(outs),
        in_specs=vmem(len(arrays)) + [pl.BlockSpec(memory_space=pl.ANY)] * len(weights),
        out_specs=tuple(vmem(len(outs))),
        scratch_shapes=[weight_scratch(w) for w in weights]
        + ([pltpu.SemaphoreType.DMA((len(weights),))] if weights else [])
        + list(scratch),
        compiler_params=pltpu.CompilerParams(vmem_limit_bytes=VMEM_LIMIT),
        cost_estimate=pl.CostEstimate(flops=flops, bytes_accessed=moved, transcendentals=0),
        name=name,
    )(*arrays, *[w[0] for w in weights])


VMEM_LIMIT = 44 * 2**20


def chunk_route(count, k):
    n_dp, n_seq = lax.axis_size("dp"), lax.axis_size("seq")
    chips = n_seq // (2 * count)
    pairs = []
    for dp in range(n_dp):
        for i in range(n_seq):
            chunk = i // count
            sequence = (dp % 2) * count + (i + k) % count
            target_dp = dp - dp % 2 + chunk % 2
            pairs.append((dp * n_seq + i, target_dp * n_seq + sequence * chips + chunk // 2))
    return pairs


def place(count):
    chips = lax.axis_size("seq") // (2 * count)
    return (lax.axis_index("seq") // chips) % count


def to_long(block):
    count = block.shape[0]
    me = lax.axis_index("seq")
    received = []
    for k in range(count):
        piece = lax.dynamic_index_in_dim(block, (me + k) % count, 0, keepdims=False)
        received.append(lax.ppermute(piece, ALL, chunk_route(count, k)))
    twice = jnp.stack((received[::-1] * 2)[: 2 * count - 1])
    long = lax.dynamic_slice_in_dim(twice, count - 1 - place(count), count, 0)
    return long.reshape((count * block.shape[1],) + block.shape[2:])


def to_short(long, count):
    me = lax.axis_index("seq")
    parts = long.reshape((count, long.shape[0] // count) + long.shape[1:])
    received = []
    for k in range(count):
        piece = lax.dynamic_index_in_dim(parts, (place(count) - k) % count, 0, keepdims=False)
        route = [(j, i) for i, j in chunk_route(count, k)]
        received.append(lax.ppermute(piece, ALL, route))
    twice = jnp.stack((received * 2)[: 2 * count - 1])
    return lax.dynamic_slice_in_dim(twice, (count - me % count) % count, count, 0)


def neighbour(block, count, back):
    n_dp, n_seq = lax.axis_size("dp"), lax.axis_size("seq")
    chips = n_seq // (2 * count)
    pairs = []
    for dp in range(n_dp):
        for i in range(n_seq):
            if dp % 2 == 0:
                pairs.append((dp * n_seq + i, (dp + 1) * n_seq + i))
            elif (i + 1) % chips:
                pairs.append((dp * n_seq + i, (dp - 1) * n_seq + i + 1))
    if back:
        pairs = [(j, i) for i, j in pairs]
    return lax.ppermute(block, ALL, pairs)


def bits(axis):
    out, bit = [], 1
    while bit < lax.axis_size(axis):
        out.append((axis, bit))
        bit *= 2
    return out


def order(first):
    core, *wide = bits("dp")
    near, *far = bits("seq")
    if first == "dp":
        return [core] + wide + [near] + far[::-1]
    return [core, near] + wide + far[::-1]


def swap(array, step):
    axis, bit = step
    return lax.ppermute(array, axis, [(i, i ^ bit) for i in range(lax.axis_size(axis))])


def advance(value, chains):
    if not chains:
        return value
    held = lax.optimization_barrier((value,) + tuple(chain.got for chain in chains))
    for chain, got in zip(chains, held[1:]):
        chain.got = got
        chain.advance()
    return held[0]


def halving(array):
    n_seq = lax.axis_size("seq")
    dims = bits("dp")[::-1] + bits("seq")[::-1]
    me = lax.axis_index("dp") * n_seq + lax.axis_index("seq")
    rest = array.shape[1:]
    array = jnp.take(array, me ^ jnp.arange(array.shape[0]), axis=0)
    array = array.reshape((2,) * len(dims) + rest)
    for step in order("dp"):
        at = dims.index(step)
        dims.remove(step)
        keep = lax.index_in_dim(array, 0, at, keepdims=False)
        array = keep + swap(lax.index_in_dim(array, 1, at, keepdims=False), step)
    return array


def block_numbers():
    me = lax.axis_index("dp")
    core = me % 2
    wide = [me // 2, (me // 2) ^ 1]
    leave = [2 * w + 1 - core for w in wide]
    stay = [2 * w + core for w in wide]
    return jnp.stack(leave + stay + [lax.axis_index("seq")]).astype(jnp.int32)


def product_kernel(rows, split, added, numbers_ref, a_ref, b_ref, *refs):
    got_ref = refs[0] if added else None
    outs, acc = refs[1 if added else 0 : -1], refs[-1]
    acc[...] = dot(a_ref[...], b_ref[...], 0, 0)
    me = numbers_ref[4]
    for entry in range(a_ref.shape[1] // rows):
        source = pl.multiple_of((me ^ entry) * rows, TILE)
        value = acc[pl.ds(source, rows), :]
        if added:
            value = value + got_ref[0, entry].astype(F32)
        if split:
            outs[entry % 2][0, entry // 2] = value.astype(BF16)
        else:
            outs[0][0, entry] = value.astype(BF16)


def product(left, right, numbers, first, blocks, got=None, got_first=0, split=False):
    tokens, n_seq = left.shape[0], lax.axis_size("seq")
    width = left.shape[1] // lax.axis_size("dp")
    rows = width // n_seq
    out_entries = n_seq // 2 if split else n_seq
    specs = [
        pl.BlockSpec((tokens, width), lambda i, n: (0, n[first + i])),
        pl.BlockSpec((tokens, D), lambda i, n: (0, 0)),
    ]
    operands = [left, right]
    if got is not None:
        specs.append(pl.BlockSpec((1, n_seq, rows, D), lambda i, n: (i + got_first, 0, 0, 0)))
        operands.append(got)
    shape = jax.ShapeDtypeStruct((blocks, out_entries, rows, D), BF16)
    count = 2 if split else 1
    return pl.pallas_call(
        partial(product_kernel, rows, split, got is not None),
        grid_spec=pltpu.PrefetchScalarGridSpec(
            num_scalar_prefetch=1,
            grid=(blocks,),
            in_specs=specs,
            out_specs=[pl.BlockSpec((1, out_entries, rows, D), lambda i, n: (i, 0, 0, 0))] * count,
            scratch_shapes=[pltpu.VMEM((width, D), F32)],
        ),
        out_shape=[shape] * count,
        compiler_params=pltpu.CompilerParams(vmem_limit_bytes=24 * 2**20),
        cost_estimate=pl.CostEstimate(
            flops=2 * tokens * width * blocks * D,
            bytes_accessed=2 * (tokens * width * blocks + tokens * D + 2 * width * blocks * D),
            transcendentals=0,
        ),
        name="weight_gradient",
    )(numbers, *operands)


class Chain:
    def __init__(self, left, right, first):
        self.steps = order(first)
        self.dims = bits("dp")[::-1] + bits("seq")[::-1]
        n_dp, n_seq = lax.axis_size("dp"), lax.axis_size("seq")
        width = left.shape[1] // n_dp
        self.rows = width // n_seq
        self.factors = None
        step = self.steps[0]
        if n_dp == 4 and width % 128 == 0 and self.rows % TILE == 0 and width % n_seq == 0:
            self.factors = (left, right, block_numbers())
            (send,) = product(left, right, self.factors[2], 0, 2)
            self.dims.remove(step)
            self.got = swap(send, step)
        else:
            whole = dot(left, right, 0, 0).astype(BF16).reshape(n_dp * n_seq, self.rows, D)
            me = lax.axis_index("dp") * n_seq + lax.axis_index("seq")
            self.send(jnp.take(whole, me ^ jnp.arange(n_dp * n_seq), axis=0))

    def send(self, array):
        step = self.steps[0]
        array = array.reshape((2,) * len(self.dims) + (self.rows, D))
        at = self.dims.index(step)
        self.dims.remove(step)
        self.keep = lax.index_in_dim(array, 0, at, keepdims=False)
        self.got = swap(lax.index_in_dim(array, 1, at, keepdims=False), step)

    def advance(self):
        self.steps = self.steps[1:]
        if self.factors:
            left, right, numbers = self.factors
            self.factors = None
            step = self.steps[0]
            if step[0] == "dp":
                (send,) = product(left, right, numbers, 3, 1, self.got, 1)
                (self.keep,) = product(left, right, numbers, 2, 1, self.got, 0)
            else:
                self.keep, send = product(left, right, numbers, 2, 2, self.got, 0, True)
            self.dims.remove(step)
            self.got = swap(send, step)
            return
        array = self.keep.astype(F32) + self.got.reshape(self.keep.shape).astype(F32)
        if self.steps:
            self.send(array.astype(BF16))
        else:
            self.result = array.reshape(self.rows, D)

    def finish(self):
        while self.steps:
            self.advance()
        return self.result


def allowed_pairs(start, key_count, reach, lanes):
    key_at = lax.broadcasted_iota(jnp.int32, (key_count, lanes), 0)
    query_at = lax.broadcasted_iota(jnp.int32, (key_count, lanes), 1) % QUERY_BLOCK
    distance = query_at + WINDOW - key_at
    return (distance >= 0) & (distance <= reach)


def stacked_heads(ref, start):
    return jnp.concatenate(
        [
            ref[start : start + QUERY_BLOCK, h * HEAD_DIM : (h + 1) * HEAD_DIM]
            for h in range(HEADS)
        ],
        axis=0,
    )


def window_rows(before_ref, own_ref, start, count, columns):
    return jnp.concatenate(
        [before_ref[start:, columns], own_ref[: count - (WINDOW - start), columns]], axis=0
    )


KEYS, VALUES = slice(0, HEAD_DIM), slice(HEAD_DIM, 2 * HEAD_DIM)
KEY_COUNT = QUERY_BLOCK + WINDOW


def key_value_kernel(weights, stream_ref, gains_ref, cos_ref, sin_ref, w_any, normed_ref, raw_ref, own_ref, w_ref, sem):
    copy = fetch(weights[0], w_any, w_ref, sem.at[0])
    normed = rms_norm(stream_ref[...], gain_of(gains_ref, PRE_ATTN)).astype(BF16)
    normed_ref[...] = normed
    copy.wait()
    raw = dot(normed, weight_rows(w_ref, QUERY_COLS, 2 * HEAD_DIM), 1, 1)
    raw_ref[...] = raw[:, KEYS]
    keys = rms_norm(raw[:, KEYS], gain_of(gains_ref, KEY_GAIN))
    own_ref[:, KEYS] = rotate(keys, cos_ref[...], sin_ref[...]).astype(BF16)
    own_ref[:, VALUES] = raw[:, VALUES].astype(BF16)


def query_kernel(weights, normed_ref, gains_ref, cos_ref, sin_ref, w_any, raw_ref, q_ref, w_ref, sem):
    copy = fetch(weights[0], w_any, w_ref, sem.at[0])
    copy.wait()
    cosine_tab, sine_tab = cos_ref[...], sin_ref[...]
    normed = normed_ref[...]
    for h in range(HEADS):
        columns = slice(h * HEAD_DIM, (h + 1) * HEAD_DIM)
        raw = dot(normed, weight_rows(w_ref, h * HEAD_DIM, HEAD_DIM), 1, 1)
        raw_ref[:, columns] = raw
        queries = rotate(rms_norm(raw, gain_of(gains_ref, QUERY_GAIN)), cosine_tab, sine_tab)
        q_ref[:, columns] = queries.astype(BF16) * SCORE_SCALE


def gelu_parts(gate):
    inner = GELU_A * (gate + GELU_B * gate * gate * gate)
    tanh = jnp.tanh(inner)
    return tanh, 0.5 * gate * (1.0 + tanh)


def block_kernel(
    weights, q_ref, before_ref, own_ref, reach_ref, stream_ref, gains_ref, wa_any, wi_any, wo_any,
    ctx_ref, lse_ref, branch_ref, middle_ref, fn_ref, gu_ref, inner_ref, fb_ref, result_ref,
    wa_ref, wi_ref, wo_ref, sem,
):
    copies = [
        fetch(weight, source, target, sem.at[i])
        for i, (weight, source, target) in enumerate(
            zip(weights, (wa_any, wi_any, wo_any), (wa_ref, wi_ref, wo_ref))
        )
    ]
    for block in range(q_ref.shape[0] // QUERY_BLOCK):
        start = block * QUERY_BLOCK
        queries = stacked_heads(q_ref, start)
        keys = window_rows(before_ref, own_ref, start, KEY_COUNT, KEYS)
        values = window_rows(before_ref, own_ref, start, KEY_COUNT, VALUES)
        allowed = allowed_pairs(start, KEY_COUNT, reach_ref[block : block + 1, :], HEADS * QUERY_BLOCK)
        scores = jnp.where(allowed, dot(keys, queries, 1, 1), MASKED_SCORE)
        row_max = jnp.max(scores, axis=0, keepdims=True)
        exps = jnp.exp(scores - row_max)
        row_sum = jnp.sum(exps, axis=0, keepdims=True)
        probs = (exps * (1.0 / row_sum)).astype(BF16)
        lse_ref[block : block + 1, :] = row_max + jnp.log(row_sum)
        context = dot(probs, values, 0, 0).astype(BF16)
        for h in range(HEADS):
            ctx_ref[start : start + QUERY_BLOCK, h * HEAD_DIM : (h + 1) * HEAD_DIM] = context[
                h * QUERY_BLOCK : (h + 1) * QUERY_BLOCK
            ]
    copies[0].wait()
    branch = dot(ctx_ref[...], weight_rows(wa_ref, 0, QUERY_COLS), 1, 0)
    branch_ref[...] = branch
    middle = stream_ref[...] + rms_norm(branch, gain_of(gains_ref, POST_ATTN))
    middle_ref[...] = middle
    ffn_normed = rms_norm(middle, gain_of(gains_ref, PRE_FFN)).astype(BF16)
    fn_ref[...] = ffn_normed
    copies[1].wait()
    copies[2].wait()
    hidden = inner_ref.shape[1]
    total = jnp.zeros(branch_ref.shape, F32)
    for start in range(0, hidden, HIDDEN_BLOCK):
        gate_cols = slice(start, start + HIDDEN_BLOCK)
        up_cols = slice(hidden + start, hidden + start + HIDDEN_BLOCK)
        gate = dot(ffn_normed, weight_rows(wi_ref, start, HIDDEN_BLOCK), 1, 1)
        up = dot(ffn_normed, weight_rows(wi_ref, hidden + start, HIDDEN_BLOCK), 1, 1)
        gu_ref[:, gate_cols] = gate.astype(BF16)
        gu_ref[:, up_cols] = up.astype(BF16)
        inner = (gelu_parts(gate)[1] * up).astype(BF16)
        inner_ref[:, gate_cols] = inner
        total += dot(inner, weight_rows(wo_ref, start, HIDDEN_BLOCK), 1, 0)
    fb_ref[...] = total
    result_ref[...] = middle + rms_norm(total, gain_of(gains_ref, POST_FFN))


def forward_layer(stream, weights, gains, tables, reach, count):
    tokens = stream.shape[0]
    cosine_tab, sine_tab = tables
    attn_in, attn_out, ffn_in, ffn_out = weights
    hidden = ffn_out[0].shape[0] * ffn_out[2]
    normed, key_raw, own = call(
        partial(key_value_kernel, [attn_in]), "key_value",
        (stream, gains, cosine_tab, sine_tab), [attn_in],
        [((tokens, D), BF16), ((tokens, HEAD_DIM), F32), ((tokens, 2 * HEAD_DIM), BF16)],
        4 * tokens * D * HEAD_DIM,
    )
    before = neighbour(own, count, False)
    query_raw, queries = call(
        partial(query_kernel, [attn_in]), "query",
        (normed, gains, cosine_tab, sine_tab), [attn_in],
        [((tokens, QUERY_COLS), F32), ((tokens, QUERY_COLS), BF16)],
        2 * tokens * D * QUERY_COLS,
    )
    context, lse, branch, middle, ffn_normed, gate_up, inner, ffn_branch, result = call(
        partial(block_kernel, [attn_out, ffn_in, ffn_out]), "block_forward",
        (queries, before, own, reach, stream, gains), [attn_out, ffn_in, ffn_out],
        [
            ((tokens, QUERY_COLS), BF16), (reach.shape, F32), ((tokens, D), F32), ((tokens, D), F32),
            ((tokens, D), BF16), ((tokens, 2 * hidden), BF16), ((tokens, hidden), BF16),
            ((tokens, D), F32), ((tokens, D), F32),
        ],
        2 * tokens * (D * (QUERY_COLS + 3 * hidden) + 2 * QUERY_COLS * KEY_COUNT),
    )
    record = (
        stream, normed, query_raw, key_raw, queries, before, own, lse, context,
        branch, middle, ffn_normed, gate_up, inner, ffn_branch,
    )
    return record, result


def block_backward_kernel(
    weights, grad_ref, fb_ref, gu_ref, middle_ref, branch_ref, gains_ref, wa_any, wi_any, wo_any,
    gfb_ref, ggu_ref, gb_ref, gctx_ref, gmid_ref, sums_ref,
    wa_ref, wi_ref, wo_ref, sem,
):
    copies = [
        fetch(weight, source, target, sem.at[i])
        for i, (weight, source, target) in enumerate(
            zip(weights, (wa_any, wi_any, wo_any), (wa_ref, wi_ref, wo_ref))
        )
    ]
    grad_out = grad_ref[...]
    grad_ffn_branch, post_ffn = rms_backward(fb_ref[...], gain_of(gains_ref, POST_FFN), grad_out)
    grad_ffn_branch = grad_ffn_branch.astype(BF16)
    gfb_ref[...] = grad_ffn_branch
    copies[2].wait()
    copies[1].wait()
    hidden = gu_ref.shape[1] // 2
    total = jnp.zeros(grad_ref.shape, F32)
    for start in range(0, hidden, HIDDEN_BLOCK):
        gate_cols = slice(start, start + HIDDEN_BLOCK)
        up_cols = slice(hidden + start, hidden + start + HIDDEN_BLOCK)
        grad_inner = dot(grad_ffn_branch, weight_rows(wo_ref, start, HIDDEN_BLOCK), 1, 1)
        gate = gu_ref[:, gate_cols].astype(F32)
        up = gu_ref[:, up_cols].astype(F32)
        tanh, value = gelu_parts(gate)
        slope = 0.5 * (1.0 + tanh) + 0.5 * gate * (1.0 - tanh * tanh) * GELU_A * (
            1.0 + 3.0 * GELU_B * gate * gate
        )
        grad_gate = (grad_inner * up * slope).astype(BF16)
        grad_up = (grad_inner * value).astype(BF16)
        ggu_ref[:, gate_cols] = grad_gate
        ggu_ref[:, up_cols] = grad_up
        total += dot(grad_gate, weight_rows(wi_ref, start, HIDDEN_BLOCK), 1, 0)
        total += dot(grad_up, weight_rows(wi_ref, hidden + start, HIDDEN_BLOCK), 1, 0)
    grad_part, pre_ffn = rms_backward(middle_ref[...], gain_of(gains_ref, PRE_FFN), total)
    grad_middle = grad_out + grad_part
    gmid_ref[...] = grad_middle
    grad_branch, post_attn = rms_backward(branch_ref[...], gain_of(gains_ref, POST_ATTN), grad_middle)
    grad_branch = grad_branch.astype(BF16)
    gb_ref[...] = grad_branch
    sums_ref[0:1, :] = post_attn
    sums_ref[1:2, :] = pre_ffn
    sums_ref[2:3, :] = post_ffn
    copies[0].wait()
    gctx_ref[...] = dot(grad_branch, weight_rows(wa_ref, 0, QUERY_COLS), 1, 1).astype(BF16)


def attention_backward_kernel(
    q_ref, before_ref, own_ref, reach_ref, lse_ref, g_ref, dq_ref, gbefore_ref, gown_ref, acc
):
    acc[...] = jnp.zeros_like(acc)
    for block in range(q_ref.shape[0] // QUERY_BLOCK):
        start = block * QUERY_BLOCK
        queries = stacked_heads(q_ref, start)
        grads = stacked_heads(g_ref, start)
        keys = window_rows(before_ref, own_ref, start, KEY_COUNT, KEYS)
        values = window_rows(before_ref, own_ref, start, KEY_COUNT, VALUES)
        allowed = allowed_pairs(start, KEY_COUNT, reach_ref[block : block + 1, :], HEADS * QUERY_BLOCK)
        scores = jnp.where(allowed, dot(keys, queries, 1, 1), MASKED_SCORE)
        probs = jnp.exp(scores - lse_ref[block : block + 1, :])
        grad_probs = dot(values, grads, 1, 1)
        inner = jnp.sum(probs * grad_probs, axis=0, keepdims=True)
        grad_scores = (probs * (grad_probs - inner)).astype(BF16)
        acc[start : start + KEY_COUNT, VALUES] += dot(probs.astype(BF16), grads, 1, 0)
        acc[start : start + KEY_COUNT, KEYS] += dot(grad_scores, queries, 1, 0)
        grad_queries = dot(grad_scores, keys, 0, 0) * SCORE_SCALE
        for h in range(HEADS):
            dq_ref[start : start + QUERY_BLOCK, h * HEAD_DIM : (h + 1) * HEAD_DIM] = grad_queries[
                h * QUERY_BLOCK : (h + 1) * QUERY_BLOCK
            ]
    gbefore_ref[...] = acc[:WINDOW, :].astype(BF16)
    gown_ref[...] = acc[WINDOW:, :]


def query_backward_kernel(dq_ref, raw_ref, gains_ref, cos_ref, sin_ref, gq_ref, sums_ref):
    cosine_tab, sine_tab = cos_ref[...], sin_ref[...]
    sums = jnp.zeros((1, HEAD_DIM), F32)
    for h in range(HEADS):
        columns = slice(h * HEAD_DIM, (h + 1) * HEAD_DIM)
        grad = rotate_back(dq_ref[:, columns], cosine_tab, sine_tab)
        grad, part = rms_backward(raw_ref[:, columns], gain_of(gains_ref, QUERY_GAIN), grad)
        gq_ref[:, columns] = grad.astype(BF16)
        sums += part
    sums_ref[...] = sums


def input_backward_kernel(
    weights, gq_ref, gown_ref, got_ref, kraw_ref, gmid_ref, stream_ref, gains_ref, cos_ref, sin_ref, w_any,
    gproj_ref, gin_ref, sums_ref, key_sums_ref, w_ref, sem,
):
    copy = fetch(weights[0], w_any, w_ref, sem.at[0])
    total = gown_ref[...] + got_ref[...].astype(F32)
    grad_keys = rotate_back(total[:, KEYS], cos_ref[...], sin_ref[...])
    grad_keys, key_sums = rms_backward(kraw_ref[...], gain_of(gains_ref, KEY_GAIN), grad_keys)
    gproj_ref[:, :QUERY_COLS] = gq_ref[...]
    gproj_ref[:, QUERY_COLS : QUERY_COLS + HEAD_DIM] = grad_keys.astype(BF16)
    gproj_ref[:, QUERY_COLS + HEAD_DIM :] = total[:, VALUES].astype(BF16)
    key_sums_ref[...] = key_sums
    copy.wait()
    grad_normed = dot(gproj_ref[...], weight_rows(w_ref, 0, QUERY_COLS + 2 * HEAD_DIM), 1, 0)
    grad_part, sums = rms_backward(stream_ref[...], gain_of(gains_ref, PRE_ATTN), grad_normed)
    gin_ref[...] = gmid_ref[...] + grad_part
    sums_ref[...] = sums


def backward_layer(grad_out, weights, gains, record, tables, reach, count, pump, chains):
    attn_in, attn_out, ffn_in, ffn_out = weights
    cosine_tab, sine_tab = tables
    (
        stream, normed, query_raw, key_raw, queries, before, own, lse, context,
        branch, middle, ffn_normed, gate_up, inner, ffn_branch,
    ) = record
    tokens = stream.shape[0]
    hidden = inner.shape[1]
    grad_out = pump(0, grad_out)
    grad_ffn_branch, grad_gate_up, grad_branch, grad_context, grad_middle, sums = call(
        partial(block_backward_kernel, [attn_out, ffn_in, ffn_out]), "block_backward",
        (grad_out, ffn_branch, gate_up, middle, branch, gains), [attn_out, ffn_in, ffn_out],
        [
            ((tokens, D), BF16), ((tokens, 2 * hidden), BF16), ((tokens, D), BF16),
            ((tokens, QUERY_COLS), BF16), ((tokens, D), F32), ((8, D), F32),
        ],
        2 * tokens * D * (QUERY_COLS + 3 * hidden),
    )
    chains["ffn_in"] = Chain(grad_gate_up, ffn_normed, "dp")
    chains["ffn_out"] = Chain(inner, grad_ffn_branch, "seq")
    chains["attn_out"] = Chain(context, grad_branch, "seq")
    grad_context = pump(1, grad_context)
    grad_queries, grad_before, grad_own = call(
        attention_backward_kernel, "attention_backward",
        (queries, before, own, reach, lse, grad_context), [],
        [((tokens, QUERY_COLS), F32), ((WINDOW, 2 * HEAD_DIM), BF16), ((tokens, 2 * HEAD_DIM), F32)],
        10 * tokens * QUERY_COLS * KEY_COUNT,
        [pltpu.VMEM((WINDOW + tokens, 2 * HEAD_DIM), F32)],
    )
    got = neighbour(grad_before, count, True)
    grad_queries = pump(2, grad_queries)
    grad_query_raw, query_sums = call(
        query_backward_kernel, "query_backward",
        (grad_queries, query_raw, gains, cosine_tab, sine_tab), [],
        [((tokens, QUERY_COLS), BF16), ((1, HEAD_DIM), F32)],
        20 * tokens * QUERY_COLS,
    )
    grad_query_raw = pump(3, grad_query_raw)
    grad_projected, grad_in, pre_sums, key_sums = call(
        partial(input_backward_kernel, [attn_in]), "input_backward",
        (grad_query_raw, grad_own, got, key_raw, grad_middle, stream, gains, cosine_tab, sine_tab),
        [attn_in],
        [
            ((tokens, QUERY_COLS + 2 * HEAD_DIM), BF16), ((tokens, D), F32), ((1, D), F32),
            ((1, HEAD_DIM), F32),
        ],
        2 * tokens * D * (QUERY_COLS + 2 * HEAD_DIM),
    )
    chains["attn_in"] = Chain(grad_projected, normed, "dp")
    grad_gain_row = jnp.concatenate(
        [pre_sums[0], sums[0], sums[1], sums[2], query_sums[0], key_sums[0]]
    )
    return grad_in, grad_gain_row


PLAN = {
    0: [(1, "attn_out"), (1, "ffn_out"), (1, "attn_in")],
    1: [(0, "ffn_in"), (0, "ffn_out"), (1, "ffn_in"), (1, "attn_in"), (1, "attn_out")],
    2: [(0, "attn_out"), (1, "ffn_out"), (1, "attn_in"), (1, "attn_out")],
    3: [(0, "ffn_out"), (1, "ffn_in"), (1, "attn_out")],
}


def gather_weights(w_attn_in, w_attn_out, w_ffn_in, w_ffn_out, gains):
    layers = w_attn_in.shape[0]
    kinds = [w_ffn_in.transpose(0, 2, 1), w_ffn_out, w_attn_in.transpose(0, 2, 1), w_attn_out]
    gain_rows = jnp.pad(gains, ((0, 16 - layers), (0, D - gains.shape[1])))
    packed = jnp.concatenate([kind.reshape(-1, D) for kind in kinds] + [gain_rows], axis=0)
    whole = lax.all_gather(packed, ALL, axis=0, tiled=False)
    out, at = [[] for _ in range(layers)], 0
    for kind in kinds:
        for layer in range(layers):
            out[layer].append((at, kind.shape[1]))
            at += kind.shape[1]
    gain_full = whole[:, at : at + layers, : gains.shape[1]].astype(F32)

    def of(layer):
        found = []
        for start, size in out[layer]:
            if size % TILE:
                found.append((whole[:, start : start + size].reshape(1, -1, D), 0, size * whole.shape[0]))
            else:
                found.append((whole, start, size))
        ffn_in, ffn_out, attn_in, attn_out = found
        return (attn_in, attn_out, ffn_in, ffn_out), gain_full[:, layer].reshape(1, -1)

    return of


def body(hidden_in, positions, out_grad, w_attn_in, w_attn_out, w_ffn_in, w_ffn_out, gains):
    count = hidden_in.shape[0]
    layer_count = w_attn_in.shape[0]
    layer_weights = gather_weights(w_attn_in, w_attn_out, w_ffn_in, w_ffn_out, gains)
    places = to_long(positions)
    stream = to_long(hidden_in).astype(F32)
    grad_stream = to_long(out_grad).astype(F32)
    tables = angle_tables(places)
    tokens = places.shape[0]
    blocks = tokens // QUERY_BLOCK
    reach = jnp.minimum(places, WINDOW - 1).reshape(blocks, QUERY_BLOCK)
    reach = jnp.tile(reach, (1, HEADS))
    records, weights = [], []
    for layer_index in range(layer_count):
        weights.append(layer_weights(layer_index))
        record, stream = forward_layer(stream, *weights[-1], tables, reach, count)
        records.append(record)
    hidden_out = to_short(stream.astype(BF16), count)
    gain_grads = [None] * layer_count
    chains = [{} for _ in range(layer_count + 1)]
    for layer_index in reversed(range(layer_count)):

        def pump(where, value):
            active = [
                chains[layer_index + above][name]
                for above, name in PLAN[where]
                if name in chains[layer_index + above]
            ]
            return advance(value, [chain for chain in active if chain.steps])

        grad_stream, gain_grads[layer_index] = backward_layer(
            grad_stream, *weights[layer_index], records[layer_index], tables, reach, count, pump,
            chains[layer_index],
        )
    input_grad = to_short(grad_stream.astype(BF16), count).astype(F32)
    devices = lax.axis_size("dp") * lax.axis_size("seq")
    gain_grads = halving(jnp.stack([entry.reshape(devices, -1) for entry in gain_grads], axis=1))
    members = {
        name: jnp.stack([chains[layer][name].finish() for layer in range(layer_count)])
        for name in chains[0]
    }
    return (
        hidden_out,
        input_grad,
        members["attn_in"].transpose(0, 2, 1),
        members["attn_out"],
        members["ffn_in"].transpose(0, 2, 1),
        members["ffn_out"],
        gain_grads,
    )


def solution(mesh):
    return jax.shard_map(
        body,
        mesh=mesh,
        in_specs=(
            P("dp", "seq", None),
            P("dp", "seq"),
            P("dp", "seq", None),
            P(None, None, ("dp", "seq")),
            P(None, ("dp", "seq"), None),
            P(None, None, ("dp", "seq")),
            P(None, ("dp", "seq"), None),
            P(None, ("dp", "seq")),
        ),
        out_specs=(
            P("dp", "seq", None),
            P("dp", "seq", None),
            P(None, None, ("dp", "seq")),
            P(None, ("dp", "seq"), None),
            P(None, None, ("dp", "seq")),
            P(None, ("dp", "seq"), None),
            P(None, ("dp", "seq")),
        ),
        check_vma=False,
    )
```

time: 723 us -> 596 us (0.82)
  Pallas kernels: 18.7 us -> 151 us
  matrix products: 82.3 us -> 0 us
  waiting for transfers between devices: 325 us -> 249 us
  local copies, waits for them, and re-layouts: 93.3 us -> 58.7 us
  starting transfers between devices: 121 us -> 86.8 us
  other arithmetic: 56.3 us -> 27.7 us
    pallas_call x4 -> x34, Pallas kernels: 18.7 us -> 151 us  [the longest x14 97.5 us: call(): pl.pallas_call(kernel, out_shape=tuple(outs), in_specs=vmem(len(arrays))...]
    dot_general x26 -> x0, matrix products: 82.3 us -> none  [dot(): lax.dot_general(a, b, (((a_dim,), (b_dim,)), ((), ())), preferred_element...]
    ppermute x69, waiting for transfers between devices: 192 us -> 123 us  [the longest x45 105 us: swap(): lax.ppermute(array, axis, [(i, i ^ bit) for i in range(lax.axis_size(axis...]
    ppermute x69, starting transfers between devices: 121 us -> 86.8 us  [the longest x45 56.5 us: swap(): lax.ppermute(array, axis, [(i, i ^ bit) for i in range(lax.axis_size(axis...]
    slice x23 -> x11, local copies, waits for them, and re-layouts: 33.4 us -> 6.84 us  [the longest x4 3.25 us: send(): self.keep = lax.index_in_dim(array, 0, at, keepdims=False)]
    unnamed x392 -> x323, local copies, waits for them, and re-layouts: 34.4 us -> 43.8 us
    squeeze x45 -> x23, local copies, waits for them, and re-layouts: 13.6 us -> 4.71 us  [the longest x18 3.83 us: send(): self.got = swap(lax.index_in_dim(array, 1, at, keepdims=False), step)]
    reduce_sum x14 -> x0, other arithmetic: 7.37 us -> none  [the longest x8 5.62 us: rms_norm(): values * lax.rsqrt(jnp.mean(values * values, axis=-1, keepdims=True) + EP...]
  transfers between devices with their start and end apart: 71 -> 70, of which waited for: 38 -> 29; matrix products, arithmetic and copies ran while one was open for 17% -> 9% of each run, Pallas kernels for 2% -> 12%
where the time goes in v2:
time: 596 us; the launch traced here: 590 us
  waiting for transfers between devices  249 us (42%)
  Pallas kernels  151 us (25%)
  starting transfers between devices  86.8 us (15%)
  local copies, waits for them, and re-layouts  58.7 us (10%)
  other arithmetic  27.7 us (5%)
  between operations  16.8 us (3%)
    all_gather x1, waiting for transfers between devices, gather_weights(): whole = lax.all_gather(packed, ALL, axis=0, tiled=False)  126 us
    ppermute x45, waiting for transfers between devices, swap(): lax.ppermute(array, axis, [(i, i ^ bit) for i in range(lax.axis_size(axis...  105 us
    pallas_call x14, Pallas kernels, call(): pl.pallas_call(kernel, out_shape=tuple(outs), in_specs=vmem(len(arrays))...  97.5 us
    ppermute x45, starting transfers between devices, swap(): lax.ppermute(array, axis, [(i, i ^ bit) for i in range(lax.axis_size(axis...  56.5 us
    pallas_call x20, Pallas kernels, product(): pl.pallas_call(partial(product_kernel, rows, split, got is not None), gri...  53.6 us
    unnamed x323, local copies, waits for them, and re-layouts  43.8 us
    ppermute x12, waiting for transfers between devices, to_long(): received.append(lax.ppermute(piece, ALL, chunk_route(count, k)))  18.1 us
    ppermute x12, starting transfers between devices, to_long(): received.append(lax.ppermute(piece, ALL, chunk_route(count, k)))  15.1 us
  transfers between devices with their start and end apart: 70, of which 29 were waited for; matrix products, arithmetic and copies ran while one was open for 9% of the time, Pallas kernels for 12%

profile of v2, /device:TPU:0, one launch (start us, length us, event | category | flops | bytes accessed | tf_op | source)
XLA Modules:
  0.0 589.9 jit_solution(9305526457464817752)
XLA Ops:
  9.8 4.0 collective-permute-start
  17.5 2.5 collective-permute-start.1
  29.2 2.5 collective-permute-done.14
  31.6 9.5 %collective-permute-done.15 = bf16[128,640]{1,0:T(8,128)(2,1)S(1)} collective-permute-done((bf16[128,640]{1,0:T(8,128)(2,1)S(1)}, bf16[128,640]{1,0:T(8,128)(2,1)S(1)}, u32[]{:S(2)}, u32[]{:S(2)}) %collective-permute-start.15) | collective-permute-done | bytes 163872 | tf_op jit(solution)/shard_map/ppermute | solution.py:147
  41.2 4.0 collective-permute-done.16
  47.1 125.8 %all-gather.3.cloned.1.call-done = bf16[17920,640]{1,0:T(8,128)(2,1)} async-done(((bf16[560,640]{1,0:T(8,128)(2,1)}), bf16[17920,640]{1,0:T(8,128)(2,1)}) %all-gather.3.cloned.1.call-update) | async-done | bytes 22937616 | tf_op jit(solution)/shard_map/all_gather | solution.py:660
  174.5 2.4 key_value.2
  177.7 3.1 collective-permute-start.8
  183.1 2.9 query.2
  187.3 16.2 %block_forward.2 = (bf16[512,1024]{1,0:T(8,128)(2,1)S(1)}, f32[2,1024]{1,0:T(2,128)S(1)}, f32[512,640]{1,0:T(8,128)S(1)}, f32[512,640]{1,0:T(8,128)S(1)}, bf16[5...) custom-call(bf16[512,1024]{1,0:T(8,128)(2,1)S(1)} %get-tuple-element, ...), custom_call_target="tpu_custom_call" | custom-call | flops 6308233216 | bytes 16674816 | tf_op jit(solution)/shard_map/block_forward/pallas_call | solution.py:106
  205.6 4.0 key_value.3
  211.6 2.9 query.3
  215.9 14.6 %block_forward.3 = (bf16[512,1024]{1,0:T(8,128)(2,1)S(1)}, f32[2,1024]{1,0:T(2,128)S(1)}, f32[512,640]{1,0:T(8,128)S(1)}, f32[512,640]{1,0:T(8,128)S(1)}, bf16[5...) custom-call(bf16[512,1024]{1,0:T(8,128)(2,1)S(1)} %get-tuple-element, ...), custom_call_target="tpu_custom_call" | custom-call | flops 6308233216 | bytes 16674816 | tf_op jit(solution)/shard_map/block_forward/pallas_call | solution.py:106
  232.3 16.7 %block_backward.2 = (bf16[512,640]{1,0:T(8,128)(2,1)S(1)}, bf16[512,4096]{1,0:T(8,128)(2,1)}, bf16[512,640]{1,0:T(8,128)(2,1)S(1)}, bf16[512,1024]{1,0:T(8,128)(...) custom-call(f32[512,640]{1,0:T(8,128)S(1)} %bitcast_convert_fusion.grad_ref, ...), custom_call_target="tpu_custom_call" | custom-call | flops 4697620480 | bytes 17334272 | tf_op jit(solution)/shard_map/block_backward/pallas_call | solution.py:106
  249.1 3.2 copy-done
  252.4 4.1 weight_gradient.20
  256.6 2.9 weight_gradient.21
  265.9 3.4 collective-permute-start.20
  269.4 3.5 weight_gradient.23
  274.4 5.2 attention_backward.2
  282.4 2.0 collective-permute-start.13
  289.7 2.0 collective-permute-done.21
  291.7 3.4 input_backward.2
  300.5 8.1 %collective-permute-done.24 = bf16[2,2,64,640]{3,2,1,0:T(8,128)(2,1)S(1)} collective-permute-done((bf16[2,2,64,640]{3,2,1,0:T(8,128)(2,1)S(1)}, bf16[2,2,64,640]{3,2,1,0:T(8,128)(2,1)S(1)}, u32[]{:S(2)}, u32[]{:S(2)}) %collective-permute-start.24) | collective-permute-done | bytes 327712 | tf_op jit(solution)/shard_map/ppermute | solution.py:198
  309.7 16.6 %block_backward.3 = (bf16[512,640]{1,0:T(8,128)(2,1)S(1)}, bf16[512,4096]{1,0:T(8,128)(2,1)}, bf16[512,640]{1,0:T(8,128)(2,1)S(1)}, bf16[512,1024]{1,0:T(8,128)(...) custom-call(f32[512,640]{1,0:T(8,128)S(1)} %get-tuple-element.138.grad_ref, f32[512,640]{1,0:T(8,128)S(1)} %copy-done.54, ...), custom_call_target="tpu_custom_call" | custom-call | flops 4697620480 | bytes 17334272 | tf_op jit(solution)/shard_map/block_backward/pallas_call | solution.py:106
  326.4 3.5 copy-done.2
  329.9 4.6 weight_gradient.26
  335.6 4.2 weight_gradient.28
  341.4 3.2 weight_gradient.33
  348.4 2.9 weight_gradient.27
  360.3 2.2 weight_gradient.30
  363.1 8.7 %collective-permute-done.28 = bf16[1,8,128,640]{3,2,1,0:T(8,128)(2,1)} collective-permute-done((bf16[1,8,128,640]{3,2,1,0:T(8,128)(2,1)}, bf16[1,8,128,640]{3,2,1,0:T(8,128)(2,1)}, u32[]{:S(2)}, u32[]{:S(2)}) %collective-permute-start.28) | collective-permute-done | bytes 1310752 | tf_op jit(solution)/shard_map/ppermute | solution.py:198
  371.8 13.5 %collective-permute-done.30 = bf16[2,2,32,640]{3,2,1,0:T(8,128)(2,1)S(1)} collective-permute-done((bf16[2,2,32,640]{3,2,1,0:T(8,128)(2,1)S(1)}, bf16[2,2,32,640]{3,2,1,0:T(8,128)(2,1)S(1)}, u32[]{:S(2)}, u32[]{:S(2)}) %collective-permute-start.30) | collective-permute-done | bytes 163872 | tf_op jit(solution)/shard_map/ppermute | solution.py:198
  385.4 3.3 collective-permute-start.32
  390.5 4.1 weight_gradient.32
  397.4 6.3 %attention_backward.3 = (f32[512,1024]{1,0:T(8,128)S(1)}, bf16[512,512]{1,0:T(8,128)(2,1)S(1)}, f32[512,512]{1,0:T(8,128)S(1)}) custom-call(bf16[512,1024]{1,0:T(8,128)(2,1)S(1)} %copy-done.56, bf16[512,512]{1,0:T(8,128)(2,1)} %collective-permute-done.8.before_ref, bf16[512,512]{1,0:T(8,128)(2,1)S(1)} %copy-done.69, s32[2,1024]{1,0:T(2,128)S(1)} %bitcast.335, ...), custom_call_target="tpu_custom_call" | custom-call | flops 4026531840 | bytes 6832128 | tf_op jit(solution)/shard_map/attention_backward/pallas_call | solution.py:106
  403.8 2.8 add_convert_fusion.1
  408.6 4.3 weight_gradient.39
  412.8 2.2 copy.53
  415.0 2.2 copy.59
  417.2 2.2 copy-done.4
  419.4 3.5 weight_gradient.38
  426.5 2.8 collective-permute-start.48
  436.0 2.0 collective-permute-start.63
  438.1 3.1 collective-permute-done.63
  452.3 3.4 input_backward.3
  460.3 4.2 collective-permute-start.64
  468.3 11.0 %collective-permute-done.65 = f32[2,2,2,2,96]{4,2,1,0,3:T(2,128)S(1)} collective-permute-done((f32[2,2,2,2,96]{4,2,1,0,3:T(2,128)S(1)}, f32[2,2,2,2,96]{4,2,1,0,3:T(2,128)S(1)}, u32[]{:S(2)}, u32[]{:S(2)}) %collective-permute-start.65) | collective-permute-done | bytes 6176 | tf_op jit(solution)/shard_map/ppermute | solution.py:198
  480.5 2.5 collective-permute-done.66
  484.5 2.9 collective-permute-done.67
  489.1 2.6 weight_gradient.34
  496.2 3.1 collective-permute-start.52
  500.2 6.2 %collective-permute-done.52 = bf16[2,32,640]{2,1,0:T(8,128)(2,1)S(1)} collective-permute-done((bf16[2,32,640]{2,1,0:T(8,128)(2,1)S(1)}, bf16[2,32,640]{2,1,0:T(8,128)(2,1)S(1)}, u32[]{:S(2)}, u32[]{:S(2)}) %collective-permute-start.52) | collective-permute-done | bytes 81952 | tf_op jit(solution)/shard_map/ppermute | solution.py:198
  514.4 3.5 collective-permute-start.61
  517.9 8.3 %collective-permute-done.58 = bf16[2,128,640]{1,2,0:T(8,128)(2,1)S(1)} collective-permute-done((bf16[2,128,640]{1,2,0:T(8,128)(2,1)S(1)}, bf16[2,128,640]{1,2,0:T(8,128)(2,1)S(1)}, u32[]{:S(2)}, u32[]{:S(2)}) %collective-permute-start.58) | collective-permute-done | bytes 327712 | tf_op jit(solution)/shard_map/ppermute | solution.py:198
  527.0 2.1 collective-permute-done.61
  532.7 2.2 copy.58
  539.4 2.4 collective-permute-done.62
  543.5 2.2 copy.57
  549.0 2.3 collective-permute-done.55
  552.7 5.3 collective-permute-done.44
  559.1 9.4 %collective-permute-done.56 = bf16[2,128,640]{1,2,0:T(8,128)(2,1)S(1)} collective-permute-done((bf16[2,128,640]{1,2,0:T(8,128)(2,1)S(1)}, bf16[2,128,640]{1,2,0:T(8,128)(2,1)S(1)}, u32[]{:S(2)}, u32[]{:S(2)}) %collective-permute-start.56) | collective-permute-done | bytes 327712 | tf_op jit(solution)/shard_map/ppermute | solution.py:198
  570.9 6.1 %collective-permute-done.57 = bf16[128,640]{0,1:T(8,128)(2,1)S(1)} collective-permute-done((bf16[128,640]{0,1:T(8,128)(2,1)S(1)}, bf16[128,640]{0,1:T(8,128)(2,1)S(1)}, u32[]{:S(2)}, u32[]{:S(2)}) %collective-permute-start.57) | collective-permute-done | bytes 163872 | tf_op jit(solution)/shard_map/ppermute | solution.py:198
  578.8 3.3 collective-permute-done.47
  (549 shorter events, 142.5 us)
Async XLA Ops:
  7.2 165.7 %all-gather.3.cloned.1.call-start = ((), (), s32[]{:S(2)}) async-start(), calls=%async_computation | async-start | bytes 23654400 | tf_op jit(solution)/shard_map/all_gather | solution.py:660
  9.8 15.5 %collective-permute-start = (bf16[128,640]{1,0:T(8,128)(2,1)S(1)}, bf16[128,640]{1,0:T(8,128)(2,1)S(1)}, u32[]{:S(2)}, u32[]{:S(2)}) collective-permute-start(bf16[128,640]{1,0:T(8,128)(2,1)S(1)} %get-tuple-element.221), channel_id=1, source_target_pairs={{0,3},{1,0},{2,1},{3,2},{4,11},{5,8},{6,9},{7,10},{8,7},{9,4},{10,... | collective-permute-start | bytes 491528 | tf_op jit(solution)/shard_map/ppermute | solution.py:147
  14.4 5.6 collective-permute-start.5
  14.4 7.5 %collective-permute-start.6 = (s32[128]{0:T(128)S(1)}, s32[128]{0:T(128)S(1)}, u32[]{:S(2)}, u32[]{:S(2)}) collective-permute-start(s32[128]{0:T(128)S(1)} %get-tuple-element.238), channel_id=1, source_target_pairs={{0,1},{1,2},{2,3},{3,0},{4,9},{5,10},{6,11},{7,8},{8,5},{9,6},{10,... | collective-permute-start | bytes 1544 | tf_op jit(solution)/shard_map/ppermute | solution.py:147
  16.4 6.2 %collective-permute-start.7 = (s32[128]{0:T(128)S(1)}, s32[128]{0:T(128)S(1)}, u32[]{:S(2)}, u32[]{:S(2)}) collective-permute-start(s32[128]{0:T(128)S(1)} %get-tuple-element.235), channel_id=1, source_target_pairs={{0,0},{1,1},{2,2},{3,3},{4,8},{5,9},{6,10},{7,11},{8,4},{9,5},{10,... | collective-permute-start | bytes 1544 | tf_op jit(solution)/shard_map/ppermute | solution.py:147
  17.5 8.4 %collective-permute-start.1 = (bf16[128,640]{1,0:T(8,128)(2,1)S(1)}, bf16[128,640]{1,0:T(8,128)(2,1)S(1)}, u32[]{:S(2)}, u32[]{:S(2)}) collective-permute-start(bf16[128,640]{1,0:T(8,128)(2,1)S(1)} %get-tuple-element.220), channel_id=1, source_target_pairs={{0,2},{1,3},{2,0},{3,1},{4,10},{5,11},{6,8},{7,9},{8,6},{9,7},{10,... | collective-permute-start | bytes 491528 | tf_op jit(solution)/shard_map/ppermute | solution.py:147
  20.0 8.3 %collective-permute-start.2 = (bf16[128,640]{1,0:T(8,128)(2,1)S(1)}, bf16[128,640]{1,0:T(8,128)(2,1)S(1)}, u32[]{:S(2)}, u32[]{:S(2)}) collective-permute-start(bf16[128,640]{1,0:T(8,128)(2,1)S(1)} %get-tuple-element.222), channel_id=1, source_target_pairs={{0,1},{1,2},{2,3},{3,0},{4,9},{5,10},{6,11},{7,8},{8,5},{9,6},{10,... | collective-permute-start | bytes 491528 | tf_op jit(solution)/shard_map/ppermute | solution.py:147
  21.9 7.2 %collective-permute-start.3 = (bf16[128,640]{1,0:T(8,128)(2,1)S(1)}, bf16[128,640]{1,0:T(8,128)(2,1)S(1)}, u32[]{:S(2)}, u32[]{:S(2)}) collective-permute-start(bf16[128,640]{1,0:T(8,128)(2,1)S(1)} %get-tuple-element.219), channel_id=1, source_target_pairs={{0,0},{1,1},{2,2},{3,3},{4,8},{5,9},{6,10},{7,11},{8,4},{9,5},{10,... | collective-permute-start | bytes 491528 | tf_op jit(solution)/shard_map/ppermute | solution.py:147
  22.5 9.1 %collective-permute-start.14 = (bf16[128,640]{1,0:T(8,128)(2,1)S(1)}, bf16[128,640]{1,0:T(8,128)(2,1)S(1)}, u32[]{:S(2)}, u32[]{:S(2)}) collective-permute-start(bf16[128,640]{1,0:T(8,128)(2,1)S(1)} %get-tuple-element.213), channel_id=1, source_target_pairs={{0,3},{1,0},{2,1},{3,2},{4,11},{5,8},{6,9},{7,10},{8,7},{9,4},{10,... | collective-permute-start | bytes 491528 | tf_op jit(solution)/shard_map/ppermute | solution.py:147
  25.3 15.9 %collective-permute-start.15 = (bf16[128,640]{1,0:T(8,128)(2,1)S(1)}, bf16[128,640]{1,0:T(8,128)(2,1)S(1)}, u32[]{:S(2)}, u32[]{:S(2)}) collective-permute-start(bf16[128,640]{1,0:T(8,128)(2,1)S(1)} %get-tuple-element.212), channel_id=1, source_target_pairs={{0,2},{1,3},{2,0},{3,1},{4,10},{5,11},{6,8},{7,9},{8,6},{9,7},{10,... | collective-permute-start | bytes 491528 | tf_op jit(solution)/shard_map/ppermute | solution.py:147
  25.8 19.4 %collective-permute-start.16 = (bf16[128,640]{1,0:T(8,128)(2,1)S(1)}, bf16[128,640]{1,0:T(8,128)(2,1)S(1)}, u32[]{:S(2)}, u32[]{:S(2)}) collective-permute-start(bf16[128,640]{1,0:T(8,128)(2,1)S(1)} %get-tuple-element.214), channel_id=1, source_target_pairs={{0,1},{1,2},{2,3},{3,0},{4,9},{5,10},{6,11},{7,8},{8,5},{9,6},{10,... | collective-permute-start | bytes 491528 | tf_op jit(solution)/shard_map/ppermute | solution.py:147
  28.3 17.0 %collective-permute-start.17 = (bf16[128,640]{1,0:T(8,128)(2,1)S(1)}, bf16[128,640]{1,0:T(8,128)(2,1)S(1)}, u32[]{:S(2)}, u32[]{:S(2)}) collective-permute-start(bf16[128,640]{1,0:T(8,128)(2,1)S(1)} %get-tuple-element.211), channel_id=1, source_target_pairs={{0,0},{1,1},{2,2},{3,3},{4,8},{5,9},{6,10},{7,11},{8,4},{9,5},{10,... | collective-permute-start | bytes 491528 | tf_op jit(solution)/shard_map/ppermute | solution.py:147
  177.7 9.6 %collective-permute-start.8 = (bf16[512,512]{1,0:T(8,128)(2,1)S(1)}, bf16[512,512]{1,0:T(8,128)(2,1)}, u32[]{:S(2)}, u32[]{:S(2)}) collective-permute-start(bf16[512,512]{1,0:T(8,128)(2,1)S(1)} %get-tuple-element.101.own_ref), channel_id=1, source_target_pairs={{0,8},{1,9},{2,10},{3,11},{4,12},{5,13},{6,14},{7,15},{16,24},{17,... | collective-permute-start | bytes 1572872 | tf_op jit(solution)/shard_map/ppermute | solution.py:177
  209.8 6.1 %collective-permute-start.9 = (bf16[512,512]{1,0:T(8,128)(2,1)S(1)}, bf16[512,512]{1,0:T(8,128)(2,1)S(1)}, u32[]{:S(2)}, u32[]{:S(2)}) collective-permute-start(bf16[512,512]{1,0:T(8,128)(2,1)S(1)} %get-tuple-element.105.own_ref), channel_id=1, source_target_pairs={{0,8},{1,9},{2,10},{3,11},{4,12},{5,13},{6,14},{7,15},{16,24},{17,... | collective-permute-start | bytes 1572872 | tf_op jit(solution)/shard_map/ppermute | solution.py:177
  256.5 12.8 %collective-permute-start.18 = (bf16[2,8,128,640]{3,2,1,0:T(8,128)(2,1)}, bf16[2,8,128,640]{3,2,1,0:T(8,128)(2,1)}, u32[]{:S(2)}, u32[]{:S(2)}) collective-permute-start(bf16[2,8,128,640]{3,2,1,0:T(8,128)(2,1)} %weight_gradient.20), channel_id=1, source_target_pairs={{0,8},{8,0},{16,24},{24,16},{1,9},{9,1},{17,25},{25,17},{2,10},{10... | collective-permute-start | bytes 7864328 | tf_op jit(solution)/shard_map/ppermute | solution.py:198
  259.5 9.8 %collective-permute-start.19 = (bf16[2,8,64,640]{3,2,1,0:T(8,128)(2,1)}, bf16[2,8,64,640]{3,2,1,0:T(8,128)(2,1)}, u32[]{:S(2)}, u32[]{:S(2)}) collective-permute-start(bf16[2,8,64,640]{3,2,1,0:T(8,128)(2,1)} %weight_gradient.21), channel_id=1, source_target_pairs={{0,8},{8,0},{16,24},{24,16},{1,9},{9,1},{17,25},{25,17},{2,10},{10... | collective-permute-start | bytes 3932168 | tf_op jit(solution)/shard_map/ppermute | solution.py:198
  262.7 19.7 %collective-permute-start.10 = (bf16[128,640]{1,0:T(8,128)(2,1)S(1)}, bf16[128,640]{1,0:T(8,128)(2,1)S(1)}, u32[]{:S(2)}, u32[]{:S(2)}) collective-permute-start(bf16[128,640]{1,0:T(8,128)(2,1)S(1)} %get-tuple-element.218), channel_id=1, source_target_pairs={{0,0},{1,1},{2,2},{3,3},{8,4},{9,5},{10,6},{11,7},{4,8},{5,9},{6,1... | collective-permute-start | bytes 491528 | tf_op jit(solution)/shard_map/ppermute | solution.py:160
  263.5 19.0 %collective-permute-start.11 = (bf16[128,640]{1,0:T(8,128)(2,1)S(1)}, bf16[128,640]{1,0:T(8,128)(2,1)S(1)}, u32[]{:S(2)}, u32[]{:S(2)}) collective-permute-start(bf16[128,640]{1,0:T(8,128)(2,1)S(1)} %get-tuple-element.217), channel_id=1, source_target_pairs={{1,0},{2,1},{3,2},{0,3},{9,4},{10,5},{11,6},{8,7},{5,8},{6,9},{7,1... | collective-permute-start | bytes 491528 | tf_op jit(solution)/shard_map/ppermute | solution.py:160
  265.9 18.6 %collective-permute-start.20 = (bf16[2,8,32,640]{3,2,1,0:T(8,128)(2,1)S(1)}, bf16[2,8,32,640]{3,2,1,0:T(8,128)(2,1)S(1)}, u32[]{:S(2)}, u32[]{:S(2)}) collective-permute-start(bf16[2,8,32,640]{3,2,1,0:T(8,128)(2,1)S(1)} %weight_gradient.22), channel_id=1, source_target_pairs={{0,8},{8,0},{16,24},{24,16},{1,9},{9,1},{17,25},{25,17},{2,10},{10... | collective-permute-start | bytes 1966088 | tf_op jit(solution)/shard_map/ppermute | solution.py:198
  272.9 18.8 %collective-permute-start.21 = (bf16[2,4,64,640]{3,2,1,0:T(8,128)(2,1)S(1)}, bf16[2,4,64,640]{3,2,1,0:T(8,128)(2,1)S(1)}, u32[]{:S(2)}, u32[]{:S(2)}) collective-permute-start(bf16[2,4,64,640]{3,2,1,0:T(8,128)(2,1)S(1)} %get-tuple-element.126), channel_id=1, source_target_pairs={{0,1},{1,0},{2,3},{3,2},{4,5},{5,4},{6,7},{7,6},{8,9},{9,8},{10,11... | collective-permute-start | bytes 1966088 | tf_op jit(solution)/shard_map/ppermute | solution.py:198
  279.6 12.1 %collective-permute-start.22 = (bf16[512,512]{1,0:T(8,128)(2,1)S(1)}, bf16[512,512]{1,0:T(8,128)(2,1)S(1)}, u32[]{:S(2)}, u32[]{:S(2)}) collective-permute-start(bf16[512,512]{1,0:T(8,128)(2,1)S(1)} %get-tuple-element.129), channel_id=1, source_target_pairs={{8,0},{9,1},{10,2},{11,3},{12,4},{13,5},{14,6},{15,7},{24,16},{25,... | collective-permute-start | bytes 1572872 | tf_op jit(solution)/shard_map/ppermute | solution.py:177
  282.4 18.1 %collective-permute-start.12 = (bf16[128,640]{1,0:T(8,128)(2,1)S(1)}, bf16[128,640]{1,0:T(8,128)(2,1)S(1)}, u32[]{:S(2)}, u32[]{:S(2)}) collective-permute-start(bf16[128,640]{1,0:T(8,128)(2,1)S(1)} %get-tuple-element.216), channel_id=1, source_target_pairs={{2,0},{3,1},{0,2},{1,3},{10,4},{11,5},{8,6},{9,7},{6,8},{7,9},{4,1... | collective-permute-start | bytes 491528 | tf_op jit(solution)/shard_map/ppermute | solution.py:160
  282.4 18.1 %collective-permute-start.13 = (bf16[128,640]{1,0:T(8,128)(2,1)S(1)}, bf16[128,640]{1,0:T(8,128)(2,1)S(1)}, u32[]{:S(2)}, u32[]{:S(2)}) collective-permute-start(bf16[128,640]{1,0:T(8,128)(2,1)S(1)} %get-tuple-element.215), channel_id=1, source_target_pairs={{3,0},{0,1},{1,2},{2,3},{11,4},{8,5},{9,6},{10,7},{7,8},{4,9},{5,1... | collective-permute-start | bytes 491528 | tf_op jit(solution)/shard_map/ppermute | solution.py:160
  286.9 13.7 %collective-permute-start.23 = (bf16[2,4,32,640]{3,2,1,0:T(8,128)(2,1)S(1)}, bf16[2,4,32,640]{3,2,1,0:T(8,128)(2,1)S(1)}, u32[]{:S(2)}, u32[]{:S(2)}) collective-permute-start(bf16[2,4,32,640]{3,2,1,0:T(8,128)(2,1)S(1)} %get-tuple-element.134), channel_id=1, source_target_pairs={{0,1},{1,0},{2,3},{3,2},{4,5},{5,4},{6,7},{7,6},{8,9},{9,8},{10,11... | collective-permute-start | bytes 983048 | tf_op jit(solution)/shard_map/ppermute | solution.py:198
  297.2 11.5 %collective-permute-start.25 = (bf16[2,8,48,640]{3,2,1,0:T(8,128)(2,1)S(1)}, bf16[2,8,48,640]{3,2,1,0:T(8,128)(2,1)S(1)}, u32[]{:S(2)}, u32[]{:S(2)}) collective-permute-start(bf16[2,8,48,640]{3,2,1,0:T(8,128)(2,1)S(1)} %weight_gradient.25), channel_id=1, source_target_pairs={{0,8},{8,0},{16,24},{24,16},{1,9},{9,1},{17,25},{25,17},{2,10},{10... | collective-permute-start | bytes 2949128 | tf_op jit(solution)/shard_map/ppermute | solution.py:198
  299.1 9.6 %collective-permute-start.24 = (bf16[2,2,64,640]{3,2,1,0:T(8,128)(2,1)S(1)}, bf16[2,2,64,640]{3,2,1,0:T(8,128)(2,1)S(1)}, u32[]{:S(2)}, u32[]{:S(2)}) collective-permute-start(bf16[2,2,64,640]{3,2,1,0:T(8,128)(2,1)S(1)} %bitcast.375), channel_id=1, source_target_pairs={{0,16},{8,24},{16,0},{24,8},{1,17},{9,25},{17,1},{25,9},{2,18},{10... | collective-permute-start | bytes 983048 | tf_op jit(solution)/shard_map/ppermute | solution.py:198
  334.5 54.1 %collective-permute-start.26 = (bf16[2,8,128,640]{3,2,1,0:T(8,128)(2,1)}, bf16[2,8,128,640]{3,2,1,0:T(8,128)(2,1)}, u32[]{:S(2)}, u32[]{:S(2)}) collective-permute-start(bf16[2,8,128,640]{3,2,1,0:T(8,128)(2,1)} %weight_gradient.26), channel_id=1, source_target_pairs={{0,8},{8,0},{16,24},{24,16},{1,9},{9,1},{17,25},{25,17},{2,10},{10... | collective-permute-start | bytes 7864328 | tf_op jit(solution)/shard_map/ppermute | solution.py:198
  339.9 32.0 %collective-permute-start.28 = (bf16[1,8,128,640]{3,2,1,0:T(8,128)(2,1)}, bf16[1,8,128,640]{3,2,1,0:T(8,128)(2,1)}, u32[]{:S(2)}, u32[]{:S(2)}) collective-permute-start(bf16[1,8,128,640]{3,2,1,0:T(8,128)(2,1)} %weight_gradient.28), channel_id=1, source_target_pairs={{0,16},{8,24},{16,0},{24,8},{1,17},{9,25},{17,1},{25,9},{2,18},{10... | collective-permute-start | bytes 3932168 | tf_op jit(solution)/shard_map/ppermute | solution.py:198
  351.3 37.4 %collective-permute-start.27 = (bf16[2,8,64,640]{3,2,1,0:T(8,128)(2,1)}, bf16[2,8,64,640]{3,2,1,0:T(8,128)(2,1)}, u32[]{:S(2)}, u32[]{:S(2)}) collective-permute-start(bf16[2,8,64,640]{3,2,1,0:T(8,128)(2,1)} %weight_gradient.27), channel_id=1, source_target_pairs={{0,8},{8,0},{16,24},{24,16},{1,9},{9,1},{17,25},{25,17},{2,10},{10... | collective-permute-start | bytes 3932168 | tf_op jit(solution)/shard_map/ppermute | solution.py:198
  355.1 33.6 %collective-permute-start.29 = (bf16[1,8,48,640]{3,2,1,0:T(8,128)(2,1)S(1)}, bf16[1,8,48,640]{3,2,1,0:T(8,128)(2,1)S(1)}, u32[]{:S(2)}, u32[]{:S(2)}) collective-permute-start(bf16[1,8,48,640]{3,2,1,0:T(8,128)(2,1)S(1)} %weight_gradient.29), channel_id=1, source_target_pairs={{0,16},{8,24},{16,0},{24,8},{1,17},{9,25},{17,1},{25,9},{2,18},{10... | collective-permute-start | bytes 1474568 | tf_op jit(solution)/shard_map/ppermute | solution.py:198
  355.9 29.5 %collective-permute-start.30 = (bf16[2,2,32,640]{3,2,1,0:T(8,128)(2,1)S(1)}, bf16[2,2,32,640]{3,2,1,0:T(8,128)(2,1)S(1)}, u32[]{:S(2)}, u32[]{:S(2)}) collective-permute-start(bf16[2,2,32,640]{3,2,1,0:T(8,128)(2,1)S(1)} %bitcast.376), channel_id=1, source_target_pairs={{0,16},{8,24},{16,0},{24,8},{1,17},{9,25},{17,1},{25,9},{2,18},{10... | collective-permute-start | bytes 491528 | tf_op jit(solution)/shard_map/ppermute | solution.py:198
  371.8 51.2 %collective-permute-start.31 = (bf16[2,8,32,640]{3,2,1,0:T(8,128)(2,1)}, bf16[2,8,32,640]{3,2,1,0:T(8,128)(2,1)S(1)}, u32[]{:S(2)}, u32[]{:S(2)}) collective-permute-start(bf16[2,8,32,640]{3,2,1,0:T(8,128)(2,1)} %weight_gradient.30), channel_id=1, source_target_pairs={{0,8},{8,0},{16,24},{24,16},{1,9},{9,1},{17,25},{25,17},{2,10},{10... | collective-permute-start | bytes 1966088 | tf_op jit(solution)/shard_map/ppermute | solution.py:198
  385.4 37.5 %collective-permute-start.32 = (bf16[2,64,640]{2,1,0:T(8,128)(2,1)}, bf16[2,64,640]{2,1,0:T(8,128)(2,1)S(1)}, u32[]{:S(2)}, u32[]{:S(2)}) collective-permute-start(bf16[2,64,640]{2,1,0:T(8,128)(2,1)} %slice_bitcast_fusion.15), channel_id=1, source_target_pairs={{0,4},{1,5},{2,6},{3,7},{4,0},{5,1},{6,2},{7,3},{8,12},{9,13},{10,... | collective-permute-start | bytes 491528 | tf_op jit(solution)/shard_map/ppermute | solution.py:198
  389.5 35.0 %collective-permute-start.33 = (bf16[2,2,48,640]{3,2,1,0:T(8,128)(2,1)}, bf16[2,2,48,640]{3,2,1,0:T(8,128)(2,1)}, u32[]{:S(2)}, u32[]{:S(2)}) collective-permute-start(bf16[2,2,48,640]{3,2,1,0:T(8,128)(2,1)} %slice_bitcast_fusion.7), channel_id=1, source_target_pairs={{0,1},{1,0},{2,3},{3,2},{4,5},{5,4},{6,7},{7,6},{8,9},{9,8},{10,11... | collective-permute-start | bytes 737288 | tf_op jit(solution)/shard_map/ppermute | solution.py:198
  390.2 34.3 %collective-permute-start.34 = (bf16[2,32,640]{2,1,0:T(8,128)(2,1)}, bf16[2,32,640]{2,1,0:T(8,128)(2,1)}, u32[]{:S(2)}, u32[]{:S(2)}) collective-permute-start(bf16[2,32,640]{2,1,0:T(8,128)(2,1)} %slice_bitcast_fusion.27), channel_id=1, source_target_pairs={{0,4},{1,5},{2,6},{3,7},{4,0},{5,1},{6,2},{7,3},{8,12},{9,13},{10,... | collective-permute-start | bytes 245768 | tf_op jit(solution)/shard_map/ppermute | solution.py:198
  395.5 56.7 %collective-permute-start.35 = (bf16[2,4,64,640]{3,2,1,0:T(8,128)(2,1)}, bf16[2,4,64,640]{3,2,1,0:T(8,128)(2,1)}, u32[]{:S(2)}, u32[]{:S(2)}) collective-permute-start(bf16[2,4,64,640]{3,2,1,0:T(8,128)(2,1)} %get-tuple-element.163), channel_id=1, source_target_pairs={{0,1},{1,0},{2,3},{3,2},{4,5},{5,4},{6,7},{7,6},{8,9},{9,8},{10,11... | collective-permute-start | bytes 1966088 | tf_op jit(solution)/shard_map/ppermute | solution.py:198
  422.9 29.3 %collective-permute-start.36 = (bf16[2,2,128,640]{2,3,1,0:T(8,128)(2,1)S(1)}, bf16[2,2,128,640]{2,3,1,0:T(8,128)(2,1)S(1)}, u32[]{:S(2)}, u32[]{:S(2)}) collective-permute-start(bf16[2,2,128,640]{2,3,1,0:T(8,128)(2,1)S(1)} %bitcast.370), channel_id=1, source_target_pairs={{0,1},{1,0},{2,3},{3,2},{4,5},{5,4},{6,7},{7,6},{8,9},{9,8},{10,11... | collective-permute-start | bytes 1966088 | tf_op jit(solution)/shard_map/ppermute | solution.py:198
  423.1 29.2 %collective-permute-start.38 = (bf16[512,512]{1,0:T(8,128)(2,1)S(1)}, bf16[512,512]{1,0:T(8,128)(2,1)S(1)}, u32[]{:S(2)}, u32[]{:S(2)}) collective-permute-start(bf16[512,512]{1,0:T(8,128)(2,1)S(1)} %copy-done.87), channel_id=1, source_target_pairs={{8,0},{9,1},{10,2},{11,3},{12,4},{13,5},{14,6},{15,7},{24,16},{25,... | collective-permute-start | bytes 1572872 | tf_op jit(solution)/shard_map/ppermute | solution.py:177
  426.5 9.5 %collective-permute-start.48 = (bf16[2,48,640]{2,1,0:T(8,128)(2,1)S(1)}, bf16[2,48,640]{2,1,0:T(8,128)(2,1)S(1)}, u32[]{:S(2)}, u32[]{:S(2)}) collective-permute-start(bf16[2,48,640]{2,1,0:T(8,128)(2,1)S(1)} %slice_bitcast_fusion.16), channel_id=1, source_target_pairs={{0,4},{1,5},{2,6},{3,7},{4,0},{5,1},{6,2},{7,3},{8,12},{9,13},{10,... | collective-permute-start | bytes 368648 | tf_op jit(solution)/shard_map/ppermute | solution.py:198
  431.2 15.5 %collective-permute-start.50 = (bf16[2,4,32,640]{3,2,1,0:T(8,128)(2,1)S(1)}, bf16[2,4,32,640]{3,2,1,0:T(8,128)(2,1)S(1)}, u32[]{:S(2)}, u32[]{:S(2)}) collective-permute-start(bf16[2,4,32,640]{3,2,1,0:T(8,128)(2,1)S(1)} %get-tuple-element.176), channel_id=1, source_target_pairs={{0,1},{1,0},{2,3},{3,2},{4,5},{5,4},{6,7},{7,6},{8,9},{9,8},{10,11... | collective-permute-start | bytes 983048 | tf_op jit(solution)/shard_map/ppermute | solution.py:198
  436.0 5.2 collective-permute-start.63
  445.5 84.3 %collective-permute-start.54 = (bf16[1,8,128,640]{3,2,1,0:T(8,128)(2,1)}, bf16[1,8,128,640]{3,2,1,0:T(8,128)(2,1)}, u32[]{:S(2)}, u32[]{:S(2)}) collective-permute-start(bf16[1,8,128,640]{3,2,1,0:T(8,128)(2,1)} %weight_gradient.39), channel_id=1, source_target_pairs={{0,16},{8,24},{16,0},{24,8},{1,17},{9,25},{17,1},{25,9},{2,18},{10... | collective-permute-start | bytes 3932168 | tf_op jit(solution)/shard_map/ppermute | solution.py:198
  450.7 42.5 %collective-permute-start.51 = (bf16[2,2,32,640]{3,2,1,0:T(8,128)(2,1)}, bf16[2,2,32,640]{3,2,1,0:T(8,128)(2,1)}, u32[]{:S(2)}, u32[]{:S(2)}) collective-permute-start(bf16[2,2,32,640]{3,2,1,0:T(8,128)(2,1)} %bitcast.86), channel_id=1, source_target_pairs={{0,16},{8,24},{16,0},{24,8},{1,17},{9,25},{17,1},{25,9},{2,18},{10... | collective-permute-start | bytes 491528 | tf_op jit(solution)/shard_map/ppermute | solution.py:198
  456.6 38.2 %collective-permute-start.39 = (bf16[128,640]{1,0:T(8,128)(2,1)S(1)}, bf16[128,640]{1,0:T(8,128)(2,1)S(1)}, u32[]{:S(2)}, u32[]{:S(2)}) collective-permute-start(bf16[128,640]{1,0:T(8,128)(2,1)S(1)} %get-tuple-element.208), channel_id=1, source_target_pairs={{0,0},{1,1},{2,2},{3,3},{8,4},{9,5},{10,6},{11,7},{4,8},{5,9},{6,1... | collective-permute-start | bytes 491528 | tf_op jit(solution)/shard_map/ppermute | solution.py:160
  457.3 38.9 %collective-permute-start.40 = (bf16[128,640]{1,0:T(8,128)(2,1)}, bf16[128,640]{1,0:T(8,128)(2,1)}, u32[]{:S(2)}, u32[]{:S(2)}) collective-permute-start(bf16[128,640]{1,0:T(8,128)(2,1)} %get-tuple-element.207), channel_id=1, source_target_pairs={{1,0},{2,1},{3,2},{0,3},{9,4},{10,5},{11,6},{8,7},{5,8},{6,9},{7,1... | collective-permute-start | bytes 491528 | tf_op jit(solution)/shard_map/ppermute | solution.py:160
  460.3 6.8 %collective-permute-start.64 = (f32[2,2,2,2,2,96]{5,3,2,1,0,4:T(2,128)S(1)}, f32[2,2,2,2,2,96]{5,3,2,1,0,4:T(2,128)S(1)}, u32[]{:S(2)}, u32[]{:S(2)}) collective-permute-start(f32[2,2,2,2,2,96]{5,3,2,1,0,4:T(2,128)S(1)} %slice_bitcast_fusion.36), channel_id=1, source_target_pairs={{0,8},{8,0},{16,24},{24,16},{1,9},{9,1},{17,25},{25,17},{2,10},{10... | collective-permute-start | bytes 36872 | tf_op jit(solution)/shard_map/ppermute | solution.py:198
  467.1 12.2 %collective-permute-start.65 = (f32[2,2,2,2,96]{4,2,1,0,3:T(2,128)S(1)}, f32[2,2,2,2,96]{4,2,1,0,3:T(2,128)S(1)}, u32[]{:S(2)}, u32[]{:S(2)}) collective-permute-start(f32[2,2,2,2,96]{4,2,1,0,3:T(2,128)S(1)} %slice_bitcast_fusion.38), channel_id=1, source_target_pairs={{0,16},{8,24},{16,0},{24,8},{1,17},{9,25},{17,1},{25,9},{2,18},{10... | collective-permute-start | bytes 18440 | tf_op jit(solution)/shard_map/ppermute | solution.py:198
  483.0 4.5 collective-permute-start.67
  491.7 14.7 %collective-permute-start.41 = (bf16[128,640]{1,0:T(8,128)(2,1)}, bf16[128,640]{1,0:T(8,128)(2,1)S(1)}, u32[]{:S(2)}, u32[]{:S(2)}) collective-permute-start(bf16[128,640]{1,0:T(8,128)(2,1)} %get-tuple-element.206), channel_id=1, source_target_pairs={{2,0},{3,1},{0,2},{1,3},{10,4},{11,5},{8,6},{9,7},{6,8},{7,9},{4,1... | collective-permute-start | bytes 491528 | tf_op jit(solution)/shard_map/ppermute | solution.py:160
  493.2 14.4 %collective-permute-start.42 = (bf16[128,640]{1,0:T(8,128)(2,1)}, bf16[128,640]{1,0:T(8,128)(2,1)S(1)}, u32[]{:S(2)}, u32[]{:S(2)}) collective-permute-start(bf16[128,640]{1,0:T(8,128)(2,1)} %get-tuple-element.205), channel_id=1, source_target_pairs={{3,0},{0,1},{1,2},{2,3},{11,4},{8,5},{9,6},{10,7},{7,8},{4,9},{5,1... | collective-permute-start | bytes 491528 | tf_op jit(solution)/shard_map/ppermute | solution.py:160
  494.8 50.8 %collective-permute-start.43 = (bf16[2,8,48,640]{3,2,1,0:T(8,128)(2,1)}, bf16[2,8,48,640]{3,2,1,0:T(8,128)(2,1)S(1)}, u32[]{:S(2)}, u32[]{:S(2)}) collective-permute-start(bf16[2,8,48,640]{3,2,1,0:T(8,128)(2,1)} %weight_gradient.34), channel_id=1, source_target_pairs={{0,8},{8,0},{16,24},{24,16},{1,9},{9,1},{17,25},{25,17},{2,10},{10... | collective-permute-start | bytes 2949128 | tf_op jit(solution)/shard_map/ppermute | solution.py:198
  496.2 10.2 %collective-permute-start.52 = (bf16[2,32,640]{2,1,0:T(8,128)(2,1)S(1)}, bf16[2,32,640]{2,1,0:T(8,128)(2,1)S(1)}, u32[]{:S(2)}, u32[]{:S(2)}) collective-permute-start(bf16[2,32,640]{2,1,0:T(8,128)(2,1)S(1)} %slice_bitcast_fusion.24), channel_id=1, source_target_pairs={{0,4},{1,5},{2,6},{3,7},{4,0},{5,1},{6,2},{7,3},{8,12},{9,13},{10,... | collective-permute-start | bytes 245768 | tf_op jit(solution)/shard_map/ppermute | solution.py:198
  506.4 19.8 %collective-permute-start.58 = (bf16[2,128,640]{1,2,0:T(8,128)(2,1)S(1)}, bf16[2,128,640]{1,2,0:T(8,128)(2,1)S(1)}, u32[]{:S(2)}, u32[]{:S(2)}) collective-permute-start(bf16[2,128,640]{1,2,0:T(8,128)(2,1)S(1)} %slice_bitcast_fusion), channel_id=1, source_target_pairs={{0,4},{1,5},{2,6},{3,7},{4,0},{5,1},{6,2},{7,3},{8,12},{9,13},{10,... | collective-permute-start | bytes 983048 | tf_op jit(solution)/shard_map/ppermute | solution.py:198
  506.4 7.8 %collective-permute-start.60 = (bf16[2,2,64,640]{3,2,1,0:T(8,128)(2,1)S(1)}, bf16[2,2,64,640]{3,2,1,0:T(8,128)(2,1)S(1)}, u32[]{:S(2)}, u32[]{:S(2)}) collective-permute-start(bf16[2,2,64,640]{3,2,1,0:T(8,128)(2,1)S(1)} %bitcast.374), channel_id=1, source_target_pairs={{0,16},{8,24},{16,0},{24,8},{1,17},{9,25},{17,1},{25,9},{2,18},{10... | collective-permute-start | bytes 983048 | tf_op jit(solution)/shard_map/ppermute | solution.py:198
  507.6 5.3 collective-permute-start.53
  514.4 14.7 %collective-permute-start.61 = (bf16[2,64,640]{2,1,0:T(8,128)(2,1)S(1)}, bf16[2,64,640]{2,1,0:T(8,128)(2,1)S(1)}, u32[]{:S(2)}, u32[]{:S(2)}) collective-permute-start(bf16[2,64,640]{2,1,0:T(8,128)(2,1)S(1)} %slice_bitcast_fusion.9), channel_id=1, source_target_pairs={{0,4},{1,5},{2,6},{3,7},{4,0},{5,1},{6,2},{7,3},{8,12},{9,13},{10,... | collective-permute-start | bytes 491528 | tf_op jit(solution)/shard_map/ppermute | solution.py:198
  527.0 10.6 %collective-permute-start.59 = (bf16[128,640]{0,1:T(8,128)(2,1)}, bf16[128,640]{0,1:T(8,128)(2,1)}, u32[]{:S(2)}, u32[]{:S(2)}) collective-permute-start(bf16[128,640]{0,1:T(8,128)(2,1)} %slice_bitcast_fusion.11), channel_id=1, source_target_pairs={{0,2},{1,3},{2,0},{3,1},{4,6},{5,7},{6,4},{7,5},{8,10},{9,11},{10,... | collective-permute-start | bytes 491528 | tf_op jit(solution)/shard_map/ppermute | solution.py:198
  534.9 16.4 %collective-permute-start.55 = (bf16[2,2,128,640]{2,3,1,0:T(8,128)(2,1)}, bf16[2,2,128,640]{2,3,1,0:T(8,128)(2,1)}, u32[]{:S(2)}, u32[]{:S(2)}) collective-permute-start(bf16[2,2,128,640]{2,3,1,0:T(8,128)(2,1)} %bitcast.371), channel_id=1, source_target_pairs={{0,1},{1,0},{2,3},{3,2},{4,5},{5,4},{6,7},{7,6},{8,9},{9,8},{10,11... | collective-permute-start | bytes 1966088 | tf_op jit(solution)/shard_map/ppermute | solution.py:198
  537.3 4.4 collective-permute-start.62
  546.8 11.2 %collective-permute-start.44 = (bf16[1,8,48,640]{3,2,1,0:T(8,128)(2,1)S(1)}, bf16[1,8,48,640]{3,2,1,0:T(8,128)(2,1)S(1)}, u32[]{:S(2)}, u32[]{:S(2)}) collective-permute-start(bf16[1,8,48,640]{3,2,1,0:T(8,128)(2,1)S(1)} %weight_gradient.36), channel_id=1, source_target_pairs={{0,16},{8,24},{16,0},{24,8},{1,17},{9,25},{17,1},{25,9},{2,18},{10... | collective-permute-start | bytes 1474568 | tf_op jit(solution)/shard_map/ppermute | solution.py:198
  552.6 15.9 %collective-permute-start.56 = (bf16[2,128,640]{1,2,0:T(8,128)(2,1)S(1)}, bf16[2,128,640]{1,2,0:T(8,128)(2,1)S(1)}, u32[]{:S(2)}, u32[]{:S(2)}) collective-permute-start(bf16[2,128,640]{1,2,0:T(8,128)(2,1)S(1)} %slice_bitcast_fusion.2), channel_id=1, source_target_pairs={{0,4},{1,5},{2,6},{3,7},{4,0},{5,1},{6,2},{7,3},{8,12},{9,13},{10,... | collective-permute-start | bytes 983048 | tf_op jit(solution)/shard_map/ppermute | solution.py:198
  558.1 10.6 %collective-permute-start.45 = (bf16[2,2,48,640]{3,2,1,0:T(8,128)(2,1)S(1)}, bf16[2,2,48,640]{3,2,1,0:T(8,128)(2,1)S(1)}, u32[]{:S(2)}, u32[]{:S(2)}) collective-permute-start(bf16[2,2,48,640]{3,2,1,0:T(8,128)(2,1)S(1)} %slice_bitcast_fusion.5), channel_id=1, source_target_pairs={{0,1},{1,0},{2,3},{3,2},{4,5},{5,4},{6,7},{7,6},{8,9},{9,8},{10,11... | collective-permute-start | bytes 737288 | tf_op jit(solution)/shard_map/ppermute | solution.py:198
  568.7 8.3 %collective-permute-start.57 = (bf16[128,640]{0,1:T(8,128)(2,1)S(1)}, bf16[128,640]{0,1:T(8,128)(2,1)S(1)}, u32[]{:S(2)}, u32[]{:S(2)}) collective-permute-start(bf16[128,640]{0,1:T(8,128)(2,1)S(1)} %slice_bitcast_fusion.13), channel_id=1, source_target_pairs={{0,2},{1,3},{2,0},{3,1},{4,6},{5,7},{6,4},{7,5},{8,10},{9,11},{10,... | collective-permute-start | bytes 491528 | tf_op jit(solution)/shard_map/ppermute | solution.py:198
  568.9 8.9 %collective-permute-start.46 = (bf16[2,48,640]{2,1,0:T(8,128)(2,1)S(1)}, bf16[2,48,640]{2,1,0:T(8,128)(2,1)S(1)}, u32[]{:S(2)}, u32[]{:S(2)}) collective-permute-start(bf16[2,48,640]{2,1,0:T(8,128)(2,1)S(1)} %slice_bitcast_fusion.18), channel_id=1, source_target_pairs={{0,4},{1,5},{2,6},{3,7},{4,0},{5,1},{6,2},{7,3},{8,12},{9,13},{10,... | collective-permute-start | bytes 368648 | tf_op jit(solution)/shard_map/ppermute | solution.py:198
  (145 other events, 907.2 us)
Sparse Core Ops, SparseCore 0:
  10.9 161.9 all-gather.2

commit v3 on v2

--- a/solution.py
+++ b/solution.py
@@ -198,29 +198,26 @@
     return lax.ppermute(array, axis, [(i, i ^ bit) for i in range(lax.axis_size(axis))])
 
 
+def launch(value, chains):
+    chains = [chain for chain in chains if chain.pending is not None]
+    if not chains:
+        return value
+    held = lax.optimization_barrier((value,) + tuple(chain.pending for chain in chains))
+    for chain, pending in zip(chains, held[1:]):
+        chain.got = swap(pending, chain.steps[0])
+        chain.pending = None
+    return held[0]
+
+
 def advance(value, chains):
+    chains = [chain for chain in chains if chain.steps]
     if not chains:
         return value
     held = lax.optimization_barrier((value,) + tuple(chain.got for chain in chains))
     for chain, got in zip(chains, held[1:]):
         chain.got = got
         chain.advance()
-    return held[0]
-
-
-def halving(array):
-    n_seq = lax.axis_size("seq")
-    dims = bits("dp")[::-1] + bits("seq")[::-1]
-    me = lax.axis_index("dp") * n_seq + lax.axis_index("seq")
-    rest = array.shape[1:]
-    array = jnp.take(array, me ^ jnp.arange(array.shape[0]), axis=0)
-    array = array.reshape((2,) * len(dims) + rest)
-    for step in order("dp"):
-        at = dims.index(step)
-        dims.remove(step)
-        keep = lax.index_in_dim(array, 0, at, keepdims=False)
-        array = keep + swap(lax.index_in_dim(array, 1, at, keepdims=False), step)
-    return array
+    return launch(held[0], chains)
 
 
 def block_numbers():
@@ -234,34 +231,47 @@
 
 def product_kernel(rows, split, added, numbers_ref, a_ref, b_ref, *refs):
     got_ref = refs[0] if added else None
-    outs, acc = refs[1 if added else 0 : -1], refs[-1]
-    acc[...] = dot(a_ref[...], b_ref[...], 0, 0)
+    outs = refs[1 if added else 0 :]
     me = numbers_ref[4]
-    for entry in range(a_ref.shape[1] // rows):
-        source = pl.multiple_of((me ^ entry) * rows, TILE)
-        value = acc[pl.ds(source, rows), :]
-        if added:
-            value = value + got_ref[0, entry].astype(F32)
-        if split:
-            outs[entry % 2][0, entry // 2] = value.astype(BF16)
-        else:
-            outs[0][0, entry] = value.astype(BF16)
+    width = a_ref.shape[1]
+    part = width if width <= 512 else 512
+    for start in range(0, width, part):
+        total = dot(a_ref[:, start : start + part], b_ref[...], 0, 0)
+        for at in range(0, part, rows):
+            entry = me ^ ((start + at) // rows)
+            value = total[at : at + rows]
+            if added:
+                value = value + got_ref[0, entry].astype(F32)
+            value = value.astype(BF16)
+            if split:
+                even = lax.rem(entry, 2) == 0
+
+                @pl.when(even)
+                def _():
+                    outs[0][0, entry // 2] = value
+
+                @pl.when(jnp.logical_not(even))
+                def _():
+                    outs[1][0, entry // 2] = value
+
+            else:
+                outs[0][0, entry] = value
 
 
 def product(left, right, numbers, first, blocks, got=None, got_first=0, split=False):
     tokens, n_seq = left.shape[0], lax.axis_size("seq")
-    width = left.shape[1] // lax.axis_size("dp")
+    width, columns = left.shape[1] // lax.axis_size("dp"), right.shape[1]
     rows = width // n_seq
     out_entries = n_seq // 2 if split else n_seq
     specs = [
         pl.BlockSpec((tokens, width), lambda i, n: (0, n[first + i])),
-        pl.BlockSpec((tokens, D), lambda i, n: (0, 0)),
+        pl.BlockSpec((tokens, columns), lambda i, n: (0, 0)),
     ]
     operands = [left, right]
     if got is not None:
-        specs.append(pl.BlockSpec((1, n_seq, rows, D), lambda i, n: (i + got_first, 0, 0, 0)))
+        specs.append(pl.BlockSpec((1, n_seq, rows, columns), lambda i, n: (i + got_first, 0, 0, 0)))
         operands.append(got)
-    shape = jax.ShapeDtypeStruct((blocks, out_entries, rows, D), BF16)
+    shape = jax.ShapeDtypeStruct((blocks, out_entries, rows, columns), BF16)
     count = 2 if split else 1
     return pl.pallas_call(
         partial(product_kernel, rows, split, got is not None),
@@ -269,14 +279,13 @@
             num_scalar_prefetch=1,
             grid=(blocks,),
             in_specs=specs,
-            out_specs=[pl.BlockSpec((1, out_entries, rows, D), lambda i, n: (i, 0, 0, 0))] * count,
-            scratch_shapes=[pltpu.VMEM((width, D), F32)],
+            out_specs=[pl.BlockSpec((1, out_entries, rows, columns), lambda i, n: (i, 0, 0, 0))] * count,
         ),
         out_shape=[shape] * count,
         compiler_params=pltpu.CompilerParams(vmem_limit_bytes=24 * 2**20),
         cost_estimate=pl.CostEstimate(
-            flops=2 * tokens * width * blocks * D,
-            bytes_accessed=2 * (tokens * width * blocks + tokens * D + 2 * width * blocks * D),
+            flops=2 * tokens * width * blocks * columns,
+            bytes_accessed=2 * (tokens * width * blocks + tokens * columns + 2 * width * blocks * columns),
             transcendentals=0,
         ),
         name="weight_gradient",
@@ -284,31 +293,43 @@
 
 
 class Chain:
-    def __init__(self, left, right, first):
+    def __init__(self, left, right, first, extra=None):
         self.steps = order(first)
         self.dims = bits("dp")[::-1] + bits("seq")[::-1]
         n_dp, n_seq = lax.axis_size("dp"), lax.axis_size("seq")
         width = left.shape[1] // n_dp
-        self.rows = width // n_seq
+        self.rows, self.columns = width // n_seq, right.shape[1]
         self.factors = None
+        self.extra = None
+        self.pending = None
         step = self.steps[0]
+        me = lax.axis_index("dp") * n_seq + lax.axis_index("seq")
+        if extra is not None:
+            extra = jnp.take(extra, me ^ jnp.arange(n_dp * n_seq), axis=0)
         if n_dp == 4 and width % 128 == 0 and self.rows % TILE == 0 and width % n_seq == 0:
             self.factors = (left, right, block_numbers())
             (send,) = product(left, right, self.factors[2], 0, 2)
             self.dims.remove(step)
-            self.got = swap(send, step)
+            if extra is not None:
+                extra = extra.reshape((2, 2, n_seq) + extra.shape[1:])
+                self.extra = extra[:, 0]
+                send = jnp.concatenate([send, extra[:, 1]], axis=2)
+            self.pending = send
         else:
-            whole = dot(left, right, 0, 0).astype(BF16).reshape(n_dp * n_seq, self.rows, D)
-            me = lax.axis_index("dp") * n_seq + lax.axis_index("seq")
-            self.send(jnp.take(whole, me ^ jnp.arange(n_dp * n_seq), axis=0))
+            whole = dot(left, right, 0, 0).astype(BF16).reshape(n_dp * n_seq, self.rows, self.columns)
+            whole = jnp.take(whole, me ^ jnp.arange(n_dp * n_seq), axis=0)
+            if extra is not None:
+                whole = jnp.concatenate([whole, extra], axis=1)
+                self.rows = whole.shape[1]
+            self.send(whole)
 
     def send(self, array):
         step = self.steps[0]
-        array = array.reshape((2,) * len(self.dims) + (self.rows, D))
+        array = array.reshape((2,) * len(self.dims) + (self.rows, self.columns))
         at = self.dims.index(step)
         self.dims.remove(step)
         self.keep = lax.index_in_dim(array, 0, at, keepdims=False)
-        self.got = swap(lax.index_in_dim(array, 1, at, keepdims=False), step)
+        self.pending = lax.index_in_dim(array, 1, at, keepdims=False)
 
     def advance(self):
         self.steps = self.steps[1:]
@@ -316,22 +337,33 @@
             left, right, numbers = self.factors
             self.factors = None
             step = self.steps[0]
+            self.dims.remove(step)
+            got = self.got
+            if self.extra is not None:
+                more = (self.extra.astype(F32) + got[:, :, self.rows :].astype(F32)).astype(BF16)
+                got = got[:, :, : self.rows]
             if step[0] == "dp":
-                (send,) = product(left, right, numbers, 3, 1, self.got, 1)
-                (self.keep,) = product(left, right, numbers, 2, 1, self.got, 0)
+                (send,) = product(left, right, numbers, 3, 1, got, 1)
+                (self.keep,) = product(left, right, numbers, 2, 1, got, 0)
+                if self.extra is not None:
+                    send = jnp.concatenate([send, more[1:]], axis=2)
+                    self.keep = jnp.concatenate([self.keep, more[:1]], axis=2)
+                    self.rows = send.shape[2]
             else:
-                self.keep, send = product(left, right, numbers, 2, 2, self.got, 0, True)
-            self.dims.remove(step)
-            self.got = swap(send, step)
+                self.keep, send = product(left, right, numbers, 2, 2, got, 0, True)
+            self.pending = send
             return
         array = self.keep.astype(F32) + self.got.reshape(self.keep.shape).astype(F32)
         if self.steps:
             self.send(array.astype(BF16))
         else:
-            self.result = array.reshape(self.rows, D)
+            self.result = array.reshape(self.rows, self.columns)
 
     def finish(self):
         while self.steps:
+            if self.pending is not None:
+                self.got = swap(self.pending, self.steps[0])
+                self.pending = None
             self.advance()
         return self.result
 
@@ -607,9 +639,12 @@
         ],
         2 * tokens * D * (QUERY_COLS + 3 * hidden),
     )
-    chains["ffn_in"] = Chain(grad_gate_up, ffn_normed, "dp")
-    chains["ffn_out"] = Chain(inner, grad_ffn_branch, "seq")
+    cut = 3 * D // 5
+    chains["ffn_in"] = Chain(grad_gate_up, ffn_normed[:, :cut], "dp")
+    chains["ffn_in_rest"] = Chain(grad_gate_up, ffn_normed[:, cut:], "seq")
+    chains["ffn_out"] = Chain(inner, grad_ffn_branch, "dp")
     chains["attn_out"] = Chain(context, grad_branch, "seq")
+    grad_context = launch(grad_context, list(chains.values()))
     grad_context = pump(1, grad_context)
     grad_queries, grad_before, grad_own = call(
         attention_backward_kernel, "attention_backward",
@@ -637,18 +672,26 @@
         ],
         2 * tokens * D * (QUERY_COLS + 2 * HEAD_DIM),
     )
-    chains["attn_in"] = Chain(grad_projected, normed, "dp")
-    grad_gain_row = jnp.concatenate(
-        [pre_sums[0], sums[0], sums[1], sums[2], query_sums[0], key_sums[0]]
-    )
-    return grad_in, grad_gain_row
+    gain_grads = jnp.concatenate([pre_sums[0], sums[0], sums[1], sums[2], query_sums[0], key_sums[0]])
+    devices = lax.axis_size("dp") * lax.axis_size("seq")
+    gain_grads = gain_grads.astype(BF16).reshape(devices, 1, -1)
+    extra = jnp.pad(gain_grads, ((0, 0), (0, TILE - 1), (0, D - gain_grads.shape[2])))
+    chains["attn_in"] = Chain(grad_projected, normed, "dp", extra)
+    return launch(grad_in, [chains["attn_in"]])
 
 
 PLAN = {
-    0: [(1, "attn_out"), (1, "ffn_out"), (1, "attn_in")],
-    1: [(0, "ffn_in"), (0, "ffn_out"), (1, "ffn_in"), (1, "attn_in"), (1, "attn_out")],
-    2: [(0, "attn_out"), (1, "ffn_out"), (1, "attn_in"), (1, "attn_out")],
-    3: [(0, "ffn_out"), (1, "ffn_in"), (1, "attn_out")],
+    0: [(1, "attn_in"), (1, "attn_out"), (1, "ffn_in_rest"), (1, "ffn_out")],
+    1: [
+        (0, "ffn_in"), (0, "ffn_in_rest"), (0, "ffn_out"), (0, "attn_out"),
+        (1, "ffn_in"), (1, "ffn_in_rest"), (1, "ffn_out"), (1, "attn_in"), (1, "attn_out"),
+    ],
+    2: [(1, "attn_out"), (1, "attn_in")],
+    3: [(1, "ffn_in"), (1, "ffn_in_rest"), (1, "ffn_out")],
+    4: [
+        (0, "attn_out"), (0, "ffn_in_rest"), (0, "ffn_out"), (1, "attn_in"), (1, "attn_out"),
+        (1, "ffn_in"), (1, "ffn_in_rest"), (1, "ffn_out"),
+    ],
 }
 
 
@@ -684,7 +727,6 @@
     layer_weights = gather_weights(w_attn_in, w_attn_out, w_ffn_in, w_ffn_out, gains)
     places = to_long(positions)
     stream = to_long(hidden_in).astype(F32)
-    grad_stream = to_long(out_grad).astype(F32)
     tables = angle_tables(places)
     tokens = places.shape[0]
     blocks = tokens // QUERY_BLOCK
@@ -695,8 +737,10 @@
         weights.append(layer_weights(layer_index))
         record, stream = forward_layer(stream, *weights[-1], tables, reach, count)
         records.append(record)
+        if layer_index == 0:
+            stream, out_grad = lax.optimization_barrier((stream, out_grad))
+            grad_stream = to_long(out_grad).astype(F32)
     hidden_out = to_short(stream.astype(BF16), count)
-    gain_grads = [None] * layer_count
     chains = [{} for _ in range(layer_count + 1)]
     for layer_index in reversed(range(layer_count)):
 
@@ -706,27 +750,28 @@
                 for above, name in PLAN[where]
                 if name in chains[layer_index + above]
             ]
-            return advance(value, [chain for chain in active if chain.steps])
-
-        grad_stream, gain_grads[layer_index] = backward_layer(
+            return advance(value, active)
+
+        grad_stream = backward_layer(
             grad_stream, *weights[layer_index], records[layer_index], tables, reach, count, pump,
             chains[layer_index],
         )
+    grad_stream = pump(4, grad_stream)
     input_grad = to_short(grad_stream.astype(BF16), count).astype(F32)
-    devices = lax.axis_size("dp") * lax.axis_size("seq")
-    gain_grads = halving(jnp.stack([entry.reshape(devices, -1) for entry in gain_grads], axis=1))
     members = {
         name: jnp.stack([chains[layer][name].finish() for layer in range(layer_count)])
         for name in chains[0]
     }
+    attn_in_rows = w_attn_in.shape[2]
+    ffn_in = jnp.concatenate([members["ffn_in"], members["ffn_in_rest"]], axis=2)
     return (
         hidden_out,
         input_grad,
-        members["attn_in"].transpose(0, 2, 1),
+        members["attn_in"][:, :attn_in_rows].transpose(0, 2, 1),
         members["attn_out"],
-        members["ffn_in"].transpose(0, 2, 1),
+        ffn_in.transpose(0, 2, 1),
         members["ffn_out"],
-        gain_grads,
+        members["attn_in"][:, attn_in_rows, : gains.shape[1]],
     )
 
 

time: 596 us -> 655 us (1.099)
  local copies, waits for them, and re-layouts: 58.7 us -> 118 us
  waiting for transfers between devices: 249 us -> 224 us
  other arithmetic: 27.7 us -> 42.9 us
  Pallas kernels: 151 us -> 158 us
    unnamed x323 -> x408, local copies, waits for them, and re-layouts: 43.8 us -> 75.7 us
    ppermute x45 -> x50, waiting for transfers between devices: 105 us -> 74.8 us  [swap(): lax.ppermute(array, axis, [(i, i ^ bit) for i in range(lax.axis_size(axis...]
    all_gather x1, waiting for transfers between devices: 126 us -> 140 us  [gather_weights(): whole = lax.all_gather(packed, ALL, axis=0, tiled=False)]
    pallas_call x20 -> x26, Pallas kernels: 53.6 us -> 67 us  [product(): pl.pallas_call(partial(product_kernel, rows, split, got is not None), gri...]
    ppermute x12, waiting for transfers between devices: 18.1 us -> 8.83 us  [to_long(): received.append(lax.ppermute(piece, ALL, chunk_route(count, k)))]
    convert_element_type x24 -> x30, other arithmetic: 13.9 us -> 21.8 us  [advance(): self.send(array.astype(BF16))]
    ppermute x45 -> x50, starting transfers between devices: 56.5 us -> 54.3 us  [swap(): lax.ppermute(array, axis, [(i, i ^ bit) for i in range(lax.axis_size(axis...]
  transfers between devices with their start and end apart: 70 -> 75, of which waited for: 29 -> 22; matrix products, arithmetic and copies ran while one was open for 9% -> 14% of each run, Pallas kernels for 12% -> 9%
where the time goes in v3:
time: 655 us; the launch traced here: 649 us
  waiting for transfers between devices  224 us (34%)
  Pallas kernels  158 us (24%)
  local copies, waits for them, and re-layouts  118 us (18%)
  starting transfers between devices  88.1 us (13%)
  other arithmetic  42.9 us (7%)
  between operations  16.8 us (3%)
    all_gather x1, waiting for transfers between devices, gather_weights(): whole = lax.all_gather(packed, ALL, axis=0, tiled=False)  140 us
    pallas_call x14, Pallas kernels, call(): pl.pallas_call(kernel, out_shape=tuple(outs), in_specs=vmem(len(arrays))...  91.5 us
    unnamed x408, local copies, waits for them, and re-layouts  75.7 us
    ppermute x50, waiting for transfers between devices, swap(): lax.ppermute(array, axis, [(i, i ^ bit) for i in range(lax.axis_size(axis...  74.8 us
    pallas_call x26, Pallas kernels, product(): pl.pallas_call(partial(product_kernel, rows, split, got is not None), gri...  67 us
    ppermute x50, starting transfers between devices, swap(): lax.ppermute(array, axis, [(i, i ^ bit) for i in range(lax.axis_size(axis...  54.3 us
    convert_element_type x30, other arithmetic, advance(): self.send(array.astype(BF16))  21.8 us
    ppermute x12, starting transfers between devices, to_long(): received.append(lax.ppermute(piece, ALL, chunk_route(count, k)))  15 us
  transfers between devices with their start and end apart: 75, of which 22 were waited for; matrix products, arithmetic and copies ran while one was open for 14% of the time, Pallas kernels for 9%

profile of v3, /device:TPU:0, one launch (start us, length us, event | category | flops | bytes accessed | tf_op | source)
XLA Modules:
  0.0 648.6 jit_solution(17599849916398857194)
XLA Ops:
  9.8 4.0 collective-permute-start
  17.5 2.5 collective-permute-start.1
  24.2 2.7 collective-permute-done.2
  27.3 139.9 %all-gather.3.cloned.1.call-done = bf16[17920,640]{1,0:T(8,128)(2,1)} async-done(((bf16[560,640]{1,0:T(8,128)(2,1)}), bf16[17920,640]{1,0:T(8,128)(2,1)}) %all-gather.3.cloned.1.call-update) | async-done | bytes 22937616 | tf_op jit(solution)/shard_map/all_gather | solution.py:703
  168.8 2.3 key_value.2
  172.0 2.4 collective-permute-start.8
  175.0 2.9 query.2
  182.2 14.6 %block_forward.2 = (bf16[512,1024]{1,0:T(8,128)(2,1)S(1)}, f32[2,1024]{1,0:T(2,128)S(1)}, f32[512,640]{1,0:T(8,128)S(1)}, f32[512,640]{1,0:T(8,128)S(1)}, bf16[5...) custom-call(bf16[512,1024]{1,0:T(8,128)(2,1)S(1)} %get-tuple-element, ...), custom_call_target="tpu_custom_call" | custom-call | flops 6308233216 | bytes 16674816 | tf_op jit(solution)/shard_map/block_forward/pallas_call | solution.py:106
  203.8 2.4 key_value.3
  207.0 3.7 collective-permute-start.9
  212.8 2.9 query.3
  217.9 3.6 collective-permute-done.16
  222.4 14.3 %block_forward.3 = (bf16[512,1024]{1,0:T(8,128)(2,1)S(1)}, f32[2,1024]{1,0:T(2,128)S(1)}, f32[512,640]{1,0:T(8,128)S(1)}, f32[512,640]{1,0:T(8,128)S(1)}, bf16[5...) custom-call(bf16[512,1024]{1,0:T(8,128)(2,1)S(1)} %get-tuple-element, ...), custom_call_target="tpu_custom_call" | custom-call | flops 6308233216 | bytes 16674816 | tf_op jit(solution)/shard_map/block_forward/pallas_call | solution.py:106
  238.5 16.5 %block_backward.2 = (bf16[512,640]{1,0:T(8,128)(2,1)S(1)}, bf16[512,4096]{1,0:T(8,128)(2,1)}, bf16[512,640]{1,0:T(8,128)(2,1)S(1)}, bf16[512,1024]{1,0:T(8,128)(...) custom-call(f32[512,640]{1,0:T(8,128)S(1)} %bitcast_convert_fusion.grad_ref, ...), custom_call_target="tpu_custom_call" | custom-call | flops 4697620480 | bytes 17334272 | tf_op jit(solution)/shard_map/block_backward/pallas_call | solution.py:106
  256.7 2.9 copy-done
  259.6 3.3 weight_gradient.26
  262.8 2.5 weight_gradient.27
  265.4 2.7 weight_gradient.28
  270.3 2.3 collective-permute-start.18
  273.0 7.2 %collective-permute-done.21.refs_0_ = bf16[2,8,32,640]{3,2,1,0:T(8,128)(2,1)} collective-permute-done((bf16[2,8,32,640]{3,2,1,0:T(8,128)(2,1)}, bf16[2,8,32,640]{3,2,1,0:T(8,128)(2,1)}, u32[]{:S(2)}, u32[]{:S(2)}) %collective-permute-start.21) | collective-permute-done | bytes 655392 | tf_op jit(solution)/shard_map/ppermute | solution.py:198
  282.4 3.3 weight_gradient.30
  285.7 4.5 weight_gradient.31
  290.3 3.3 weight_gradient.32
  293.6 3.4 weight_gradient.33
  297.8 5.3 attention_backward.2
  306.9 3.2 input_backward.2
  313.5 2.5 gather_fusion
  326.1 2.9 collective-permute-start.10
  335.2 2.2 weight_gradient.36
  337.5 9.7 %collective-permute-done.24 = bf16[2,4,32,640]{3,2,1,0:T(8,128)(2,1)} collective-permute-done((bf16[2,4,32,640]{3,2,1,0:T(8,128)(2,1)}, bf16[2,4,32,640]{3,2,1,0:T(8,128)(2,1)}, u32[]{:S(2)}, u32[]{:S(2)}) %collective-permute-start.24) | collective-permute-done | bytes 327712 | tf_op jit(solution)/shard_map/ppermute | solution.py:198
  347.2 2.8 collective-permute-start.13
  362.1 16.2 %block_backward.3 = (bf16[512,640]{1,0:T(8,128)(2,1)S(1)}, bf16[512,4096]{1,0:T(8,128)(2,1)}, bf16[512,640]{1,0:T(8,128)(2,1)S(1)}, bf16[512,1024]{1,0:T(8,128)(...) custom-call(f32[512,640]{1,0:T(8,128)S(1)} %copy-done.71, f32[512,640]{1,0:T(8,128)S(1)} %copy-done.69, ...), custom_call_target="tpu_custom_call" | custom-call | flops 4697620480 | bytes 17334272 | tf_op jit(solution)/shard_map/block_backward/pallas_call | solution.py:106
  379.3 3.1 copy-done.3
  387.9 2.7 weight_gradient.39
  390.7 3.1 weight_gradient.37
  400.8 2.2 collective-permute-done.35
  408.7 3.9 collective-permute-done.33
  418.8 2.2 copy-done.2
  421.0 2.4 weight_gradient.45
  433.2 3.3 weight_gradient.41
  436.5 4.7 weight_gradient.42
  441.1 3.2 weight_gradient.43
  444.4 3.5 weight_gradient.44
  459.4 2.9 collective-permute-start.36
  464.5 2.8 collective-permute-start.40
  467.3 5.2 attention_backward.3
  477.7 2.5 weight_gradient.48
  480.2 2.9 weight_gradient.51
  500.1 3.2 input_backward.3
  517.8 2.9 collective-permute-start.45
  524.1 4.4 collective-permute-done.49
  539.1 2.9 collective-permute-start.50
  547.8 4.0 collective-permute-done.59
  552.9 4.4 collective-permute-done.67
  566.7 3.2 collective-permute-start.71
  580.1 3.0 collective-permute-start.62
  585.9 4.2 collective-permute-done.69
  592.2 2.6 collective-permute-done.70
  594.9 4.8 collective-permute-done.72
  604.9 2.4 collective-permute-start.65
  609.1 9.9 %collective-permute-done.55 = bf16[1,8,64,640]{3,2,1,0:T(8,128)(2,1)S(1)} collective-permute-done((bf16[1,8,64,640]{3,2,1,0:T(8,128)(2,1)S(1)}, bf16[1,8,64,640]{3,2,1,0:T(8,128)(2,1)S(1)}, u32[]{:S(2)}, u32[]{:S(2)}) %collective-permute-start.55) | collective-permute-done | bytes 655392 | tf_op jit(solution)/shard_map/ppermute | solution.py:198
  621.7 5.3 collective-permute-done.56
  629.2 6.0 collective-permute-done.57
  636.3 3.5 collective-permute-done.58
  (685 shorter events, 219.3 us)
Async XLA Ops:
  7.2 160.0 %all-gather.3.cloned.1.call-start = ((), (), s32[]{:S(2)}) async-start(), calls=%async_computation | async-start | bytes 23654400 | tf_op jit(solution)/shard_map/all_gather | solution.py:703
  9.8 14.4 %collective-permute-start = (bf16[128,640]{1,0:T(8,128)(2,1)S(1)}, bf16[128,640]{1,0:T(8,128)(2,1)S(1)}, u32[]{:S(2)}, u32[]{:S(2)}) collective-permute-start(bf16[128,640]{1,0:T(8,128)(2,1)S(1)} %get-tuple-element.357), channel_id=1, source_target_pairs={{0,3},{1,0},{2,1},{3,2},{4,11},{5,8},{6,9},{7,10},{8,7},{9,4},{10,... | collective-permute-start | bytes 491528 | tf_op jit(solution)/shard_map/ppermute | solution.py:147
  14.4 7.5 %collective-permute-start.6 = (s32[128]{0:T(128)S(1)}, s32[128]{0:T(128)S(1)}, u32[]{:S(2)}, u32[]{:S(2)}) collective-permute-start(s32[128]{0:T(128)S(1)} %get-tuple-element.378), channel_id=1, source_target_pairs={{0,1},{1,2},{2,3},{3,0},{4,9},{5,10},{6,11},{7,8},{8,5},{9,6},{10,... | collective-permute-start | bytes 1544 | tf_op jit(solution)/shard_map/ppermute | solution.py:147
  16.4 6.2 collective-permute-start.7
  17.5 6.7 %collective-permute-start.1 = (bf16[128,640]{1,0:T(8,128)(2,1)S(1)}, bf16[128,640]{1,0:T(8,128)(2,1)S(1)}, u32[]{:S(2)}, u32[]{:S(2)}) collective-permute-start(bf16[128,640]{1,0:T(8,128)(2,1)S(1)} %get-tuple-element.356), channel_id=1, source_target_pairs={{0,2},{1,3},{2,0},{3,1},{4,10},{5,11},{6,8},{7,9},{8,6},{9,7},{10,... | collective-permute-start | bytes 491528 | tf_op jit(solution)/shard_map/ppermute | solution.py:147
  20.0 6.9 %collective-permute-start.2 = (bf16[128,640]{1,0:T(8,128)(2,1)S(1)}, bf16[128,640]{1,0:T(8,128)(2,1)S(1)}, u32[]{:S(2)}, u32[]{:S(2)}) collective-permute-start(bf16[128,640]{1,0:T(8,128)(2,1)S(1)} %get-tuple-element.358), channel_id=1, source_target_pairs={{0,1},{1,2},{2,3},{3,0},{4,9},{5,10},{6,11},{7,8},{8,5},{9,6},{10,... | collective-permute-start | bytes 491528 | tf_op jit(solution)/shard_map/ppermute | solution.py:147
  172.0 7.3 %collective-permute-start.8 = (bf16[512,512]{1,0:T(8,128)(2,1)S(1)}, bf16[512,512]{1,0:T(8,128)(2,1)S(1)}, u32[]{:S(2)}, u32[]{:S(2)}) collective-permute-start(bf16[512,512]{1,0:T(8,128)(2,1)S(1)} %get-tuple-element.161.own_ref), channel_id=1, source_target_pairs={{0,8},{1,9},{2,10},{3,11},{4,12},{5,13},{6,14},{7,15},{16,24},{17,... | collective-permute-start | bytes 1572872 | tf_op jit(solution)/shard_map/ppermute | solution.py:177
  202.9 12.8 %collective-permute-start.14 = (bf16[128,640]{1,0:T(8,128)(2,1)}, bf16[128,640]{1,0:T(8,128)(2,1)S(1)}, u32[]{:S(2)}, u32[]{:S(2)}) collective-permute-start(bf16[128,640]{1,0:T(8,128)(2,1)} %get-tuple-element.350), channel_id=1, source_target_pairs={{0,3},{1,0},{2,1},{3,2},{4,11},{5,8},{6,9},{7,10},{8,7},{9,4},{10,... | collective-permute-start | bytes 491528 | tf_op jit(solution)/shard_map/ppermute | solution.py:147
  207.0 14.9 %collective-permute-start.9 = (bf16[512,512]{1,0:T(8,128)(2,1)S(1)}, bf16[512,512]{1,0:T(8,128)(2,1)S(1)}, u32[]{:S(2)}, u32[]{:S(2)}) collective-permute-start(bf16[512,512]{1,0:T(8,128)(2,1)S(1)} %get-tuple-element.166.own_ref), channel_id=1, source_target_pairs={{0,8},{1,9},{2,10},{3,11},{4,12},{5,13},{6,14},{7,15},{16,24},{17,... | collective-permute-start | bytes 1572872 | tf_op jit(solution)/shard_map/ppermute | solution.py:177
  210.7 7.2 %collective-permute-start.15 = (bf16[128,640]{1,0:T(8,128)(2,1)S(1)}, bf16[128,640]{1,0:T(8,128)(2,1)S(1)}, u32[]{:S(2)}, u32[]{:S(2)}) collective-permute-start(bf16[128,640]{1,0:T(8,128)(2,1)S(1)} %copy-done.165), channel_id=1, source_target_pairs={{0,2},{1,3},{2,0},{3,1},{4,10},{5,11},{6,8},{7,9},{8,6},{9,7},{10,... | collective-permute-start | bytes 491528 | tf_op jit(solution)/shard_map/ppermute | solution.py:147
  211.5 10.0 %collective-permute-start.16 = (bf16[128,640]{1,0:T(8,128)(2,1)S(1)}, bf16[128,640]{1,0:T(8,128)(2,1)S(1)}, u32[]{:S(2)}, u32[]{:S(2)}) collective-permute-start(bf16[128,640]{1,0:T(8,128)(2,1)S(1)} %copy-done.164), channel_id=1, source_target_pairs={{0,1},{1,2},{2,3},{3,0},{4,9},{5,10},{6,11},{7,8},{8,5},{9,6},{10,... | collective-permute-start | bytes 491528 | tf_op jit(solution)/shard_map/ppermute | solution.py:147
  211.9 9.6 %collective-permute-start.17 = (bf16[128,640]{1,0:T(8,128)(2,1)S(1)}, bf16[128,640]{1,0:T(8,128)(2,1)S(1)}, u32[]{:S(2)}, u32[]{:S(2)}) collective-permute-start(bf16[128,640]{1,0:T(8,128)(2,1)S(1)} %copy-done.163), channel_id=1, source_target_pairs={{0,0},{1,1},{2,2},{3,3},{4,8},{5,9},{6,10},{7,11},{8,4},{9,5},{10,... | collective-permute-start | bytes 491528 | tf_op jit(solution)/shard_map/ppermute | solution.py:147
  270.3 10.0 %collective-permute-start.18 = (bf16[2,8,128,384]{3,2,1,0:T(8,128)(2,1)}, bf16[2,8,128,384]{3,2,1,0:T(8,128)(2,1)}, u32[]{:S(2)}, u32[]{:S(2)}) collective-permute-start(bf16[2,8,128,384]{3,2,1,0:T(8,128)(2,1)} %weight_gradient.26), channel_id=1, source_target_pairs={{0,8},{8,0},{16,24},{24,16},{1,9},{9,1},{17,25},{25,17},{2,10},{10... | collective-permute-start | bytes 4718600 | tf_op jit(solution)/shard_map/ppermute | solution.py:198
  272.5 7.7 %collective-permute-start.20 = (bf16[2,8,64,640]{3,2,1,0:T(8,128)(2,1)}, bf16[2,8,64,640]{3,2,1,0:T(8,128)(2,1)}, u32[]{:S(2)}, u32[]{:S(2)}) collective-permute-start(bf16[2,8,64,640]{3,2,1,0:T(8,128)(2,1)} %weight_gradient.28), channel_id=1, source_target_pairs={{0,8},{8,0},{16,24},{24,16},{1,9},{9,1},{17,25},{25,17},{2,10},{10... | collective-permute-start | bytes 3932168 | tf_op jit(solution)/shard_map/ppermute | solution.py:198
  272.5 7.7 %collective-permute-start.19 = (bf16[2,8,128,256]{3,2,1,0:T(8,128)(2,1)}, bf16[2,8,128,256]{3,2,1,0:T(8,128)(2,1)}, u32[]{:S(2)}, u32[]{:S(2)}) collective-permute-start(bf16[2,8,128,256]{3,2,1,0:T(8,128)(2,1)} %weight_gradient.27), channel_id=1, source_target_pairs={{0,8},{8,0},{16,24},{24,16},{1,9},{9,1},{17,25},{25,17},{2,10},{10... | collective-permute-start | bytes 3145736 | tf_op jit(solution)/shard_map/ppermute | solution.py:198
  273.0 7.2 %collective-permute-start.21 = (bf16[2,8,32,640]{3,2,1,0:T(8,128)(2,1)}, bf16[2,8,32,640]{3,2,1,0:T(8,128)(2,1)}, u32[]{:S(2)}, u32[]{:S(2)}) collective-permute-start(bf16[2,8,32,640]{3,2,1,0:T(8,128)(2,1)} %weight_gradient.29), channel_id=1, source_target_pairs={{0,8},{8,0},{16,24},{24,16},{1,9},{9,1},{17,25},{25,17},{2,10},{10... | collective-permute-start | bytes 1966088 | tf_op jit(solution)/shard_map/ppermute | solution.py:198
  321.1 29.5 %collective-permute-start.23 = (bf16[2,8,64,640]{3,2,1,0:T(8,128)(2,1)}, bf16[2,8,64,640]{3,2,1,0:T(8,128)(2,1)}, u32[]{:S(2)}, u32[]{:S(2)}) collective-permute-start(bf16[2,8,64,640]{3,2,1,0:T(8,128)(2,1)} %pad_maximum_fusion), channel_id=1, source_target_pairs={{0,8},{8,0},{16,24},{24,16},{1,9},{9,1},{17,25},{25,17},{2,10},{10... | collective-permute-start | bytes 3932168 | tf_op jit(solution)/shard_map/ppermute | solution.py:198
  321.9 28.1 %collective-permute-start.26 = (bf16[1,8,64,640]{3,2,1,0:T(8,128)(2,1)}, bf16[1,8,64,640]{3,2,1,0:T(8,128)(2,1)}, u32[]{:S(2)}, u32[]{:S(2)}) collective-permute-start(bf16[1,8,64,640]{3,2,1,0:T(8,128)(2,1)} %weight_gradient.32), channel_id=1, source_target_pairs={{0,16},{8,24},{16,0},{24,8},{1,17},{9,25},{17,1},{25,9},{2,18},{10... | collective-permute-start | bytes 1966088 | tf_op jit(solution)/shard_map/ppermute | solution.py:198
  323.9 23.3 %collective-permute-start.25 = (bf16[2,4,128,256]{3,2,1,0:T(8,128)(2,1)}, bf16[2,4,128,256]{3,2,1,0:T(8,128)(2,1)}, u32[]{:S(2)}, u32[]{:S(2)}) collective-permute-start(bf16[2,4,128,256]{3,2,1,0:T(8,128)(2,1)} %get-tuple-element.211), channel_id=1, source_target_pairs={{0,1},{1,0},{2,3},{3,2},{4,5},{5,4},{6,7},{7,6},{8,9},{9,8},{10,11... | collective-permute-start | bytes 1572872 | tf_op jit(solution)/shard_map/ppermute | solution.py:198
  329.0 18.2 %collective-permute-start.24 = (bf16[2,4,32,640]{3,2,1,0:T(8,128)(2,1)}, bf16[2,4,32,640]{3,2,1,0:T(8,128)(2,1)}, u32[]{:S(2)}, u32[]{:S(2)}) collective-permute-start(bf16[2,4,32,640]{3,2,1,0:T(8,128)(2,1)} %get-tuple-element.210), channel_id=1, source_target_pairs={{0,1},{1,0},{2,3},{3,2},{4,5},{5,4},{6,7},{7,6},{8,9},{9,8},{10,11... | collective-permute-start | bytes 983048 | tf_op jit(solution)/shard_map/ppermute | solution.py:198
  332.0 62.7 %collective-permute-start.11 = (bf16[128,640]{1,0:T(8,128)(2,1)S(1)}, bf16[128,640]{1,0:T(8,128)(2,1)S(1)}, u32[]{:S(2)}, u32[]{:S(2)}) collective-permute-start(bf16[128,640]{1,0:T(8,128)(2,1)S(1)} %copy-done.162), channel_id=1, source_target_pairs={{1,0},{2,1},{3,2},{0,3},{9,4},{10,5},{11,6},{8,7},{5,8},{6,9},{7,1... | collective-permute-start | bytes 491528 | tf_op jit(solution)/shard_map/ppermute | solution.py:160
  347.2 48.9 %collective-permute-start.12 = (bf16[128,640]{1,0:T(8,128)(2,1)S(1)}, bf16[128,640]{1,0:T(8,128)(2,1)S(1)}, u32[]{:S(2)}, u32[]{:S(2)}) collective-permute-start(bf16[128,640]{1,0:T(8,128)(2,1)S(1)} %copy-done.161), channel_id=1, source_target_pairs={{2,0},{3,1},{0,2},{1,3},{10,4},{11,5},{8,6},{9,7},{6,8},{7,9},{4,1... | collective-permute-start | bytes 491528 | tf_op jit(solution)/shard_map/ppermute | solution.py:160
  347.2 52.4 %collective-permute-start.13 = (bf16[128,640]{1,0:T(8,128)(2,1)}, bf16[128,640]{1,0:T(8,128)(2,1)}, u32[]{:S(2)}, u32[]{:S(2)}) collective-permute-start(bf16[128,640]{1,0:T(8,128)(2,1)} %get-tuple-element.351), channel_id=1, source_target_pairs={{3,0},{0,1},{1,2},{2,3},{11,4},{8,5},{9,6},{10,7},{7,8},{4,9},{5,1... | collective-permute-start | bytes 491528 | tf_op jit(solution)/shard_map/ppermute | solution.py:160
  350.0 49.8 %collective-permute-start.31 = (bf16[1,8,128,384]{3,2,1,0:T(8,128)(2,1)}, bf16[1,8,128,384]{3,2,1,0:T(8,128)(2,1)}, u32[]{:S(2)}, u32[]{:S(2)}) collective-permute-start(bf16[1,8,128,384]{3,2,1,0:T(8,128)(2,1)} %weight_gradient.30), channel_id=1, source_target_pairs={{0,16},{8,24},{16,0},{24,8},{1,17},{9,25},{17,1},{25,9},{2,18},{10... | collective-permute-start | bytes 2359304 | tf_op jit(solution)/shard_map/ppermute | solution.py:198
  393.8 37.2 %collective-permute-start.27 = (bf16[2,8,128,384]{3,2,1,0:T(8,128)(2,1)}, bf16[2,8,128,384]{3,2,1,0:T(8,128)(2,1)}, u32[]{:S(2)}, u32[]{:S(2)}) collective-permute-start(bf16[2,8,128,384]{3,2,1,0:T(8,128)(2,1)} %weight_gradient.37), channel_id=1, source_target_pairs={{0,8},{8,0},{16,24},{24,16},{1,9},{9,1},{17,25},{25,17},{2,10},{10... | collective-permute-start | bytes 4718600 | tf_op jit(solution)/shard_map/ppermute | solution.py:198
  396.1 34.9 %collective-permute-start.29 = (bf16[2,8,64,640]{3,2,1,0:T(8,128)(2,1)}, bf16[2,8,64,640]{3,2,1,0:T(8,128)(2,1)}, u32[]{:S(2)}, u32[]{:S(2)}) collective-permute-start(bf16[2,8,64,640]{3,2,1,0:T(8,128)(2,1)} %weight_gradient.39), channel_id=1, source_target_pairs={{0,8},{8,0},{16,24},{24,16},{1,9},{9,1},{17,25},{25,17},{2,10},{10... | collective-permute-start | bytes 3932168 | tf_op jit(solution)/shard_map/ppermute | solution.py:198
  396.1 6.9 %collective-permute-start.35 = (bf16[2,2,32,640]{3,2,1,0:T(8,128)(2,1)}, bf16[2,2,32,640]{3,2,1,0:T(8,128)(2,1)}, u32[]{:S(2)}, u32[]{:S(2)}) collective-permute-start(bf16[2,2,32,640]{3,2,1,0:T(8,128)(2,1)} %bitcast.51), channel_id=1, source_target_pairs={{0,16},{8,24},{16,0},{24,8},{1,17},{9,25},{17,1},{25,9},{2,18},{10... | collective-permute-start | bytes 491528 | tf_op jit(solution)/shard_map/ppermute | solution.py:198
  399.6 31.3 %collective-permute-start.28 = (bf16[2,8,128,256]{3,2,1,0:T(8,128)(2,1)}, bf16[2,8,128,256]{3,2,1,0:T(8,128)(2,1)}, u32[]{:S(2)}, u32[]{:S(2)}) collective-permute-start(bf16[2,8,128,256]{3,2,1,0:T(8,128)(2,1)} %copy-done.78), channel_id=1, source_target_pairs={{0,8},{8,0},{16,24},{24,16},{1,9},{9,1},{17,25},{25,17},{2,10},{10... | collective-permute-start | bytes 3145736 | tf_op jit(solution)/shard_map/ppermute | solution.py:198
  399.8 8.9 %collective-permute-start.32 = (bf16[2,2,128,256]{2,3,1,0:T(8,128)(2,1)}, bf16[2,2,128,256]{2,3,1,0:T(8,128)(2,1)}, u32[]{:S(2)}, u32[]{:S(2)}) collective-permute-start(bf16[2,2,128,256]{2,3,1,0:T(8,128)(2,1)} %copy.61), channel_id=1, source_target_pairs={{0,16},{8,24},{16,0},{24,8},{1,17},{9,25},{17,1},{25,9},{2,18},{10... | collective-permute-start | bytes 786440 | tf_op jit(solution)/shard_map/ppermute | solution.py:198
  403.0 9.6 %collective-permute-start.33 = (bf16[2,2,64,640]{3,2,1,0:T(8,128)(2,1)}, bf16[2,2,64,640]{3,2,1,0:T(8,128)(2,1)}, u32[]{:S(2)}, u32[]{:S(2)}) collective-permute-start(bf16[2,2,64,640]{3,2,1,0:T(8,128)(2,1)} %slice_bitcast_fusion.9), channel_id=1, source_target_pairs={{0,1},{1,0},{2,3},{3,2},{4,5},{5,4},{6,7},{7,6},{8,9},{9,8},{10,11... | collective-permute-start | bytes 983048 | tf_op jit(solution)/shard_map/ppermute | solution.py:198
  408.7 22.3 %collective-permute-start.30 = (bf16[2,8,32,640]{3,2,1,0:T(8,128)(2,1)}, bf16[2,8,32,640]{3,2,1,0:T(8,128)(2,1)}, u32[]{:S(2)}, u32[]{:S(2)}) collective-permute-start(bf16[2,8,32,640]{3,2,1,0:T(8,128)(2,1)} %copy-done.79), channel_id=1, source_target_pairs={{0,8},{8,0},{16,24},{24,16},{1,9},{9,1},{17,25},{25,17},{2,10},{10... | collective-permute-start | bytes 1966088 | tf_op jit(solution)/shard_map/ppermute | solution.py:198
  412.6 18.3 %collective-permute-start.34 = (bf16[1,8,64,640]{3,2,1,0:T(8,128)(2,1)}, bf16[1,8,64,640]{3,2,1,0:T(8,128)(2,1)}, u32[]{:S(2)}, u32[]{:S(2)}) collective-permute-start(bf16[1,8,64,640]{3,2,1,0:T(8,128)(2,1)} %pad_maximum_fusion.2), channel_id=1, source_target_pairs={{0,16},{8,24},{16,0},{24,8},{1,17},{9,25},{17,1},{25,9},{2,18},{10... | collective-permute-start | bytes 1966088 | tf_op jit(solution)/shard_map/ppermute | solution.py:198
  459.4 24.7 %collective-permute-start.36 = (bf16[2,32,640]{2,1,0:T(8,128)(2,1)S(1)}, bf16[2,32,640]{2,1,0:T(8,128)(2,1)}, u32[]{:S(2)}, u32[]{:S(2)}) collective-permute-start(bf16[2,32,640]{2,1,0:T(8,128)(2,1)S(1)} %slice_bitcast_fusion.43), channel_id=1, source_target_pairs={{0,4},{1,5},{2,6},{3,7},{4,0},{5,1},{6,2},{7,3},{8,12},{9,13},{10,... | collective-permute-start | bytes 245768 | tf_op jit(solution)/shard_map/ppermute | solution.py:198
  462.3 23.4 %collective-permute-start.37 = (bf16[2,2,64,640]{3,2,1,0:T(8,128)(2,1)}, bf16[2,2,64,640]{3,2,1,0:T(8,128)(2,1)}, u32[]{:S(2)}, u32[]{:S(2)}) collective-permute-start(bf16[2,2,64,640]{3,2,1,0:T(8,128)(2,1)} %slice_bitcast_fusion.7), channel_id=1, source_target_pairs={{0,1},{1,0},{2,3},{3,2},{4,5},{5,4},{6,7},{7,6},{8,9},{9,8},{10,11... | collective-permute-start | bytes 983048 | tf_op jit(solution)/shard_map/ppermute | solution.py:198
  462.6 31.8 %collective-permute-start.38 = (bf16[2,2,128,384]{2,3,1,0:T(8,128)(2,1)}, bf16[2,2,128,384]{2,3,1,0:T(8,128)(2,1)}, u32[]{:S(2)}, u32[]{:S(2)}) collective-permute-start(bf16[2,2,128,384]{2,3,1,0:T(8,128)(2,1)} %bitcast.56), channel_id=1, source_target_pairs={{0,1},{1,0},{2,3},{3,2},{4,5},{5,4},{6,7},{7,6},{8,9},{9,8},{10,11... | collective-permute-start | bytes 1179656 | tf_op jit(solution)/shard_map/ppermute | solution.py:198
  464.4 26.9 %collective-permute-start.39 = (bf16[2,128,256]{1,2,0:T(8,128)(2,1)}, bf16[2,128,256]{1,2,0:T(8,128)(2,1)}, u32[]{:S(2)}, u32[]{:S(2)}) collective-permute-start(bf16[2,128,256]{1,2,0:T(8,128)(2,1)} %slice_bitcast_fusion.27), channel_id=1, source_target_pairs={{0,4},{1,5},{2,6},{3,7},{4,0},{5,1},{6,2},{7,3},{8,12},{9,13},{10,... | collective-permute-start | bytes 393224 | tf_op jit(solution)/shard_map/ppermute | solution.py:198
  464.5 28.5 %collective-permute-start.40 = (bf16[2,64,640]{2,1,0:T(8,128)(2,1)}, bf16[2,64,640]{2,1,0:T(8,128)(2,1)}, u32[]{:S(2)}, u32[]{:S(2)}) collective-permute-start(bf16[2,64,640]{2,1,0:T(8,128)(2,1)} %slice_bitcast_fusion.23), channel_id=1, source_target_pairs={{0,4},{1,5},{2,6},{3,7},{4,0},{5,1},{6,2},{7,3},{8,12},{9,13},{10,... | collective-permute-start | bytes 491528 | tf_op jit(solution)/shard_map/ppermute | solution.py:198
  484.1 15.4 %collective-permute-start.41 = (bf16[512,512]{1,0:T(8,128)(2,1)S(1)}, bf16[512,512]{1,0:T(8,128)(2,1)S(1)}, u32[]{:S(2)}, u32[]{:S(2)}) collective-permute-start(bf16[512,512]{1,0:T(8,128)(2,1)S(1)} %get-tuple-element.273), channel_id=1, source_target_pairs={{8,0},{9,1},{10,2},{11,3},{12,4},{13,5},{14,6},{15,7},{24,16},{25,... | collective-permute-start | bytes 1572872 | tf_op jit(solution)/shard_map/ppermute | solution.py:177
  485.7 30.8 %collective-permute-start.42 = (bf16[2,4,32,640]{3,2,1,0:T(8,128)(2,1)}, bf16[2,4,32,640]{3,2,1,0:T(8,128)(2,1)}, u32[]{:S(2)}, u32[]{:S(2)}) collective-permute-start(bf16[2,4,32,640]{3,2,1,0:T(8,128)(2,1)} %get-tuple-element.283), channel_id=1, source_target_pairs={{0,1},{1,0},{2,3},{3,2},{4,5},{5,4},{6,7},{7,6},{8,9},{9,8},{10,11... | collective-permute-start | bytes 983048 | tf_op jit(solution)/shard_map/ppermute | solution.py:198
  491.3 37.8 %collective-permute-start.43 = (bf16[2,4,128,256]{3,2,1,0:T(8,128)(2,1)}, bf16[2,4,128,256]{3,2,1,0:T(8,128)(2,1)}, u32[]{:S(2)}, u32[]{:S(2)}) collective-permute-start(bf16[2,4,128,256]{3,2,1,0:T(8,128)(2,1)} %get-tuple-element.284), channel_id=1, source_target_pairs={{0,1},{1,0},{2,3},{3,2},{4,5},{5,4},{6,7},{7,6},{8,9},{9,8},{10,11... | collective-permute-start | bytes 1572872 | tf_op jit(solution)/shard_map/ppermute | solution.py:198
  493.0 36.0 %collective-permute-start.44 = (bf16[1,8,64,640]{3,2,1,0:T(8,128)(2,1)}, bf16[1,8,64,640]{3,2,1,0:T(8,128)(2,1)}, u32[]{:S(2)}, u32[]{:S(2)}) collective-permute-start(bf16[1,8,64,640]{3,2,1,0:T(8,128)(2,1)} %weight_gradient.43), channel_id=1, source_target_pairs={{0,16},{8,24},{16,0},{24,8},{1,17},{9,25},{17,1},{25,9},{2,18},{10... | collective-permute-start | bytes 1966088 | tf_op jit(solution)/shard_map/ppermute | solution.py:198
  494.4 23.4 %collective-permute-start.46 = (bf16[32,640]{1,0:T(8,128)(2,1)}, bf16[32,640]{1,0:T(8,128)(2,1)S(1)}, u32[]{:S(2)}, u32[]{:S(2)}) collective-permute-start(bf16[32,640]{1,0:T(8,128)(2,1)} %slice_bitcast_fusion.51), channel_id=1, source_target_pairs={{0,2},{1,3},{2,0},{3,1},{4,6},{5,7},{6,4},{7,5},{8,10},{9,11},{10,... | collective-permute-start | bytes 122888 | tf_op jit(solution)/shard_map/ppermute | solution.py:198
  499.5 29.5 %collective-permute-start.47 = (bf16[2,128,384]{1,2,0:T(8,128)(2,1)}, bf16[2,128,384]{1,2,0:T(8,128)(2,1)}, u32[]{:S(2)}, u32[]{:S(2)}) collective-permute-start(bf16[2,128,384]{1,2,0:T(8,128)(2,1)} %slice_bitcast_fusion.15), channel_id=1, source_target_pairs={{0,4},{1,5},{2,6},{3,7},{4,0},{5,1},{6,2},{7,3},{8,12},{9,13},{10,... | collective-permute-start | bytes 589832 | tf_op jit(solution)/shard_map/ppermute | solution.py:198
  517.8 11.2 %collective-permute-start.45 = (bf16[2,64,640]{2,1,0:T(8,128)(2,1)S(1)}, bf16[2,64,640]{2,1,0:T(8,128)(2,1)S(1)}, u32[]{:S(2)}, u32[]{:S(2)}) collective-permute-start(bf16[2,64,640]{2,1,0:T(8,128)(2,1)S(1)} %copy-done.167), channel_id=1, source_target_pairs={{0,4},{1,5},{2,6},{3,7},{4,0},{5,1},{6,2},{7,3},{8,12},{9,13},{10,... | collective-permute-start | bytes 491528 | tf_op jit(solution)/shard_map/ppermute | solution.py:198
  528.6 30.6 %collective-permute-start.63 = (bf16[1,8,128,384]{3,2,1,0:T(8,128)(2,1)}, bf16[1,8,128,384]{3,2,1,0:T(8,128)(2,1)}, u32[]{:S(2)}, u32[]{:S(2)}) collective-permute-start(bf16[1,8,128,384]{3,2,1,0:T(8,128)(2,1)} %weight_gradient.41), channel_id=1, source_target_pairs={{0,16},{8,24},{16,0},{24,8},{1,17},{9,25},{17,1},{25,9},{2,18},{10... | collective-permute-start | bytes 2359304 | tf_op jit(solution)/shard_map/ppermute | solution.py:198
  529.0 70.7 %collective-permute-start.54 = (bf16[2,8,64,640]{3,2,1,0:T(8,128)(2,1)}, bf16[2,8,64,640]{3,2,1,0:T(8,128)(2,1)}, u32[]{:S(2)}, u32[]{:S(2)}) collective-permute-start(bf16[2,8,64,640]{3,2,1,0:T(8,128)(2,1)} %pad_maximum_fusion.1), channel_id=1, source_target_pairs={{0,8},{8,0},{16,24},{24,16},{1,9},{9,1},{17,25},{25,17},{2,10},{10... | collective-permute-start | bytes 3932168 | tf_op jit(solution)/shard_map/ppermute | solution.py:198
  539.1 23.6 %collective-permute-start.50 = (bf16[128,640]{1,0:T(8,128)(2,1)}, bf16[128,640]{1,0:T(8,128)(2,1)}, u32[]{:S(2)}, u32[]{:S(2)}) collective-permute-start(bf16[128,640]{1,0:T(8,128)(2,1)} %get-tuple-element.346), channel_id=1, source_target_pairs={{0,0},{1,1},{2,2},{3,3},{8,4},{9,5},{10,6},{11,7},{4,8},{5,9},{6,1... | collective-permute-start | bytes 491528 | tf_op jit(solution)/shard_map/ppermute | solution.py:160
  542.0 22.7 %collective-permute-start.51 = (bf16[128,640]{1,0:T(8,128)(2,1)}, bf16[128,640]{1,0:T(8,128)(2,1)}, u32[]{:S(2)}, u32[]{:S(2)}) collective-permute-start(bf16[128,640]{1,0:T(8,128)(2,1)} %get-tuple-element.345), channel_id=1, source_target_pairs={{1,0},{2,1},{3,2},{0,3},{9,4},{10,5},{11,6},{8,7},{5,8},{6,9},{7,1... | collective-permute-start | bytes 491528 | tf_op jit(solution)/shard_map/ppermute | solution.py:160
  542.5 9.4 %collective-permute-start.59 = (bf16[64,640]{1,0:T(8,128)(2,1)}, bf16[64,640]{1,0:T(8,128)(2,1)}, u32[]{:S(2)}, u32[]{:S(2)}) collective-permute-start(bf16[64,640]{1,0:T(8,128)(2,1)} %slice_bitcast_fusion.40), channel_id=1, source_target_pairs={{0,2},{1,3},{2,0},{3,1},{4,6},{5,7},{6,4},{7,5},{8,10},{9,11},{10,... | collective-permute-start | bytes 245768 | tf_op jit(solution)/shard_map/ppermute | solution.py:198
  557.3 9.4 %collective-permute-start.52 = (bf16[128,640]{1,0:T(8,128)(2,1)}, bf16[128,640]{1,0:T(8,128)(2,1)}, u32[]{:S(2)}, u32[]{:S(2)}) collective-permute-start(bf16[128,640]{1,0:T(8,128)(2,1)} %get-tuple-element.344), channel_id=1, source_target_pairs={{2,0},{3,1},{0,2},{1,3},{10,4},{11,5},{8,6},{9,7},{6,8},{7,9},{4,1... | collective-permute-start | bytes 491528 | tf_op jit(solution)/shard_map/ppermute | solution.py:160
  559.2 13.8 %collective-permute-start.53 = (bf16[128,640]{1,0:T(8,128)(2,1)}, bf16[128,640]{1,0:T(8,128)(2,1)}, u32[]{:S(2)}, u32[]{:S(2)}) collective-permute-start(bf16[128,640]{1,0:T(8,128)(2,1)} %get-tuple-element.343), channel_id=1, source_target_pairs={{3,0},{0,1},{1,2},{2,3},{11,4},{8,5},{9,6},{10,7},{7,8},{4,9},{5,1... | collective-permute-start | bytes 491528 | tf_op jit(solution)/shard_map/ppermute | solution.py:160
  562.7 8.2 %collective-permute-start.60 = (bf16[2,2,32,640]{3,2,1,0:T(8,128)(2,1)}, bf16[2,2,32,640]{3,2,1,0:T(8,128)(2,1)S(1)}, u32[]{:S(2)}, u32[]{:S(2)}) collective-permute-start(bf16[2,2,32,640]{3,2,1,0:T(8,128)(2,1)} %bitcast.417), channel_id=1, source_target_pairs={{0,16},{8,24},{16,0},{24,8},{1,17},{9,25},{17,1},{25,9},{2,18},{10... | collective-permute-start | bytes 491528 | tf_op jit(solution)/shard_map/ppermute | solution.py:198
  564.8 18.4 %collective-permute-start.68 = (bf16[2,2,128,256]{2,3,1,0:T(8,128)(2,1)}, bf16[2,2,128,256]{2,3,1,0:T(8,128)(2,1)S(1)}, u32[]{:S(2)}, u32[]{:S(2)}) collective-permute-start(bf16[2,2,128,256]{2,3,1,0:T(8,128)(2,1)} %copy.76), channel_id=1, source_target_pairs={{0,16},{8,24},{16,0},{24,8},{1,17},{9,25},{17,1},{25,9},{2,18},{10... | collective-permute-start | bytes 786440 | tf_op jit(solution)/shard_map/ppermute | solution.py:198
  566.7 19.1 %collective-permute-start.71 = (bf16[2,2,64,640]{3,2,1,0:T(8,128)(2,1)}, bf16[2,2,64,640]{3,2,1,0:T(8,128)(2,1)S(1)}, u32[]{:S(2)}, u32[]{:S(2)}) collective-permute-start(bf16[2,2,64,640]{3,2,1,0:T(8,128)(2,1)} %slice_bitcast_fusion.4), channel_id=1, source_target_pairs={{0,1},{1,0},{2,3},{3,2},{4,5},{5,4},{6,7},{7,6},{8,9},{9,8},{10,11... | collective-permute-start | bytes 983048 | tf_op jit(solution)/shard_map/ppermute | solution.py:198
  570.9 33.8 %collective-permute-start.64 = (bf16[2,2,128,384]{2,3,1,0:T(8,128)(2,1)}, bf16[2,2,128,384]{2,3,1,0:T(8,128)(2,1)S(1)}, u32[]{:S(2)}, u32[]{:S(2)}) collective-permute-start(bf16[2,2,128,384]{2,3,1,0:T(8,128)(2,1)} %bitcast.115), channel_id=1, source_target_pairs={{0,1},{1,0},{2,3},{3,2},{4,5},{5,4},{6,7},{7,6},{8,9},{9,8},{10,11... | collective-permute-start | bytes 1179656 | tf_op jit(solution)/shard_map/ppermute | solution.py:198
  573.0 7.1 %collective-permute-start.61 = (bf16[2,32,640]{2,1,0:T(8,128)(2,1)S(1)}, bf16[2,32,640]{2,1,0:T(8,128)(2,1)S(1)}, u32[]{:S(2)}, u32[]{:S(2)}) collective-permute-start(bf16[2,32,640]{2,1,0:T(8,128)(2,1)S(1)} %slice_bitcast_fusion.35), channel_id=1, source_target_pairs={{0,4},{1,5},{2,6},{3,7},{4,0},{5,1},{6,2},{7,3},{8,12},{9,13},{10,... | collective-permute-start | bytes 245768 | tf_op jit(solution)/shard_map/ppermute | solution.py:198
  583.2 6.9 %collective-permute-start.69 = (bf16[2,128,256]{1,2,0:T(8,128)(2,1)S(1)}, bf16[2,128,256]{1,2,0:T(8,128)(2,1)S(1)}, u32[]{:S(2)}, u32[]{:S(2)}) collective-permute-start(bf16[2,128,256]{1,2,0:T(8,128)(2,1)S(1)} %slice_bitcast_fusion.24), channel_id=1, source_target_pairs={{0,4},{1,5},{2,6},{3,7},{4,0},{5,1},{6,2},{7,3},{8,12},{9,13},{10,... | collective-permute-start | bytes 393224 | tf_op jit(solution)/shard_map/ppermute | solution.py:198
  590.2 9.4 %collective-permute-start.72 = (bf16[2,64,640]{2,1,0:T(8,128)(2,1)S(1)}, bf16[2,64,640]{2,1,0:T(8,128)(2,1)S(1)}, u32[]{:S(2)}, u32[]{:S(2)}) collective-permute-start(bf16[2,64,640]{2,1,0:T(8,128)(2,1)S(1)} %slice_bitcast_fusion.16), channel_id=1, source_target_pairs={{0,4},{1,5},{2,6},{3,7},{4,0},{5,1},{6,2},{7,3},{8,12},{9,13},{10,... | collective-permute-start | bytes 491528 | tf_op jit(solution)/shard_map/ppermute | solution.py:198
  599.7 7.6 %collective-permute-start.73 = (bf16[64,640]{1,0:T(8,128)(2,1)S(1)}, bf16[64,640]{1,0:T(8,128)(2,1)S(1)}, u32[]{:S(2)}, u32[]{:S(2)}) collective-permute-start(bf16[64,640]{1,0:T(8,128)(2,1)S(1)} %slice_bitcast_fusion.33), channel_id=1, source_target_pairs={{0,2},{1,3},{2,0},{3,1},{4,6},{5,7},{6,4},{7,5},{8,10},{9,11},{10,... | collective-permute-start | bytes 245768 | tf_op jit(solution)/shard_map/ppermute | solution.py:198
  603.3 15.7 %collective-permute-start.55 = (bf16[1,8,64,640]{3,2,1,0:T(8,128)(2,1)S(1)}, bf16[1,8,64,640]{3,2,1,0:T(8,128)(2,1)S(1)}, u32[]{:S(2)}, u32[]{:S(2)}) collective-permute-start(bf16[1,8,64,640]{3,2,1,0:T(8,128)(2,1)S(1)} %pad_maximum_fusion.3), channel_id=1, source_target_pairs={{0,16},{8,24},{16,0},{24,8},{1,17},{9,25},{17,1},{25,9},{2,18},{10... | collective-permute-start | bytes 1966088 | tf_op jit(solution)/shard_map/ppermute | solution.py:198
  604.9 14.9 %collective-permute-start.65 = (bf16[2,128,384]{1,2,0:T(8,128)(2,1)S(1)}, bf16[2,128,384]{1,2,0:T(8,128)(2,1)S(1)}, u32[]{:S(2)}, u32[]{:S(2)}) collective-permute-start(bf16[2,128,384]{1,2,0:T(8,128)(2,1)S(1)} %slice_bitcast_fusion.12), channel_id=1, source_target_pairs={{0,4},{1,5},{2,6},{3,7},{4,0},{5,1},{6,2},{7,3},{8,12},{9,13},{10,... | collective-permute-start | bytes 589832 | tf_op jit(solution)/shard_map/ppermute | solution.py:198
  619.2 7.8 %collective-permute-start.56 = (bf16[2,2,64,640]{3,2,1,0:T(8,128)(2,1)S(1)}, bf16[2,2,64,640]{3,2,1,0:T(8,128)(2,1)S(1)}, u32[]{:S(2)}, u32[]{:S(2)}) collective-permute-start(bf16[2,2,64,640]{3,2,1,0:T(8,128)(2,1)S(1)} %slice_bitcast_fusion.1), channel_id=1, source_target_pairs={{0,1},{1,0},{2,3},{3,2},{4,5},{5,4},{6,7},{7,6},{8,9},{9,8},{10,11... | collective-permute-start | bytes 983048 | tf_op jit(solution)/shard_map/ppermute | solution.py:198
  619.9 9.3 %collective-permute-start.66 = (bf16[128,384]{0,1:T(8,128)(2,1)S(1)}, bf16[128,384]{0,1:T(8,128)(2,1)S(1)}, u32[]{:S(2)}, u32[]{:S(2)}) collective-permute-start(bf16[128,384]{0,1:T(8,128)(2,1)S(1)} %slice_bitcast_fusion.29), channel_id=1, source_target_pairs={{0,2},{1,3},{2,0},{3,1},{4,6},{5,7},{6,4},{7,5},{8,10},{9,11},{10,... | collective-permute-start | bytes 294920 | tf_op jit(solution)/shard_map/ppermute | solution.py:198
  627.1 8.1 %collective-permute-start.57 = (bf16[2,64,640]{2,1,0:T(8,128)(2,1)S(1)}, bf16[2,64,640]{2,1,0:T(8,128)(2,1)S(1)}, u32[]{:S(2)}, u32[]{:S(2)}) collective-permute-start(bf16[2,64,640]{2,1,0:T(8,128)(2,1)S(1)} %slice_bitcast_fusion.18), channel_id=1, source_target_pairs={{0,4},{1,5},{2,6},{3,7},{4,0},{5,1},{6,2},{7,3},{8,12},{9,13},{10,... | collective-permute-start | bytes 491528 | tf_op jit(solution)/shard_map/ppermute | solution.py:198
  (192 other events, 1125.2 us)
Sparse Core Ops, SparseCore 0:
  11.5 155.6 all-gather.2

commit v4 on v2

--- a/solution.py
+++ b/solution.py
@@ -185,9 +185,11 @@
     return out
 
 
-def order(first):
+def order(first, scatter):
     core, *wide = bits("dp")
     near, *far = bits("seq")
+    if scatter:
+        return [core] + wide
     if first == "dp":
         return [core] + wide + [near] + far[::-1]
     return [core, near] + wide + far[::-1]
@@ -198,85 +200,117 @@
     return lax.ppermute(array, axis, [(i, i ^ bit) for i in range(lax.axis_size(axis))])
 
 
+def launch(value, chains):
+    chains = [chain for chain in chains if chain.pending is not None]
+    if not chains:
+        return value
+    held = lax.optimization_barrier((value,) + tuple(chain.pending for chain in chains))
+    for chain, pending in zip(chains, held[1:]):
+        chain.got = swap(pending, chain.steps[0])
+        chain.pending = None
+    return held[0]
+
+
 def advance(value, chains):
+    chains = [chain for chain in chains if chain.steps]
     if not chains:
         return value
     held = lax.optimization_barrier((value,) + tuple(chain.got for chain in chains))
     for chain, got in zip(chains, held[1:]):
         chain.got = got
         chain.advance()
-    return held[0]
-
-
-def halving(array):
-    n_seq = lax.axis_size("seq")
-    dims = bits("dp")[::-1] + bits("seq")[::-1]
-    me = lax.axis_index("dp") * n_seq + lax.axis_index("seq")
-    rest = array.shape[1:]
-    array = jnp.take(array, me ^ jnp.arange(array.shape[0]), axis=0)
-    array = array.reshape((2,) * len(dims) + rest)
-    for step in order("dp"):
-        at = dims.index(step)
-        dims.remove(step)
-        keep = lax.index_in_dim(array, 0, at, keepdims=False)
-        array = keep + swap(lax.index_in_dim(array, 1, at, keepdims=False), step)
-    return array
-
-
-def block_numbers():
+    return launch(held[0], chains)
+
+
+def block_numbers(scatter):
     me = lax.axis_index("dp")
     core = me % 2
     wide = [me // 2, (me // 2) ^ 1]
     leave = [2 * w + 1 - core for w in wide]
     stay = [2 * w + core for w in wide]
-    return jnp.stack(leave + stay + [lax.axis_index("seq")]).astype(jnp.int32)
-
-
-def product_kernel(rows, split, added, numbers_ref, a_ref, b_ref, *refs):
-    got_ref = refs[0] if added else None
-    outs, acc = refs[1 if added else 0 : -1], refs[-1]
-    acc[...] = dot(a_ref[...], b_ref[...], 0, 0)
+    along = lax.axis_index("seq") * (0 if scatter else 1)
+    return jnp.stack(leave + stay + [along]).astype(jnp.int32)
+
+
+def product_kernel(pairs, extra, added, split, scatter, columns, n_seq, numbers_ref, *refs):
+    lefts, rights, refs = refs[:pairs], refs[pairs : 2 * pairs], refs[2 * pairs :]
+    if extra:
+        extra_ref, refs = refs[0], refs[1:]
+    if added:
+        got_ref, refs = refs[0], refs[1:]
     me = numbers_ref[4]
-    for entry in range(a_ref.shape[1] // rows):
-        source = pl.multiple_of((me ^ entry) * rows, TILE)
-        value = acc[pl.ds(source, rows), :]
+
+    def store(shard, base, value):
+        entry = me ^ shard
+        if not scatter:
+            entry = lax.rem(entry, 2) * (n_seq // 2) + entry // 2
+        place = slice(base, base + value.shape[0])
         if added:
-            value = value + got_ref[0, entry].astype(F32)
+            value = value + got_ref[0, entry, place].astype(F32)
+        value = value.astype(BF16)
         if split:
-            outs[entry % 2][0, entry // 2] = value.astype(BF16)
+            stays = entry < n_seq // 2
+
+            @pl.when(stays)
+            def _():
+                refs[0][0, entry, place] = value
+
+            @pl.when(jnp.logical_not(stays))
+            def _():
+                refs[1][0, entry - n_seq // 2, place] = value
+
         else:
-            outs[0][0, entry] = value.astype(BF16)
-
-
-def product(left, right, numbers, first, blocks, got=None, got_first=0, split=False):
-    tokens, n_seq = left.shape[0], lax.axis_size("seq")
-    width = left.shape[1] // lax.axis_size("dp")
-    rows = width // n_seq
-    out_entries = n_seq // 2 if split else n_seq
-    specs = [
-        pl.BlockSpec((tokens, width), lambda i, n: (0, n[first + i])),
-        pl.BlockSpec((tokens, D), lambda i, n: (0, 0)),
-    ]
-    operands = [left, right]
+            refs[0][0, entry, place] = value
+
+    base = 0
+    for left, right in zip(lefts, rights):
+        width = left.shape[1]
+        rows = width // n_seq
+        part = min(width, 512)
+        for start in range(0, width, part):
+            total = dot(left[:, start : start + part], right[:, columns], 0, 0)
+            for at in range(0, part, rows):
+                store((start + at) // rows, base, total[at : at + rows])
+        base += rows
+    if extra:
+        for shard in range(n_seq):
+            store(shard, base, extra_ref[0, shard].astype(F32))
+
+
+def product(factors, first, blocks, got=None, got_first=0, split=False):
+    pairs, extra, numbers, columns, scatter = factors
+    n_dp, n_seq = lax.axis_size("dp"), lax.axis_size("seq")
+    tokens = pairs[0][0].shape[0]
+    wide = columns.stop - columns.start
+    widths = [left.shape[1] // n_dp for left, _ in pairs]
+    rows = sum(widths) // n_seq + (0 if extra is None else extra.shape[2])
+    entries = n_seq // 2 if split else n_seq
+    specs = [pl.BlockSpec((tokens, w), lambda i, n: (0, n[first + i])) for w in widths]
+    specs += [pl.BlockSpec(right.shape, lambda i, n: (0, 0)) for _, right in pairs]
+    operands = [left for left, _ in pairs] + [right for _, right in pairs]
+    if extra is not None:
+        specs.append(pl.BlockSpec((1,) + extra.shape[1:], lambda i, n: (n[first + i], 0, 0, 0)))
+        operands.append(extra)
     if got is not None:
-        specs.append(pl.BlockSpec((1, n_seq, rows, D), lambda i, n: (i + got_first, 0, 0, 0)))
+        specs.append(pl.BlockSpec((1, n_seq, rows, wide), lambda i, n: (i + got_first, 0, 0, 0)))
         operands.append(got)
-    shape = jax.ShapeDtypeStruct((blocks, out_entries, rows, D), BF16)
+    shape = jax.ShapeDtypeStruct((blocks, entries, rows, wide), BF16)
     count = 2 if split else 1
     return pl.pallas_call(
-        partial(product_kernel, rows, split, got is not None),
+        partial(
+            product_kernel, len(pairs), extra is not None, got is not None, split, scatter, columns, n_seq
+        ),
         grid_spec=pltpu.PrefetchScalarGridSpec(
             num_scalar_prefetch=1,
             grid=(blocks,),
             in_specs=specs,
-            out_specs=[pl.BlockSpec((1, out_entries, rows, D), lambda i, n: (i, 0, 0, 0))] * count,
-            scratch_shapes=[pltpu.VMEM((width, D), F32)],
+            out_specs=[pl.BlockSpec((1, entries, rows, wide), lambda i, n: (i, 0, 0, 0))] * count,
         ),
         out_shape=[shape] * count,
-        compiler_params=pltpu.CompilerParams(vmem_limit_bytes=24 * 2**20),
+        compiler_params=pltpu.CompilerParams(vmem_limit_bytes=28 * 2**20),
         cost_estimate=pl.CostEstimate(
-            flops=2 * tokens * width * blocks * D,
-            bytes_accessed=2 * (tokens * width * blocks + tokens * D + 2 * width * blocks * D),
+            flops=2 * tokens * sum(widths) * blocks * wide,
+            bytes_accessed=2 * (tokens + 2 * wide) * sum(widths) * blocks,
             transcendentals=0,
         ),
         name="weight_gradient",
@@ -284,54 +318,63 @@
 
 
 class Chain:
-    def __init__(self, left, right, first):
-        self.steps = order(first)
-        self.dims = bits("dp")[::-1] + bits("seq")[::-1]
+    def __init__(self, pairs, first="dp", scatter=False, columns=slice(0, D), extra=None):
+        self.steps = order(first, scatter)
         n_dp, n_seq = lax.axis_size("dp"), lax.axis_size("seq")
-        width = left.shape[1] // n_dp
-        self.rows = width // n_seq
+        widths = [left.shape[1] // n_dp for left, _ in pairs]
         self.factors = None
-        step = self.steps[0]
-        if n_dp == 4 and width % 128 == 0 and self.rows % TILE == 0 and width % n_seq == 0:
-            self.factors = (left, right, block_numbers())
-            (send,) = product(left, right, self.factors[2], 0, 2)
-            self.dims.remove(step)
-            self.got = swap(send, step)
-        else:
-            whole = dot(left, right, 0, 0).astype(BF16).reshape(n_dp * n_seq, self.rows, D)
-            me = lax.axis_index("dp") * n_seq + lax.axis_index("seq")
-            self.send(jnp.take(whole, me ^ jnp.arange(n_dp * n_seq), axis=0))
-
-    def send(self, array):
-        step = self.steps[0]
-        array = array.reshape((2,) * len(self.dims) + (self.rows, D))
-        at = self.dims.index(step)
-        self.dims.remove(step)
-        self.keep = lax.index_in_dim(array, 0, at, keepdims=False)
-        self.got = swap(lax.index_in_dim(array, 1, at, keepdims=False), step)
+        self.shape = (-1, sum(widths) // n_seq + (0 if extra is None else extra.shape[2]), columns.stop - columns.start)
+        if n_dp == 4 and all(w % 128 == 0 and w % (n_seq * TILE) == 0 for w in widths):
+            self.factors = (pairs, extra, block_numbers(scatter), columns, scatter)
+            (self.pending,) = product(self.factors, 0, 2)
+            return
+        devices = n_dp * n_seq
+        parts = [
+            dot(left, right[:, columns], 0, 0).astype(BF16).reshape(devices, -1, self.shape[2])
+            for left, right in pairs
+        ]
+        if extra is not None:
+            parts.append(extra.reshape(devices, -1, self.shape[2]))
+        target = jnp.arange(devices)
+        source, left_over = jnp.zeros_like(target), devices
+        for axis, bit in self.steps:
+            left_over //= 2
+            weight = bit * n_seq if axis == "dp" else bit
+            source = source + (target // left_over) % 2 * weight
+        if scatter:
+            source = source + target % n_seq
+        me = lax.axis_index("dp") * n_seq
+        if not scatter:
+            me = me + lax.axis_index("seq")
+        self.cut(jnp.take(jnp.concatenate(parts, axis=1), me ^ source, axis=0))
+
+    def cut(self, array):
+        half = array.shape[0] // 2
+        self.keep, self.pending = array[:half], array[half:]
 
     def advance(self):
         self.steps = self.steps[1:]
         if self.factors:
-            left, right, numbers = self.factors
-            self.factors = None
-            step = self.steps[0]
-            if step[0] == "dp":
-                (send,) = product(left, right, numbers, 3, 1, self.got, 1)
-                (self.keep,) = product(left, right, numbers, 2, 1, self.got, 0)
+            factors, self.factors = self.factors, None
+            if self.steps[0][0] == "dp":
+                (self.pending,) = product(factors, 3, 1, self.got, 1)
+                (self.keep,) = product(factors, 2, 1, self.got, 0)
             else:
-                self.keep, send = product(left, right, numbers, 2, 2, self.got, 0, True)
-            self.dims.remove(step)
-            self.got = swap(send, step)
+                self.keep, self.pending = product(factors, 2, 2, self.got, 0, True)
+            self.keep = self.keep.reshape(self.shape)
+            self.pending = self.pending.reshape(self.shape)
             return
-        array = self.keep.astype(F32) + self.got.reshape(self.keep.shape).astype(F32)
+        array = self.keep.astype(F32) + self.got.astype(F32)
         if self.steps:
-            self.send(array.astype(BF16))
+            self.cut(array.astype(BF16))
         else:
-            self.result = array.reshape(self.rows, D)
+            self.result = array
 
     def finish(self):
         while self.steps:
+            if self.pending is not None:
+                self.got = swap(self.pending, self.steps[0])
+                self.pending = None
             self.advance()
         return self.result
 
@@ -570,8 +613,8 @@
 
 
 def input_backward_kernel(
-    weights, gq_ref, gown_ref, got_ref, kraw_ref, gmid_ref, stream_ref, gains_ref, cos_ref, sin_ref, w_any,
-    gproj_ref, gin_ref, sums_ref, key_sums_ref, w_ref, sem,
+    weights, gq_ref, gown_ref, got_ref, kraw_ref, gmid_ref, stream_ref, gains_ref, cos_ref, sin_ref,
+    sums_ref, qsums_ref, w_any, gproj_ref, gin_ref, ggains_ref, w_ref, sem,
 ):
     copy = fetch(weights[0], w_any, w_ref, sem.at[0])
     total = gown_ref[...] + got_ref[...].astype(F32)
@@ -580,15 +623,15 @@
     gproj_ref[:, :QUERY_COLS] = gq_ref[...]
     gproj_ref[:, QUERY_COLS : QUERY_COLS + HEAD_DIM] = grad_keys.astype(BF16)
     gproj_ref[:, QUERY_COLS + HEAD_DIM :] = total[:, VALUES].astype(BF16)
-    key_sums_ref[...] = key_sums
     copy.wait()
     grad_normed = dot(gproj_ref[...], weight_rows(w_ref, 0, QUERY_COLS + 2 * HEAD_DIM), 1, 0)
     grad_part, sums = rms_backward(stream_ref[...], gain_of(gains_ref, PRE_ATTN), grad_normed)
     gin_ref[...] = gmid_ref[...] + grad_part
-    sums_ref[...] = sums
-
-
-def backward_layer(grad_out, weights, gains, record, tables, reach, count, pump, chains):
+    found = [sums] + [sums_ref[i : i + 1, :] for i in range(3)] + [qsums_ref[...], key_sums]
+    ggains_ref[...] = jnp.concatenate(found, axis=1)
+
+
+def backward_layer(grad_out, weights, gains, record, tables, reach, count, pump, chains, last):
     attn_in, attn_out, ffn_in, ffn_out = weights
     cosine_tab, sine_tab = tables
     (
@@ -607,9 +650,14 @@
         ],
         2 * tokens * D * (QUERY_COLS + 3 * hidden),
     )
-    chains["ffn_in"] = Chain(grad_gate_up, ffn_normed, "dp")
-    chains["ffn_out"] = Chain(inner, grad_ffn_branch, "seq")
-    chains["attn_out"] = Chain(context, grad_branch, "seq")
+    ffn = [(grad_gate_up, ffn_normed), (inner, grad_ffn_branch)]
+    if last:
+        chains["ffn"] = Chain(ffn, "dp", True)
+    else:
+        cut = 3 * D // 5
+        chains["ffn_a"] = Chain(ffn, "dp", columns=slice(0, cut))
+        chains["ffn_b"] = Chain(ffn, "seq", columns=slice(cut, D))
+    grad_context = launch(grad_context, list(chains.values()))
     grad_context = pump(1, grad_context)
     grad_queries, grad_before, grad_own = call(
         attention_backward_kernel, "attention_backward",
@@ -627,28 +675,30 @@
         20 * tokens * QUERY_COLS,
     )
     grad_query_raw = pump(3, grad_query_raw)
-    grad_projected, grad_in, pre_sums, key_sums = call(
+    grad_projected, grad_in, gain_grads = call(
         partial(input_backward_kernel, [attn_in]), "input_backward",
-        (grad_query_raw, grad_own, got, key_raw, grad_middle, stream, gains, cosine_tab, sine_tab),
+        (
+            grad_query_raw, grad_own, got, key_raw, grad_middle, stream, gains, cosine_tab, sine_tab,
+            sums, query_sums,
+        ),
         [attn_in],
-        [
-            ((tokens, QUERY_COLS + 2 * HEAD_DIM), BF16), ((tokens, D), F32), ((1, D), F32),
-            ((1, HEAD_DIM), F32),
-        ],
+        [((tokens, QUERY_COLS + 2 * HEAD_DIM), BF16), ((tokens, D), F32), (gains.shape, F32)],
         2 * tokens * D * (QUERY_COLS + 2 * HEAD_DIM),
     )
-    chains["attn_in"] = Chain(grad_projected, normed, "dp")
-    grad_gain_row = jnp.concatenate(
-        [pre_sums[0], sums[0], sums[1], sums[2], query_sums[0], key_sums[0]]
-    )
-    return grad_in, grad_gain_row
+    n_dp, n_seq = lax.axis_size("dp"), lax.axis_size("seq")
+    gain_grads = gain_grads.astype(BF16).reshape(n_dp, n_seq, 1, -1)
+    extra = jnp.pad(gain_grads, ((0, 0), (0, 0), (0, TILE - 1), (0, D - gain_grads.shape[3])))
+    attn = [(grad_projected, normed), (context, grad_branch)]
+    chains["attn"] = Chain(attn, "dp" if last else "seq", last, extra=extra)
+    return launch(grad_in, [chains["attn"]])
 
 
 PLAN = {
-    0: [(1, "attn_out"), (1, "ffn_out"), (1, "attn_in")],
-    1: [(0, "ffn_in"), (0, "ffn_out"), (1, "ffn_in"), (1, "attn_in"), (1, "attn_out")],
-    2: [(0, "attn_out"), (1, "ffn_out"), (1, "attn_in"), (1, "attn_out")],
-    3: [(0, "ffn_out"), (1, "ffn_in"), (1, "attn_out")],
+    0: [(1, "attn")],
+    1: [(0, "ffn"), (0, "ffn_a"), (0, "ffn_b"), (1, "ffn")],
+    2: [],
+    3: [(1, "attn")],
+    4: [(0, "ffn_a"), (0, "ffn_b")],
 }
 
 
@@ -684,7 +734,6 @@
     layer_weights = gather_weights(w_attn_in, w_attn_out, w_ffn_in, w_ffn_out, gains)
     places = to_long(positions)
     stream = to_long(hidden_in).astype(F32)
-    grad_stream = to_long(out_grad).astype(F32)
     tables = angle_tables(places)
     tokens = places.shape[0]
     blocks = tokens // QUERY_BLOCK
@@ -695,9 +744,12 @@
         weights.append(layer_weights(layer_index))
         record, stream = forward_layer(stream, *weights[-1], tables, reach, count)
         records.append(record)
+        if layer_index == 0:
+            stream, out_grad = lax.optimization_barrier((stream, out_grad))
+            grad_stream = to_long(out_grad).astype(F32)
     hidden_out = to_short(stream.astype(BF16), count)
-    gain_grads = [None] * layer_count
     chains = [{} for _ in range(layer_count + 1)]
+    sums = [None] * layer_count
     for layer_index in reversed(range(layer_count)):
 
         def pump(where, value):
@@ -706,27 +758,37 @@
                 for above, name in PLAN[where]
                 if name in chains[layer_index + above]
             ]
-            return advance(value, [chain for chain in active if chain.steps])
-
-        grad_stream, gain_grads[layer_index] = backward_layer(
+            value = advance(value, active)
+            if where == 3 and layer_index + 1 < layer_count:
+                above = chains[layer_index + 1]
+                packed = jnp.concatenate([above["ffn"].finish(), above["attn"].finish()], axis=1)
+                value, packed = lax.optimization_barrier((value, packed.astype(BF16)))
+                sums[layer_index + 1] = lax.psum_scatter(packed, "seq", scatter_dimension=0)
+            return value
+
+        grad_stream = backward_layer(
             grad_stream, *weights[layer_index], records[layer_index], tables, reach, count, pump,
-            chains[layer_index],
+            chains[layer_index], layer_index > 0,
         )
+    grad_stream = pump(4, grad_stream)
     input_grad = to_short(grad_stream.astype(BF16), count).astype(F32)
-    devices = lax.axis_size("dp") * lax.axis_size("seq")
-    gain_grads = halving(jnp.stack([entry.reshape(devices, -1) for entry in gain_grads], axis=1))
-    members = {
-        name: jnp.stack([chains[layer][name].finish() for layer in range(layer_count)])
-        for name in chains[0]
-    }
+    found = chains[0]
+    ffn = jnp.concatenate([found["ffn_a"].finish(), found["ffn_b"].finish()], axis=2)
+    sums[0] = jnp.concatenate([ffn, found["attn"].finish()], axis=1)[0]
+    packed = jnp.stack([entry.astype(F32) for entry in sums])
+    sizes = [w_ffn_in.shape[2], w_ffn_out.shape[1], w_attn_in.shape[2], w_attn_out.shape[1]]
+    parts, at = [], 0
+    for size in sizes:
+        parts.append(packed[:, at : at + size])
+        at += size
     return (
         hidden_out,
         input_grad,
-        members["attn_in"].transpose(0, 2, 1),
-        members["attn_out"],
-        members["ffn_in"].transpose(0, 2, 1),
-        members["ffn_out"],
-        gain_grads,
+        parts[2].transpose(0, 2, 1),
+        parts[3],
+        parts[0].transpose(0, 2, 1),
+        parts[1],
+        packed[:, at, : gains.shape[1]],
     )
 
 

time: 596 us -> 546 us (0.916)
  starting transfers between devices: 86.8 us -> 68.1 us
  other arithmetic: 27.7 us -> 17 us
  Pallas kernels: 151 us -> 141 us
    ppermute x45 -> x19, starting transfers between devices: 56.5 us -> 27.4 us  [swap(): lax.ppermute(array, axis, [(i, i ^ bit) for i in range(lax.axis_size(axis...]
    ppermute x45 -> x19, waiting for transfers between devices: 105 us -> 77.3 us  [swap(): lax.ppermute(array, axis, [(i, i ^ bit) for i in range(lax.axis_size(axis...]
    ppermute x8, waiting for transfers between devices: 0.02 us -> 20.8 us  [to_short(): received.append(lax.ppermute(piece, ALL, route))]
    all_gather x1, waiting for transfers between devices: 126 us -> 141 us  [gather_weights(): whole = lax.all_gather(packed, ALL, axis=0, tiled=False)]
    ppermute x12, waiting for transfers between devices: 18.1 us -> 5.51 us  [to_long(): received.append(lax.ppermute(piece, ALL, chunk_route(count, k)))]
    pallas_call x20 -> x13, Pallas kernels: 53.6 us -> 43.8 us  [product(): pl.pallas_call(partial(product_kernel, len(pairs), extra is not None, got...]
    convert_element_type x24 -> x12, other arithmetic: 13.9 us -> 5.14 us  [the longest x9 4.03 us: advance(): self.cut(array.astype(BF16))]
    ppermute x8, starting transfers between devices: 7.75 us -> 14.9 us  [to_short(): received.append(lax.ppermute(piece, ALL, route))]
  transfers between devices with their start and end apart: 70 -> 45, of which waited for: 29 -> 18; matrix products, arithmetic and copies ran while one was open for 9% -> 3% of each run, Pallas kernels for 12% -> 8%
where the time goes in v4:
time: 546 us; the launch traced here: 541 us
  waiting for transfers between devices  246 us (45%)
  Pallas kernels  141 us (26%)
  starting transfers between devices  68.1 us (12%)
  local copies, waits for them, and re-layouts  52.9 us (10%)
  other arithmetic  17 us (3%)
  between operations  15.8 us (3%)
    all_gather x1, waiting for transfers between devices, gather_weights(): whole = lax.all_gather(packed, ALL, axis=0, tiled=False)  141 us
    pallas_call x14, Pallas kernels, call(): pl.pallas_call(kernel, out_shape=tuple(outs), in_specs=vmem(len(arrays))...  97.3 us
    ppermute x19, waiting for transfers between devices, swap(): lax.ppermute(array, axis, [(i, i ^ bit) for i in range(lax.axis_size(axis...  77.3 us
    unnamed x210, local copies, waits for them, and re-layouts  48.8 us
    pallas_call x13, Pallas kernels, product(): pl.pallas_call(partial(product_kernel, len(pairs), extra is not None, got...  43.8 us
    ppermute x19, starting transfers between devices, swap(): lax.ppermute(array, axis, [(i, i ^ bit) for i in range(lax.axis_size(axis...  27.4 us
    ppermute x8, waiting for transfers between devices, to_short(): received.append(lax.ppermute(piece, ALL, route))  20.8 us
    ppermute x8, starting transfers between devices, to_short(): received.append(lax.ppermute(piece, ALL, route))  14.9 us
  transfers between devices with their start and end apart: 45, of which 18 were waited for; matrix products, arithmetic and copies ran while one was open for 3% of the time, Pallas kernels for 8%

profile of v4, /device:TPU:0, one launch (start us, length us, event | category | flops | bytes accessed | tf_op | source)
XLA Modules:
  0.0 541.2 jit_solution(17849948432494531865)
XLA Ops:
  10.4 3.1 collective-permute-start.5
  17.3 2.9 collective-permute-start
  21.3 1.8 collective-permute-done
  23.2 3.6 collective-permute-done.2
  27.2 141.3 %all-gather.3.cloned.1.call-done = bf16[17920,640]{1,0:T(8,128)(2,1)} async-done(((bf16[560,640]{1,0:T(8,128)(2,1)}), bf16[17920,640]{1,0:T(8,128)(2,1)}) %all-gather.3.cloned.1.call-update) | async-done | bytes 22937616 | tf_op jit(solution)/shard_map/all_gather | solution.py:710
  169.6 3.1 key_value.2
  172.8 3.2 collective-permute-start.8
  176.0 2.9 query.2
  180.2 16.0 %block_forward.2 = (bf16[512,1024]{1,0:T(8,128)(2,1)S(1)}, f32[2,1024]{1,0:T(2,128)S(1)}, f32[512,640]{1,0:T(8,128)S(1)}, f32[512,640]{1,0:T(8,128)S(1)}, bf16[5...) custom-call(bf16[512,1024]{1,0:T(8,128)(2,1)S(1)} %get-tuple-element, ...), custom_call_target="tpu_custom_call" | custom-call | flops 6308233216 | bytes 16674816 | tf_op jit(solution)/shard_map/block_forward/pallas_call | solution.py:106
  207.0 2.3 key_value.3
  209.3 4.9 collective-permute-start.9
  214.2 2.9 query.3
  217.6 14.3 %block_forward.3 = (bf16[512,1024]{1,0:T(8,128)(2,1)S(1)}, f32[2,1024]{1,0:T(2,128)S(1)}, f32[512,640]{1,0:T(8,128)S(1)}, f32[512,640]{1,0:T(8,128)S(1)}, bf16[5...) custom-call(bf16[512,1024]{1,0:T(8,128)(2,1)S(1)} %get-tuple-element, ...), custom_call_target="tpu_custom_call" | custom-call | flops 6308233216 | bytes 16674816 | tf_op jit(solution)/shard_map/block_forward/pallas_call | solution.py:106
  234.0 16.7 %block_backward.2 = (bf16[512,640]{1,0:T(8,128)(2,1)S(1)}, bf16[512,4096]{1,0:T(8,128)(2,1)}, bf16[512,640]{1,0:T(8,128)(2,1)S(1)}, bf16[512,1024]{1,0:T(8,128)(...) custom-call(f32[512,640]{1,0:T(8,128)S(1)} %bitcast_convert_fusion.grad_ref, ...), custom_call_target="tpu_custom_call" | custom-call | flops 4697620480 | bytes 17334272 | tf_op jit(solution)/shard_map/block_backward/pallas_call | solution.py:106
  250.8 3.1 copy-done.4
  253.9 3.9 weight_gradient.13
  258.5 6.4 %collective-permute-done.18.refs_4_ = bf16[2,8,192,640]{3,2,1,0:T(8,128)(2,1)S(1)} collective-permute-done((bf16[2,8,192,640]{3,2,1,0:T(8,128)(2,1)S(1)}, bf16[2,8,192,640]{3,2,1,0:T(8,128)(2,1)S(1)}, u32[]{:S(2)}, u32[]{:S(2)}) %collective-permute-start.18) | collective-permute-done | bytes 3932192 | tf_op jit(solution)/shard_map/ppermute | solution.py:200
  264.9 3.3 weight_gradient.14
  268.2 5.2 attention_backward.2
  277.2 3.5 input_backward.2
  285.8 3.4 weight_gradient.15
  289.6 3.9 collective-permute-done.20.refs_5_
  298.0 2.7 weight_gradient.16
  301.8 16.4 %block_backward.3 = (bf16[512,640]{1,0:T(8,128)(2,1)S(1)}, bf16[512,4096]{1,0:T(8,128)(2,1)}, bf16[512,640]{1,0:T(8,128)(2,1)S(1)}, bf16[512,1024]{1,0:T(8,128)(...) custom-call(f32[512,640]{1,0:T(8,128)S(1)} %copy-done.63, f32[512,640]{1,0:T(8,128)S(1)} %copy-done.61, ...), custom_call_target="tpu_custom_call" | custom-call | flops 4697620480 | bytes 17334272 | tf_op jit(solution)/shard_map/block_backward/pallas_call | solution.py:106
  318.2 3.5 copy-done
  321.7 3.0 weight_gradient.18
  324.7 4.4 weight_gradient.17
  334.4 2.7 collective-permute-start.13
  337.1 1.8 collective-permute-start.11
  339.0 4.9 collective-permute-done.11
  343.8 3.1 collective-permute-start.12
  346.9 5.2 collective-permute-done.12
  355.2 2.2 copy-done.5
  358.9 2.1 copy-done.14
  361.1 2.0 weight_gradient.21
  363.3 2.7 weight_gradient.22
  366.1 9.3 %collective-permute-done.23 = bf16[8,192,640]{2,1,0:T(8,128)(2,1)} collective-permute-done((bf16[8,192,640]{2,1,0:T(8,128)(2,1)}, bf16[8,192,640]{2,1,0:T(8,128)(2,1)}, u32[]{:S(2)}, u32[]{:S(2)}) %collective-permute-start.23) | collective-permute-done | bytes 1966112 | tf_op jit(solution)/shard_map/ppermute | solution.py:200
  375.4 4.0 weight_gradient.19
  379.4 5.6 %weight_gradient.20 = (bf16[2,4,192,256]{3,2,1,0:T(8,128)(2,1)S(1)}, bf16[2,4,192,256]{3,2,1,0:T(8,128)(2,1)}) custom-call(s32[5]{0:T(128)S(1)} %stack.162.numbers_ref, bf16[512,4096]{1,0:T(8,128)(2,1)S(1)} %copy-done.1, bf16[512,2048]{1,0:T(8,128)(2,1)S(1)} %copy-done.3, bf16[512,640]{1,0:T(8,128)(2,1)S(1)} %get-tuple-element.155.refs_2_, ...), custom_call_target="tpu_custom_call" | custom-call | flops 805306368 | bytes 6291456 | tf_op jit(solution)/shard_map/weight_gradient/pallas_call | solution.py:299
  386.0 7.1 %attention_backward.3 = (f32[512,1024]{1,0:T(8,128)S(1)}, bf16[512,512]{1,0:T(8,128)(2,1)}, f32[512,512]{1,0:T(8,128)S(1)}) custom-call(bf16[512,1024]{1,0:T(8,128)(2,1)S(1)} %copy-done.65, bf16[512,512]{1,0:T(8,128)(2,1)} %collective-permute-done.8.before_ref, bf16[512,512]{1,0:T(8,128)(2,1)} %get-tuple-element.105.own_ref, s32[2,1024]{1,0:T(2,128)S(1)} %bitcast.144, ...), custom_call_target="tpu_custom_call" | custom-call | flops 4026531840 | bytes 6832128 | tf_op jit(solution)/shard_map/attention_backward/pallas_call | solution.py:106
  394.5 3.4 collective-permute-start.27
  398.4 2.2 fusion
  402.8 1.8 pad_maximum_fusion
  404.6 1.6 bitcast_dynamic-update-slice_fusion.18
  406.2 2.2 copy-done.2
  409.5 3.3 weight_gradient.24
  413.8 4.7 input_backward.3
  422.1 2.2 weight_gradient.23
  424.4 1.7 collective-permute-start.38
  427.9 1.7 fusion.1
  431.9 2.9 collective-permute-start.30
  434.9 2.0 collective-permute-start.29
  437.8 10.6 %collective-permute-done.29 = bf16[128,640]{1,0:T(8,128)(2,1)S(1)} collective-permute-done((bf16[128,640]{1,0:T(8,128)(2,1)S(1)}, bf16[128,640]{1,0:T(8,128)(2,1)S(1)}, u32[]{:S(2)}, u32[]{:S(2)}) %collective-permute-start.29) | collective-permute-done | bytes 163872 | tf_op jit(solution)/shard_map/ppermute | solution.py:160
  448.4 1.6 collective-permute-start.32
  450.2 3.4 weight_gradient.25
  454.2 8.7 %collective-permute-start.36 = (bf16[2,192,256]{2,1,0:T(8,128)(2,1)S(1)}, bf16[2,192,256]{2,1,0:T(8,128)(2,1)S(1)}, u32[]{:S(2)}, u32[]{:S(2)}) collective-permute-start(bf16[2,192,256]{2,1,0:T(8,128)(2,1)S(1)} %slice.116), channel_id=1, source_target_pairs={{0,4},{1,5},{2,6},{3,7},{4,0},{5,1},{6,2},{7,3},{8,12},{9,13},{10,... | collective-permute-start | bytes 589832 | tf_op jit(solution)/shard_map/ppermute | solution.py:200
  464.1 8.3 %collective-permute-done.36 = bf16[2,192,256]{2,1,0:T(8,128)(2,1)S(1)} collective-permute-done((bf16[2,192,256]{2,1,0:T(8,128)(2,1)S(1)}, bf16[2,192,256]{2,1,0:T(8,128)(2,1)S(1)}, u32[]{:S(2)}, u32[]{:S(2)}) %collective-permute-start.36) | collective-permute-done | bytes 196640 | tf_op jit(solution)/shard_map/ppermute | solution.py:200
  472.6 20.3 %collective-permute-done.39 = bf16[8,96,640]{2,1,0:T(8,128)(2,1)S(1)} collective-permute-done((bf16[8,96,640]{2,1,0:T(8,128)(2,1)S(1)}, bf16[8,96,640]{2,1,0:T(8,128)(2,1)S(1)}, u32[]{:S(2)}, u32[]{:S(2)}) %collective-permute-start.39) | collective-permute-done | bytes 983072 | tf_op jit(solution)/shard_map/ppermute | solution.py:200
  493.6 5.2 collective-permute-start.33
  498.8 7.2 %collective-permute-done.40 = bf16[4,96,640]{2,1,0:T(8,128)(2,1)S(1)} collective-permute-done((bf16[4,96,640]{2,1,0:T(8,128)(2,1)S(1)}, bf16[4,96,640]{2,1,0:T(8,128)(2,1)S(1)}, u32[]{:S(2)}, u32[]{:S(2)}) %collective-permute-start.40) | collective-permute-done | bytes 491552 | tf_op jit(solution)/shard_map/ppermute | solution.py:200
  507.3 10.9 %collective-permute-done.33 = bf16[2,192,384]{2,1,0:T(8,128)(2,1)S(1)} collective-permute-done((bf16[2,192,384]{2,1,0:T(8,128)(2,1)S(1)}, bf16[2,192,384]{2,1,0:T(8,128)(2,1)S(1)}, u32[]{:S(2)}, u32[]{:S(2)}) %collective-permute-start.33) | collective-permute-done | bytes 294944 | tf_op jit(solution)/shard_map/ppermute | solution.py:200
  518.4 5.0 collective-permute-done.41
  523.6 3.0 collective-permute-done.34
  526.6 2.5 collective-permute-done.42
  (331 shorter events, 74.6 us)
Async XLA Ops:
  7.2 161.4 %all-gather.3.cloned.1.call-start = ((), (), s32[]{:S(2)}) async-start(), calls=%async_computation.2 | async-start | bytes 23654400 | tf_op jit(solution)/shard_map/all_gather | solution.py:710
  8.5 7.0 %copy-start.78 = (bf16[4,128,640]{2,1,0:T(8,128)(2,1)S(1)}, bf16[4,128,640]{2,1,0:T(8,128)(2,1)}, u32[]{:S(2)}) copy-start(bf16[4,128,640]{2,1,0:T(8,128)(2,1)} %param.8) | copy-start | bytes 1966084
  9.6 519.6 %reduce-scatter.2.cloned.1.call-start = ((), (), s32[]{:S(2)}) async-start(), calls=%async_computation.1 | async-start | bytes 3317760 | tf_op jit(solution)/shard_map/reduce_scatter | solution.py:766
  9.8 6.6 %collective-permute-start.7 = (s32[128]{0:T(128)S(1)}, s32[128]{0:T(128)S(1)}, u32[]{:S(2)}, u32[]{:S(2)}) collective-permute-start(s32[128]{0:T(128)S(1)} %get-tuple-element.235), channel_id=1, source_target_pairs={{0,0},{1,1},{2,2},{3,3},{4,8},{5,9},{6,10},{7,11},{8,4},{9,5},{10,... | collective-permute-start | bytes 1544 | tf_op jit(solution)/shard_map/ppermute | solution.py:147
  10.4 6.9 %collective-permute-start.5 = (s32[128]{0:T(128)S(1)}, s32[128]{0:T(128)S(1)}, u32[]{:S(2)}, u32[]{:S(2)}) collective-permute-start(s32[128]{0:T(128)S(1)} %get-tuple-element.236), channel_id=1, source_target_pairs={{0,2},{1,3},{2,0},{3,1},{4,10},{5,11},{6,8},{7,9},{8,6},{9,7},{10,... | collective-permute-start | bytes 1544 | tf_op jit(solution)/shard_map/ppermute | solution.py:147
  13.5 6.8 %collective-permute-start.4 = (s32[128]{0:T(128)S(1)}, s32[128]{0:T(128)S(1)}, u32[]{:S(2)}, u32[]{:S(2)}) collective-permute-start(s32[128]{0:T(128)S(1)} %get-tuple-element.237), channel_id=1, source_target_pairs={{0,3},{1,0},{2,1},{3,2},{4,11},{5,8},{6,9},{7,10},{8,7},{9,4},{10,... | collective-permute-start | bytes 1544 | tf_op jit(solution)/shard_map/ppermute | solution.py:147
  14.9 5.4 collective-permute-start.6
  15.6 11.3 %collective-permute-start.3 = (bf16[128,640]{1,0:T(8,128)(2,1)S(1)}, bf16[128,640]{1,0:T(8,128)(2,1)S(1)}, u32[]{:S(2)}, u32[]{:S(2)}) collective-permute-start(bf16[128,640]{1,0:T(8,128)(2,1)S(1)} %get-tuple-element.227), channel_id=1, source_target_pairs={{0,0},{1,1},{2,2},{3,3},{4,8},{5,9},{6,10},{7,11},{8,4},{9,5},{10,... | collective-permute-start | bytes 491528 | tf_op jit(solution)/shard_map/ppermute | solution.py:147
  16.3 6.9 %collective-permute-start.1 = (bf16[128,640]{1,0:T(8,128)(2,1)S(1)}, bf16[128,640]{1,0:T(8,128)(2,1)S(1)}, u32[]{:S(2)}, u32[]{:S(2)}) collective-permute-start(bf16[128,640]{1,0:T(8,128)(2,1)S(1)} %get-tuple-element.228), channel_id=1, source_target_pairs={{0,2},{1,3},{2,0},{3,1},{4,10},{5,11},{6,8},{7,9},{8,6},{9,7},{10,... | collective-permute-start | bytes 491528 | tf_op jit(solution)/shard_map/ppermute | solution.py:147
  17.3 5.8 %collective-permute-start = (bf16[128,640]{1,0:T(8,128)(2,1)S(1)}, bf16[128,640]{1,0:T(8,128)(2,1)S(1)}, u32[]{:S(2)}, u32[]{:S(2)}) collective-permute-start(bf16[128,640]{1,0:T(8,128)(2,1)S(1)} %get-tuple-element.229), channel_id=1, source_target_pairs={{0,3},{1,0},{2,1},{3,2},{4,11},{5,8},{6,9},{7,10},{8,7},{9,4},{10,... | collective-permute-start | bytes 491528 | tf_op jit(solution)/shard_map/ppermute | solution.py:147
  20.3 6.6 %collective-permute-start.2 = (bf16[128,640]{1,0:T(8,128)(2,1)S(1)}, bf16[128,640]{1,0:T(8,128)(2,1)S(1)}, u32[]{:S(2)}, u32[]{:S(2)}) collective-permute-start(bf16[128,640]{1,0:T(8,128)(2,1)S(1)} %get-tuple-element.230), channel_id=1, source_target_pairs={{0,1},{1,2},{2,3},{3,0},{4,9},{5,10},{6,11},{7,8},{8,5},{9,6},{10,... | collective-permute-start | bytes 491528 | tf_op jit(solution)/shard_map/ppermute | solution.py:147
  27.2 153.0 %copy-start.6 = (f32[512,640]{1,0:T(8,128)}, f32[512,640]{1,0:T(8,128)S(1)}, u32[]{:S(2)}) copy-start(f32[512,640]{1,0:T(8,128)S(1)} %bitcast_convert_fusion.1.stream_ref) | copy-start | bytes 3932164
  172.8 7.4 %collective-permute-start.8 = (bf16[512,512]{1,0:T(8,128)(2,1)}, bf16[512,512]{1,0:T(8,128)(2,1)}, u32[]{:S(2)}, u32[]{:S(2)}) collective-permute-start(bf16[512,512]{1,0:T(8,128)(2,1)} %get-tuple-element.105.own_ref), channel_id=1, source_target_pairs={{0,8},{1,9},{2,10},{3,11},{4,12},{5,13},{6,14},{7,15},{16,24},{17,... | collective-permute-start | bytes 1572872 | tf_op jit(solution)/shard_map/ppermute | solution.py:177
  180.2 16.0 %copy-start.64 = (bf16[512,1024]{1,0:T(8,128)(2,1)}, bf16[512,1024]{1,0:T(8,128)(2,1)S(1)}, u32[]{:S(2)}) copy-start(bf16[512,1024]{1,0:T(8,128)(2,1)S(1)} %get-tuple-element.104.q_ref) | copy-start | bytes 3145732
  180.2 21.2 %copy-start.79 = (bf16[4,128,640]{2,1,0:T(8,128)(2,1)S(1)}, bf16[4,128,640]{2,1,0:T(8,128)(2,1)}, u32[]{:S(2)}) copy-start(bf16[4,128,640]{2,1,0:T(8,128)(2,1)} %param.10) | copy-start | bytes 1966084
  202.3 14.8 %collective-permute-start.14 = (bf16[128,640]{1,0:T(8,128)(2,1)}, bf16[128,640]{1,0:T(8,128)(2,1)S(1)}, u32[]{:S(2)}, u32[]{:S(2)}) collective-permute-start(bf16[128,640]{1,0:T(8,128)(2,1)} %get-tuple-element.222), channel_id=1, source_target_pairs={{0,3},{1,0},{2,1},{3,2},{4,11},{5,8},{6,9},{7,10},{8,7},{9,4},{10,... | collective-permute-start | bytes 491528 | tf_op jit(solution)/shard_map/ppermute | solution.py:147
  203.1 14.1 %collective-permute-start.17 = (bf16[128,640]{1,0:T(8,128)(2,1)}, bf16[128,640]{1,0:T(8,128)(2,1)S(1)}, u32[]{:S(2)}, u32[]{:S(2)}) collective-permute-start(bf16[128,640]{1,0:T(8,128)(2,1)} %get-tuple-element.219), channel_id=1, source_target_pairs={{0,0},{1,1},{2,2},{3,3},{4,8},{5,9},{6,10},{7,11},{8,4},{9,5},{10,... | collective-permute-start | bytes 491528 | tf_op jit(solution)/shard_map/ppermute | solution.py:147
  204.7 12.5 %collective-permute-start.16 = (bf16[128,640]{1,0:T(8,128)(2,1)}, bf16[128,640]{1,0:T(8,128)(2,1)S(1)}, u32[]{:S(2)}, u32[]{:S(2)}) collective-permute-start(bf16[128,640]{1,0:T(8,128)(2,1)} %get-tuple-element.220), channel_id=1, source_target_pairs={{0,1},{1,2},{2,3},{3,0},{4,9},{5,10},{6,11},{7,8},{8,5},{9,6},{10,... | collective-permute-start | bytes 491528 | tf_op jit(solution)/shard_map/ppermute | solution.py:147
  206.0 11.1 %collective-permute-start.15 = (bf16[128,640]{1,0:T(8,128)(2,1)}, bf16[128,640]{1,0:T(8,128)(2,1)S(1)}, u32[]{:S(2)}, u32[]{:S(2)}) collective-permute-start(bf16[128,640]{1,0:T(8,128)(2,1)} %get-tuple-element.221), channel_id=1, source_target_pairs={{0,2},{1,3},{2,0},{3,1},{4,10},{5,11},{6,8},{7,9},{8,6},{9,7},{10,... | collective-permute-start | bytes 491528 | tf_op jit(solution)/shard_map/ppermute | solution.py:147
  209.3 7.8 %copy-start.20 = (bf16[512,640]{1,0:T(8,128)(2,1)}, bf16[512,640]{1,0:T(8,128)(2,1)S(1)}, u32[]{:S(2)}) copy-start(bf16[512,640]{1,0:T(8,128)(2,1)S(1)} %get-tuple-element.108.normed_ref.refs_2_) | copy-start | bytes 1966084
  209.3 8.3 %collective-permute-start.9 = (bf16[512,512]{1,0:T(8,128)(2,1)S(1)}, bf16[512,512]{1,0:T(8,128)(2,1)S(1)}, u32[]{:S(2)}, u32[]{:S(2)}) collective-permute-start(bf16[512,512]{1,0:T(8,128)(2,1)S(1)} %get-tuple-element.110.own_ref), channel_id=1, source_target_pairs={{0,8},{1,9},{2,10},{3,11},{4,12},{5,13},{6,14},{7,15},{16,24},{17,... | collective-permute-start | bytes 1572872 | tf_op jit(solution)/shard_map/ppermute | solution.py:177
  234.0 30.9 %copy-start.33 = (bf16[512,640]{1,0:T(8,128)(2,1)}, bf16[512,640]{1,0:T(8,128)(2,1)S(1)}, u32[]{:S(2)}) copy-start(bf16[512,640]{1,0:T(8,128)(2,1)S(1)} %get-tuple-element.122.refs_2_) | copy-start | bytes 1966084
  234.0 16.8 %copy-start.8 = (bf16[512,2048]{1,0:T(8,128)(2,1)S(1)}, bf16[512,2048]{1,0:T(8,128)(2,1)}, u32[]{:S(2)}) copy-start(bf16[512,2048]{1,0:T(8,128)(2,1)} %get-tuple-element.121.refs_1_) | copy-start | bytes 6291460
  250.7 7.1 %copy-start.37 = (bf16[512,640]{1,0:T(8,128)(2,1)}, bf16[512,640]{1,0:T(8,128)(2,1)S(1)}, u32[]{:S(2)}) copy-start(bf16[512,640]{1,0:T(8,128)(2,1)S(1)} %get-tuple-element.141.refs_3_) | copy-start | bytes 1966084
  250.7 7.1 %copy-start.51 = (f32[512,640]{1,0:T(8,128)}, f32[512,640]{1,0:T(8,128)S(1)}, u32[]{:S(2)}) copy-start(f32[512,640]{1,0:T(8,128)S(1)} %get-tuple-element.135.gmid_ref) | copy-start | bytes 3932164
  250.7 14.2 %copy-start.35 = (bf16[512,640]{1,0:T(8,128)(2,1)}, bf16[512,640]{1,0:T(8,128)(2,1)S(1)}, u32[]{:S(2)}) copy-start(bf16[512,640]{1,0:T(8,128)(2,1)S(1)} %get-tuple-element.123.refs_3_) | copy-start | bytes 1966084
  257.8 7.1 %collective-permute-start.18 = (bf16[2,8,192,640]{3,2,1,0:T(8,128)(2,1)S(1)}, bf16[2,8,192,640]{3,2,1,0:T(8,128)(2,1)S(1)}, u32[]{:S(2)}, u32[]{:S(2)}) collective-permute-start(bf16[2,8,192,640]{3,2,1,0:T(8,128)(2,1)S(1)} %weight_gradient.13), channel_id=1, source_target_pairs={{0,8},{8,0},{16,24},{24,16},{1,9},{9,1},{17,25},{25,17},{2,10},{10... | collective-permute-start | bytes 11796488 | tf_op jit(solution)/shard_map/ppermute | solution.py:200
  273.4 3.8 collective-permute-start.19
  281.7 11.8 %copy-start.15 = (bf16[512,1536]{1,0:T(8,128)(2,1)}, bf16[512,1536]{1,0:T(8,128)(2,1)S(1)}, u32[]{:S(2)}) copy-start(bf16[512,1536]{1,0:T(8,128)(2,1)S(1)} %get-tuple-element.139.refs_0_) | copy-start | bytes 4718596
  281.9 7.3 %copy-start.24 = (bf16[4,8,16,640]{3,2,1,0:T(8,128)(2,1)}, bf16[4,8,16,640]{3,2,1,0:T(8,128)(2,1)S(1)}, u32[]{:S(2)}) copy-start(bf16[4,8,16,640]{3,2,1,0:T(8,128)(2,1)S(1)} %pad.12.refs_4_) | copy-start | bytes 1966084
  289.2 4.3 collective-permute-start.20
  301.7 16.4 %copy-start.3 = (bf16[512,2048]{1,0:T(8,128)(2,1)S(1)}, bf16[512,2048]{1,0:T(8,128)(2,1)}, u32[]{:S(2)}) copy-start(bf16[512,2048]{1,0:T(8,128)(2,1)} %get-tuple-element.154.refs_1_) | copy-start | bytes 6291460
  329.1 46.3 %collective-permute-start.21 = (bf16[2,8,192,384]{3,2,1,0:T(8,128)(2,1)}, bf16[2,8,192,384]{3,2,1,0:T(8,128)(2,1)}, u32[]{:S(2)}, u32[]{:S(2)}) collective-permute-start(bf16[2,8,192,384]{3,2,1,0:T(8,128)(2,1)} %weight_gradient.17), channel_id=1, source_target_pairs={{0,8},{8,0},{16,24},{24,16},{1,9},{9,1},{17,25},{25,17},{2,10},{10... | collective-permute-start | bytes 7077896 | tf_op jit(solution)/shard_map/ppermute | solution.py:200
  329.4 46.0 %collective-permute-start.23 = (bf16[8,192,640]{2,1,0:T(8,128)(2,1)}, bf16[8,192,640]{2,1,0:T(8,128)(2,1)}, u32[]{:S(2)}, u32[]{:S(2)}) collective-permute-start(bf16[8,192,640]{2,1,0:T(8,128)(2,1)} %bitcast.47), channel_id=1, source_target_pairs={{0,16},{8,24},{16,0},{24,8},{1,17},{9,25},{17,1},{25,9},{2,18},{10... | collective-permute-start | bytes 5898248 | tf_op jit(solution)/shard_map/ppermute | solution.py:200
  331.9 43.5 %collective-permute-start.22 = (bf16[2,8,192,256]{3,2,1,0:T(8,128)(2,1)}, bf16[2,8,192,256]{3,2,1,0:T(8,128)(2,1)}, u32[]{:S(2)}, u32[]{:S(2)}) collective-permute-start(bf16[2,8,192,256]{3,2,1,0:T(8,128)(2,1)} %weight_gradient.18), channel_id=1, source_target_pairs={{0,8},{8,0},{16,24},{24,16},{1,9},{9,1},{17,25},{25,17},{2,10},{10... | collective-permute-start | bytes 4718600 | tf_op jit(solution)/shard_map/ppermute | solution.py:200
  332.9 4.3 collective-permute-start.10
  334.4 20.7 %copy-start.34 = (bf16[512,640]{1,0:T(8,128)(2,1)S(1)}, bf16[512,640]{1,0:T(8,128)(2,1)}, u32[]{:S(2)}) copy-start(bf16[512,640]{1,0:T(8,128)(2,1)} %copy-done.33) | copy-start | bytes 1966084
  334.4 20.7 %copy-start.36 = (bf16[512,640]{1,0:T(8,128)(2,1)S(1)}, bf16[512,640]{1,0:T(8,128)(2,1)}, u32[]{:S(2)}) copy-start(bf16[512,640]{1,0:T(8,128)(2,1)} %copy-done.35) | copy-start | bytes 1966084
  334.4 17.8 %collective-permute-start.13 = (bf16[128,640]{1,0:T(8,128)(2,1)}, bf16[128,640]{1,0:T(8,128)(2,1)S(1)}, u32[]{:S(2)}, u32[]{:S(2)}) collective-permute-start(bf16[128,640]{1,0:T(8,128)(2,1)} %get-tuple-element.223), channel_id=1, source_target_pairs={{3,0},{0,1},{1,2},{2,3},{11,4},{8,5},{9,6},{10,7},{7,8},{4,9},{5,1... | collective-permute-start | bytes 491528 | tf_op jit(solution)/shard_map/ppermute | solution.py:160
  337.1 6.7 %collective-permute-start.11 = (bf16[128,640]{1,0:T(8,128)(2,1)}, bf16[128,640]{1,0:T(8,128)(2,1)S(1)}, u32[]{:S(2)}, u32[]{:S(2)}) collective-permute-start(bf16[128,640]{1,0:T(8,128)(2,1)} %get-tuple-element.225), channel_id=1, source_target_pairs={{1,0},{2,1},{3,2},{0,3},{9,4},{10,5},{11,6},{8,7},{5,8},{6,9},{7,1... | collective-permute-start | bytes 491528 | tf_op jit(solution)/shard_map/ppermute | solution.py:160
  343.8 9.3 %copy-start.80 = (bf16[128,640]{1,0:T(8,128)(2,1)}, bf16[128,640]{1,0:T(8,128)(2,1)S(1)}, u32[]{:S(2)}) copy-start(bf16[128,640]{1,0:T(8,128)(2,1)S(1)} %collective-permute-done.11) | copy-start | bytes 491524
  343.8 8.3 %collective-permute-start.12 = (bf16[128,640]{1,0:T(8,128)(2,1)}, bf16[128,640]{1,0:T(8,128)(2,1)S(1)}, u32[]{:S(2)}, u32[]{:S(2)}) collective-permute-start(bf16[128,640]{1,0:T(8,128)(2,1)} %get-tuple-element.224), channel_id=1, source_target_pairs={{2,0},{3,1},{0,2},{1,3},{10,4},{11,5},{8,6},{9,7},{6,8},{7,9},{4,1... | collective-permute-start | bytes 491528 | tf_op jit(solution)/shard_map/ppermute | solution.py:160
  354.2 47.6 %collective-permute-start.24 = (bf16[8,96,640]{2,1,0:T(8,128)(2,1)}, bf16[8,96,640]{2,1,0:T(8,128)(2,1)S(1)}, u32[]{:S(2)}, u32[]{:S(2)}) collective-permute-start(bf16[8,96,640]{2,1,0:T(8,128)(2,1)} %bitcast.140), channel_id=1, source_target_pairs={{0,16},{8,24},{16,0},{24,8},{1,17},{9,25},{17,1},{25,9},{2,18},{10... | collective-permute-start | bytes 2949128 | tf_op jit(solution)/shard_map/ppermute | solution.py:200
  363.3 12.1 %copy-start.1 = (bf16[512,4096]{1,0:T(8,128)(2,1)S(1)}, bf16[512,4096]{1,0:T(8,128)(2,1)}, u32[]{:S(2)}) copy-start(bf16[512,4096]{1,0:T(8,128)(2,1)} %get-tuple-element.153.refs_0_) | copy-start | bytes 12582916
  363.3 12.1 %copy-start.11 = (bf16[512,640]{1,0:T(8,128)(2,1)S(1)}, bf16[512,640]{1,0:T(8,128)(2,1)}, u32[]{:S(2)}) copy-start(bf16[512,640]{1,0:T(8,128)(2,1)} %copy-done.10) | copy-start | bytes 1966084
  393.0 7.5 %copy-start.66 = (f32[512,512]{1,0:T(8,128)}, f32[512,512]{1,0:T(8,128)S(1)}, u32[]{:S(2)}) copy-start(f32[512,512]{1,0:T(8,128)S(1)} %get-tuple-element.174.gown_ref) | copy-start | bytes 3145732
  393.0 20.8 %collective-permute-start.25 = (bf16[512,512]{1,0:T(8,128)(2,1)}, bf16[512,512]{1,0:T(8,128)(2,1)}, u32[]{:S(2)}, u32[]{:S(2)}) collective-permute-start(bf16[512,512]{1,0:T(8,128)(2,1)} %get-tuple-element.175), channel_id=1, source_target_pairs={{8,0},{9,1},{10,2},{11,3},{12,4},{13,5},{14,6},{15,7},{24,16},{25,... | collective-permute-start | bytes 1572872 | tf_op jit(solution)/shard_map/ppermute | solution.py:177
  394.5 31.6 %collective-permute-start.27 = (bf16[8,192,256]{2,1,0:T(8,128)(2,1)}, bf16[8,192,256]{2,1,0:T(8,128)(2,1)}, u32[]{:S(2)}, u32[]{:S(2)}) collective-permute-start(bf16[8,192,256]{2,1,0:T(8,128)(2,1)} %bitcast.51), channel_id=1, source_target_pairs={{0,1},{1,0},{2,3},{3,2},{4,5},{5,4},{6,7},{7,6},{8,9},{9,8},{10,11... | collective-permute-start | bytes 2359304 | tf_op jit(solution)/shard_map/ppermute | solution.py:200
  397.8 28.5 %collective-permute-start.26 = (bf16[8,192,384]{2,1,0:T(8,128)(2,1)}, bf16[8,192,384]{2,1,0:T(8,128)(2,1)}, u32[]{:S(2)}, u32[]{:S(2)}) collective-permute-start(bf16[8,192,384]{2,1,0:T(8,128)(2,1)} %bitcast.50), channel_id=1, source_target_pairs={{0,16},{8,24},{16,0},{24,8},{1,17},{9,25},{17,1},{25,9},{2,18},{10... | collective-permute-start | bytes 3538952 | tf_op jit(solution)/shard_map/ppermute | solution.py:200
  424.4 25.8 %collective-permute-start.38 = (bf16[2,8,96,640]{3,2,1,0:T(8,128)(2,1)S(1)}, bf16[2,8,96,640]{3,2,1,0:T(8,128)(2,1)S(1)}, u32[]{:S(2)}, u32[]{:S(2)}) collective-permute-start(bf16[2,8,96,640]{3,2,1,0:T(8,128)(2,1)S(1)} %weight_gradient.23), channel_id=1, source_target_pairs={{0,8},{8,0},{16,24},{24,16},{1,9},{9,1},{17,25},{25,17},{2,10},{10... | collective-permute-start | bytes 5898248 | tf_op jit(solution)/shard_map/ppermute | solution.py:200
  429.9 7.0 %collective-permute-start.28 = (bf16[128,640]{1,0:T(8,128)(2,1)S(1)}, bf16[128,640]{1,0:T(8,128)(2,1)S(1)}, u32[]{:S(2)}, u32[]{:S(2)}) collective-permute-start(bf16[128,640]{1,0:T(8,128)(2,1)S(1)} %get-tuple-element.218), channel_id=1, source_target_pairs={{0,0},{1,1},{2,2},{3,3},{8,4},{9,5},{10,6},{11,7},{4,8},{5,9},{6,1... | collective-permute-start | bytes 491528 | tf_op jit(solution)/shard_map/ppermute | solution.py:160
  431.9 18.2 %collective-permute-start.31 = (bf16[128,640]{1,0:T(8,128)(2,1)S(1)}, bf16[128,640]{1,0:T(8,128)(2,1)S(1)}, u32[]{:S(2)}, u32[]{:S(2)}) collective-permute-start(bf16[128,640]{1,0:T(8,128)(2,1)S(1)} %get-tuple-element.215), channel_id=1, source_target_pairs={{3,0},{0,1},{1,2},{2,3},{11,4},{8,5},{9,6},{10,7},{7,8},{4,9},{5,1... | collective-permute-start | bytes 491528 | tf_op jit(solution)/shard_map/ppermute | solution.py:160
  431.9 18.2 %collective-permute-start.30 = (bf16[128,640]{1,0:T(8,128)(2,1)S(1)}, bf16[128,640]{1,0:T(8,128)(2,1)S(1)}, u32[]{:S(2)}, u32[]{:S(2)}) collective-permute-start(bf16[128,640]{1,0:T(8,128)(2,1)S(1)} %get-tuple-element.216), channel_id=1, source_target_pairs={{2,0},{3,1},{0,2},{1,3},{10,4},{11,5},{8,6},{9,7},{6,8},{7,9},{4,1... | collective-permute-start | bytes 491528 | tf_op jit(solution)/shard_map/ppermute | solution.py:160
  434.9 13.6 %collective-permute-start.29 = (bf16[128,640]{1,0:T(8,128)(2,1)S(1)}, bf16[128,640]{1,0:T(8,128)(2,1)S(1)}, u32[]{:S(2)}, u32[]{:S(2)}) collective-permute-start(bf16[128,640]{1,0:T(8,128)(2,1)S(1)} %get-tuple-element.217), channel_id=1, source_target_pairs={{1,0},{2,1},{3,2},{0,3},{9,4},{10,5},{11,6},{8,7},{5,8},{6,9},{7,1... | collective-permute-start | bytes 491528 | tf_op jit(solution)/shard_map/ppermute | solution.py:160
  436.9 17.2 %collective-permute-start.35 = (bf16[4,192,256]{2,1,0:T(8,128)(2,1)S(1)}, bf16[4,192,256]{2,1,0:T(8,128)(2,1)S(1)}, u32[]{:S(2)}, u32[]{:S(2)}) collective-permute-start(bf16[4,192,256]{2,1,0:T(8,128)(2,1)S(1)} %slice.108), channel_id=1, source_target_pairs={{0,16},{8,24},{16,0},{24,8},{1,17},{9,25},{17,1},{25,9},{2,18},{10... | collective-permute-start | bytes 1179656 | tf_op jit(solution)/shard_map/ppermute | solution.py:200
  448.4 44.9 %collective-permute-start.32 = (bf16[4,192,384]{2,1,0:T(8,128)(2,1)S(1)}, bf16[4,192,384]{2,1,0:T(8,128)(2,1)S(1)}, u32[]{:S(2)}, u32[]{:S(2)}) collective-permute-start(bf16[4,192,384]{2,1,0:T(8,128)(2,1)S(1)} %slice.107), channel_id=1, source_target_pairs={{0,1},{1,0},{2,3},{3,2},{4,5},{5,4},{6,7},{7,6},{8,9},{9,8},{10,11... | collective-permute-start | bytes 1769480 | tf_op jit(solution)/shard_map/ppermute | solution.py:200
  453.6 39.3 %collective-permute-start.39 = (bf16[8,96,640]{2,1,0:T(8,128)(2,1)S(1)}, bf16[8,96,640]{2,1,0:T(8,128)(2,1)S(1)}, u32[]{:S(2)}, u32[]{:S(2)}) collective-permute-start(bf16[8,96,640]{2,1,0:T(8,128)(2,1)S(1)} %bitcast.145), channel_id=1, source_target_pairs={{0,1},{1,0},{2,3},{3,2},{4,5},{5,4},{6,7},{7,6},{8,9},{9,8},{10,11... | collective-permute-start | bytes 2949128 | tf_op jit(solution)/shard_map/ppermute | solution.py:200
  454.2 18.2 %collective-permute-start.36 = (bf16[2,192,256]{2,1,0:T(8,128)(2,1)S(1)}, bf16[2,192,256]{2,1,0:T(8,128)(2,1)S(1)}, u32[]{:S(2)}, u32[]{:S(2)}) collective-permute-start(bf16[2,192,256]{2,1,0:T(8,128)(2,1)S(1)} %slice.116), channel_id=1, source_target_pairs={{0,4},{1,5},{2,6},{3,7},{4,0},{5,1},{6,2},{7,3},{8,12},{9,13},{10,... | collective-permute-start | bytes 589832 | tf_op jit(solution)/shard_map/ppermute | solution.py:200
  472.5 26.3 %collective-permute-start.37 = (bf16[1,192,256]{2,1,0:T(8,128)(2,1)S(1)}, bf16[1,192,256]{2,1,0:T(8,128)(2,1)S(1)}, u32[]{:S(2)}, u32[]{:S(2)}) collective-permute-start(bf16[1,192,256]{2,1,0:T(8,128)(2,1)S(1)} %slice.118), channel_id=1, source_target_pairs={{0,2},{1,3},{2,0},{3,1},{4,6},{5,7},{6,4},{7,5},{8,10},{9,11},{10,... | collective-permute-start | bytes 294920 | tf_op jit(solution)/shard_map/ppermute | solution.py:200
  493.3 12.8 %collective-permute-start.40 = (bf16[4,96,640]{2,1,0:T(8,128)(2,1)S(1)}, bf16[4,96,640]{2,1,0:T(8,128)(2,1)S(1)}, u32[]{:S(2)}, u32[]{:S(2)}) collective-permute-start(bf16[4,96,640]{2,1,0:T(8,128)(2,1)S(1)} %slice.120), channel_id=1, source_target_pairs={{0,16},{8,24},{16,0},{24,8},{1,17},{9,25},{17,1},{25,9},{2,18},{10... | collective-permute-start | bytes 1474568 | tf_op jit(solution)/shard_map/ppermute | solution.py:200
  493.6 24.7 %collective-permute-start.33 = (bf16[2,192,384]{2,1,0:T(8,128)(2,1)S(1)}, bf16[2,192,384]{2,1,0:T(8,128)(2,1)S(1)}, u32[]{:S(2)}, u32[]{:S(2)}) collective-permute-start(bf16[2,192,384]{2,1,0:T(8,128)(2,1)S(1)} %slice.111), channel_id=1, source_target_pairs={{0,4},{1,5},{2,6},{3,7},{4,0},{5,1},{6,2},{7,3},{8,12},{9,13},{10,... | collective-permute-start | bytes 884744 | tf_op jit(solution)/shard_map/ppermute | solution.py:200
  506.2 17.2 %collective-permute-start.41 = (bf16[2,96,640]{2,1,0:T(8,128)(2,1)S(1)}, bf16[2,96,640]{2,1,0:T(8,128)(2,1)S(1)}, u32[]{:S(2)}, u32[]{:S(2)}) collective-permute-start(bf16[2,96,640]{2,1,0:T(8,128)(2,1)S(1)} %slice.122), channel_id=1, source_target_pairs={{0,4},{1,5},{2,6},{3,7},{4,0},{5,1},{6,2},{7,3},{8,12},{9,13},{10,... | collective-permute-start | bytes 737288 | tf_op jit(solution)/shard_map/ppermute | solution.py:200
  518.3 8.3 %collective-permute-start.34 = (bf16[1,192,384]{2,1,0:T(8,128)(2,1)S(1)}, bf16[1,192,384]{2,1,0:T(8,128)(2,1)S(1)}, u32[]{:S(2)}, u32[]{:S(2)}) collective-permute-start(bf16[1,192,384]{2,1,0:T(8,128)(2,1)S(1)} %slice.113), channel_id=1, source_target_pairs={{0,2},{1,3},{2,0},{3,1},{4,6},{5,7},{6,4},{7,5},{8,10},{9,11},{10,... | collective-permute-start | bytes 442376 | tf_op jit(solution)/shard_map/ppermute | solution.py:200
  523.5 5.6 %collective-permute-start.42 = (bf16[1,96,640]{2,1,0:T(8,128)(2,1)S(1)}, bf16[1,96,640]{2,1,0:T(8,128)(2,1)S(1)}, u32[]{:S(2)}, u32[]{:S(2)}) collective-permute-start(bf16[1,96,640]{2,1,0:T(8,128)(2,1)S(1)} %slice.124), channel_id=1, source_target_pairs={{0,2},{1,3},{2,0},{3,1},{4,6},{5,7},{6,4},{7,5},{8,10},{9,11},{10,... | collective-permute-start | bytes 368648 | tf_op jit(solution)/shard_map/ppermute | solution.py:200
  (70 other events, 185.9 us)
Sparse Core Ops, SparseCore 0:
  11.5 157.0 all-gather.2
  404.8 90.2 reduce-scatter.1

commit v5 on v4

--- a/solution.py
+++ b/solution.py
@@ -100,24 +100,21 @@
     return [pl.BlockSpec(memory_space=pltpu.VMEM)] * count
 
 
-def call(kernel, name, arrays, weights, outs, flops, scratch=()):
+def call(kernel, name, arrays, weights, outs, flops, limit, scratch=(), handed=False):
     outs = [jax.ShapeDtypeStruct(shape, dtype) for shape, dtype in outs]
     moved = sum(a.size * a.dtype.itemsize for a in list(arrays) + outs)
     return pl.pallas_call(
         kernel,
         out_shape=tuple(outs),
-        in_specs=vmem(len(arrays)) + [pl.BlockSpec(memory_space=pl.ANY)] * len(weights),
+        in_specs=vmem(len(arrays)) + [pl.BlockSpec(memory_space=pltpu.HBM)] * len(weights),
         out_specs=tuple(vmem(len(outs))),
-        scratch_shapes=[weight_scratch(w) for w in weights]
+        scratch_shapes=[weight_scratch(w) for w in weights if not handed]
         + ([pltpu.SemaphoreType.DMA((len(weights),))] if weights else [])
         + list(scratch),
-        compiler_params=pltpu.CompilerParams(vmem_limit_bytes=VMEM_LIMIT),
+        compiler_params=pltpu.CompilerParams(vmem_limit_bytes=limit * 2**20),
         cost_estimate=pl.CostEstimate(flops=flops, bytes_accessed=moved, transcendentals=0),
         name=name,
     )(*arrays, *[w[0] for w in weights])
-
-
-VMEM_LIMIT = 44 * 2**20
 
 
 def chunk_route(count, k):
@@ -219,7 +216,7 @@
     for chain, got in zip(chains, held[1:]):
         chain.got = got
         chain.advance()
-    return launch(held[0], chains)
+    return launch(held[0], chains + [part for chain in chains for part in chain.parts])
 
 
 def block_numbers(scatter):
@@ -232,35 +229,32 @@
     return jnp.stack(leave + stay + [along]).astype(jnp.int32)
 
 
-def product_kernel(pairs, extra, added, split, scatter, columns, n_seq, numbers_ref, *refs):
+def product_kernel(pairs, extra, added, outs, scatter, n_seq, numbers_ref, *refs):
     lefts, rights, refs = refs[:pairs], refs[pairs : 2 * pairs], refs[2 * pairs :]
     if extra:
         extra_ref, refs = refs[0], refs[1:]
     if added:
         got_ref, refs = refs[0], refs[1:]
-    me = numbers_ref[4]
+    me, step = numbers_ref[4], pl.program_id(0)
+    half = n_seq // 2
 
     def store(shard, base, value):
         entry = me ^ shard
         if not scatter:
-            entry = lax.rem(entry, 2) * (n_seq // 2) + entry // 2
+            entry = lax.rem(entry, 2) * half + entry // 2
         place = slice(base, base + value.shape[0])
         if added:
             value = value + got_ref[0, entry, place].astype(F32)
         value = value.astype(BF16)
-        if split:
-            stays = entry < n_seq // 2
-
-            @pl.when(stays)
+        for (kind, which, columns), ref in zip(outs, refs):
+            if kind == "all":
+                ref[0, entry, place] = value[:, columns]
+                continue
+            at = entry - which * half if kind == "half" else entry
+
+            @pl.when((entry // half if kind == "half" else step) == which)
             def _():
-                refs[0][0, entry, place] = value
-
-            @pl.when(jnp.logical_not(stays))
-            def _():
-                refs[1][0, entry - n_seq // 2, place] = value
-
-        else:
-            refs[0][0, entry, place] = value
+                ref[0, at, place] = value[:, columns]
 
     base = 0
     for left, right in zip(lefts, rights):
@@ -268,7 +262,7 @@
         rows = width // n_seq
         part = min(width, 512)
         for start in range(0, width, part):
-            total = dot(left[:, start : start + part], right[:, columns], 0, 0)
+            total = dot(left[:, start : start + part], right[...], 0, 0)
             for at in range(0, part, rows):
                 store((start + at) // rows, base, total[at : at + rows])
         base += rows
@@ -277,14 +271,12 @@
             store(shard, base, extra_ref[0, shard].astype(F32))
 
 
-def product(factors, first, blocks, got=None, got_first=0, split=False):
-    pairs, extra, numbers, columns, scatter = factors
+def product(factors, first, outs, got=None):
+    pairs, extra, numbers, scatter = factors
     n_dp, n_seq = lax.axis_size("dp"), lax.axis_size("seq")
     tokens = pairs[0][0].shape[0]
-    wide = columns.stop - columns.start
     widths = [left.shape[1] // n_dp for left, _ in pairs]
     rows = sum(widths) // n_seq + (0 if extra is None else extra.shape[2])
-    entries = n_seq // 2 if split else n_seq
     specs = [pl.BlockSpec((tokens, w), lambda i, n: (0, n[first + i])) for w in widths]
     specs += [pl.BlockSpec(right.shape, lambda i, n: (0, 0)) for _, right in pairs]
     operands = [left for left, _ in pairs] + [right for _, right in pairs]
@@ -292,55 +284,58 @@
         specs.append(pl.BlockSpec((1,) + extra.shape[1:], lambda i, n: (n[first + i], 0, 0, 0)))
         operands.append(extra)
     if got is not None:
-        specs.append(pl.BlockSpec((1, n_seq, rows, wide), lambda i, n: (i + got_first, 0, 0, 0)))
+        specs.append(pl.BlockSpec((1, n_seq, rows, D), lambda i, n: (i, 0, 0, 0)))
         operands.append(got)
-    shape = jax.ShapeDtypeStruct((blocks, entries, rows, wide), BF16)
-    count = 2 if split else 1
+    shapes, out_specs = [], []
+    for kind, _, columns in outs:
+        wide = columns.stop - columns.start
+        entries = n_seq // 2 if kind == "half" else n_seq
+        shapes.append(jax.ShapeDtypeStruct((1 if kind == "block" else 2, entries, rows, wide), BF16))
+        index = (lambda i, n: (0, 0, 0, 0)) if kind == "block" else (lambda i, n: (i, 0, 0, 0))
+        out_specs.append(pl.BlockSpec((1, entries, rows, wide), index))
     return pl.pallas_call(
-        partial(
-            product_kernel, len(pairs), extra is not None, got is not None, split, scatter, columns, n_seq
+        partial(product_kernel, len(pairs), extra is not None, got is not None, outs, scatter, n_seq),
+        grid_spec=pltpu.PrefetchScalarGridSpec(
+            num_scalar_prefetch=1, grid=(2,), in_specs=specs, out_specs=out_specs
         ),
-        grid_spec=pltpu.PrefetchScalarGridSpec(
-            num_scalar_prefetch=1,
-            grid=(blocks,),
-            in_specs=specs,
-            out_specs=[pl.BlockSpec((1, entries, rows, wide), lambda i, n: (i, 0, 0, 0))] * count,
-        ),
-        out_shape=[shape] * count,
-        compiler_params=pltpu.CompilerParams(vmem_limit_bytes=28 * 2**20),
+        out_shape=shapes,
+        compiler_params=pltpu.CompilerParams(vmem_limit_bytes=26 * 2**20),
         cost_estimate=pl.CostEstimate(
-            flops=2 * tokens * sum(widths) * blocks * wide,
-            bytes_accessed=2 * (tokens + 2 * wide) * sum(widths) * blocks,
+            flops=4 * tokens * sum(widths) * D,
+            bytes_accessed=4 * (tokens + 2 * D) * sum(widths),
             transcendentals=0,
         ),
         name="weight_gradient",
     )(numbers, *operands)
 
 
+WHOLE, CUT = slice(0, D), 3 * D // 5
+
+
 class Chain:
-    def __init__(self, pairs, first="dp", scatter=False, columns=slice(0, D), extra=None):
-        self.steps = order(first, scatter)
+    def __init__(self, pairs, scatter=False, extra=None, fork=False):
+        self.steps = order("dp", scatter)
+        self.fork = fork
+        self.parts = []
         n_dp, n_seq = lax.axis_size("dp"), lax.axis_size("seq")
         widths = [left.shape[1] // n_dp for left, _ in pairs]
         self.factors = None
-        self.shape = (-1, sum(widths) // n_seq + (0 if extra is None else extra.shape[2]), columns.stop - columns.start)
+        self.rows = sum(widths) // n_seq + (0 if extra is None else extra.shape[2])
         if n_dp == 4 and all(w % 128 == 0 and w % (n_seq * TILE) == 0 for w in widths):
-            self.factors = (pairs, extra, block_numbers(scatter), columns, scatter)
-            (self.pending,) = product(self.factors, 0, 2)
+            self.factors = (pairs, extra, block_numbers(scatter), scatter)
+            (self.pending,) = product(self.factors, 0, [("all", 0, WHOLE)])
             return
         devices = n_dp * n_seq
         parts = [
-            dot(left, right[:, columns], 0, 0).astype(BF16).reshape(devices, -1, self.shape[2])
-            for left, right in pairs
+            dot(left, right, 0, 0).astype(BF16).reshape(devices, -1, D) for left, right in pairs
         ]
         if extra is not None:
-            parts.append(extra.reshape(devices, -1, self.shape[2]))
+            parts.append(extra.reshape(devices, -1, D))
         target = jnp.arange(devices)
         source, left_over = jnp.zeros_like(target), devices
         for axis, bit in self.steps:
             left_over //= 2
-            weight = bit * n_seq if axis == "dp" else bit
-            source = source + (target // left_over) % 2 * weight
+            source = source + (target // left_over) % 2 * (bit * n_seq if axis == "dp" else bit)
         if scatter:
             source = source + target % n_seq
         me = lax.axis_index("dp") * n_seq
@@ -348,6 +343,12 @@
             me = me + lax.axis_index("seq")
         self.cut(jnp.take(jnp.concatenate(parts, axis=1), me ^ source, axis=0))
 
+    def part(self, steps, keep, pending):
+        chain = object.__new__(Chain)
+        chain.steps, chain.factors, chain.fork, chain.parts = steps, None, False, []
+        chain.keep, chain.pending = keep, pending
+        self.parts.append(chain)
+
     def cut(self, array):
         half = array.shape[0] // 2
         self.keep, self.pending = array[:half], array[half:]
@@ -356,13 +357,19 @@
         self.steps = self.steps[1:]
         if self.factors:
             factors, self.factors = self.factors, None
-            if self.steps[0][0] == "dp":
-                (self.pending,) = product(factors, 3, 1, self.got, 1)
-                (self.keep,) = product(factors, 2, 1, self.got, 0)
+            outs = [("block", 0, WHOLE), ("block", 1, WHOLE)]
+            if self.fork:
+                a, b = slice(0, CUT), slice(CUT, D)
+                outs = [("block", 0, a), ("block", 1, a), ("half", 0, b), ("half", 1, b)]
+            found = product(factors, 2, outs, self.got)
+            found = [array.reshape((-1, self.rows) + array.shape[3:]) for array in found]
+            if self.fork:
+                self.pending = None
+                self.part(order("dp", False)[1:], *found[:2])
+                self.part(order("seq", False)[1:], *found[2:])
+                self.steps = []
             else:
-                self.keep, self.pending = product(factors, 2, 2, self.got, 0, True)
-            self.keep = self.keep.reshape(self.shape)
-            self.pending = self.pending.reshape(self.shape)
+                self.keep, self.pending = found
             return
         array = self.keep.astype(F32) + self.got.astype(F32)
         if self.steps:
@@ -371,6 +378,8 @@
             self.result = array
 
     def finish(self):
+        if self.parts:
+            return jnp.concatenate([part.finish() for part in self.parts], axis=2)
         while self.steps:
             if self.pending is not None:
                 self.got = swap(self.pending, self.steps[0])
@@ -418,9 +427,7 @@
     own_ref[:, VALUES] = raw[:, VALUES].astype(BF16)
 
 
-def query_kernel(weights, normed_ref, gains_ref, cos_ref, sin_ref, w_any, raw_ref, q_ref, w_ref, sem):
-    copy = fetch(weights[0], w_any, w_ref, sem.at[0])
-    copy.wait()
+def query_kernel(normed_ref, gains_ref, cos_ref, sin_ref, w_ref, raw_ref, q_ref):
     cosine_tab, sine_tab = cos_ref[...], sin_ref[...]
     normed = normed_ref[...]
     for h in range(HEADS):
@@ -495,18 +502,20 @@
     cosine_tab, sine_tab = tables
     attn_in, attn_out, ffn_in, ffn_out = weights
     hidden = ffn_out[0].shape[0] * ffn_out[2]
-    normed, key_raw, own = call(
+    normed, key_raw, own, fetched = call(
         partial(key_value_kernel, [attn_in]), "key_value",
         (stream, gains, cosine_tab, sine_tab), [attn_in],
-        [((tokens, D), BF16), ((tokens, HEAD_DIM), F32), ((tokens, 2 * HEAD_DIM), BF16)],
-        4 * tokens * D * HEAD_DIM,
+        [
+            ((tokens, D), BF16), ((tokens, HEAD_DIM), F32), ((tokens, 2 * HEAD_DIM), BF16),
+            ((attn_in[0].shape[0], attn_in[2], D), BF16),
+        ],
+        4 * tokens * D * HEAD_DIM, 12, handed=True,
     )
     before = neighbour(own, count, False)
     query_raw, queries = call(
-        partial(query_kernel, [attn_in]), "query",
-        (normed, gains, cosine_tab, sine_tab), [attn_in],
+        query_kernel, "query", (normed, gains, cosine_tab, sine_tab, fetched), [],
         [((tokens, QUERY_COLS), F32), ((tokens, QUERY_COLS), BF16)],
-        2 * tokens * D * QUERY_COLS,
+        2 * tokens * D * QUERY_COLS, 12,
     )
     context, lse, branch, middle, ffn_normed, gate_up, inner, ffn_branch, result = call(
         partial(block_kernel, [attn_out, ffn_in, ffn_out]), "block_forward",
@@ -516,7 +525,7 @@
             ((tokens, D), BF16), ((tokens, 2 * hidden), BF16), ((tokens, hidden), BF16),
             ((tokens, D), F32), ((tokens, D), F32),
         ],
-        2 * tokens * (D * (QUERY_COLS + 3 * hidden) + 2 * QUERY_COLS * KEY_COUNT),
+        2 * tokens * (D * (QUERY_COLS + 3 * hidden) + 2 * QUERY_COLS * KEY_COUNT), 32,
     )
     record = (
         stream, normed, query_raw, key_raw, queries, before, own, lse, context,
@@ -530,18 +539,14 @@
     gfb_ref, ggu_ref, gb_ref, gctx_ref, gmid_ref, sums_ref,
     wa_ref, wi_ref, wo_ref, sem,
 ):
-    copies = [
-        fetch(weight, source, target, sem.at[i])
-        for i, (weight, source, target) in enumerate(
-            zip(weights, (wa_any, wi_any, wo_any), (wa_ref, wi_ref, wo_ref))
-        )
-    ]
+    copies = [None] * 3
+    for i, source, target in ((2, wo_any, wo_ref), (1, wi_any, wi_ref), (0, wa_any, wa_ref)):
+        copies[i] = fetch(weights[i], source, target, sem.at[i])
     grad_out = grad_ref[...]
     grad_ffn_branch, post_ffn = rms_backward(fb_ref[...], gain_of(gains_ref, POST_FFN), grad_out)
     grad_ffn_branch = grad_ffn_branch.astype(BF16)
     gfb_ref[...] = grad_ffn_branch
     copies[2].wait()
-    copies[1].wait()
     hidden = gu_ref.shape[1] // 2
     total = jnp.zeros(grad_ref.shape, F32)
     for start in range(0, hidden, HIDDEN_BLOCK):
@@ -558,6 +563,8 @@
         grad_up = (grad_inner * value).astype(BF16)
         ggu_ref[:, gate_cols] = grad_gate
         ggu_ref[:, up_cols] = grad_up
+        if start == 0:
+            copies[1].wait()
         total += dot(grad_gate, weight_rows(wi_ref, start, HIDDEN_BLOCK), 1, 0)
         total += dot(grad_up, weight_rows(wi_ref, hidden + start, HIDDEN_BLOCK), 1, 0)
     grad_part, pre_ffn = rms_backward(middle_ref[...], gain_of(gains_ref, PRE_FFN), total)
@@ -648,22 +655,17 @@
             ((tokens, D), BF16), ((tokens, 2 * hidden), BF16), ((tokens, D), BF16),
             ((tokens, QUERY_COLS), BF16), ((tokens, D), F32), ((8, D), F32),
         ],
-        2 * tokens * D * (QUERY_COLS + 3 * hidden),
-    )
+        2 * tokens * D * (QUERY_COLS + 3 * hidden), 26,
+    )
+    grad_context = pump(1, grad_context)
     ffn = [(grad_gate_up, ffn_normed), (inner, grad_ffn_branch)]
-    if last:
-        chains["ffn"] = Chain(ffn, "dp", True)
-    else:
-        cut = 3 * D // 5
-        chains["ffn_a"] = Chain(ffn, "dp", columns=slice(0, cut))
-        chains["ffn_b"] = Chain(ffn, "seq", columns=slice(cut, D))
+    chains["ffn"] = Chain(ffn, last, fork=not last)
     grad_context = launch(grad_context, list(chains.values()))
-    grad_context = pump(1, grad_context)
     grad_queries, grad_before, grad_own = call(
         attention_backward_kernel, "attention_backward",
         (queries, before, own, reach, lse, grad_context), [],
         [((tokens, QUERY_COLS), F32), ((WINDOW, 2 * HEAD_DIM), BF16), ((tokens, 2 * HEAD_DIM), F32)],
-        10 * tokens * QUERY_COLS * KEY_COUNT,
+        10 * tokens * QUERY_COLS * KEY_COUNT, 26,
         [pltpu.VMEM((WINDOW + tokens, 2 * HEAD_DIM), F32)],
     )
     got = neighbour(grad_before, count, True)
@@ -672,7 +674,7 @@
         query_backward_kernel, "query_backward",
         (grad_queries, query_raw, gains, cosine_tab, sine_tab), [],
         [((tokens, QUERY_COLS), BF16), ((1, HEAD_DIM), F32)],
-        20 * tokens * QUERY_COLS,
+        20 * tokens * QUERY_COLS, 12,
     )
     grad_query_raw = pump(3, grad_query_raw)
     grad_projected, grad_in, gain_grads = call(
@@ -683,55 +685,52 @@
         ),
         [attn_in],
         [((tokens, QUERY_COLS + 2 * HEAD_DIM), BF16), ((tokens, D), F32), (gains.shape, F32)],
-        2 * tokens * D * (QUERY_COLS + 2 * HEAD_DIM),
+        2 * tokens * D * (QUERY_COLS + 2 * HEAD_DIM), 14,
     )
     n_dp, n_seq = lax.axis_size("dp"), lax.axis_size("seq")
     gain_grads = gain_grads.astype(BF16).reshape(n_dp, n_seq, 1, -1)
     extra = jnp.pad(gain_grads, ((0, 0), (0, 0), (0, TILE - 1), (0, D - gain_grads.shape[3])))
     attn = [(grad_projected, normed), (context, grad_branch)]
-    chains["attn"] = Chain(attn, "dp" if last else "seq", last, extra=extra)
+    chains["attn"] = Chain(attn, last, extra)
     return launch(grad_in, [chains["attn"]])
 
 
 PLAN = {
     0: [(1, "attn")],
-    1: [(0, "ffn"), (0, "ffn_a"), (0, "ffn_b"), (1, "ffn")],
-    2: [],
-    3: [(1, "attn")],
-    4: [(0, "ffn_a"), (0, "ffn_b")],
+    1: [(1, "ffn")],
+    2: [(0, "ffn"), (1, "attn")],
+    3: [],
 }
 
 
-def gather_weights(w_attn_in, w_attn_out, w_ffn_in, w_ffn_out, gains):
-    layers = w_attn_in.shape[0]
-    kinds = [w_ffn_in.transpose(0, 2, 1), w_ffn_out, w_attn_in.transpose(0, 2, 1), w_attn_out]
-    gain_rows = jnp.pad(gains, ((0, 16 - layers), (0, D - gains.shape[1])))
-    packed = jnp.concatenate([kind.reshape(-1, D) for kind in kinds] + [gain_rows], axis=0)
+def pack_weights(w_attn_in, w_attn_out, w_ffn_in, w_ffn_out, gains):
+    gain_rows = jnp.pad(gains[None, :], ((0, TILE - 1), (0, D - gains.shape[0])))
+    return jnp.concatenate([w_ffn_in.T, w_ffn_out, w_attn_in.T, w_attn_out, gain_rows], axis=0)
+
+
+def gather_weights(packed, sizes, gain_count):
     whole = lax.all_gather(packed, ALL, axis=0, tiled=False)
-    out, at = [[] for _ in range(layers)], 0
-    for kind in kinds:
-        for layer in range(layers):
-            out[layer].append((at, kind.shape[1]))
-            at += kind.shape[1]
-    gain_full = whole[:, at : at + layers, : gains.shape[1]].astype(F32)
-
-    def of(layer):
-        found = []
-        for start, size in out[layer]:
-            if size % TILE:
-                found.append((whole[:, start : start + size].reshape(1, -1, D), 0, size * whole.shape[0]))
-            else:
-                found.append((whole, start, size))
-        ffn_in, ffn_out, attn_in, attn_out = found
-        return (attn_in, attn_out, ffn_in, ffn_out), gain_full[:, layer].reshape(1, -1)
-
-    return of
+    found, at = [], 0
+    for size in sizes:
+        if size % TILE:
+            found.append((whole[:, at : at + size].reshape(1, -1, D), 0, size * whole.shape[0]))
+        else:
+            found.append((whole, at, size))
+        at += size
+    ffn_in, ffn_out, attn_in, attn_out = found
+    gain_full = whole[:, at, :gain_count].astype(F32).reshape(1, -1)
+    return (attn_in, attn_out, ffn_in, ffn_out), gain_full
 
 
 def body(hidden_in, positions, out_grad, w_attn_in, w_attn_out, w_ffn_in, w_ffn_out, gains):
     count = hidden_in.shape[0]
     layer_count = w_attn_in.shape[0]
-    layer_weights = gather_weights(w_attn_in, w_attn_out, w_ffn_in, w_ffn_out, gains)
+    sizes = [w_ffn_in.shape[2], w_ffn_out.shape[1], w_attn_in.shape[2], w_attn_out.shape[1]]
+    packed = [
+        pack_weights(w_attn_in[l], w_attn_out[l], w_ffn_in[l], w_ffn_out[l], gains[l])
+        for l in range(layer_count)
+    ]
+    weights = [gather_weights(packed[0], sizes, gains.shape[1])]
     places = to_long(positions)
     stream = to_long(hidden_in).astype(F32)
     tables = angle_tables(places)
@@ -739,15 +738,17 @@
     blocks = tokens // QUERY_BLOCK
     reach = jnp.minimum(places, WINDOW - 1).reshape(blocks, QUERY_BLOCK)
     reach = jnp.tile(reach, (1, HEADS))
-    records, weights = [], []
+    records = []
+    stream, later = lax.optimization_barrier((stream, packed[1:]))
+    weights += [gather_weights(entry, sizes, gains.shape[1]) for entry in later]
     for layer_index in range(layer_count):
-        weights.append(layer_weights(layer_index))
-        record, stream = forward_layer(stream, *weights[-1], tables, reach, count)
+        record, stream = forward_layer(stream, *weights[layer_index], tables, reach, count)
         records.append(record)
         if layer_index == 0:
             stream, out_grad = lax.optimization_barrier((stream, out_grad))
             grad_stream = to_long(out_grad).astype(F32)
     hidden_out = to_short(stream.astype(BF16), count)
+    outputs = {"hidden": hidden_out}
     chains = [{} for _ in range(layer_count + 1)]
     sums = [None] * layer_count
     for layer_index in reversed(range(layer_count)):
@@ -759,7 +760,9 @@
                 if name in chains[layer_index + above]
             ]
             value = advance(value, active)
-            if where == 3 and layer_index + 1 < layer_count:
+            if where == 1 and layer_index + 1 == layer_count:
+                value, outputs["hidden"] = lax.optimization_barrier((value, outputs["hidden"]))
+            if where == 2 and layer_index + 1 < layer_count:
                 above = chains[layer_index + 1]
                 packed = jnp.concatenate([above["ffn"].finish(), above["attn"].finish()], axis=1)
                 value, packed = lax.optimization_barrier((value, packed.astype(BF16)))
@@ -770,20 +773,26 @@
             grad_stream, *weights[layer_index], records[layer_index], tables, reach, count, pump,
             chains[layer_index], layer_index > 0,
         )
-    grad_stream = pump(4, grad_stream)
-    input_grad = to_short(grad_stream.astype(BF16), count).astype(F32)
-    found = chains[0]
-    ffn = jnp.concatenate([found["ffn_a"].finish(), found["ffn_b"].finish()], axis=2)
-    sums[0] = jnp.concatenate([ffn, found["attn"].finish()], axis=1)[0]
+    attn, ffn = [chains[0]["attn"]], chains[0]["ffn"].parts or [chains[0]["ffn"]]
+    grad_stream = advance(grad_stream, ffn)
+    grad_stream = advance(grad_stream, attn)
+    grad_stream = advance(grad_stream, ffn)
+    short = to_short(grad_stream.astype(BF16), count)
+    mark = advance(grad_stream[:8], attn)
+    mark = advance(mark, ffn)
+    mark = advance(mark, attn)
+    mark = advance(mark, ffn)
+    mark, short = lax.optimization_barrier((mark, short))
+    mark = advance(mark, attn)
+    sums[0] = jnp.concatenate([chains[0]["ffn"].finish(), chains[0]["attn"].finish()], axis=1)[0]
     packed = jnp.stack([entry.astype(F32) for entry in sums])
-    sizes = [w_ffn_in.shape[2], w_ffn_out.shape[1], w_attn_in.shape[2], w_attn_out.shape[1]]
     parts, at = [], 0
     for size in sizes:
         parts.append(packed[:, at : at + size])
         at += size
     return (
-        hidden_out,
-        input_grad,
+        outputs["hidden"],
+        short.astype(F32),
         parts[2].transpose(0, 2, 1),
         parts[3],
         parts[0].transpose(0, 2, 1),

time: 546 us -> 570 us (1.044)
  local copies, waits for them, and re-layouts: 52.9 us -> 91 us
  Pallas kernels: 141 us -> 109 us
  waiting for transfers between devices: 246 us -> 270 us
  starting transfers between devices: 68.1 us -> 61.6 us
    unnamed x210 -> x257, local copies, waits for them, and re-layouts: 48.8 us -> 86.7 us
    pallas_call x14, Pallas kernels: 97.3 us -> 72 us  [call(): pl.pallas_call(kernel, out_shape=tuple(outs), in_specs=vmem(len(arrays))...]
    ppermute x8, waiting for transfers between devices: 20.8 us -> 40.6 us  [to_short(): received.append(lax.ppermute(piece, ALL, route))]
    all_gather x1 -> x2, waiting for transfers between devices: 141 us -> 132 us  [gather_weights(): whole = lax.all_gather(packed, ALL, axis=0, tiled=False)]
    ppermute x8, starting transfers between devices: 14.9 us -> 7.2 us  [to_short(): received.append(lax.ppermute(piece, ALL, route))]
    ppermute x12, waiting for transfers between devices: 5.51 us -> 13 us  [to_long(): received.append(lax.ppermute(piece, ALL, chunk_route(count, k)))]
    ppermute x19 -> x18, waiting for transfers between devices: 77.3 us -> 84.2 us  [swap(): lax.ppermute(array, axis, [(i, i ^ bit) for i in range(lax.axis_size(axis...]
    pallas_call x13 -> x8, Pallas kernels: 43.8 us -> 37.3 us  [product(): pl.pallas_call(partial(product_kernel, len(pairs), extra is not None, got...]
  transfers between devices with their start and end apart: 45 -> 45, of which waited for: 18 -> 20; matrix products, arithmetic and copies ran while one was open for 3% -> 3% of each run, Pallas kernels for 8% -> 15%
where the time goes in v5:
time: 570 us; the launch traced here: 564 us
  waiting for transfers between devices  270 us (47%)
  Pallas kernels  109 us (19%)
  local copies, waits for them, and re-layouts  91 us (16%)
  starting transfers between devices  61.6 us (11%)
  other arithmetic  16.6 us (3%)
  between operations  15.6 us (3%)
    all_gather x2, waiting for transfers between devices, gather_weights(): whole = lax.all_gather(packed, ALL, axis=0, tiled=False)  132 us
    unnamed x257, local copies, waits for them, and re-layouts  86.7 us
    ppermute x18, waiting for transfers between devices, swap(): lax.ppermute(array, axis, [(i, i ^ bit) for i in range(lax.axis_size(axis...  84.2 us
    pallas_call x14, Pallas kernels, call(): pl.pallas_call(kernel, out_shape=tuple(outs), in_specs=vmem(len(arrays))...  72 us
    ppermute x8, waiting for transfers between devices, to_short(): received.append(lax.ppermute(piece, ALL, route))  40.6 us
    pallas_call x8, Pallas kernels, product(): pl.pallas_call(partial(product_kernel, len(pairs), extra is not None, got...  37.3 us
    ppermute x18, starting transfers between devices, swap(): lax.ppermute(array, axis, [(i, i ^ bit) for i in range(lax.axis_size(axis...  29 us
    ppermute x12, starting transfers between devices, to_long(): received.append(lax.ppermute(piece, ALL, chunk_route(count, k)))  17.4 us
  transfers between devices with their start and end apart: 45, of which 20 were waited for; matrix products, arithmetic and copies ran while one was open for 3% of the time, Pallas kernels for 15%

profile of v5, /device:TPU:0, one launch (start us, length us, event | category | flops | bytes accessed | tf_op | source)
XLA Modules:
  0.0 564.4 jit_solution(13364093332924652779)
XLA Ops:
  9.9 4.0 collective-permute-start
  15.7 1.8 collective-permute-done
  17.5 3.7 collective-permute-done.1
  24.1 2.0 collective-permute-start.5
  26.1 1.9 collective-permute-start.6
  28.7 1.8 collective-permute-done.6
  31.5 77.4 %all-gather.5.cloned.1.call-done = bf16[9216,640]{1,0:T(8,128)(2,1)} async-done(((bf16[288,640]{1,0:T(8,128)(2,1)}), bf16[9216,640]{1,0:T(8,128)(2,1)}) %all-gather.5.cloned.1.call-update) | async-done | bytes 11796496 | tf_op jit(solution)/shard_map/all_gather | solution.py:712
  109.9 4.3 copy-done
  117.4 3.1 collective-permute-start.8
  126.4 13.6 %block_forward.2 = (bf16[512,1024]{1,0:T(8,128)(2,1)S(1)}, f32[2,1024]{1,0:T(2,128)S(1)}, f32[512,640]{1,0:T(8,128)S(1)}, f32[512,640]{1,0:T(8,128)S(1)}, bf16[5...) custom-call(bf16[512,1024]{1,0:T(8,128)(2,1)S(1)} %get-tuple-element, ...), custom_call_target="tpu_custom_call" | custom-call | flops 6308233216 | bytes 16674816 | tf_op jit(solution)/shard_map/block_forward/pallas_call | solution.py:106
  141.4 2.1 copy-done.18
  149.4 2.0 collective-permute-start.9
  151.4 55.0 %all-gather.7.cloned.1.call-done = bf16[9216,640]{1,0:T(8,128)(2,1)} async-done(((bf16[288,640]{1,0:T(8,128)(2,1)}), bf16[9216,640]{1,0:T(8,128)(2,1)}) %all-gather.7.cloned.1.call-update) | async-done | bytes 11796496 | tf_op jit(solution)/shard_map/all_gather | solution.py:712
  207.4 4.3 copy-done.3
  213.6 2.2 collective-permute-start.13
  223.0 4.4 collective-permute-done.11
  227.8 12.6 %block_forward.3 = (bf16[512,1024]{1,0:T(8,128)(2,1)S(1)}, f32[2,1024]{1,0:T(2,128)S(1)}, f32[512,640]{1,0:T(8,128)S(1)}, f32[512,640]{1,0:T(8,128)S(1)}, bf16[5...) custom-call(bf16[512,1024]{1,0:T(8,128)(2,1)S(1)} %get-tuple-element, ...), custom_call_target="tpu_custom_call" | custom-call | flops 6308233216 | bytes 16674816 | tf_op jit(solution)/shard_map/block_forward/pallas_call | solution.py:106
  240.4 1.9 copy-done.20
  248.0 2.3 collective-permute-start.17
  250.3 4.4 copy-done.4
  254.7 2.2 copy-done.21
  258.2 11.0 %block_backward.2 = (bf16[512,640]{1,0:T(8,128)(2,1)S(1)}, bf16[512,4096]{1,0:T(8,128)(2,1)S(1)}, bf16[512,640]{1,0:T(8,128)(2,1)S(1)}, bf16[512,1024]{1,0:T(8,1...) custom-call(f32[512,640]{1,0:T(8,128)S(1)} %bitcast_convert_fusion.grad_ref, f32[512,640]{1,0:T(8,128)S(1)} %copy-done.66, ...), custom_call_target="tpu_custom_call" | custom-call | flops 4697620480 | bytes 17334272 | tf_op jit(solution)/shard_map/block_backward/pallas_call | solution.py:106
  269.2 3.9 weight_gradient.8
  274.3 5.6 collective-permute-start.18
  279.9 5.2 attention_backward.2
  288.8 1.8 copy-done.27
  290.6 2.1 copy-done.28
  292.7 6.9 %weight_gradient.9 = (bf16[1,8,192,640]{3,2,1,0:T(8,128)(2,1)S(1)}, bf16[1,8,192,640]{3,2,1,0:T(8,128)(2,1)}) custom-call(s32[5]{0:T(128)S(1)} %stack.154.numbers_ref, bf16[512,4096]{1,0:T(8,128)(2,1)S(1)} %get-tuple-element.152.refs_0_, bf16[512,2048]{1,0:T(8,128)(2,1)S(1)} %get-tuple-element.153.refs_1_, bf16[512,640]{1,0:T(8,128)(2,1)S(1)} %get-tuple-element.154.refs_2_, ...), custom_call_target="tpu_custom_call" | custom-call | flops 2013265920 | bytes 11010048 | tf_op jit(solution)/shard_map/weight_gradient/pallas_call | solution.py:296
  302.1 2.3 input_backward.2
  306.8 1.6 copy-done.8
  311.9 3.2 weight_gradient.10
  317.6 2.6 collective-permute-done.20.refs_5_
  324.7 4.6 weight_gradient.11
  331.2 4.4 copy-done.1
  339.5 11.4 %block_backward.3 = (bf16[512,640]{1,0:T(8,128)(2,1)S(1)}, bf16[512,4096]{1,0:T(8,128)(2,1)S(1)}, bf16[512,640]{1,0:T(8,128)(2,1)S(1)}, bf16[512,1024]{1,0:T(8,1...) custom-call(f32[512,640]{1,0:T(8,128)S(1)} %copy-done.60, f32[512,640]{1,0:T(8,128)S(1)} %copy-done.54, ...), custom_call_target="tpu_custom_call" | custom-call | flops 4697620480 | bytes 17334272 | tf_op jit(solution)/shard_map/block_backward/pallas_call | solution.py:106
  351.0 10.3 %collective-permute-done.21 = bf16[8,192,640]{2,1,0:T(8,128)(2,1)} collective-permute-done((bf16[8,192,640]{2,1,0:T(8,128)(2,1)}, bf16[8,192,640]{2,1,0:T(8,128)(2,1)}, u32[]{:S(2)}, u32[]{:S(2)}) %collective-permute-start.21) | collective-permute-done | bytes 1966112 | tf_op jit(solution)/shard_map/ppermute | solution.py:197
  361.3 3.9 weight_gradient.12
  366.6 6.4 %attention_backward.3 = (f32[512,1024]{1,0:T(8,128)S(1)}, bf16[512,512]{1,0:T(8,128)(2,1)S(1)}, f32[512,512]{1,0:T(8,128)S(1)}) custom-call(bf16[512,1024]{1,0:T(8,128)(2,1)S(1)} %copy-done.72, bf16[512,512]{1,0:T(8,128)(2,1)} %collective-permute-done.8.before_ref, bf16[512,512]{1,0:T(8,128)(2,1)S(1)} %copy-done.84, s32[2,1024]{1,0:T(2,128)S(1)} %bitcast.180, ...), custom_call_target="tpu_custom_call" | custom-call | flops 4026531840 | bytes 6832128 | tf_op jit(solution)/shard_map/attention_backward/pallas_call | solution.py:106
  374.4 2.0 fusion
  376.4 13.0 %collective-permute-done.23 = bf16[8,96,640]{2,1,0:T(8,128)(2,1)S(1)} collective-permute-done((bf16[8,96,640]{2,1,0:T(8,128)(2,1)S(1)}, bf16[8,96,640]{2,1,0:T(8,128)(2,1)S(1)}, u32[]{:S(2)}, u32[]{:S(2)}) %collective-permute-start.23) | collective-permute-done | bytes 983072 | tf_op jit(solution)/shard_map/ppermute | solution.py:197
  389.5 7.2 %weight_gradient.13 = (bf16[1,8,192,384]{3,2,1,0:T(8,128)(2,1)S(1)}, bf16[1,8,192,384]{3,2,1,0:T(8,128)(2,1)}, bf16[2,4,192,256]{3,2,1,0:T(8,128)(2,1)S(1)}, bf16[2,4,192,256]{3,2,1,0:T(8,128)(2,1)}) custom-call(s32[5]{0:T(128)S(1)} %stack.156.numbers_ref, bf16[512,4096]{1,0:T(8,128)(2,1)S(1)} %get-tuple-element.189.refs_0_, ...), custom_call_target="tpu_custom_call" | custom-call | flops 2013265920 | bytes 11010048 | tf_op jit(solution)/shard_map/weight_gradient/pallas_call | solution.py:296
  398.2 1.8 pad_maximum_fusion
  400.0 1.6 copy-done.38
  401.6 1.6 copy-done.42
  405.2 4.3 copy-done.2
  410.6 2.3 input_backward.3
  417.6 3.2 weight_gradient.14
  420.8 2.9 collective-permute-start.26
  423.7 22.5 %collective-permute-done.26 = bf16[8,192,256]{2,1,0:T(8,128)(2,1)} collective-permute-done((bf16[8,192,256]{2,1,0:T(8,128)(2,1)}, bf16[8,192,256]{2,1,0:T(8,128)(2,1)}, u32[]{:S(2)}, u32[]{:S(2)}) %collective-permute-start.26) | collective-permute-done | bytes 786464 | tf_op jit(solution)/shard_map/ppermute | solution.py:197
  446.1 1.7 fusion.4
  447.9 1.7 fusion.1
  449.7 1.8 collective-permute-start.28
  452.6 4.4 weight_gradient.15
  457.0 5.0 collective-permute-done.29
  462.0 7.0 %collective-permute-done.28 = bf16[4,192,384]{2,1,0:T(8,128)(2,1)S(1)} collective-permute-done((bf16[4,192,384]{2,1,0:T(8,128)(2,1)S(1)}, bf16[4,192,384]{2,1,0:T(8,128)(2,1)S(1)}, u32[]{:S(2)}, u32[]{:S(2)}) %collective-permute-start.28) | collective-permute-done | bytes 589856 | tf_op jit(solution)/shard_map/ppermute | solution.py:197
  471.2 4.0 collective-permute-start.34
  478.7 16.3 %collective-permute-done.31 = bf16[128,640]{1,0:T(8,128)(2,1)S(1)} collective-permute-done((bf16[128,640]{1,0:T(8,128)(2,1)S(1)}, bf16[128,640]{1,0:T(8,128)(2,1)S(1)}, u32[]{:S(2)}, u32[]{:S(2)}) %collective-permute-start.31) | collective-permute-done | bytes 163872 | tf_op jit(solution)/shard_map/ppermute | solution.py:157
  495.0 6.4 %collective-permute-done.32 = bf16[128,640]{1,0:T(8,128)(2,1)S(1)} collective-permute-done((bf16[128,640]{1,0:T(8,128)(2,1)S(1)}, bf16[128,640]{1,0:T(8,128)(2,1)S(1)}, u32[]{:S(2)}, u32[]{:S(2)}) %collective-permute-start.32) | collective-permute-done | bytes 163872 | tf_op jit(solution)/shard_map/ppermute | solution.py:157
  501.4 17.9 %collective-permute-done.33 = bf16[128,640]{1,0:T(8,128)(2,1)S(1)} collective-permute-done((bf16[128,640]{1,0:T(8,128)(2,1)S(1)}, bf16[128,640]{1,0:T(8,128)(2,1)S(1)}, u32[]{:S(2)}, u32[]{:S(2)}) %collective-permute-start.33) | collective-permute-done | bytes 163872 | tf_op jit(solution)/shard_map/ppermute | solution.py:157
  520.2 1.9 collective-permute-start.37
  522.1 9.5 %collective-permute-done.39 = bf16[4,96,640]{2,1,0:T(8,128)(2,1)S(1)} collective-permute-done((bf16[4,96,640]{2,1,0:T(8,128)(2,1)S(1)}, bf16[4,96,640]{2,1,0:T(8,128)(2,1)S(1)}, u32[]{:S(2)}, u32[]{:S(2)}) %collective-permute-start.39) | collective-permute-done | bytes 491552 | tf_op jit(solution)/shard_map/ppermute | solution.py:197
  531.8 5.1 collective-permute-start.40
  538.1 9.0 %collective-permute-done.40 = bf16[2,96,640]{2,1,0:T(8,128)(2,1)S(1)} collective-permute-done((bf16[2,96,640]{2,1,0:T(8,128)(2,1)S(1)}, bf16[2,96,640]{2,1,0:T(8,128)(2,1)S(1)}, u32[]{:S(2)}, u32[]{:S(2)}) %collective-permute-start.40) | collective-permute-done | bytes 245792 | tf_op jit(solution)/shard_map/ppermute | solution.py:197
  547.3 5.3 collective-permute-done.41
  (379 shorter events, 95.0 us)
Async XLA Ops:
  7.2 101.7 %all-gather.5.cloned.1.call-start = ((), (), s32[]{:S(2)}) async-start(), calls=%async_computation.2 | async-start | bytes 12165120 | tf_op jit(solution)/shard_map/all_gather | solution.py:712
  9.7 196.7 %all-gather.7.cloned.1.call-start = ((), (), s32[]{:S(2)}) async-start(), calls=%async_computation.3 | async-start | bytes 12165120 | tf_op jit(solution)/shard_map/all_gather | solution.py:712
  9.9 7.6 %collective-permute-start = (bf16[128,640]{1,0:T(8,128)(2,1)S(1)}, bf16[128,640]{1,0:T(8,128)(2,1)S(1)}, u32[]{:S(2)}, u32[]{:S(2)}) collective-permute-start(bf16[128,640]{1,0:T(8,128)(2,1)S(1)} %get-tuple-element.286), channel_id=1, source_target_pairs={{0,3},{1,0},{2,1},{3,2},{4,11},{5,8},{6,9},{7,10},{8,7},{9,4},{10,... | collective-permute-start | bytes 491528 | tf_op jit(solution)/shard_map/ppermute | solution.py:144
  13.9 7.3 %collective-permute-start.1 = (bf16[128,640]{1,0:T(8,128)(2,1)S(1)}, bf16[128,640]{1,0:T(8,128)(2,1)S(1)}, u32[]{:S(2)}, u32[]{:S(2)}) collective-permute-start(bf16[128,640]{1,0:T(8,128)(2,1)S(1)} %get-tuple-element.285), channel_id=1, source_target_pairs={{0,2},{1,3},{2,0},{3,1},{4,10},{5,11},{6,8},{7,9},{8,6},{9,7},{10,... | collective-permute-start | bytes 491528 | tf_op jit(solution)/shard_map/ppermute | solution.py:144
  14.3 7.2 %collective-permute-start.2 = (bf16[128,640]{1,0:T(8,128)(2,1)S(1)}, bf16[128,640]{1,0:T(8,128)(2,1)S(1)}, u32[]{:S(2)}, u32[]{:S(2)}) collective-permute-start(bf16[128,640]{1,0:T(8,128)(2,1)S(1)} %get-tuple-element.287), channel_id=1, source_target_pairs={{0,1},{1,2},{2,3},{3,0},{4,9},{5,10},{6,11},{7,8},{8,5},{9,6},{10,... | collective-permute-start | bytes 491528 | tf_op jit(solution)/shard_map/ppermute | solution.py:144
  15.0 6.6 %collective-permute-start.3 = (bf16[128,640]{1,0:T(8,128)(2,1)S(1)}, bf16[128,640]{1,0:T(8,128)(2,1)S(1)}, u32[]{:S(2)}, u32[]{:S(2)}) collective-permute-start(bf16[128,640]{1,0:T(8,128)(2,1)S(1)} %get-tuple-element.284), channel_id=1, source_target_pairs={{0,0},{1,1},{2,2},{3,3},{4,8},{5,9},{6,10},{7,11},{8,4},{9,5},{10,... | collective-permute-start | bytes 491528 | tf_op jit(solution)/shard_map/ppermute | solution.py:144
  22.0 530.7 %reduce-scatter.2.cloned.1.call-start = ((), (), s32[]{:S(2)}) async-start(), calls=%async_computation.1 | async-start | bytes 3317760 | tf_op jit(solution)/shard_map/reduce_scatter | solution.py:769
  22.5 6.2 %collective-permute-start.4 = (s32[128]{0:T(128)S(1)}, s32[128]{0:T(128)S(1)}, u32[]{:S(2)}, u32[]{:S(2)}) collective-permute-start(s32[128]{0:T(128)S(1)} %get-tuple-element.302), channel_id=1, source_target_pairs={{0,3},{1,0},{2,1},{3,2},{4,11},{5,8},{6,9},{7,10},{8,7},{9,4},{10,... | collective-permute-start | bytes 1544 | tf_op jit(solution)/shard_map/ppermute | solution.py:144
  24.1 4.6 collective-permute-start.5
  26.1 4.4 collective-permute-start.6
  28.0 2.5 collective-permute-start.7
  117.4 7.6 %collective-permute-start.8 = (bf16[512,512]{1,0:T(8,128)(2,1)S(1)}, bf16[512,512]{1,0:T(8,128)(2,1)}, u32[]{:S(2)}, u32[]{:S(2)}) collective-permute-start(bf16[512,512]{1,0:T(8,128)(2,1)S(1)} %get-tuple-element.133.own_ref), channel_id=1, source_target_pairs={{0,8},{1,9},{2,10},{3,11},{4,12},{5,13},{6,14},{7,15},{16,24},{17,... | collective-permute-start | bytes 1572872 | tf_op jit(solution)/shard_map/ppermute | solution.py:174
  125.0 15.1 %copy-start.71 = (bf16[512,1024]{1,0:T(8,128)(2,1)}, bf16[512,1024]{1,0:T(8,128)(2,1)S(1)}, u32[]{:S(2)}) copy-start(bf16[512,1024]{1,0:T(8,128)(2,1)S(1)} %get-tuple-element.132.q_ref) | copy-start | bytes 3145732
  126.4 22.1 %copy-start.100 = (bf16[4,128,640]{2,1,0:T(8,128)(2,1)S(1)}, bf16[4,128,640]{2,1,0:T(8,128)(2,1)}, u32[]{:S(2)}) copy-start(bf16[4,128,640]{2,1,0:T(8,128)(2,1)} %param.10) | copy-start | bytes 1966084
  149.4 72.6 %collective-permute-start.9 = (bf16[128,640]{1,0:T(8,128)(2,1)}, bf16[128,640]{1,0:T(8,128)(2,1)S(1)}, u32[]{:S(2)}, u32[]{:S(2)}) collective-permute-start(bf16[128,640]{1,0:T(8,128)(2,1)} %get-tuple-element.283), channel_id=1, source_target_pairs={{0,3},{1,0},{2,1},{3,2},{4,11},{5,8},{6,9},{7,10},{8,7},{9,4},{10,... | collective-permute-start | bytes 491528 | tf_op jit(solution)/shard_map/ppermute | solution.py:144
  211.7 6.7 %copy-start.101 = (bf16[128,640]{1,0:T(8,128)(2,1)S(1)}, bf16[128,640]{1,0:T(8,128)(2,1)}, u32[]{:S(2)}) copy-start(bf16[128,640]{1,0:T(8,128)(2,1)} %get-tuple-element.280) | copy-start | bytes 491524
  213.6 7.0 %copy-start.15 = (bf16[512,640]{1,0:T(8,128)(2,1)}, bf16[512,640]{1,0:T(8,128)(2,1)S(1)}, u32[]{:S(2)}) copy-start(bf16[512,640]{1,0:T(8,128)(2,1)S(1)} %get-tuple-element.138.normed_ref.refs_2_) | copy-start | bytes 1966084
  213.6 14.2 %copy-start.85 = (bf16[512,512]{1,0:T(8,128)(2,1)}, bf16[512,512]{1,0:T(8,128)(2,1)S(1)}, u32[]{:S(2)}) copy-start(bf16[512,512]{1,0:T(8,128)(2,1)S(1)} %get-tuple-element.141.own_ref) | copy-start | bytes 1572868
  213.6 14.1 %collective-permute-start.13 = (bf16[512,512]{1,0:T(8,128)(2,1)S(1)}, bf16[512,512]{1,0:T(8,128)(2,1)S(1)}, u32[]{:S(2)}, u32[]{:S(2)}) collective-permute-start(bf16[512,512]{1,0:T(8,128)(2,1)S(1)} %get-tuple-element.141.own_ref), channel_id=1, source_target_pairs={{0,8},{1,9},{2,10},{3,11},{4,12},{5,13},{6,14},{7,15},{16,24},{17,... | collective-permute-start | bytes 1572872 | tf_op jit(solution)/shard_map/ppermute | solution.py:174
  215.8 7.2 %collective-permute-start.10 = (bf16[128,640]{1,0:T(8,128)(2,1)S(1)}, bf16[128,640]{1,0:T(8,128)(2,1)S(1)}, u32[]{:S(2)}, u32[]{:S(2)}) collective-permute-start(bf16[128,640]{1,0:T(8,128)(2,1)S(1)} %copy-done.103), channel_id=1, source_target_pairs={{0,2},{1,3},{2,0},{3,1},{4,10},{5,11},{6,8},{7,9},{8,6},{9,7},{10,... | collective-permute-start | bytes 491528 | tf_op jit(solution)/shard_map/ppermute | solution.py:144
  217.0 10.4 %collective-permute-start.11 = (bf16[128,640]{1,0:T(8,128)(2,1)S(1)}, bf16[128,640]{1,0:T(8,128)(2,1)S(1)}, u32[]{:S(2)}, u32[]{:S(2)}) collective-permute-start(bf16[128,640]{1,0:T(8,128)(2,1)S(1)} %copy-done.102), channel_id=1, source_target_pairs={{0,1},{1,2},{2,3},{3,0},{4,9},{5,10},{6,11},{7,8},{8,5},{9,6},{10,... | collective-permute-start | bytes 491528 | tf_op jit(solution)/shard_map/ppermute | solution.py:144
  218.4 9.0 %collective-permute-start.12 = (bf16[128,640]{1,0:T(8,128)(2,1)S(1)}, bf16[128,640]{1,0:T(8,128)(2,1)S(1)}, u32[]{:S(2)}, u32[]{:S(2)}) collective-permute-start(bf16[128,640]{1,0:T(8,128)(2,1)S(1)} %copy-done.101), channel_id=1, source_target_pairs={{0,0},{1,1},{2,2},{3,3},{4,8},{5,9},{6,10},{7,11},{8,4},{9,5},{10,... | collective-permute-start | bytes 491528 | tf_op jit(solution)/shard_map/ppermute | solution.py:144
  227.8 12.6 %copy-start.87 = (bf16[512,512]{1,0:T(8,128)(2,1)}, bf16[512,512]{1,0:T(8,128)(2,1)S(1)}, u32[]{:S(2)}) copy-start(bf16[512,512]{1,0:T(8,128)(2,1)S(1)} %collective-permute-done.13.before_ref) | copy-start | bytes 1572868
  246.0 27.1 %collective-permute-start.14 = (bf16[128,640]{1,0:T(8,128)(2,1)S(1)}, bf16[128,640]{1,0:T(8,128)(2,1)S(1)}, u32[]{:S(2)}, u32[]{:S(2)}) collective-permute-start(bf16[128,640]{1,0:T(8,128)(2,1)S(1)} %get-tuple-element.279), channel_id=1, source_target_pairs={{0,0},{1,1},{2,2},{3,3},{8,4},{9,5},{10,6},{11,7},{4,8},{5,9},{6,1... | collective-permute-start | bytes 491528 | tf_op jit(solution)/shard_map/ppermute | solution.py:157
  246.8 26.3 %collective-permute-start.15 = (bf16[128,640]{1,0:T(8,128)(2,1)S(1)}, bf16[128,640]{1,0:T(8,128)(2,1)S(1)}, u32[]{:S(2)}, u32[]{:S(2)}) collective-permute-start(bf16[128,640]{1,0:T(8,128)(2,1)S(1)} %get-tuple-element.278), channel_id=1, source_target_pairs={{1,0},{2,1},{3,2},{0,3},{9,4},{10,5},{11,6},{8,7},{5,8},{6,9},{7,1... | collective-permute-start | bytes 491528 | tf_op jit(solution)/shard_map/ppermute | solution.py:157
  246.9 26.3 %collective-permute-start.16 = (bf16[128,640]{1,0:T(8,128)(2,1)S(1)}, bf16[128,640]{1,0:T(8,128)(2,1)S(1)}, u32[]{:S(2)}, u32[]{:S(2)}) collective-permute-start(bf16[128,640]{1,0:T(8,128)(2,1)S(1)} %get-tuple-element.277), channel_id=1, source_target_pairs={{2,0},{3,1},{0,2},{1,3},{10,4},{11,5},{8,6},{9,7},{6,8},{7,9},{4,1... | collective-permute-start | bytes 491528 | tf_op jit(solution)/shard_map/ppermute | solution.py:157
  248.0 25.2 %collective-permute-start.17 = (bf16[128,640]{1,0:T(8,128)(2,1)S(1)}, bf16[128,640]{1,0:T(8,128)(2,1)S(1)}, u32[]{:S(2)}, u32[]{:S(2)}) collective-permute-start(bf16[128,640]{1,0:T(8,128)(2,1)S(1)} %get-tuple-element.276), channel_id=1, source_target_pairs={{3,0},{0,1},{1,2},{2,3},{11,4},{8,5},{9,6},{10,7},{7,8},{4,9},{5,1... | collective-permute-start | bytes 491528 | tf_op jit(solution)/shard_map/ppermute | solution.py:157
  274.3 14.5 %collective-permute-start.18 = (bf16[2,8,192,640]{3,2,1,0:T(8,128)(2,1)S(1)}, bf16[2,8,192,640]{3,2,1,0:T(8,128)(2,1)S(1)}, u32[]{:S(2)}, u32[]{:S(2)}) collective-permute-start(bf16[2,8,192,640]{3,2,1,0:T(8,128)(2,1)S(1)} %weight_gradient.8), channel_id=1, source_target_pairs={{0,8},{8,0},{16,24},{24,16},{1,9},{9,1},{17,25},{25,17},{2,10},{10... | collective-permute-start | bytes 11796488 | tf_op jit(solution)/shard_map/ppermute | solution.py:197
  279.9 21.0 %slice-start = ((s8[11796480]{0:T(1024)(128)(4,1)}), s8[4194304]{0:T(1024)(128)(4,1)S(1)}, s32[]{:S(2)}) async-start(s8[11796480]{0:T(1024)(128)(4,1)} %bitcast.174), calls=%async_computation.4 | async-start | bytes 8388608
  279.9 21.0 %slice-start.1 = ((s8[11796480]{0:T(1024)(128)(4,1)}), s8[4194304]{0:T(1024)(128)(4,1)S(1)}, s32[]{:S(2)}) async-start(s8[11796480]{0:T(1024)(128)(4,1)} %bitcast.174), calls=%async_computation.5 | async-start | bytes 8388608
  287.5 13.4 %collective-permute-start.19 = (bf16[512,512]{1,0:T(8,128)(2,1)S(1)}, bf16[512,512]{1,0:T(8,128)(2,1)S(1)}, u32[]{:S(2)}, u32[]{:S(2)}) collective-permute-start(bf16[512,512]{1,0:T(8,128)(2,1)S(1)} %get-tuple-element.166), channel_id=1, source_target_pairs={{8,0},{9,1},{10,2},{11,3},{12,4},{13,5},{14,6},{15,7},{24,16},{25,... | collective-permute-start | bytes 1572872 | tf_op jit(solution)/shard_map/ppermute | solution.py:174
  292.7 6.9 %copy-start.40 = (f32[512,1024]{1,0:T(8,128)S(1)}, f32[512,1024]{1,0:T(8,128)}, u32[]{:S(2)}) copy-start(f32[512,1024]{1,0:T(8,128)} %copy-done.39) | copy-start | bytes 6291460
  292.7 6.9 %copy-start.44 = (f32[512,1024]{1,0:T(8,128)S(1)}, f32[512,1024]{1,0:T(8,128)}, u32[]{:S(2)}) copy-start(f32[512,1024]{1,0:T(8,128)} %copy-done.43) | copy-start | bytes 6291460
  292.7 8.2 %slice-start.2 = ((s8[11796480]{0:T(1024)(128)(4,1)}), s8[3407872]{0:T(1024)(128)(4,1)S(1)}, s32[]{:S(2)}) async-start(s8[11796480]{0:T(1024)(128)(4,1)} %bitcast.174), calls=%async_computation.6 | async-start | bytes 6815744
  306.8 8.3 %copy-start.10 = (bf16[4,8,16,640]{3,2,1,0:T(8,128)(2,1)}, bf16[4,8,16,640]{3,2,1,0:T(8,128)(2,1)S(1)}, u32[]{:S(2)}) copy-start(bf16[4,8,16,640]{3,2,1,0:T(8,128)(2,1)S(1)} %pad.16.refs_4_) | copy-start | bytes 1966084
  311.9 8.3 %copy-start.9 = (bf16[512,1536]{1,0:T(8,128)(2,1)S(1)}, bf16[512,1536]{1,0:T(8,128)(2,1)}, u32[]{:S(2)}) copy-start(bf16[512,1536]{1,0:T(8,128)(2,1)} %copy-done.7) | copy-start | bytes 4718596
  315.1 5.1 collective-permute-start.20
  316.2 45.0 %collective-permute-start.21 = (bf16[8,192,640]{2,1,0:T(8,128)(2,1)}, bf16[8,192,640]{2,1,0:T(8,128)(2,1)}, u32[]{:S(2)}, u32[]{:S(2)}) collective-permute-start(bf16[8,192,640]{2,1,0:T(8,128)(2,1)} %bitcast.54), channel_id=1, source_target_pairs={{0,16},{8,24},{16,0},{24,8},{1,17},{9,25},{17,1},{25,9},{2,18},{10... | collective-permute-start | bytes 5898248 | tf_op jit(solution)/shard_map/ppermute | solution.py:197
  339.5 21.7 %copy-start.6 = (bf16[512,2048]{1,0:T(8,128)(2,1)S(1)}, bf16[512,2048]{1,0:T(8,128)(2,1)}, u32[]{:S(2)}) copy-start(bf16[512,2048]{1,0:T(8,128)(2,1)} %copy-done.5) | copy-start | bytes 6291460
  339.5 21.7 %copy-start.30 = (bf16[512,640]{1,0:T(8,128)(2,1)S(1)}, bf16[512,640]{1,0:T(8,128)(2,1)}, u32[]{:S(2)}) copy-start(bf16[512,640]{1,0:T(8,128)(2,1)} %copy-done.29) | copy-start | bytes 1966084
  351.0 14.2 %copy-start.31 = (bf16[512,640]{1,0:T(8,128)(2,1)}, bf16[512,640]{1,0:T(8,128)(2,1)S(1)}, u32[]{:S(2)}) copy-start(bf16[512,640]{1,0:T(8,128)(2,1)S(1)} %get-tuple-element.218.refs_3_) | copy-start | bytes 1966084
  351.0 14.2 %copy-start.57 = (f32[512,640]{1,0:T(8,128)}, f32[512,640]{1,0:T(8,128)S(1)}, u32[]{:S(2)}) copy-start(f32[512,640]{1,0:T(8,128)S(1)} %get-tuple-element.212.gmid_ref) | copy-start | bytes 3932164
  365.2 24.3 %collective-permute-start.22 = (bf16[2,8,192,640]{3,2,1,0:T(8,128)(2,1)S(1)}, bf16[2,8,192,640]{3,2,1,0:T(8,128)(2,1)S(1)}, u32[]{:S(2)}, u32[]{:S(2)}) collective-permute-start(bf16[2,8,192,640]{3,2,1,0:T(8,128)(2,1)S(1)} %weight_gradient.12), channel_id=1, source_target_pairs={{0,8},{8,0},{16,24},{24,16},{1,9},{9,1},{17,25},{25,17},{2,10},{10... | collective-permute-start | bytes 11796488 | tf_op jit(solution)/shard_map/ppermute | solution.py:197
  365.3 24.2 %collective-permute-start.23 = (bf16[8,96,640]{2,1,0:T(8,128)(2,1)S(1)}, bf16[8,96,640]{2,1,0:T(8,128)(2,1)S(1)}, u32[]{:S(2)}, u32[]{:S(2)}) collective-permute-start(bf16[8,96,640]{2,1,0:T(8,128)(2,1)S(1)} %bitcast.182), channel_id=1, source_target_pairs={{0,16},{8,24},{16,0},{24,8},{1,17},{9,25},{17,1},{25,9},{2,18},{10... | collective-permute-start | bytes 2949128 | tf_op jit(solution)/shard_map/ppermute | solution.py:197
  366.6 7.7 %copy-start.48 = (bf16[1,8,192,640]{3,2,1,0:T(8,128)(2,1)S(1)}, bf16[1,8,192,640]{3,2,1,0:T(8,128)(2,1)}, u32[]{:S(2)}) copy-start(bf16[1,8,192,640]{3,2,1,0:T(8,128)(2,1)} %copy-done.47) | copy-start | bytes 5898244
  373.0 31.4 %collective-permute-start.24 = (bf16[512,512]{1,0:T(8,128)(2,1)S(1)}, bf16[512,512]{1,0:T(8,128)(2,1)S(1)}, u32[]{:S(2)}, u32[]{:S(2)}) collective-permute-start(bf16[512,512]{1,0:T(8,128)(2,1)S(1)} %get-tuple-element.210), channel_id=1, source_target_pairs={{8,0},{9,1},{10,2},{11,3},{12,4},{13,5},{14,6},{15,7},{24,16},{25,... | collective-permute-start | bytes 1572872 | tf_op jit(solution)/shard_map/ppermute | solution.py:174
  389.5 8.5 %copy-start.80 = (bf16[1,8,96,640]{3,2,1,0:T(8,128)(2,1)S(1)}, bf16[1,8,96,640]{3,2,1,0:T(8,128)(2,1)}, u32[]{:S(2)}) copy-start(bf16[1,8,96,640]{3,2,1,0:T(8,128)(2,1)} %copy-done.79) | copy-start | bytes 2949124
  396.7 49.5 %collective-permute-start.25 = (bf16[8,192,384]{2,1,0:T(8,128)(2,1)}, bf16[8,192,384]{2,1,0:T(8,128)(2,1)}, u32[]{:S(2)}, u32[]{:S(2)}) collective-permute-start(bf16[8,192,384]{2,1,0:T(8,128)(2,1)} %bitcast.57), channel_id=1, source_target_pairs={{0,16},{8,24},{16,0},{24,8},{1,17},{9,25},{17,1},{25,9},{2,18},{10... | collective-permute-start | bytes 3538952 | tf_op jit(solution)/shard_map/ppermute | solution.py:197
  420.8 31.8 %collective-permute-start.27 = (bf16[2,8,96,640]{3,2,1,0:T(8,128)(2,1)}, bf16[2,8,96,640]{3,2,1,0:T(8,128)(2,1)}, u32[]{:S(2)}, u32[]{:S(2)}) collective-permute-start(bf16[2,8,96,640]{3,2,1,0:T(8,128)(2,1)} %weight_gradient.14), channel_id=1, source_target_pairs={{0,8},{8,0},{16,24},{24,16},{1,9},{9,1},{17,25},{25,17},{2,10},{10... | collective-permute-start | bytes 5898248 | tf_op jit(solution)/shard_map/ppermute | solution.py:197
  420.8 25.3 %collective-permute-start.26 = (bf16[8,192,256]{2,1,0:T(8,128)(2,1)}, bf16[8,192,256]{2,1,0:T(8,128)(2,1)}, u32[]{:S(2)}, u32[]{:S(2)}) collective-permute-start(bf16[8,192,256]{2,1,0:T(8,128)(2,1)} %bitcast.58), channel_id=1, source_target_pairs={{0,1},{1,0},{2,3},{3,2},{4,5},{5,4},{6,7},{7,6},{8,9},{9,8},{10,11... | collective-permute-start | bytes 2359304 | tf_op jit(solution)/shard_map/ppermute | solution.py:197
  449.7 19.3 %collective-permute-start.28 = (bf16[4,192,384]{2,1,0:T(8,128)(2,1)S(1)}, bf16[4,192,384]{2,1,0:T(8,128)(2,1)S(1)}, u32[]{:S(2)}, u32[]{:S(2)}) collective-permute-start(bf16[4,192,384]{2,1,0:T(8,128)(2,1)S(1)} %slice.143), channel_id=1, source_target_pairs={{0,1},{1,0},{2,3},{3,2},{4,5},{5,4},{6,7},{7,6},{8,9},{9,8},{10,11... | collective-permute-start | bytes 1769480 | tf_op jit(solution)/shard_map/ppermute | solution.py:197
  451.5 10.5 %collective-permute-start.29 = (bf16[4,192,256]{2,1,0:T(8,128)(2,1)S(1)}, bf16[4,192,256]{2,1,0:T(8,128)(2,1)S(1)}, u32[]{:S(2)}, u32[]{:S(2)}) collective-permute-start(bf16[4,192,256]{2,1,0:T(8,128)(2,1)S(1)} %slice.144), channel_id=1, source_target_pairs={{0,16},{8,24},{16,0},{24,8},{1,17},{9,25},{17,1},{25,9},{2,18},{10... | collective-permute-start | bytes 1179656 | tf_op jit(solution)/shard_map/ppermute | solution.py:197
  470.6 7.3 %collective-permute-start.30 = (bf16[128,640]{1,0:T(8,128)(2,1)S(1)}, bf16[128,640]{1,0:T(8,128)(2,1)S(1)}, u32[]{:S(2)}, u32[]{:S(2)}) collective-permute-start(bf16[128,640]{1,0:T(8,128)(2,1)S(1)} %get-tuple-element.275), channel_id=1, source_target_pairs={{0,0},{1,1},{2,2},{3,3},{8,4},{9,5},{10,6},{11,7},{4,8},{5,9},{6,1... | collective-permute-start | bytes 491528 | tf_op jit(solution)/shard_map/ppermute | solution.py:157
  471.2 48.6 %collective-permute-start.34 = (bf16[2,192,384]{2,1,0:T(8,128)(2,1)S(1)}, bf16[2,192,384]{2,1,0:T(8,128)(2,1)S(1)}, u32[]{:S(2)}, u32[]{:S(2)}) collective-permute-start(bf16[2,192,384]{2,1,0:T(8,128)(2,1)S(1)} %slice.146), channel_id=1, source_target_pairs={{0,4},{1,5},{2,6},{3,7},{4,0},{5,1},{6,2},{7,3},{8,12},{9,13},{10,... | collective-permute-start | bytes 884744 | tf_op jit(solution)/shard_map/ppermute | solution.py:197
  475.3 44.5 %collective-permute-start.35 = (bf16[2,192,256]{2,1,0:T(8,128)(2,1)S(1)}, bf16[2,192,256]{2,1,0:T(8,128)(2,1)S(1)}, u32[]{:S(2)}, u32[]{:S(2)}) collective-permute-start(bf16[2,192,256]{2,1,0:T(8,128)(2,1)S(1)} %slice.148), channel_id=1, source_target_pairs={{0,4},{1,5},{2,6},{3,7},{4,0},{5,1},{6,2},{7,3},{8,12},{9,13},{10,... | collective-permute-start | bytes 589832 | tf_op jit(solution)/shard_map/ppermute | solution.py:197
  475.4 44.0 %collective-permute-start.38 = (bf16[8,96,640]{2,1,0:T(8,128)(2,1)S(1)}, bf16[8,96,640]{2,1,0:T(8,128)(2,1)S(1)}, u32[]{:S(2)}, u32[]{:S(2)}) collective-permute-start(bf16[8,96,640]{2,1,0:T(8,128)(2,1)S(1)} %bitcast.181), channel_id=1, source_target_pairs={{0,16},{8,24},{16,0},{24,8},{1,17},{9,25},{17,1},{25,9},{2,18},{10... | collective-permute-start | bytes 2949128 | tf_op jit(solution)/shard_map/ppermute | solution.py:197
  476.4 18.5 %collective-permute-start.31 = (bf16[128,640]{1,0:T(8,128)(2,1)S(1)}, bf16[128,640]{1,0:T(8,128)(2,1)S(1)}, u32[]{:S(2)}, u32[]{:S(2)}) collective-permute-start(bf16[128,640]{1,0:T(8,128)(2,1)S(1)} %get-tuple-element.274), channel_id=1, source_target_pairs={{1,0},{2,1},{3,2},{0,3},{9,4},{10,5},{11,6},{8,7},{5,8},{6,9},{7,1... | collective-permute-start | bytes 491528 | tf_op jit(solution)/shard_map/ppermute | solution.py:157
  477.9 23.5 %collective-permute-start.32 = (bf16[128,640]{1,0:T(8,128)(2,1)S(1)}, bf16[128,640]{1,0:T(8,128)(2,1)S(1)}, u32[]{:S(2)}, u32[]{:S(2)}) collective-permute-start(bf16[128,640]{1,0:T(8,128)(2,1)S(1)} %get-tuple-element.273), channel_id=1, source_target_pairs={{2,0},{3,1},{0,2},{1,3},{10,4},{11,5},{8,6},{9,7},{6,8},{7,9},{4,1... | collective-permute-start | bytes 491528 | tf_op jit(solution)/shard_map/ppermute | solution.py:157
  495.0 24.3 %collective-permute-start.33 = (bf16[128,640]{1,0:T(8,128)(2,1)S(1)}, bf16[128,640]{1,0:T(8,128)(2,1)S(1)}, u32[]{:S(2)}, u32[]{:S(2)}) collective-permute-start(bf16[128,640]{1,0:T(8,128)(2,1)S(1)} %get-tuple-element.272), channel_id=1, source_target_pairs={{3,0},{0,1},{1,2},{2,3},{11,4},{8,5},{9,6},{10,7},{7,8},{4,9},{5,1... | collective-permute-start | bytes 491528 | tf_op jit(solution)/shard_map/ppermute | solution.py:157
  519.7 11.9 %collective-permute-start.39 = (bf16[4,96,640]{2,1,0:T(8,128)(2,1)S(1)}, bf16[4,96,640]{2,1,0:T(8,128)(2,1)S(1)}, u32[]{:S(2)}, u32[]{:S(2)}) collective-permute-start(bf16[4,96,640]{2,1,0:T(8,128)(2,1)S(1)} %slice.156), channel_id=1, source_target_pairs={{0,1},{1,0},{2,3},{3,2},{4,5},{5,4},{6,7},{7,6},{8,9},{9,8},{10,11... | collective-permute-start | bytes 1474568 | tf_op jit(solution)/shard_map/ppermute | solution.py:197
  520.0 18.1 %collective-permute-start.36 = (bf16[1,192,384]{2,1,0:T(8,128)(2,1)S(1)}, bf16[1,192,384]{2,1,0:T(8,128)(2,1)S(1)}, u32[]{:S(2)}, u32[]{:S(2)}) collective-permute-start(bf16[1,192,384]{2,1,0:T(8,128)(2,1)S(1)} %slice.151), channel_id=1, source_target_pairs={{0,2},{1,3},{2,0},{3,1},{4,6},{5,7},{6,4},{7,5},{8,10},{9,11},{10,... | collective-permute-start | bytes 442376 | tf_op jit(solution)/shard_map/ppermute | solution.py:197
  520.2 17.9 %collective-permute-start.37 = (bf16[1,192,256]{2,1,0:T(8,128)(2,1)S(1)}, bf16[1,192,256]{2,1,0:T(8,128)(2,1)S(1)}, u32[]{:S(2)}, u32[]{:S(2)}) collective-permute-start(bf16[1,192,256]{2,1,0:T(8,128)(2,1)S(1)} %slice.153), channel_id=1, source_target_pairs={{0,2},{1,3},{2,0},{3,1},{4,6},{5,7},{6,4},{7,5},{8,10},{9,11},{10,... | collective-permute-start | bytes 294920 | tf_op jit(solution)/shard_map/ppermute | solution.py:197
  531.8 15.4 %collective-permute-start.40 = (bf16[2,96,640]{2,1,0:T(8,128)(2,1)S(1)}, bf16[2,96,640]{2,1,0:T(8,128)(2,1)S(1)}, u32[]{:S(2)}, u32[]{:S(2)}) collective-permute-start(bf16[2,96,640]{2,1,0:T(8,128)(2,1)S(1)} %slice.158), channel_id=1, source_target_pairs={{0,4},{1,5},{2,6},{3,7},{4,0},{5,1},{6,2},{7,3},{8,12},{9,13},{10,... | collective-permute-start | bytes 737288 | tf_op jit(solution)/shard_map/ppermute | solution.py:197
  547.2 5.4 collective-permute-start.41
  (93 other events, 226.9 us)
Sparse Core Ops, SparseCore 0:
  11.5 97.3 all-gather.4
  112.4 93.9 all-gather.6
  423.8 87.5 reduce-scatter.1

commit v6 on v5

--- a/solution.py
+++ b/solution.py
@@ -18,6 +18,8 @@
 SCORE_SCALE = 0.0625
 MASKED_SCORE = -1e30
 BF16 = jnp.bfloat16
+VMEM_LIMIT = 44 * 2**20
+VMEM_LIMIT_PRODUCT = 44 * 2**20
 F32 = jnp.float32
 ALL = ("dp", "seq")
 TILE = 16
@@ -111,8 +113,8 @@
         scratch_shapes=[weight_scratch(w) for w in weights if not handed]
         + ([pltpu.SemaphoreType.DMA((len(weights),))] if weights else [])
         + list(scratch),
-        compiler_params=pltpu.CompilerParams(vmem_limit_bytes=limit * 2**20),
-        cost_estimate=pl.CostEstimate(flops=flops, bytes_accessed=moved, transcendentals=0),
+        compiler_params=pltpu.CompilerParams(vmem_limit_bytes=VMEM_LIMIT),
+        cost_estimate=pl.CostEstimate(flops=flops // 64, bytes_accessed=moved // 64, transcendentals=0),
         name=name,
     )(*arrays, *[w[0] for w in weights])
 
@@ -299,10 +301,10 @@
             num_scalar_prefetch=1, grid=(2,), in_specs=specs, out_specs=out_specs
         ),
         out_shape=shapes,
-        compiler_params=pltpu.CompilerParams(vmem_limit_bytes=26 * 2**20),
+        compiler_params=pltpu.CompilerParams(vmem_limit_bytes=VMEM_LIMIT_PRODUCT),
         cost_estimate=pl.CostEstimate(
-            flops=4 * tokens * sum(widths) * D,
-            bytes_accessed=4 * (tokens + 2 * D) * sum(widths),
+            flops=tokens * sum(widths) * D // 16,
+            bytes_accessed=(tokens + 2 * D) * sum(widths) // 16,
             transcendentals=0,
         ),
         name="weight_gradient",
@@ -697,40 +699,48 @@
 
 PLAN = {
     0: [(1, "attn")],
-    1: [(1, "ffn")],
-    2: [(0, "ffn"), (1, "attn")],
+    1: [(1, "ffn"), (1, "attn")],
+    2: [(0, "ffn")],
     3: [],
 }
 
 
-def pack_weights(w_attn_in, w_attn_out, w_ffn_in, w_ffn_out, gains):
-    gain_rows = jnp.pad(gains[None, :], ((0, TILE - 1), (0, D - gains.shape[0])))
-    return jnp.concatenate([w_ffn_in.T, w_ffn_out, w_attn_in.T, w_attn_out, gain_rows], axis=0)
-
-
-def gather_weights(packed, sizes, gain_count):
-    whole = lax.all_gather(packed, ALL, axis=0, tiled=False)
-    found, at = [], 0
-    for size in sizes:
-        if size % TILE:
-            found.append((whole[:, at : at + size].reshape(1, -1, D), 0, size * whole.shape[0]))
-        else:
-            found.append((whole, at, size))
-        at += size
-    ffn_in, ffn_out, attn_in, attn_out = found
-    gain_full = whole[:, at, :gain_count].astype(F32).reshape(1, -1)
-    return (attn_in, attn_out, ffn_in, ffn_out), gain_full
+def gather_weights(shards, gains, behind):
+    layers = gains.shape[0]
+    gain_rows = jnp.pad(gains, ((0, TILE - layers), (0, D - gains.shape[1])))
+    first = [(kind, l) for l in range(layers) for kind in range(len(shards)) if l == 0 or kind >= 2]
+    later = [(kind, l) for l in range(1, layers) for kind in range(2)]
+    found, rest = {}, None
+    for names in (first, later):
+        parts = [shards[kind][l] for kind, l in names]
+        if names is first:
+            parts.append(gain_rows)
+        packed = jnp.concatenate(parts, axis=0)
+        if names is later:
+            behind, packed = lax.optimization_barrier((behind, packed))
+        whole = lax.all_gather(packed, ALL, axis=0, tiled=False)
+        at = 0
+        for kind, l in names:
+            size = shards[kind].shape[1]
+            if size % TILE:
+                found[kind, l] = (whole[:, at : at + size].reshape(1, -1, D), 0, size * whole.shape[0])
+            else:
+                found[kind, l] = (whole, at, size)
+            at += size
+        if names is first:
+            gain_full = whole[:, at : at + layers, : gains.shape[1]].astype(F32)
+    out = []
+    for l in range(layers):
+        ffn_in, ffn_out, attn_in, attn_out = [found[kind, l] for kind in range(4)]
+        out.append(((attn_in, attn_out, ffn_in, ffn_out), gain_full[:, l].reshape(1, -1)))
+    return out, behind
 
 
 def body(hidden_in, positions, out_grad, w_attn_in, w_attn_out, w_ffn_in, w_ffn_out, gains):
     count = hidden_in.shape[0]
     layer_count = w_attn_in.shape[0]
     sizes = [w_ffn_in.shape[2], w_ffn_out.shape[1], w_attn_in.shape[2], w_attn_out.shape[1]]
-    packed = [
-        pack_weights(w_attn_in[l], w_attn_out[l], w_ffn_in[l], w_ffn_out[l], gains[l])
-        for l in range(layer_count)
-    ]
-    weights = [gather_weights(packed[0], sizes, gains.shape[1])]
+    shards = [w_ffn_in.transpose(0, 2, 1), w_ffn_out, w_attn_in.transpose(0, 2, 1), w_attn_out]
     places = to_long(positions)
     stream = to_long(hidden_in).astype(F32)
     tables = angle_tables(places)
@@ -739,8 +749,7 @@
     reach = jnp.minimum(places, WINDOW - 1).reshape(blocks, QUERY_BLOCK)
     reach = jnp.tile(reach, (1, HEADS))
     records = []
-    stream, later = lax.optimization_barrier((stream, packed[1:]))
-    weights += [gather_weights(entry, sizes, gains.shape[1]) for entry in later]
+    weights, stream = gather_weights(shards, gains, stream)
     for layer_index in range(layer_count):
         record, stream = forward_layer(stream, *weights[layer_index], tables, reach, count)
         records.append(record)
@@ -762,7 +771,7 @@
             value = advance(value, active)
             if where == 1 and layer_index + 1 == layer_count:
                 value, outputs["hidden"] = lax.optimization_barrier((value, outputs["hidden"]))
-            if where == 2 and layer_index + 1 < layer_count:
+            if where == 1 and layer_index + 1 < layer_count:
                 above = chains[layer_index + 1]
                 packed = jnp.concatenate([above["ffn"].finish(), above["attn"].finish()], axis=1)
                 value, packed = lax.optimization_barrier((value, packed.astype(BF16)))
@@ -774,15 +783,16 @@
             chains[layer_index], layer_index > 0,
         )
     attn, ffn = [chains[0]["attn"]], chains[0]["ffn"].parts or [chains[0]["ffn"]]
-    grad_stream = advance(grad_stream, ffn)
-    grad_stream = advance(grad_stream, attn)
-    grad_stream = advance(grad_stream, ffn)
-    short = to_short(grad_stream.astype(BF16), count)
-    mark = advance(grad_stream[:8], attn)
+    mark = grad_stream[:8]
     mark = advance(mark, ffn)
     mark = advance(mark, attn)
     mark = advance(mark, ffn)
-    mark, short = lax.optimization_barrier((mark, short))
+    mark = advance(mark, attn)
+    mark = advance(mark, ffn)
+    mark, grad_stream = lax.optimization_barrier((mark, grad_stream))
+    short = to_short(grad_stream.astype(BF16), count)
+    mark = advance(mark, attn)
+    mark = advance(mark, ffn)
     mark = advance(mark, attn)
     sums[0] = jnp.concatenate([chains[0]["ffn"].finish(), chains[0]["attn"].finish()], axis=1)[0]
     packed = jnp.stack([entry.astype(F32) for entry in sums])

time: 570 us -> 510 us (0.89)
  waiting for transfers between devices: 270 us -> 230 us
  local copies, waits for them, and re-layouts: 91 us -> 58.2 us
  Pallas kernels: 109 us -> 130 us
  starting transfers between devices: 61.6 us -> 54.3 us
    unnamed x257 -> x220, local copies, waits for them, and re-layouts: 86.7 us -> 52.8 us
    all_gather x2, waiting for transfers between devices: 132 us -> 111 us  [gather_weights(): whole = lax.all_gather(packed, ALL, axis=0, tiled=False)]
    pallas_call x14, Pallas kernels: 72 us -> 89.5 us  [call(): pl.pallas_call(kernel, out_shape=tuple(outs), in_specs=vmem(len(arrays))...]
    ppermute x8, waiting for transfers between devices: 40.6 us -> 29.2 us  [to_short(): received.append(lax.ppermute(piece, ALL, route))]
    ppermute x18, waiting for transfers between devices: 84.2 us -> 73.1 us  [swap(): lax.ppermute(array, axis, [(i, i ^ bit) for i in range(lax.axis_size(axis...]
  transfers between devices with their start and end apart: 45 -> 45, of which waited for: 20 -> 19; matrix products, arithmetic and copies ran while one was open for 3% -> 3% of each run, Pallas kernels for 15% -> 22%
where the time goes in v6:
time: 510 us; the launch traced here: 505 us
  waiting for transfers between devices  230 us (45%)
  Pallas kernels  130 us (25%)
  local copies, waits for them, and re-layouts  58.2 us (11%)
  starting transfers between devices  54.3 us (11%)
  other arithmetic  16.6 us (3%)
  between operations  15.4 us (3%)
    all_gather x2, waiting for transfers between devices, gather_weights(): whole = lax.all_gather(packed, ALL, axis=0, tiled=False)  111 us
    pallas_call x14, Pallas kernels, call(): pl.pallas_call(kernel, out_shape=tuple(outs), in_specs=vmem(len(arrays))...  89.5 us
    ppermute x18, waiting for transfers between devices, swap(): lax.ppermute(array, axis, [(i, i ^ bit) for i in range(lax.axis_size(axis...  73.1 us
    unnamed x220, local copies, waits for them, and re-layouts  52.8 us
    pallas_call x8, Pallas kernels, product(): pl.pallas_call(partial(product_kernel, len(pairs), extra is not None, got...  40.5 us
    ppermute x8, waiting for transfers between devices, to_short(): received.append(lax.ppermute(piece, ALL, route))  29.2 us
    ppermute x18, starting transfers between devices, swap(): lax.ppermute(array, axis, [(i, i ^ bit) for i in range(lax.axis_size(axis...  23.3 us
    ppermute x12, waiting for transfers between devices, to_long(): received.append(lax.ppermute(piece, ALL, chunk_route(count, k)))  17.2 us
  transfers between devices with their start and end apart: 45, of which 19 were waited for; matrix products, arithmetic and copies ran while one was open for 3% of the time, Pallas kernels for 22%

profile of v6, /device:TPU:0, one launch (start us, length us, event | category | flops | bytes accessed | tf_op | source)
XLA Modules:
  0.0 504.8 jit_solution(12541348768811097467)
XLA Ops:
  10.6 4.0 collective-permute-start
  18.2 3.7 collective-permute-done.1
  23.2 1.6 collective-permute-start.4
  24.8 2.0 collective-permute-start.5
  26.7 1.9 collective-permute-start.6
  29.4 1.8 collective-permute-done.6
  32.8 91.9 %all-gather.5.cloned.1.call-done = bf16[11776,640]{1,0:T(8,128)(2,1)} async-done(((bf16[368,640]{1,0:T(8,128)(2,1)}), bf16[11776,640]{1,0:T(8,128)(2,1)}) %all-gather.5.cloned.1.call-update) | async-done | bytes 15073296 | tf_op jit(solution)/shard_map/all_gather | solution.py:721
  126.3 2.3 key_value.2
  128.6 1.3 copy-done.43
  130.8 2.4 collective-permute-start.8
  133.8 1.6 copy-done.44
  135.5 1.3 query.2
  141.1 14.7 %block_forward.2 = (bf16[512,1024]{1,0:T(8,128)(2,1)S(1)}, f32[2,1024]{1,0:T(2,128)S(1)}, f32[512,640]{1,0:T(8,128)S(1)}, f32[512,640]{1,0:T(8,128)S(1)}, bf16[5...) custom-call(bf16[512,1024]{1,0:T(8,128)(2,1)S(1)} %get-tuple-element, ...), custom_call_target="tpu_custom_call" | custom-call | flops 98566144 | bytes 260544 | tf_op jit(solution)/shard_map/block_forward/pallas_call | solution.py:108
  161.7 1.5 collective-permute-start.9
  163.4 3.3 key_value.3
  166.7 3.7 collective-permute-start.13
  172.3 1.4 query.3
  174.7 1.4 copy-done.37
  176.1 1.5 collective-permute-done.10
  177.7 8.8 %collective-permute-done.11 = bf16[128,640]{1,0:T(8,128)(2,1)S(1)} collective-permute-done((bf16[128,640]{1,0:T(8,128)(2,1)S(1)}, bf16[128,640]{1,0:T(8,128)(2,1)S(1)}, u32[]{:S(2)}, u32[]{:S(2)}) %collective-permute-start.11) | collective-permute-done | bytes 163872 | tf_op jit(solution)/shard_map/ppermute | solution.py:146
  187.6 18.9 %all-gather.7.cloned.1.call-done = bf16[6144,640]{1,0:T(8,128)(2,1)} async-done(((bf16[192,640]{1,0:T(8,128)(2,1)}), bf16[6144,640]{1,0:T(8,128)(2,1)}) %all-gather.7.cloned.1.call-update) | async-done | bytes 7864336 | tf_op jit(solution)/shard_map/all_gather | solution.py:721
  207.7 15.6 %block_forward.3 = (bf16[512,1024]{1,0:T(8,128)(2,1)S(1)}, f32[2,1024]{1,0:T(2,128)S(1)}, f32[512,640]{1,0:T(8,128)S(1)}, f32[512,640]{1,0:T(8,128)S(1)}, bf16[5...) custom-call(bf16[512,1024]{1,0:T(8,128)(2,1)S(1)} %copy-done.12, ...), custom_call_target="tpu_custom_call" | custom-call | flops 98566144 | bytes 260544 | tf_op jit(solution)/shard_map/block_forward/pallas_call | solution.py:108
  225.3 2.6 collective-permute-start.16
  228.5 14.9 %block_backward.2 = (bf16[512,640]{1,0:T(8,128)(2,1)S(1)}, bf16[512,4096]{1,0:T(8,128)(2,1)}, bf16[512,640]{1,0:T(8,128)(2,1)S(1)}, bf16[512,1024]{1,0:T(8,128)(...) custom-call(f32[512,640]{1,0:T(8,128)S(1)} %bitcast_convert_fusion.grad_ref, ...), custom_call_target="tpu_custom_call" | custom-call | flops 73400320 | bytes 270848 | tf_op jit(solution)/shard_map/block_backward/pallas_call | solution.py:108
  244.5 4.9 weight_gradient.8
  250.6 4.2 collective-permute-start.18
  254.8 6.4 %attention_backward.2 = (f32[512,1024]{1,0:T(8,128)S(1)}, bf16[512,512]{1,0:T(8,128)(2,1)S(1)}, f32[512,512]{1,0:T(8,128)S(1)}) custom-call(bf16[512,1024]{1,0:T(8,128)(2,1)S(1)} %copy-done.13, bf16[512,512]{1,0:T(8,128)(2,1)} %collective-permute-done.13.before_ref, bf16[512,512]{1,0:T(8,128)(2,1)} %get-tuple-element.133.own_ref, s32[2,1024]{1,0:T(2,128)S(1)} %bitcast.159, ...), custom_call_target="tpu_custom_call" | custom-call | flops 62914560 | bytes 106752 | tf_op jit(solution)/shard_map/attention_backward/pallas_call | solution.py:108
  261.2 1.4 copy-done.39
  263.9 9.0 %weight_gradient.9 = (bf16[1,8,192,640]{3,2,1,0:T(8,128)(2,1)S(1)}, bf16[1,8,192,640]{3,2,1,0:T(8,128)(2,1)}) custom-call(s32[5]{0:T(128)S(1)} %stack.154.numbers_ref, bf16[512,4096]{1,0:T(8,128)(2,1)} %get-tuple-element.145.refs_0_, bf16[512,2048]{1,0:T(8,128)(2,1)S(1)} %copy-done.2, bf16[512,640]{1,0:T(8,128)(2,1)S(1)} %get-tuple-element.147.refs_2_, ...), custom_call_target="tpu_custom_call" | custom-call | flops 31457280 | bytes 172032 | tf_op jit(solution)/shard_map/weight_gradient/pallas_call | solution.py:298
  275.0 3.5 input_backward.2
  281.0 1.4 copy-done.4
  285.8 2.2 weight_gradient.10
  290.2 2.6 collective-permute-done.20.refs_5_
  292.8 4.3 weight_gradient.11
  298.3 1.3 copy-done.46
  299.6 1.3 copy-done.48
  302.3 1.3 copy-done.52
  303.6 14.9 %block_backward.3 = (bf16[512,640]{1,0:T(8,128)(2,1)S(1)}, bf16[512,4096]{1,0:T(8,128)(2,1)}, bf16[512,640]{1,0:T(8,128)(2,1)S(1)}, bf16[512,1024]{1,0:T(8,128)(...) custom-call(f32[512,640]{1,0:T(8,128)S(1)} %copy-done.52, f32[512,640]{1,0:T(8,128)S(1)} %copy-done.50, ...), custom_call_target="tpu_custom_call" | custom-call | flops 73400320 | bytes 270848 | tf_op jit(solution)/shard_map/block_backward/pallas_call | solution.py:108
  320.6 5.7 %weight_gradient.12 = bf16[2,8,192,640]{3,2,1,0:T(8,128)(2,1)S(1)} custom-call(s32[5]{0:T(128)S(1)} %stack.156.numbers_ref, bf16[512,4096]{1,0:T(8,128)(2,1)} %get-tuple-element.188.refs_0_, bf16[512,2048]{1,0:T(8,128)(2,1)S(1)} %copy-done, bf16[512,640]{1,0:T(8,128)(2,1)S(1)} %copy-done.20, bf16[512,640]{1,0:T(8,128)(2,1)S(1)} %get-tuple-element.191.refs_3_), custom_call_target="tpu_custom_call" | custom-call | flops 31457280 | bytes 172032 | tf_op jit(solution)/shard_map/weight_gradient/pallas_call | solution.py:298
  326.3 8.9 %collective-permute-done.21 = bf16[8,192,640]{2,1,0:T(8,128)(2,1)} collective-permute-done((bf16[8,192,640]{2,1,0:T(8,128)(2,1)}, bf16[8,192,640]{2,1,0:T(8,128)(2,1)}, u32[]{:S(2)}, u32[]{:S(2)}) %collective-permute-start.21) | collective-permute-done | bytes 1966112 | tf_op jit(solution)/shard_map/ppermute | solution.py:199
  335.2 20.2 %collective-permute-done.22 = bf16[8,96,640]{2,1,0:T(8,128)(2,1)} collective-permute-done((bf16[8,96,640]{2,1,0:T(8,128)(2,1)}, bf16[8,96,640]{2,1,0:T(8,128)(2,1)}, u32[]{:S(2)}, u32[]{:S(2)}) %collective-permute-start.22) | collective-permute-done | bytes 983072 | tf_op jit(solution)/shard_map/ppermute | solution.py:199
  355.4 2.1 fusion
  357.5 1.4 fusion.3
  358.9 1.8 pad_maximum_fusion
  366.7 5.2 %attention_backward.3 = (f32[512,1024]{1,0:T(8,128)S(1)}, bf16[512,512]{1,0:T(8,128)(2,1)S(1)}, f32[512,512]{1,0:T(8,128)S(1)}) custom-call(bf16[512,1024]{1,0:T(8,128)(2,1)S(1)} %copy-done.10, bf16[512,512]{1,0:T(8,128)(2,1)S(1)} %copy-done.34, bf16[512,512]{1,0:T(8,128)(2,1)S(1)} %copy-done.31, s32[2,1024]{1,0:T(2,128)S(1)} %bitcast.160, ...), custom_call_target="tpu_custom_call" | custom-call | flops 62914560 | bytes 106752 | tf_op jit(solution)/shard_map/attention_backward/pallas_call | solution.py:108
  373.2 8.8 %weight_gradient.13 = (bf16[1,8,192,384]{3,2,1,0:T(8,128)(2,1)S(1)}, bf16[1,8,192,384]{3,2,1,0:T(8,128)(2,1)}, bf16[2,4,192,256]{3,2,1,0:T(8,128)(2,1)S(1)}, bf16[2,4,192,256]{3,2,1,0:T(8,128)(2,1)S(1)}) custom-call(s32[5]{0:T(128)S(1)} %stack.156.numbers_ref, bf16[512,4096]{1,0:T(8,128)(2,1)} %get-tuple-element.188.refs_0_, ...), custom_call_target="tpu_custom_call" | custom-call | flops 31457280 | bytes 172032 | tf_op jit(solution)/shard_map/weight_gradient/pallas_call | solution.py:298
  385.5 3.5 input_backward.3
  393.6 2.2 weight_gradient.14
  397.8 1.5 collective-permute-start.30
  399.3 2.0 collective-permute-start.26
  401.4 25.3 %collective-permute-done.26 = bf16[128,640]{1,0:T(8,128)(2,1)S(1)} collective-permute-done((bf16[128,640]{1,0:T(8,128)(2,1)S(1)}, bf16[128,640]{1,0:T(8,128)(2,1)S(1)}, u32[]{:S(2)}, u32[]{:S(2)}) %collective-permute-start.26) | collective-permute-done | bytes 163872 | tf_op jit(solution)/shard_map/ppermute | solution.py:159
  428.1 1.6 fusion.1
  429.7 4.7 collective-permute-start.31
  434.5 3.8 collective-permute-done.28
  438.3 1.5 collective-permute-start.32
  439.8 3.3 weight_gradient.15
  443.8 6.6 %collective-permute-done.32 = bf16[4,192,256]{2,1,0:T(8,128)(2,1)S(1)} collective-permute-done((bf16[4,192,256]{2,1,0:T(8,128)(2,1)S(1)}, bf16[4,192,256]{2,1,0:T(8,128)(2,1)S(1)}, u32[]{:S(2)}, u32[]{:S(2)}) %collective-permute-start.32) | collective-permute-done | bytes 393248 | tf_op jit(solution)/shard_map/ppermute | solution.py:199
  450.8 2.9 collective-permute-start.34
  453.8 12.8 %collective-permute-done.38 = bf16[8,96,640]{2,1,0:T(8,128)(2,1)S(1)} collective-permute-done((bf16[8,96,640]{2,1,0:T(8,128)(2,1)S(1)}, bf16[8,96,640]{2,1,0:T(8,128)(2,1)S(1)}, u32[]{:S(2)}, u32[]{:S(2)}) %collective-permute-start.38) | collective-permute-done | bytes 983072 | tf_op jit(solution)/shard_map/ppermute | solution.py:199
  467.3 6.4 %collective-permute-done.34 = bf16[2,192,256]{2,1,0:T(8,128)(2,1)S(1)} collective-permute-done((bf16[2,192,256]{2,1,0:T(8,128)(2,1)S(1)}, bf16[2,192,256]{2,1,0:T(8,128)(2,1)S(1)}, u32[]{:S(2)}, u32[]{:S(2)}) %collective-permute-start.34) | collective-permute-done | bytes 196640 | tf_op jit(solution)/shard_map/ppermute | solution.py:199
  474.0 2.0 collective-permute-start.36
  478.4 5.8 %collective-permute-done.36 = bf16[1,192,256]{2,1,0:T(8,128)(2,1)S(1)} collective-permute-done((bf16[1,192,256]{2,1,0:T(8,128)(2,1)S(1)}, bf16[1,192,256]{2,1,0:T(8,128)(2,1)S(1)}, u32[]{:S(2)}, u32[]{:S(2)}) %collective-permute-start.36) | collective-permute-done | bytes 98336 | tf_op jit(solution)/shard_map/ppermute | solution.py:199
  484.3 4.8 collective-permute-done.40
  489.3 4.8 collective-permute-done.41
  (340 shorter events, 76.5 us)
Async XLA Ops:
  7.2 117.5 %all-gather.5.cloned.1.call-start = ((), (), s32[]{:S(2)}) async-start(), calls=%async_computation.2 | async-start | bytes 15544320 | tf_op jit(solution)/shard_map/all_gather | solution.py:721
  10.4 196.1 %all-gather.7.cloned.1.call-start = ((), (), s32[]{:S(2)}) async-start(), calls=%async_computation.3 | async-start | bytes 8110080 | tf_op jit(solution)/shard_map/all_gather | solution.py:721
  10.6 7.6 %collective-permute-start = (bf16[128,640]{1,0:T(8,128)(2,1)S(1)}, bf16[128,640]{1,0:T(8,128)(2,1)S(1)}, u32[]{:S(2)}, u32[]{:S(2)}) collective-permute-start(bf16[128,640]{1,0:T(8,128)(2,1)S(1)} %get-tuple-element.274), channel_id=1, source_target_pairs={{0,3},{1,0},{2,1},{3,2},{4,11},{5,8},{6,9},{7,10},{8,7},{9,4},{10,... | collective-permute-start | bytes 491528 | tf_op jit(solution)/shard_map/ppermute | solution.py:146
  14.6 7.3 %collective-permute-start.1 = (bf16[128,640]{1,0:T(8,128)(2,1)S(1)}, bf16[128,640]{1,0:T(8,128)(2,1)S(1)}, u32[]{:S(2)}, u32[]{:S(2)}) collective-permute-start(bf16[128,640]{1,0:T(8,128)(2,1)S(1)} %get-tuple-element.273), channel_id=1, source_target_pairs={{0,2},{1,3},{2,0},{3,1},{4,10},{5,11},{6,8},{7,9},{8,6},{9,7},{10,... | collective-permute-start | bytes 491528 | tf_op jit(solution)/shard_map/ppermute | solution.py:146
  15.1 7.2 %collective-permute-start.2 = (bf16[128,640]{1,0:T(8,128)(2,1)S(1)}, bf16[128,640]{1,0:T(8,128)(2,1)S(1)}, u32[]{:S(2)}, u32[]{:S(2)}) collective-permute-start(bf16[128,640]{1,0:T(8,128)(2,1)S(1)} %get-tuple-element.275), channel_id=1, source_target_pairs={{0,1},{1,2},{2,3},{3,0},{4,9},{5,10},{6,11},{7,8},{8,5},{9,6},{10,... | collective-permute-start | bytes 491528 | tf_op jit(solution)/shard_map/ppermute | solution.py:146
  15.7 6.6 %collective-permute-start.3 = (bf16[128,640]{1,0:T(8,128)(2,1)S(1)}, bf16[128,640]{1,0:T(8,128)(2,1)S(1)}, u32[]{:S(2)}, u32[]{:S(2)}) collective-permute-start(bf16[128,640]{1,0:T(8,128)(2,1)S(1)} %get-tuple-element.272), channel_id=1, source_target_pairs={{0,0},{1,1},{2,2},{3,3},{4,8},{5,9},{6,10},{7,11},{8,4},{9,5},{10,... | collective-permute-start | bytes 491528 | tf_op jit(solution)/shard_map/ppermute | solution.py:146
  22.7 454.7 %reduce-scatter.2.cloned.1.call-start = ((), (), s32[]{:S(2)}) async-start(), calls=%async_computation.1 | async-start | bytes 3317760 | tf_op jit(solution)/shard_map/reduce_scatter | solution.py:778
  23.2 6.2 %collective-permute-start.4 = (s32[128]{0:T(128)S(1)}, s32[128]{0:T(128)S(1)}, u32[]{:S(2)}, u32[]{:S(2)}) collective-permute-start(s32[128]{0:T(128)S(1)} %get-tuple-element.282), channel_id=1, source_target_pairs={{0,3},{1,0},{2,1},{3,2},{4,11},{5,8},{6,9},{7,10},{8,7},{9,4},{10,... | collective-permute-start | bytes 1544 | tf_op jit(solution)/shard_map/ppermute | solution.py:146
  24.8 4.6 collective-permute-start.5
  26.7 4.4 collective-permute-start.6
  28.7 2.5 collective-permute-start.7
  130.8 7.4 %collective-permute-start.8 = (bf16[512,512]{1,0:T(8,128)(2,1)S(1)}, bf16[512,512]{1,0:T(8,128)(2,1)S(1)}, u32[]{:S(2)}, u32[]{:S(2)}) collective-permute-start(bf16[512,512]{1,0:T(8,128)(2,1)S(1)} %get-tuple-element.126.own_ref), channel_id=1, source_target_pairs={{0,8},{1,9},{2,10},{3,11},{4,12},{5,13},{6,14},{7,15},{16,24},{17,... | collective-permute-start | bytes 1572872 | tf_op jit(solution)/shard_map/ppermute | solution.py:176
  138.1 17.6 %copy-start.9 = (bf16[512,1024]{1,0:T(8,128)(2,1)}, bf16[512,1024]{1,0:T(8,128)(2,1)S(1)}, u32[]{:S(2)}) copy-start(bf16[512,1024]{1,0:T(8,128)(2,1)S(1)} %get-tuple-element.125.q_ref) | copy-start | bytes 3145732
  141.1 19.8 %copy-start.83 = (bf16[4,128,640]{2,1,0:T(8,128)(2,1)S(1)}, bf16[4,128,640]{2,1,0:T(8,128)(2,1)}, u32[]{:S(2)}) copy-start(bf16[4,128,640]{2,1,0:T(8,128)(2,1)} %param.10) | copy-start | bytes 1966084
  161.7 14.4 %collective-permute-start.9 = (bf16[128,640]{1,0:T(8,128)(2,1)}, bf16[128,640]{1,0:T(8,128)(2,1)S(1)}, u32[]{:S(2)}, u32[]{:S(2)}) collective-permute-start(bf16[128,640]{1,0:T(8,128)(2,1)} %get-tuple-element.271), channel_id=1, source_target_pairs={{0,3},{1,0},{2,1},{3,2},{4,11},{5,8},{6,9},{7,10},{8,7},{9,4},{10,... | collective-permute-start | bytes 491528 | tf_op jit(solution)/shard_map/ppermute | solution.py:146
  163.3 7.0 %copy-start.86 = (bf16[128,640]{1,0:T(8,128)(2,1)S(1)}, bf16[128,640]{1,0:T(8,128)(2,1)}, u32[]{:S(2)}) copy-start(bf16[128,640]{1,0:T(8,128)(2,1)} %get-tuple-element.270) | copy-start | bytes 491524
  163.4 7.6 %copy-start.85 = (bf16[128,640]{1,0:T(8,128)(2,1)S(1)}, bf16[128,640]{1,0:T(8,128)(2,1)}, u32[]{:S(2)}) copy-start(bf16[128,640]{1,0:T(8,128)(2,1)} %get-tuple-element.269) | copy-start | bytes 491524
  163.4 8.1 %copy-start.84 = (bf16[128,640]{1,0:T(8,128)(2,1)S(1)}, bf16[128,640]{1,0:T(8,128)(2,1)}, u32[]{:S(2)}) copy-start(bf16[128,640]{1,0:T(8,128)(2,1)} %get-tuple-element.268) | copy-start | bytes 491524
  166.7 7.0 %copy-start.7 = (bf16[512,640]{1,0:T(8,128)(2,1)}, bf16[512,640]{1,0:T(8,128)(2,1)S(1)}, u32[]{:S(2)}) copy-start(bf16[512,640]{1,0:T(8,128)(2,1)S(1)} %get-tuple-element.130.normed_ref.refs_2_) | copy-start | bytes 1966084
  166.7 7.0 %copy-start.69 = (f32[512,256]{1,0:T(8,128)}, f32[512,256]{1,0:T(8,128)S(1)}, u32[]{:S(2)}) copy-start(f32[512,256]{1,0:T(8,128)S(1)} %get-tuple-element.160.kraw_ref) | copy-start | bytes 1572868
  166.7 39.8 %collective-permute-start.13 = (bf16[512,512]{1,0:T(8,128)(2,1)}, bf16[512,512]{1,0:T(8,128)(2,1)}, u32[]{:S(2)}, u32[]{:S(2)}) collective-permute-start(bf16[512,512]{1,0:T(8,128)(2,1)} %get-tuple-element.133.own_ref), channel_id=1, source_target_pairs={{0,8},{1,9},{2,10},{3,11},{4,12},{5,13},{6,14},{7,15},{16,24},{17,... | collective-permute-start | bytes 1572872 | tf_op jit(solution)/shard_map/ppermute | solution.py:176
  170.4 7.3 %collective-permute-start.10 = (bf16[128,640]{1,0:T(8,128)(2,1)S(1)}, bf16[128,640]{1,0:T(8,128)(2,1)S(1)}, u32[]{:S(2)}, u32[]{:S(2)}) collective-permute-start(bf16[128,640]{1,0:T(8,128)(2,1)S(1)} %copy-done.86), channel_id=1, source_target_pairs={{0,2},{1,3},{2,0},{3,1},{4,10},{5,11},{6,8},{7,9},{8,6},{9,7},{10,... | collective-permute-start | bytes 491528 | tf_op jit(solution)/shard_map/ppermute | solution.py:146
  171.0 15.5 %collective-permute-start.11 = (bf16[128,640]{1,0:T(8,128)(2,1)S(1)}, bf16[128,640]{1,0:T(8,128)(2,1)S(1)}, u32[]{:S(2)}, u32[]{:S(2)}) collective-permute-start(bf16[128,640]{1,0:T(8,128)(2,1)S(1)} %copy-done.85), channel_id=1, source_target_pairs={{0,1},{1,2},{2,3},{3,0},{4,9},{5,10},{6,11},{7,8},{8,5},{9,6},{10,... | collective-permute-start | bytes 491528 | tf_op jit(solution)/shard_map/ppermute | solution.py:146
  171.5 15.1 %collective-permute-start.12 = (bf16[128,640]{1,0:T(8,128)(2,1)S(1)}, bf16[128,640]{1,0:T(8,128)(2,1)S(1)}, u32[]{:S(2)}, u32[]{:S(2)}) collective-permute-start(bf16[128,640]{1,0:T(8,128)(2,1)S(1)} %copy-done.84), channel_id=1, source_target_pairs={{0,0},{1,1},{2,2},{3,3},{4,8},{5,9},{6,10},{7,11},{8,4},{9,5},{10,... | collective-permute-start | bytes 491528 | tf_op jit(solution)/shard_map/ppermute | solution.py:146
  186.6 19.9 %copy-start.72 = (s32[1,2,4,256]{3,1,2,0:T(2,128)S(1)}, s32[1,2,4,256]{3,1,2,0:T(2,128)}, u32[]{:S(2)}) copy-start(s32[1,2,4,256]{3,1,2,0:T(2,128)} %copy-done.71) | copy-start | bytes 24580
  224.3 25.1 %collective-permute-start.14 = (bf16[128,640]{1,0:T(8,128)(2,1)S(1)}, bf16[128,640]{1,0:T(8,128)(2,1)S(1)}, u32[]{:S(2)}, u32[]{:S(2)}) collective-permute-start(bf16[128,640]{1,0:T(8,128)(2,1)S(1)} %get-tuple-element.267), channel_id=1, source_target_pairs={{0,0},{1,1},{2,2},{3,3},{8,4},{9,5},{10,6},{11,7},{4,8},{5,9},{6,1... | collective-permute-start | bytes 491528 | tf_op jit(solution)/shard_map/ppermute | solution.py:159
  225.2 24.3 %collective-permute-start.15 = (bf16[128,640]{1,0:T(8,128)(2,1)S(1)}, bf16[128,640]{1,0:T(8,128)(2,1)S(1)}, u32[]{:S(2)}, u32[]{:S(2)}) collective-permute-start(bf16[128,640]{1,0:T(8,128)(2,1)S(1)} %get-tuple-element.266), channel_id=1, source_target_pairs={{1,0},{2,1},{3,2},{0,3},{9,4},{10,5},{11,6},{8,7},{5,8},{6,9},{7,1... | collective-permute-start | bytes 491528 | tf_op jit(solution)/shard_map/ppermute | solution.py:159
  225.3 24.2 %collective-permute-start.16 = (bf16[128,640]{1,0:T(8,128)(2,1)S(1)}, bf16[128,640]{1,0:T(8,128)(2,1)S(1)}, u32[]{:S(2)}, u32[]{:S(2)}) collective-permute-start(bf16[128,640]{1,0:T(8,128)(2,1)S(1)} %get-tuple-element.265), channel_id=1, source_target_pairs={{2,0},{3,1},{0,2},{1,3},{10,4},{11,5},{8,6},{9,7},{6,8},{7,9},{4,1... | collective-permute-start | bytes 491528 | tf_op jit(solution)/shard_map/ppermute | solution.py:159
  227.9 21.6 %collective-permute-start.17 = (bf16[128,640]{1,0:T(8,128)(2,1)S(1)}, bf16[128,640]{1,0:T(8,128)(2,1)S(1)}, u32[]{:S(2)}, u32[]{:S(2)}) collective-permute-start(bf16[128,640]{1,0:T(8,128)(2,1)S(1)} %get-tuple-element.264), channel_id=1, source_target_pairs={{3,0},{0,1},{1,2},{2,3},{11,4},{8,5},{9,6},{10,7},{7,8},{4,9},{5,1... | collective-permute-start | bytes 491528 | tf_op jit(solution)/shard_map/ppermute | solution.py:159
  228.5 16.0 %copy-start.2 = (bf16[512,2048]{1,0:T(8,128)(2,1)S(1)}, bf16[512,2048]{1,0:T(8,128)(2,1)}, u32[]{:S(2)}) copy-start(bf16[512,2048]{1,0:T(8,128)(2,1)} %get-tuple-element.146.refs_1_) | copy-start | bytes 6291460
  250.6 13.3 %collective-permute-start.18 = (bf16[2,8,192,640]{3,2,1,0:T(8,128)(2,1)S(1)}, bf16[2,8,192,640]{3,2,1,0:T(8,128)(2,1)}, u32[]{:S(2)}, u32[]{:S(2)}) collective-permute-start(bf16[2,8,192,640]{3,2,1,0:T(8,128)(2,1)S(1)} %weight_gradient.8), channel_id=1, source_target_pairs={{0,8},{8,0},{16,24},{24,16},{1,9},{9,1},{17,25},{25,17},{2,10},{10... | collective-permute-start | bytes 11796488 | tf_op jit(solution)/shard_map/ppermute | solution.py:199
  262.5 11.6 %collective-permute-start.19 = (bf16[512,512]{1,0:T(8,128)(2,1)S(1)}, bf16[512,512]{1,0:T(8,128)(2,1)S(1)}, u32[]{:S(2)}, u32[]{:S(2)}) collective-permute-start(bf16[512,512]{1,0:T(8,128)(2,1)S(1)} %get-tuple-element.159), channel_id=1, source_target_pairs={{8,0},{9,1},{10,2},{11,3},{12,4},{13,5},{14,6},{15,7},{24,16},{25,... | collective-permute-start | bytes 1572872 | tf_op jit(solution)/shard_map/ppermute | solution.py:176
  263.8 9.0 %copy-start.38 = (f32[512,1024]{1,0:T(8,128)S(1)}, f32[512,1024]{1,0:T(8,128)}, u32[]{:S(2)}) copy-start(f32[512,1024]{1,0:T(8,128)} %copy-done.37) | copy-start | bytes 6291460
  263.8 9.0 %copy-start.40 = (f32[512,1024]{1,0:T(8,128)S(1)}, f32[512,1024]{1,0:T(8,128)}, u32[]{:S(2)}) copy-start(f32[512,1024]{1,0:T(8,128)} %copy-done.39) | copy-start | bytes 6291460
  285.8 7.1 %copy-start.28 = (bf16[512,640]{1,0:T(8,128)(2,1)S(1)}, bf16[512,640]{1,0:T(8,128)(2,1)}, u32[]{:S(2)}) copy-start(bf16[512,640]{1,0:T(8,128)(2,1)} %copy-done.26) | copy-start | bytes 1966084
  288.0 4.8 collective-permute-start.20
  289.2 46.0 %collective-permute-start.21 = (bf16[8,192,640]{2,1,0:T(8,128)(2,1)}, bf16[8,192,640]{2,1,0:T(8,128)(2,1)}, u32[]{:S(2)}, u32[]{:S(2)}) collective-permute-start(bf16[8,192,640]{2,1,0:T(8,128)(2,1)} %bitcast.52), channel_id=1, source_target_pairs={{0,16},{8,24},{16,0},{24,8},{1,17},{9,25},{17,1},{25,9},{2,18},{10... | collective-permute-start | bytes 5898248 | tf_op jit(solution)/shard_map/ppermute | solution.py:199
  297.2 58.3 %collective-permute-start.22 = (bf16[8,96,640]{2,1,0:T(8,128)(2,1)}, bf16[8,96,640]{2,1,0:T(8,128)(2,1)}, u32[]{:S(2)}, u32[]{:S(2)}) collective-permute-start(bf16[8,96,640]{2,1,0:T(8,128)(2,1)} %bitcast.53), channel_id=1, source_target_pairs={{0,16},{8,24},{16,0},{24,8},{1,17},{9,25},{17,1},{25,9},{2,18},{10... | collective-permute-start | bytes 2949128 | tf_op jit(solution)/shard_map/ppermute | solution.py:199
  303.6 17.0 %copy-start = (bf16[512,2048]{1,0:T(8,128)(2,1)S(1)}, bf16[512,2048]{1,0:T(8,128)(2,1)}, u32[]{:S(2)}) copy-start(bf16[512,2048]{1,0:T(8,128)(2,1)} %get-tuple-element.189.refs_1_) | copy-start | bytes 6291460
  303.6 17.0 %copy-start.20 = (bf16[512,640]{1,0:T(8,128)(2,1)S(1)}, bf16[512,640]{1,0:T(8,128)(2,1)}, u32[]{:S(2)}) copy-start(bf16[512,640]{1,0:T(8,128)(2,1)} %copy-done.19) | copy-start | bytes 1966084
  320.6 34.8 %copy-start.42 = (bf16[1,8,192,640]{3,2,1,0:T(8,128)(2,1)S(1)}, bf16[1,8,192,640]{3,2,1,0:T(8,128)(2,1)}, u32[]{:S(2)}) copy-start(bf16[1,8,192,640]{3,2,1,0:T(8,128)(2,1)} %copy-done.41) | copy-start | bytes 5898244
  326.3 31.2 %copy-start.18 = (bf16[2,8,192,640]{3,2,1,0:T(8,128)(2,1)}, bf16[2,8,192,640]{3,2,1,0:T(8,128)(2,1)S(1)}, u32[]{:S(2)}) copy-start(bf16[2,8,192,640]{3,2,1,0:T(8,128)(2,1)S(1)} %weight_gradient.12) | copy-start | bytes 11796484
  360.8 12.4 %collective-permute-start.23 = (bf16[2,8,192,640]{3,2,1,0:T(8,128)(2,1)}, bf16[2,8,192,640]{3,2,1,0:T(8,128)(2,1)}, u32[]{:S(2)}, u32[]{:S(2)}) collective-permute-start(bf16[2,8,192,640]{3,2,1,0:T(8,128)(2,1)} %copy-done.18), channel_id=1, source_target_pairs={{0,8},{8,0},{16,24},{24,16},{1,9},{9,1},{17,25},{25,17},{2,10},{10... | collective-permute-start | bytes 11796488 | tf_op jit(solution)/shard_map/ppermute | solution.py:199
  371.9 13.3 %collective-permute-start.24 = (bf16[512,512]{1,0:T(8,128)(2,1)S(1)}, bf16[512,512]{1,0:T(8,128)(2,1)S(1)}, u32[]{:S(2)}, u32[]{:S(2)}) collective-permute-start(bf16[512,512]{1,0:T(8,128)(2,1)S(1)} %get-tuple-element.203), channel_id=1, source_target_pairs={{8,0},{9,1},{10,2},{11,3},{12,4},{13,5},{14,6},{15,7},{24,16},{25,... | collective-permute-start | bytes 1572872 | tf_op jit(solution)/shard_map/ppermute | solution.py:176
  373.2 10.7 %copy-start.36 = (f32[512,1024]{1,0:T(8,128)S(1)}, f32[512,1024]{1,0:T(8,128)}, u32[]{:S(2)}) copy-start(f32[512,1024]{1,0:T(8,128)} %copy-done.35) | copy-start | bytes 6291460
  383.0 43.8 %collective-permute-start.29 = (bf16[8,192,384]{2,1,0:T(8,128)(2,1)}, bf16[8,192,384]{2,1,0:T(8,128)(2,1)}, u32[]{:S(2)}, u32[]{:S(2)}) collective-permute-start(bf16[8,192,384]{2,1,0:T(8,128)(2,1)} %bitcast.57), channel_id=1, source_target_pairs={{0,16},{8,24},{16,0},{24,8},{1,17},{9,25},{17,1},{25,9},{2,18},{10... | collective-permute-start | bytes 3538952 | tf_op jit(solution)/shard_map/ppermute | solution.py:199
  395.9 43.9 %collective-permute-start.37 = (bf16[2,8,96,640]{3,2,1,0:T(8,128)(2,1)S(1)}, bf16[2,8,96,640]{3,2,1,0:T(8,128)(2,1)S(1)}, u32[]{:S(2)}, u32[]{:S(2)}) collective-permute-start(bf16[2,8,96,640]{3,2,1,0:T(8,128)(2,1)S(1)} %weight_gradient.14), channel_id=1, source_target_pairs={{0,8},{8,0},{16,24},{24,16},{1,9},{9,1},{17,25},{25,17},{2,10},{10... | collective-permute-start | bytes 5898248 | tf_op jit(solution)/shard_map/ppermute | solution.py:199
  396.9 29.9 %copy-start.66 = (bf16[2,4,192,256]{3,2,1,0:T(8,128)(2,1)S(1)}, bf16[2,4,192,256]{3,2,1,0:T(8,128)(2,1)}, u32[]{:S(2)}) copy-start(bf16[2,4,192,256]{3,2,1,0:T(8,128)(2,1)} %copy-done.65) | copy-start | bytes 2359300
  397.0 4.4 collective-permute-start.25
  397.8 29.0 %collective-permute-start.30 = (bf16[8,192,256]{2,1,0:T(8,128)(2,1)S(1)}, bf16[8,192,256]{2,1,0:T(8,128)(2,1)S(1)}, u32[]{:S(2)}, u32[]{:S(2)}) collective-permute-start(bf16[8,192,256]{2,1,0:T(8,128)(2,1)S(1)} %bitcast.162), channel_id=1, source_target_pairs={{0,1},{1,0},{2,3},{3,2},{4,5},{5,4},{6,7},{7,6},{8,9},{9,8},{10,11... | collective-permute-start | bytes 2359304 | tf_op jit(solution)/shard_map/ppermute | solution.py:199
  399.3 27.4 %collective-permute-start.26 = (bf16[128,640]{1,0:T(8,128)(2,1)S(1)}, bf16[128,640]{1,0:T(8,128)(2,1)S(1)}, u32[]{:S(2)}, u32[]{:S(2)}) collective-permute-start(bf16[128,640]{1,0:T(8,128)(2,1)S(1)} %get-tuple-element.262), channel_id=1, source_target_pairs={{1,0},{2,1},{3,2},{0,3},{9,4},{10,5},{11,6},{8,7},{5,8},{6,9},{7,1... | collective-permute-start | bytes 491528 | tf_op jit(solution)/shard_map/ppermute | solution.py:159
  401.4 25.4 %collective-permute-start.27 = (bf16[128,640]{1,0:T(8,128)(2,1)S(1)}, bf16[128,640]{1,0:T(8,128)(2,1)S(1)}, u32[]{:S(2)}, u32[]{:S(2)}) collective-permute-start(bf16[128,640]{1,0:T(8,128)(2,1)S(1)} %get-tuple-element.261), channel_id=1, source_target_pairs={{2,0},{3,1},{0,2},{1,3},{10,4},{11,5},{8,6},{9,7},{6,8},{7,9},{4,1... | collective-permute-start | bytes 491528 | tf_op jit(solution)/shard_map/ppermute | solution.py:159
  426.7 11.6 %collective-permute-start.28 = (bf16[128,640]{1,0:T(8,128)(2,1)S(1)}, bf16[128,640]{1,0:T(8,128)(2,1)S(1)}, u32[]{:S(2)}, u32[]{:S(2)}) collective-permute-start(bf16[128,640]{1,0:T(8,128)(2,1)S(1)} %get-tuple-element.260), channel_id=1, source_target_pairs={{3,0},{0,1},{1,2},{2,3},{11,4},{8,5},{9,6},{10,7},{7,8},{4,9},{5,1... | collective-permute-start | bytes 491528 | tf_op jit(solution)/shard_map/ppermute | solution.py:159
  429.6 10.2 %copy-start.25 = (bf16[512,640]{1,0:T(8,128)(2,1)S(1)}, bf16[512,640]{1,0:T(8,128)(2,1)}, u32[]{:S(2)}) copy-start(bf16[512,640]{1,0:T(8,128)(2,1)} %copy-done.23) | copy-start | bytes 1966084
  429.7 20.7 %collective-permute-start.31 = (bf16[4,192,384]{2,1,0:T(8,128)(2,1)S(1)}, bf16[4,192,384]{2,1,0:T(8,128)(2,1)S(1)}, u32[]{:S(2)}, u32[]{:S(2)}) collective-permute-start(bf16[4,192,384]{2,1,0:T(8,128)(2,1)S(1)} %slice.148), channel_id=1, source_target_pairs={{0,1},{1,0},{2,3},{3,2},{4,5},{5,4},{6,7},{7,6},{8,9},{9,8},{10,11... | collective-permute-start | bytes 1769480 | tf_op jit(solution)/shard_map/ppermute | solution.py:199
  438.3 12.1 %collective-permute-start.32 = (bf16[4,192,256]{2,1,0:T(8,128)(2,1)S(1)}, bf16[4,192,256]{2,1,0:T(8,128)(2,1)S(1)}, u32[]{:S(2)}, u32[]{:S(2)}) collective-permute-start(bf16[4,192,256]{2,1,0:T(8,128)(2,1)S(1)} %slice.149), channel_id=1, source_target_pairs={{0,16},{8,24},{16,0},{24,8},{1,17},{9,25},{17,1},{25,9},{2,18},{10... | collective-permute-start | bytes 1179656 | tf_op jit(solution)/shard_map/ppermute | solution.py:199
  443.1 23.5 %collective-permute-start.38 = (bf16[8,96,640]{2,1,0:T(8,128)(2,1)S(1)}, bf16[8,96,640]{2,1,0:T(8,128)(2,1)S(1)}, u32[]{:S(2)}, u32[]{:S(2)}) collective-permute-start(bf16[8,96,640]{2,1,0:T(8,128)(2,1)S(1)} %bitcast.161), channel_id=1, source_target_pairs={{0,16},{8,24},{16,0},{24,8},{1,17},{9,25},{17,1},{25,9},{2,18},{10... | collective-permute-start | bytes 2949128 | tf_op jit(solution)/shard_map/ppermute | solution.py:199
  450.8 23.0 %collective-permute-start.33 = (bf16[2,192,384]{2,1,0:T(8,128)(2,1)S(1)}, bf16[2,192,384]{2,1,0:T(8,128)(2,1)S(1)}, u32[]{:S(2)}, u32[]{:S(2)}) collective-permute-start(bf16[2,192,384]{2,1,0:T(8,128)(2,1)S(1)} %slice.151), channel_id=1, source_target_pairs={{0,4},{1,5},{2,6},{3,7},{4,0},{5,1},{6,2},{7,3},{8,12},{9,13},{10,... | collective-permute-start | bytes 884744 | tf_op jit(solution)/shard_map/ppermute | solution.py:199
  450.8 22.9 %collective-permute-start.34 = (bf16[2,192,256]{2,1,0:T(8,128)(2,1)S(1)}, bf16[2,192,256]{2,1,0:T(8,128)(2,1)S(1)}, u32[]{:S(2)}, u32[]{:S(2)}) collective-permute-start(bf16[2,192,256]{2,1,0:T(8,128)(2,1)S(1)} %slice.153), channel_id=1, source_target_pairs={{0,4},{1,5},{2,6},{3,7},{4,0},{5,1},{6,2},{7,3},{8,12},{9,13},{10,... | collective-permute-start | bytes 589832 | tf_op jit(solution)/shard_map/ppermute | solution.py:199
  466.9 9.1 %collective-permute-start.39 = (bf16[4,96,640]{2,1,0:T(8,128)(2,1)S(1)}, bf16[4,96,640]{2,1,0:T(8,128)(2,1)S(1)}, u32[]{:S(2)}, u32[]{:S(2)}) collective-permute-start(bf16[4,96,640]{2,1,0:T(8,128)(2,1)S(1)} %slice.160), channel_id=1, source_target_pairs={{0,1},{1,0},{2,3},{3,2},{4,5},{5,4},{6,7},{7,6},{8,9},{9,8},{10,11... | collective-permute-start | bytes 1474568 | tf_op jit(solution)/shard_map/ppermute | solution.py:199
  473.9 10.3 %collective-permute-start.35 = (bf16[1,192,384]{2,1,0:T(8,128)(2,1)S(1)}, bf16[1,192,384]{2,1,0:T(8,128)(2,1)S(1)}, u32[]{:S(2)}, u32[]{:S(2)}) collective-permute-start(bf16[1,192,384]{2,1,0:T(8,128)(2,1)S(1)} %slice.155), channel_id=1, source_target_pairs={{0,2},{1,3},{2,0},{3,1},{4,6},{5,7},{6,4},{7,5},{8,10},{9,11},{10,... | collective-permute-start | bytes 442376 | tf_op jit(solution)/shard_map/ppermute | solution.py:199
  474.0 10.2 %collective-permute-start.36 = (bf16[1,192,256]{2,1,0:T(8,128)(2,1)S(1)}, bf16[1,192,256]{2,1,0:T(8,128)(2,1)S(1)}, u32[]{:S(2)}, u32[]{:S(2)}) collective-permute-start(bf16[1,192,256]{2,1,0:T(8,128)(2,1)S(1)} %slice.157), channel_id=1, source_target_pairs={{0,2},{1,3},{2,0},{3,1},{4,6},{5,7},{6,4},{7,5},{8,10},{9,11},{10,... | collective-permute-start | bytes 294920 | tf_op jit(solution)/shard_map/ppermute | solution.py:199
  476.2 12.9 %collective-permute-start.40 = (bf16[2,96,640]{2,1,0:T(8,128)(2,1)S(1)}, bf16[2,96,640]{2,1,0:T(8,128)(2,1)S(1)}, u32[]{:S(2)}, u32[]{:S(2)}) collective-permute-start(bf16[2,96,640]{2,1,0:T(8,128)(2,1)S(1)} %slice.162), channel_id=1, source_target_pairs={{0,4},{1,5},{2,6},{3,7},{4,0},{5,1},{6,2},{7,3},{8,12},{9,13},{10,... | collective-permute-start | bytes 737288 | tf_op jit(solution)/shard_map/ppermute | solution.py:199
  489.2 4.9 collective-permute-start.41
  (74 other events, 159.1 us)
Sparse Core Ops, SparseCore 0:
  11.5 113.1 all-gather.4
  128.2 78.2 all-gather.6
  360.9 81.2 reduce-scatter.1

commit v7 on v6

--- a/solution.py
+++ b/solution.py
@@ -206,18 +206,18 @@
     held = lax.optimization_barrier((value,) + tuple(chain.pending for chain in chains))
     for chain, pending in zip(chains, held[1:]):
         chain.got = swap(pending, chain.steps[0])
-        chain.pending = None
+        chain.sent, chain.pending = pending, None
     return held[0]
 
 
-def advance(value, chains):
+def advance(value, chains, after=()):
     chains = [chain for chain in chains if chain.steps]
     if not chains:
         return value
     held = lax.optimization_barrier((value,) + tuple(chain.got for chain in chains))
     for chain, got in zip(chains, held[1:]):
         chain.got = got
-        chain.advance()
+        chain.advance(after)
     return launch(held[0], chains + [part for chain in chains for part in chain.parts])
 
 
@@ -314,9 +314,31 @@
 WHOLE, CUT = slice(0, D), 3 * D // 5
 
 
+def fold_kernel(k0_ref, k1_ref, g0_ref, g1_ref, *refs):
+    keep_ref, send_ref = refs[-2:]
+    keep_ref[...] = (k0_ref[...].astype(F32) + g0_ref[...].astype(F32)).astype(BF16)
+    send_ref[...] = (k1_ref[...].astype(F32) + g1_ref[...].astype(F32)).astype(BF16)
+
+
+def fold(keep, got, after):
+    half = keep.shape[0] // 2
+    block = (1,) + keep.shape[1:]
+    near = pl.BlockSpec(block, lambda i: (i, 0, 0))
+    far = pl.BlockSpec(block, lambda i: (i + half, 0, 0))
+    return pl.pallas_call(
+        fold_kernel,
+        grid=(half,),
+        in_specs=[near, far, near, far] + [pl.BlockSpec(memory_space=pltpu.HBM)] * len(after),
+        out_specs=[near, near],
+        out_shape=[jax.ShapeDtypeStruct((half,) + keep.shape[1:], BF16)] * 2,
+        compiler_params=pltpu.CompilerParams(vmem_limit_bytes=VMEM_LIMIT_PRODUCT),
+        name="fold_sums",
+    )(keep, keep, got, got, *after)
+
+
 class Chain:
-    def __init__(self, pairs, scatter=False, extra=None, fork=False):
-        self.steps = order("dp", scatter)
+    def __init__(self, pairs, scatter=False, extra=None, fork=False, first="dp"):
+        self.steps = order(first, scatter)
         self.fork = fork
         self.parts = []
         n_dp, n_seq = lax.axis_size("dp"), lax.axis_size("seq")
@@ -348,6 +370,7 @@
     def part(self, steps, keep, pending):
         chain = object.__new__(Chain)
         chain.steps, chain.factors, chain.fork, chain.parts = steps, None, False, []
+        chain.rows = self.rows
         chain.keep, chain.pending = keep, pending
         self.parts.append(chain)
 
@@ -355,11 +378,15 @@
         half = array.shape[0] // 2
         self.keep, self.pending = array[:half], array[half:]
 
-    def advance(self):
+    def advance(self, after=()):
         self.steps = self.steps[1:]
+        if after and self.steps and not self.factors and self.rows % TILE == 0:
+            self.keep, self.pending = fold(self.keep, self.got, after)
+            return
         if self.factors:
             factors, self.factors = self.factors, None
-            outs = [("block", 0, WHOLE), ("block", 1, WHOLE)]
+            kind = "block" if self.steps[0][0] == "dp" else "half"
+            outs = [(kind, 0, WHOLE), (kind, 1, WHOLE)]
             if self.fork:
                 a, b = slice(0, CUT), slice(CUT, D)
                 outs = [("block", 0, a), ("block", 1, a), ("half", 0, b), ("half", 1, b)]
@@ -388,6 +415,21 @@
                 self.pending = None
             self.advance()
         return self.result
+
+
+def round_kernel(waits, value_ref, *refs):
+    refs[waits][...] = value_ref[...].astype(BF16)
+
+
+def rounded(value, after):
+    return pl.pallas_call(
+        partial(round_kernel, len(after)),
+        in_specs=[pl.BlockSpec(memory_space=pltpu.VMEM)] + [pl.BlockSpec(memory_space=pltpu.HBM)] * len(after),
+        out_specs=pl.BlockSpec(memory_space=pltpu.VMEM),
+        out_shape=jax.ShapeDtypeStruct(value.shape, BF16),
+        compiler_params=pltpu.CompilerParams(vmem_limit_bytes=VMEM_LIMIT_PRODUCT),
+        name="round_gradient",
+    )(value, *after)
 
 
 def allowed_pairs(start, key_count, reach, lanes):
@@ -693,15 +735,15 @@
     gain_grads = gain_grads.astype(BF16).reshape(n_dp, n_seq, 1, -1)
     extra = jnp.pad(gain_grads, ((0, 0), (0, 0), (0, TILE - 1), (0, D - gain_grads.shape[3])))
     attn = [(grad_projected, normed), (context, grad_branch)]
-    chains["attn"] = Chain(attn, last, extra)
+    chains["attn"] = Chain(attn, extra=extra, first="seq" if last else "dp")
     return launch(grad_in, [chains["attn"]])
 
 
 PLAN = {
     0: [(1, "attn")],
-    1: [(1, "ffn"), (1, "attn")],
-    2: [(0, "ffn")],
-    3: [],
+    1: [(1, "ffn")],
+    2: [(0, "ffn"), (1, "attn")],
+    3: [(1, "attn")],
 }
 
 
@@ -773,8 +815,7 @@
                 value, outputs["hidden"] = lax.optimization_barrier((value, outputs["hidden"]))
             if where == 1 and layer_index + 1 < layer_count:
                 above = chains[layer_index + 1]
-                packed = jnp.concatenate([above["ffn"].finish(), above["attn"].finish()], axis=1)
-                value, packed = lax.optimization_barrier((value, packed.astype(BF16)))
+                packed = above["ffn"].finish().astype(BF16)
                 sums[layer_index + 1] = lax.psum_scatter(packed, "seq", scatter_dimension=0)
             return value
 
@@ -784,16 +825,15 @@
         )
     attn, ffn = [chains[0]["attn"]], chains[0]["ffn"].parts or [chains[0]["ffn"]]
     mark = grad_stream[:8]
-    mark = advance(mark, ffn)
-    mark = advance(mark, attn)
-    mark = advance(mark, ffn)
-    mark = advance(mark, attn)
-    mark = advance(mark, ffn)
-    mark, grad_stream = lax.optimization_barrier((mark, grad_stream))
-    short = to_short(grad_stream.astype(BF16), count)
-    mark = advance(mark, attn)
-    mark = advance(mark, ffn)
-    mark = advance(mark, attn)
+    mark = advance(mark, ffn, [chain.sent for chain in attn])
+    for chains_now in (attn, ffn):
+        mark = advance(mark, chains_now)
+    short = to_short(rounded(grad_stream, [chain.keep for chain in ffn]), count)
+    for layer in range(1, layer_count):
+        found = chains[layer]["attn"].finish()[0]
+        sums[layer] = jnp.concatenate([sums[layer].astype(F32), found], axis=0)
+    for chains_now in (attn, ffn, attn, ffn, attn):
+        mark = advance(mark, chains_now)
     sums[0] = jnp.concatenate([chains[0]["ffn"].finish(), chains[0]["attn"].finish()], axis=1)[0]
     packed = jnp.stack([entry.astype(F32) for entry in sums])
     parts, at = [], 0

time: 510 us -> 567 us (1.11)
  waiting for transfers between devices: 230 us -> 253 us
  starting transfers between devices: 54.3 us -> 73.6 us
  Pallas kernels: 130 us -> 141 us
    ppermute x18 -> x21, waiting for transfers between devices: 73.1 us -> 114 us  [swap(): lax.ppermute(array, axis, [(i, i ^ bit) for i in range(lax.axis_size(axis...]
    ppermute x18 -> x21, starting transfers between devices: 23.3 us -> 42.5 us  [swap(): lax.ppermute(array, axis, [(i, i ^ bit) for i in range(lax.axis_size(axis...]
    ppermute x8, waiting for transfers between devices: 29.2 us -> 11.1 us  [to_short(): received.append(lax.ppermute(piece, ALL, route))]
    pallas_call x0 -> x3, Pallas kernels: none -> 6.8 us  [the longest x2 6.73 us: fold(): pl.pallas_call(fold_kernel, grid=(half,), in_specs=[near, far, near, far]...]
    unnamed x220 -> x246, local copies, waits for them, and re-layouts: 52.8 us -> 56.1 us
  transfers between devices with their start and end apart: 45 -> 48, of which waited for: 19 -> 21; matrix products, arithmetic and copies ran while one was open for 3% -> 3% of each run, Pallas kernels for 22% -> 20%
where the time goes in v7:
time: 567 us; the launch traced here: 562 us
  waiting for transfers between devices  253 us (45%)
  Pallas kernels  141 us (25%)
  starting transfers between devices  73.6 us (13%)
  local copies, waits for them, and re-layouts  62.3 us (11%)
  other arithmetic  16.6 us (3%)
  between operations  15.5 us (3%)
    ppermute x21, waiting for transfers between devices, swap(): lax.ppermute(array, axis, [(i, i ^ bit) for i in range(lax.axis_size(axis...  114 us
    all_gather x2, waiting for transfers between devices, gather_weights(): whole = lax.all_gather(packed, ALL, axis=0, tiled=False)  109 us
    pallas_call x14, Pallas kernels, call(): pl.pallas_call(kernel, out_shape=tuple(outs), in_specs=vmem(len(arrays))...  92 us
    unnamed x246, local copies, waits for them, and re-layouts  56.1 us
    ppermute x21, starting transfers between devices, swap(): lax.ppermute(array, axis, [(i, i ^ bit) for i in range(lax.axis_size(axis...  42.5 us
    pallas_call x8, Pallas kernels, product(): pl.pallas_call(partial(product_kernel, len(pairs), extra is not None, got...  42.1 us
    ppermute x12, waiting for transfers between devices, to_long(): received.append(lax.ppermute(piece, ALL, chunk_route(count, k)))  18.8 us
    ppermute x12, starting transfers between devices, to_long(): received.append(lax.ppermute(piece, ALL, chunk_route(count, k)))  15.4 us
  transfers between devices with their start and end apart: 48, of which 21 were waited for; matrix products, arithmetic and copies ran while one was open for 3% of the time, Pallas kernels for 20%

profile of v7, /device:TPU:0, one launch (start us, length us, event | category | flops | bytes accessed | tf_op | source)
XLA Modules:
  0.0 561.7 jit_solution(5686022665898468117)
XLA Ops:
  10.6 4.0 collective-permute-start
  18.2 3.7 collective-permute-done.1
  23.2 1.6 collective-permute-start.4
  24.8 2.0 collective-permute-start.5
  26.7 1.9 collective-permute-start.6
  29.4 1.8 collective-permute-done.6
  32.8 91.9 %all-gather.5.cloned.1.call-done = bf16[11776,640]{1,0:T(8,128)(2,1)} async-done(((bf16[368,640]{1,0:T(8,128)(2,1)}), bf16[11776,640]{1,0:T(8,128)(2,1)}) %all-gather.5.cloned.1.call-update) | async-done | bytes 15073296 | tf_op jit(solution)/shard_map/all_gather | solution.py:763
  126.3 2.3 key_value.2
  130.7 2.4 collective-permute-start.8
  133.8 1.6 copy-done.55
  135.5 1.3 query.2
  141.1 14.9 %block_forward.2 = (bf16[512,1024]{1,0:T(8,128)(2,1)S(1)}, f32[2,1024]{1,0:T(2,128)S(1)}, f32[512,640]{1,0:T(8,128)S(1)}, f32[512,640]{1,0:T(8,128)S(1)}, bf16[5...) custom-call(bf16[512,1024]{1,0:T(8,128)(2,1)S(1)} %get-tuple-element, ...), custom_call_target="tpu_custom_call" | custom-call | flops 98566144 | bytes 260544 | tf_op jit(solution)/shard_map/block_forward/pallas_call | solution.py:108
  162.5 1.5 collective-permute-start.9
  164.2 3.3 key_value.3
  167.5 3.7 collective-permute-start.13
  173.2 1.3 query.3
  175.6 1.4 copy-done.48
  177.0 3.3 collective-permute-done.10
  180.3 8.6 %collective-permute-done.11 = bf16[128,640]{1,0:T(8,128)(2,1)S(1)} collective-permute-done((bf16[128,640]{1,0:T(8,128)(2,1)S(1)}, bf16[128,640]{1,0:T(8,128)(2,1)S(1)}, u32[]{:S(2)}, u32[]{:S(2)}) %collective-permute-start.11) | collective-permute-done | bytes 163872 | tf_op jit(solution)/shard_map/ppermute | solution.py:146
  190.0 17.1 %all-gather.7.cloned.1.call-done = bf16[6144,640]{1,0:T(8,128)(2,1)} async-done(((bf16[192,640]{1,0:T(8,128)(2,1)}), bf16[6144,640]{1,0:T(8,128)(2,1)}) %all-gather.7.cloned.1.call-update) | async-done | bytes 7864336 | tf_op jit(solution)/shard_map/all_gather | solution.py:763
  208.3 15.6 %block_forward.3 = (bf16[512,1024]{1,0:T(8,128)(2,1)S(1)}, f32[2,1024]{1,0:T(2,128)S(1)}, f32[512,640]{1,0:T(8,128)S(1)}, f32[512,640]{1,0:T(8,128)S(1)}, bf16[5...) custom-call(bf16[512,1024]{1,0:T(8,128)(2,1)S(1)} %copy-done.18, ...), custom_call_target="tpu_custom_call" | custom-call | flops 98566144 | bytes 260544 | tf_op jit(solution)/shard_map/block_forward/pallas_call | solution.py:108
  225.8 2.1 collective-permute-start.16
  228.7 15.0 %block_backward.2 = (bf16[512,640]{1,0:T(8,128)(2,1)S(1)}, bf16[512,4096]{1,0:T(8,128)(2,1)}, bf16[512,640]{1,0:T(8,128)(2,1)S(1)}, bf16[512,1024]{1,0:T(8,128)(...) custom-call(f32[512,640]{1,0:T(8,128)S(1)} %bitcast_convert_fusion.grad_ref, ...), custom_call_target="tpu_custom_call" | custom-call | flops 73400320 | bytes 270848 | tf_op jit(solution)/shard_map/block_backward/pallas_call | solution.py:108
  244.5 6.3 %weight_gradient.8 = bf16[2,8,192,640]{3,2,1,0:T(8,128)(2,1)} custom-call(s32[5]{0:T(128)S(1)} %stack.157.numbers_ref, bf16[512,4096]{1,0:T(8,128)(2,1)} %get-tuple-element.151.refs_0_, bf16[512,2048]{1,0:T(8,128)(2,1)S(1)} %copy-done.2, bf16[512,640]{1,0:T(8,128)(2,1)S(1)} %get-tuple-element.153.refs_2_, bf16[512,640]{1,0:T(8,128)(2,1)S(1)} %get-tuple-element.154.refs_3_), custom_call_target="tpu_custom_call" | custom-call | flops 31457280 | bytes 172032 | tf_op jit(solution)/shard_map/weight_gradient/pallas_call | solution.py:298
  252.0 4.2 collective-permute-start.18
  256.2 7.1 %attention_backward.2 = (f32[512,1024]{1,0:T(8,128)S(1)}, bf16[512,512]{1,0:T(8,128)(2,1)}, f32[512,512]{1,0:T(8,128)S(1)}) custom-call(bf16[512,1024]{1,0:T(8,128)(2,1)S(1)} %copy-done.19, bf16[512,512]{1,0:T(8,128)(2,1)} %collective-permute-done.13.before_ref, bf16[512,512]{1,0:T(8,128)(2,1)} %get-tuple-element.139.own_ref, s32[2,1024]{1,0:T(2,128)S(1)} %bitcast.167, ...), custom_call_target="tpu_custom_call" | custom-call | flops 62914560 | bytes 106752 | tf_op jit(solution)/shard_map/attention_backward/pallas_call | solution.py:108
  263.2 1.3 copy-done.50
  266.9 1.6 copy-done.3
  270.7 9.0 %weight_gradient.9 = (bf16[1,8,192,640]{3,2,1,0:T(8,128)(2,1)S(1)}, bf16[1,8,192,640]{3,2,1,0:T(8,128)(2,1)}) custom-call(s32[5]{0:T(128)S(1)} %stack.157.numbers_ref, bf16[512,4096]{1,0:T(8,128)(2,1)} %get-tuple-element.151.refs_0_, bf16[512,2048]{1,0:T(8,128)(2,1)S(1)} %copy-done.3, bf16[512,640]{1,0:T(8,128)(2,1)S(1)} %copy-done.30, ...), custom_call_target="tpu_custom_call" | custom-call | flops 31457280 | bytes 172032 | tf_op jit(solution)/shard_map/weight_gradient/pallas_call | solution.py:298
  279.7 1.3 copy-done.52
  281.1 1.3 query_backward.2
  282.8 4.8 input_backward.2
  290.9 1.4 copy-done.5
  294.7 2.3 weight_gradient.10
  297.0 2.0 collective-permute-start.20
  299.8 2.7 collective-permute-done.20.refs_5_
  302.6 3.7 weight_gradient.11
  307.3 15.1 %block_backward.3 = (bf16[512,640]{1,0:T(8,128)(2,1)S(1)}, bf16[512,4096]{1,0:T(8,128)(2,1)}, bf16[512,640]{1,0:T(8,128)(2,1)S(1)}, bf16[512,1024]{1,0:T(8,128)(...) custom-call(f32[512,640]{1,0:T(8,128)S(1)} %copy-done.63, f32[512,640]{1,0:T(8,128)S(1)} %copy-done.61, ...), custom_call_target="tpu_custom_call" | custom-call | flops 73400320 | bytes 270848 | tf_op jit(solution)/shard_map/block_backward/pallas_call | solution.py:108
  324.2 19.8 %collective-permute-done.21 = bf16[8,192,640]{2,1,0:T(8,128)(2,1)} collective-permute-done((bf16[8,192,640]{2,1,0:T(8,128)(2,1)}, bf16[8,192,640]{2,1,0:T(8,128)(2,1)}, u32[]{:S(2)}, u32[]{:S(2)}) %collective-permute-start.21) | collective-permute-done | bytes 1966112 | tf_op jit(solution)/shard_map/ppermute | solution.py:199
  344.1 6.5 %weight_gradient.12 = bf16[2,8,192,640]{3,2,1,0:T(8,128)(2,1)} custom-call(s32[5]{0:T(128)S(1)} %stack.159.numbers_ref, bf16[512,4096]{1,0:T(8,128)(2,1)} %get-tuple-element.188.refs_0_, bf16[512,2048]{1,0:T(8,128)(2,1)S(1)} %copy-done, bf16[512,640]{1,0:T(8,128)(2,1)S(1)} %copy-done.28, bf16[512,640]{1,0:T(8,128)(2,1)S(1)} %get-tuple-element.191.refs_3_), custom_call_target="tpu_custom_call" | custom-call | flops 31457280 | bytes 172032 | tf_op jit(solution)/shard_map/weight_gradient/pallas_call | solution.py:298
  350.7 3.3 fusion
  360.0 5.2 attention_backward.3
  365.2 18.6 %collective-permute-done.23 = bf16[8,96,640]{2,1,0:T(8,128)(2,1)S(1)} collective-permute-done((bf16[8,96,640]{2,1,0:T(8,128)(2,1)}, bf16[8,96,640]{2,1,0:T(8,128)(2,1)S(1)}, u32[]{:S(2)}, u32[]{:S(2)}) %collective-permute-start.23) | collective-permute-done | bytes 983072 | tf_op jit(solution)/shard_map/ppermute | solution.py:199
  385.5 8.9 %weight_gradient.13 = (bf16[1,8,192,384]{3,2,1,0:T(8,128)(2,1)S(1)}, bf16[1,8,192,384]{3,2,1,0:T(8,128)(2,1)}, bf16[2,4,192,256]{3,2,1,0:T(8,128)(2,1)S(1)}, bf16[2,4,192,256]{3,2,1,0:T(8,128)(2,1)}) custom-call(s32[5]{0:T(128)S(1)} %stack.159.numbers_ref, bf16[512,4096]{1,0:T(8,128)(2,1)} %get-tuple-element.188.refs_0_, bf16[512,2048]{1,0:T(8,128)(2,1)S(1)} %copy-done.1, ...), custom_call_target="tpu_custom_call" | custom-call | flops 31457280 | bytes 172032 | tf_op jit(solution)/shard_map/weight_gradient/pallas_call | solution.py:298
  399.5 1.5 collective-permute-start.25
  401.0 1.3 query_backward.3
  402.3 32.3 %collective-permute-done.24 = bf16[4,96,640]{2,1,0:T(8,128)(2,1)S(1)} collective-permute-done((bf16[4,96,640]{2,1,0:T(8,128)(2,1)S(1)}, bf16[4,96,640]{2,1,0:T(8,128)(2,1)S(1)}, u32[]{:S(2)}, u32[]{:S(2)}) %collective-permute-start.24) | collective-permute-done | bytes 491552 | tf_op jit(solution)/shard_map/ppermute | solution.py:199
  435.7 3.5 input_backward.3
  444.1 2.2 weight_gradient.14.refs_0_
  446.4 3.3 fold_sums.3
  450.5 3.4 fold_sums.2
  455.9 2.0 collective-permute-start.43
  457.9 1.6 collective-permute-start.29
  460.6 8.2 %collective-permute-done.43 = bf16[2,96,640]{2,1,0:T(8,128)(2,1)} collective-permute-done((bf16[2,96,640]{2,1,0:T(8,128)(2,1)}, bf16[2,96,640]{2,1,0:T(8,128)(2,1)}, u32[]{:S(2)}, u32[]{:S(2)}) %collective-permute-start.43) | collective-permute-done | bytes 245792 | tf_op jit(solution)/shard_map/ppermute | solution.py:199
  475.0 3.4 collective-permute-start.34
  480.9 3.3 weight_gradient.15
  484.2 9.3 %collective-permute-done.31 = bf16[128,640]{1,0:T(8,128)(2,1)S(1)} collective-permute-done((bf16[128,640]{1,0:T(8,128)(2,1)S(1)}, bf16[128,640]{1,0:T(8,128)(2,1)S(1)}, u32[]{:S(2)}, u32[]{:S(2)}) %collective-permute-start.31) | collective-permute-done | bytes 163872 | tf_op jit(solution)/shard_map/ppermute | solution.py:159
  494.5 1.8 collective-permute-done.32
  496.4 11.2 %collective-permute-done.39 = bf16[8,96,640]{2,1,0:T(8,128)(2,1)S(1)} collective-permute-done((bf16[8,96,640]{2,1,0:T(8,128)(2,1)S(1)}, bf16[8,96,640]{2,1,0:T(8,128)(2,1)S(1)}, u32[]{:S(2)}, u32[]{:S(2)}) %collective-permute-start.39) | collective-permute-done | bytes 983072 | tf_op jit(solution)/shard_map/ppermute | solution.py:199
  509.2 3.0 collective-permute-start.36
  512.3 4.5 collective-permute-done.40
  517.0 18.4 %collective-permute-start.41 = (bf16[2,96,640]{2,1,0:T(8,128)(2,1)S(1)}, bf16[2,96,640]{2,1,0:T(8,128)(2,1)S(1)}, u32[]{:S(2)}, u32[]{:S(2)}) collective-permute-start(bf16[2,96,640]{2,1,0:T(8,128)(2,1)S(1)} %slice.169), channel_id=1, source_target_pairs={{0,4},{1,5},{2,6},{3,7},{4,0},{5,1},{6,2},{7,3},{8,12},{9,13},{10,... | collective-permute-start | bytes 737288 | tf_op jit(solution)/shard_map/ppermute | solution.py:199
  536.5 9.1 %collective-permute-done.41 = bf16[2,96,640]{2,1,0:T(8,128)(2,1)S(1)} collective-permute-done((bf16[2,96,640]{2,1,0:T(8,128)(2,1)S(1)}, bf16[2,96,640]{2,1,0:T(8,128)(2,1)S(1)}, u32[]{:S(2)}, u32[]{:S(2)}) %collective-permute-start.41) | collective-permute-done | bytes 245792 | tf_op jit(solution)/shard_map/ppermute | solution.py:199
  545.8 5.2 collective-permute-done.42
  (376 shorter events, 89.2 us)
Async XLA Ops:
  7.2 117.5 %all-gather.5.cloned.1.call-start = ((), (), s32[]{:S(2)}) async-start(), calls=%async_computation.2 | async-start | bytes 15544320 | tf_op jit(solution)/shard_map/all_gather | solution.py:763
  10.4 196.7 %all-gather.7.cloned.1.call-start = ((), (), s32[]{:S(2)}) async-start(), calls=%async_computation.3 | async-start | bytes 8110080 | tf_op jit(solution)/shard_map/all_gather | solution.py:763
  10.6 7.6 %collective-permute-start = (bf16[128,640]{1,0:T(8,128)(2,1)S(1)}, bf16[128,640]{1,0:T(8,128)(2,1)S(1)}, u32[]{:S(2)}, u32[]{:S(2)}) collective-permute-start(bf16[128,640]{1,0:T(8,128)(2,1)S(1)} %get-tuple-element.286), channel_id=1, source_target_pairs={{0,3},{1,0},{2,1},{3,2},{4,11},{5,8},{6,9},{7,10},{8,7},{9,4},{10,... | collective-permute-start | bytes 491528 | tf_op jit(solution)/shard_map/ppermute | solution.py:146
  14.6 7.3 %collective-permute-start.1 = (bf16[128,640]{1,0:T(8,128)(2,1)S(1)}, bf16[128,640]{1,0:T(8,128)(2,1)S(1)}, u32[]{:S(2)}, u32[]{:S(2)}) collective-permute-start(bf16[128,640]{1,0:T(8,128)(2,1)S(1)} %get-tuple-element.285), channel_id=1, source_target_pairs={{0,2},{1,3},{2,0},{3,1},{4,10},{5,11},{6,8},{7,9},{8,6},{9,7},{10,... | collective-permute-start | bytes 491528 | tf_op jit(solution)/shard_map/ppermute | solution.py:146
  15.1 7.2 %collective-permute-start.2 = (bf16[128,640]{1,0:T(8,128)(2,1)S(1)}, bf16[128,640]{1,0:T(8,128)(2,1)S(1)}, u32[]{:S(2)}, u32[]{:S(2)}) collective-permute-start(bf16[128,640]{1,0:T(8,128)(2,1)S(1)} %get-tuple-element.287), channel_id=1, source_target_pairs={{0,1},{1,2},{2,3},{3,0},{4,9},{5,10},{6,11},{7,8},{8,5},{9,6},{10,... | collective-permute-start | bytes 491528 | tf_op jit(solution)/shard_map/ppermute | solution.py:146
  15.7 6.6 %collective-permute-start.3 = (bf16[128,640]{1,0:T(8,128)(2,1)S(1)}, bf16[128,640]{1,0:T(8,128)(2,1)S(1)}, u32[]{:S(2)}, u32[]{:S(2)}) collective-permute-start(bf16[128,640]{1,0:T(8,128)(2,1)S(1)} %get-tuple-element.284), channel_id=1, source_target_pairs={{0,0},{1,1},{2,2},{3,3},{4,8},{5,9},{6,10},{7,11},{8,4},{9,5},{10,... | collective-permute-start | bytes 491528 | tf_op jit(solution)/shard_map/ppermute | solution.py:146
  22.7 436.8 %reduce-scatter.2.cloned.1.call-start = ((), (), s32[]{:S(2)}) async-start(), calls=%async_computation.1 | async-start | bytes 2211840 | tf_op jit(solution)/shard_map/reduce_scatter | solution.py:819
  23.2 6.2 %collective-permute-start.4 = (s32[128]{0:T(128)S(1)}, s32[128]{0:T(128)S(1)}, u32[]{:S(2)}, u32[]{:S(2)}) collective-permute-start(s32[128]{0:T(128)S(1)} %get-tuple-element.298), channel_id=1, source_target_pairs={{0,3},{1,0},{2,1},{3,2},{4,11},{5,8},{6,9},{7,10},{8,7},{9,4},{10,... | collective-permute-start | bytes 1544 | tf_op jit(solution)/shard_map/ppermute | solution.py:146
  24.8 4.6 collective-permute-start.5
  26.7 4.4 collective-permute-start.6
  28.7 2.5 collective-permute-start.7
  130.7 7.4 %collective-permute-start.8 = (bf16[512,512]{1,0:T(8,128)(2,1)S(1)}, bf16[512,512]{1,0:T(8,128)(2,1)S(1)}, u32[]{:S(2)}, u32[]{:S(2)}) collective-permute-start(bf16[512,512]{1,0:T(8,128)(2,1)S(1)} %get-tuple-element.132.own_ref), channel_id=1, source_target_pairs={{0,8},{1,9},{2,10},{3,11},{4,12},{5,13},{6,14},{7,15},{16,24},{17,... | collective-permute-start | bytes 1572872 | tf_op jit(solution)/shard_map/ppermute | solution.py:176
  138.1 17.8 %copy-start.15 = (bf16[512,1024]{1,0:T(8,128)(2,1)}, bf16[512,1024]{1,0:T(8,128)(2,1)S(1)}, u32[]{:S(2)}) copy-start(bf16[512,1024]{1,0:T(8,128)(2,1)S(1)} %get-tuple-element.131.q_ref) | copy-start | bytes 3145732
  141.1 20.6 %copy-start.96 = (bf16[4,128,640]{2,1,0:T(8,128)(2,1)S(1)}, bf16[4,128,640]{2,1,0:T(8,128)(2,1)}, u32[]{:S(2)}) copy-start(bf16[4,128,640]{2,1,0:T(8,128)(2,1)} %param.10) | copy-start | bytes 1966084
  162.5 14.4 %collective-permute-start.9 = (bf16[128,640]{1,0:T(8,128)(2,1)}, bf16[128,640]{1,0:T(8,128)(2,1)S(1)}, u32[]{:S(2)}, u32[]{:S(2)}) collective-permute-start(bf16[128,640]{1,0:T(8,128)(2,1)} %get-tuple-element.283), channel_id=1, source_target_pairs={{0,3},{1,0},{2,1},{3,2},{4,11},{5,8},{6,9},{7,10},{8,7},{9,4},{10,... | collective-permute-start | bytes 491528 | tf_op jit(solution)/shard_map/ppermute | solution.py:146
  167.5 39.6 %collective-permute-start.13 = (bf16[512,512]{1,0:T(8,128)(2,1)}, bf16[512,512]{1,0:T(8,128)(2,1)}, u32[]{:S(2)}, u32[]{:S(2)}) collective-permute-start(bf16[512,512]{1,0:T(8,128)(2,1)} %get-tuple-element.139.own_ref), channel_id=1, source_target_pairs={{0,8},{1,9},{2,10},{3,11},{4,12},{5,13},{6,14},{7,15},{16,24},{17,... | collective-permute-start | bytes 1572872 | tf_op jit(solution)/shard_map/ppermute | solution.py:176
  171.2 9.1 %collective-permute-start.10 = (bf16[128,640]{1,0:T(8,128)(2,1)S(1)}, bf16[128,640]{1,0:T(8,128)(2,1)S(1)}, u32[]{:S(2)}, u32[]{:S(2)}) collective-permute-start(bf16[128,640]{1,0:T(8,128)(2,1)S(1)} %copy-done.99), channel_id=1, source_target_pairs={{0,2},{1,3},{2,0},{3,1},{4,10},{5,11},{6,8},{7,9},{8,6},{9,7},{10,... | collective-permute-start | bytes 491528 | tf_op jit(solution)/shard_map/ppermute | solution.py:146
  171.8 17.1 %collective-permute-start.11 = (bf16[128,640]{1,0:T(8,128)(2,1)S(1)}, bf16[128,640]{1,0:T(8,128)(2,1)S(1)}, u32[]{:S(2)}, u32[]{:S(2)}) collective-permute-start(bf16[128,640]{1,0:T(8,128)(2,1)S(1)} %copy-done.98), channel_id=1, source_target_pairs={{0,1},{1,2},{2,3},{3,0},{4,9},{5,10},{6,11},{7,8},{8,5},{9,6},{10,... | collective-permute-start | bytes 491528 | tf_op jit(solution)/shard_map/ppermute | solution.py:146
  172.3 16.6 %collective-permute-start.12 = (bf16[128,640]{1,0:T(8,128)(2,1)S(1)}, bf16[128,640]{1,0:T(8,128)(2,1)S(1)}, u32[]{:S(2)}, u32[]{:S(2)}) collective-permute-start(bf16[128,640]{1,0:T(8,128)(2,1)S(1)} %copy-done.97), channel_id=1, source_target_pairs={{0,0},{1,1},{2,2},{3,3},{4,8},{5,9},{6,10},{7,11},{8,4},{9,5},{10,... | collective-permute-start | bytes 491528 | tf_op jit(solution)/shard_map/ppermute | solution.py:146
  189.0 18.1 %copy-start.85 = (s32[1,2,4,256]{3,1,2,0:T(2,128)S(1)}, s32[1,2,4,256]{3,1,2,0:T(2,128)}, u32[]{:S(2)}) copy-start(s32[1,2,4,256]{3,1,2,0:T(2,128)} %copy-done.84) | copy-start | bytes 24580
  223.9 20.6 %copy-start.29 = (bf16[512,640]{1,0:T(8,128)(2,1)}, bf16[512,640]{1,0:T(8,128)(2,1)S(1)}, u32[]{:S(2)}) copy-start(bf16[512,640]{1,0:T(8,128)(2,1)S(1)} %get-tuple-element.153.refs_2_) | copy-start | bytes 1966084
  224.9 25.9 %collective-permute-start.14 = (bf16[128,640]{1,0:T(8,128)(2,1)S(1)}, bf16[128,640]{1,0:T(8,128)(2,1)S(1)}, u32[]{:S(2)}, u32[]{:S(2)}) collective-permute-start(bf16[128,640]{1,0:T(8,128)(2,1)S(1)} %get-tuple-element.279), channel_id=1, source_target_pairs={{0,0},{1,1},{2,2},{3,3},{8,4},{9,5},{10,6},{11,7},{4,8},{5,9},{6,1... | collective-permute-start | bytes 491528 | tf_op jit(solution)/shard_map/ppermute | solution.py:159
  225.7 25.1 %collective-permute-start.15 = (bf16[128,640]{1,0:T(8,128)(2,1)S(1)}, bf16[128,640]{1,0:T(8,128)(2,1)S(1)}, u32[]{:S(2)}, u32[]{:S(2)}) collective-permute-start(bf16[128,640]{1,0:T(8,128)(2,1)S(1)} %get-tuple-element.278), channel_id=1, source_target_pairs={{1,0},{2,1},{3,2},{0,3},{9,4},{10,5},{11,6},{8,7},{5,8},{6,9},{7,1... | collective-permute-start | bytes 491528 | tf_op jit(solution)/shard_map/ppermute | solution.py:159
  225.8 25.1 %collective-permute-start.16 = (bf16[128,640]{1,0:T(8,128)(2,1)S(1)}, bf16[128,640]{1,0:T(8,128)(2,1)S(1)}, u32[]{:S(2)}, u32[]{:S(2)}) collective-permute-start(bf16[128,640]{1,0:T(8,128)(2,1)S(1)} %get-tuple-element.277), channel_id=1, source_target_pairs={{2,0},{3,1},{0,2},{1,3},{10,4},{11,5},{8,6},{9,7},{6,8},{7,9},{4,1... | collective-permute-start | bytes 491528 | tf_op jit(solution)/shard_map/ppermute | solution.py:159
  227.9 23.0 %collective-permute-start.17 = (bf16[128,640]{1,0:T(8,128)(2,1)S(1)}, bf16[128,640]{1,0:T(8,128)(2,1)S(1)}, u32[]{:S(2)}, u32[]{:S(2)}) collective-permute-start(bf16[128,640]{1,0:T(8,128)(2,1)S(1)} %get-tuple-element.276), channel_id=1, source_target_pairs={{3,0},{0,1},{1,2},{2,3},{11,4},{8,5},{9,6},{10,7},{7,8},{4,9},{5,1... | collective-permute-start | bytes 491528 | tf_op jit(solution)/shard_map/ppermute | solution.py:159
  228.7 15.8 %copy-start.2 = (bf16[512,2048]{1,0:T(8,128)(2,1)S(1)}, bf16[512,2048]{1,0:T(8,128)(2,1)}, u32[]{:S(2)}) copy-start(bf16[512,2048]{1,0:T(8,128)(2,1)} %get-tuple-element.152.refs_1_) | copy-start | bytes 6291460
  252.0 15.0 %collective-permute-start.18 = (bf16[2,8,192,640]{3,2,1,0:T(8,128)(2,1)}, bf16[2,8,192,640]{3,2,1,0:T(8,128)(2,1)}, u32[]{:S(2)}, u32[]{:S(2)}) collective-permute-start(bf16[2,8,192,640]{3,2,1,0:T(8,128)(2,1)} %weight_gradient.8), channel_id=1, source_target_pairs={{0,8},{8,0},{16,24},{24,16},{1,9},{9,1},{17,25},{25,17},{2,10},{10... | collective-permute-start | bytes 11796488 | tf_op jit(solution)/shard_map/ppermute | solution.py:199
  265.6 16.8 %collective-permute-start.19 = (bf16[512,512]{1,0:T(8,128)(2,1)}, bf16[512,512]{1,0:T(8,128)(2,1)}, u32[]{:S(2)}, u32[]{:S(2)}) collective-permute-start(bf16[512,512]{1,0:T(8,128)(2,1)} %get-tuple-element.165), channel_id=1, source_target_pairs={{8,0},{9,1},{10,2},{11,3},{12,4},{13,5},{14,6},{15,7},{24,16},{25,... | collective-permute-start | bytes 1572872 | tf_op jit(solution)/shard_map/ppermute | solution.py:176
  297.0 5.6 collective-permute-start.20
  299.0 45.1 %collective-permute-start.21 = (bf16[8,192,640]{2,1,0:T(8,128)(2,1)}, bf16[8,192,640]{2,1,0:T(8,128)(2,1)}, u32[]{:S(2)}, u32[]{:S(2)}) collective-permute-start(bf16[8,192,640]{2,1,0:T(8,128)(2,1)} %bitcast.52), channel_id=1, source_target_pairs={{0,16},{8,24},{16,0},{24,8},{1,17},{9,25},{17,1},{25,9},{2,18},{10... | collective-permute-start | bytes 5898248 | tf_op jit(solution)/shard_map/ppermute | solution.py:199
  306.3 16.1 %copy-start.74 = (bf16[2,4,96,640]{3,2,1,0:T(8,128)(2,1)}, bf16[2,4,96,640]{3,2,1,0:T(8,128)(2,1)S(1)}, u32[]{:S(2)}) copy-start(bf16[2,4,96,640]{3,2,1,0:T(8,128)(2,1)S(1)} %get-tuple-element.197) | copy-start | bytes 2949124
  307.2 36.8 %copy-start = (bf16[512,2048]{1,0:T(8,128)(2,1)S(1)}, bf16[512,2048]{1,0:T(8,128)(2,1)}, u32[]{:S(2)}) copy-start(bf16[512,2048]{1,0:T(8,128)(2,1)} %get-tuple-element.189.refs_1_) | copy-start | bytes 6291460
  307.2 36.8 %copy-start.28 = (bf16[512,640]{1,0:T(8,128)(2,1)S(1)}, bf16[512,640]{1,0:T(8,128)(2,1)}, u32[]{:S(2)}) copy-start(bf16[512,640]{1,0:T(8,128)(2,1)} %copy-done.27) | copy-start | bytes 1966084
  324.2 26.4 %copy-start.33 = (bf16[512,640]{1,0:T(8,128)(2,1)}, bf16[512,640]{1,0:T(8,128)(2,1)S(1)}, u32[]{:S(2)}) copy-start(bf16[512,640]{1,0:T(8,128)(2,1)S(1)} %get-tuple-element.191.refs_3_) | copy-start | bytes 1966084
  324.2 26.4 %copy-start.66 = (f32[512,640]{1,0:T(8,128)}, f32[512,640]{1,0:T(8,128)S(1)}, u32[]{:S(2)}) copy-start(f32[512,640]{1,0:T(8,128)S(1)} %get-tuple-element.212.gmid_ref) | copy-start | bytes 3932164
  324.2 26.4 %copy-start.87 = (f32[8,640]{1,0:T(8,128)}, f32[8,640]{1,0:T(8,128)S(1)}, u32[]{:S(2)}) copy-start(f32[8,640]{1,0:T(8,128)S(1)} %get-tuple-element.213.sums_ref) | copy-start | bytes 61444
  350.6 33.1 %collective-permute-start.22 = (bf16[2,8,192,640]{3,2,1,0:T(8,128)(2,1)}, bf16[2,8,192,640]{3,2,1,0:T(8,128)(2,1)}, u32[]{:S(2)}, u32[]{:S(2)}) collective-permute-start(bf16[2,8,192,640]{3,2,1,0:T(8,128)(2,1)} %weight_gradient.12), channel_id=1, source_target_pairs={{0,8},{8,0},{16,24},{24,16},{1,9},{9,1},{17,25},{25,17},{2,10},{10... | collective-permute-start | bytes 11796488 | tf_op jit(solution)/shard_map/ppermute | solution.py:199
  354.1 29.7 %collective-permute-start.23 = (bf16[8,96,640]{2,1,0:T(8,128)(2,1)}, bf16[8,96,640]{2,1,0:T(8,128)(2,1)S(1)}, u32[]{:S(2)}, u32[]{:S(2)}) collective-permute-start(bf16[8,96,640]{2,1,0:T(8,128)(2,1)} %bitcast.169), channel_id=1, source_target_pairs={{0,1},{1,0},{2,3},{3,2},{4,5},{5,4},{6,7},{7,6},{8,9},{9,8},{10,11... | collective-permute-start | bytes 2949128 | tf_op jit(solution)/shard_map/ppermute | solution.py:199
  360.0 23.7 %copy-start.75 = (bf16[2,4,96,640]{3,2,1,0:T(8,128)(2,1)S(1)}, bf16[2,4,96,640]{3,2,1,0:T(8,128)(2,1)}, u32[]{:S(2)}) copy-start(bf16[2,4,96,640]{3,2,1,0:T(8,128)(2,1)} %copy-done.74) | copy-start | bytes 2949124
  385.5 15.4 %copy-start.47 = (f32[512,1024]{1,0:T(8,128)S(1)}, f32[512,1024]{1,0:T(8,128)}, u32[]{:S(2)}) copy-start(f32[512,1024]{1,0:T(8,128)} %copy-done.46) | copy-start | bytes 6291460
  396.3 50.1 %collective-permute-start.26 = (bf16[8,192,384]{2,1,0:T(8,128)(2,1)}, bf16[8,192,384]{2,1,0:T(8,128)(2,1)}, u32[]{:S(2)}, u32[]{:S(2)}) collective-permute-start(bf16[8,192,384]{2,1,0:T(8,128)(2,1)} %bitcast.56), channel_id=1, source_target_pairs={{0,16},{8,24},{16,0},{24,8},{1,17},{9,25},{17,1},{25,9},{2,18},{10... | collective-permute-start | bytes 3538952 | tf_op jit(solution)/shard_map/ppermute | solution.py:199
  397.2 37.5 %collective-permute-start.24 = (bf16[4,96,640]{2,1,0:T(8,128)(2,1)S(1)}, bf16[4,96,640]{2,1,0:T(8,128)(2,1)S(1)}, u32[]{:S(2)}, u32[]{:S(2)}) collective-permute-start(bf16[4,96,640]{2,1,0:T(8,128)(2,1)S(1)} %slice.155), channel_id=1, source_target_pairs={{0,16},{8,24},{16,0},{24,8},{1,17},{9,25},{17,1},{25,9},{2,18},{10... | collective-permute-start | bytes 1474568 | tf_op jit(solution)/shard_map/ppermute | solution.py:199
  398.3 48.0 %collective-permute-start.27 = (bf16[8,192,256]{2,1,0:T(8,128)(2,1)}, bf16[8,192,256]{2,1,0:T(8,128)(2,1)}, u32[]{:S(2)}, u32[]{:S(2)}) collective-permute-start(bf16[8,192,256]{2,1,0:T(8,128)(2,1)} %bitcast.57), channel_id=1, source_target_pairs={{0,1},{1,0},{2,3},{3,2},{4,5},{5,4},{6,7},{7,6},{8,9},{9,8},{10,11... | collective-permute-start | bytes 2359304 | tf_op jit(solution)/shard_map/ppermute | solution.py:199
  399.5 36.1 %collective-permute-start.25 = (bf16[512,512]{1,0:T(8,128)(2,1)S(1)}, bf16[512,512]{1,0:T(8,128)(2,1)S(1)}, u32[]{:S(2)}, u32[]{:S(2)}) collective-permute-start(bf16[512,512]{1,0:T(8,128)(2,1)S(1)} %get-tuple-element.210), channel_id=1, source_target_pairs={{8,0},{9,1},{10,2},{11,3},{12,4},{13,5},{14,6},{15,7},{24,16},{25,... | collective-permute-start | bytes 1572872 | tf_op jit(solution)/shard_map/ppermute | solution.py:176
  402.3 33.4 %copy-start.67 = (f32[512,640]{1,0:T(8,128)S(1)}, f32[512,640]{1,0:T(8,128)}, u32[]{:S(2)}) copy-start(f32[512,640]{1,0:T(8,128)} %copy-done.66) | copy-start | bytes 3932164
  402.3 33.3 %copy-start.79 = (f32[512,256]{1,0:T(8,128)S(1)}, f32[512,256]{1,0:T(8,128)}, u32[]{:S(2)}) copy-start(f32[512,256]{1,0:T(8,128)} %copy-done.78) | copy-start | bytes 1572868
  402.3 33.3 %copy-start.88 = (f32[8,640]{1,0:T(8,128)S(1)}, f32[8,640]{1,0:T(8,128)}, u32[]{:S(2)}) copy-start(f32[8,640]{1,0:T(8,128)} %copy-done.87) | copy-start | bytes 61444
  454.7 15.3 %collective-permute-start.28 = (bf16[4,192,384]{2,1,0:T(8,128)(2,1)}, bf16[4,192,384]{2,1,0:T(8,128)(2,1)}, u32[]{:S(2)}, u32[]{:S(2)}) collective-permute-start(bf16[4,192,384]{2,1,0:T(8,128)(2,1)} %get-tuple-element.231), channel_id=1, source_target_pairs={{0,1},{1,0},{2,3},{3,2},{4,5},{5,4},{6,7},{7,6},{8,9},{9,8},{10,11... | collective-permute-start | bytes 1769480 | tf_op jit(solution)/shard_map/ppermute | solution.py:199
  455.9 12.9 %collective-permute-start.43 = (bf16[2,96,640]{2,1,0:T(8,128)(2,1)}, bf16[2,96,640]{2,1,0:T(8,128)(2,1)}, u32[]{:S(2)}, u32[]{:S(2)}) collective-permute-start(bf16[2,96,640]{2,1,0:T(8,128)(2,1)} %slice.157), channel_id=1, source_target_pairs={{0,4},{1,5},{2,6},{3,7},{4,0},{5,1},{6,2},{7,3},{8,12},{9,13},{10,... | collective-permute-start | bytes 737288 | tf_op jit(solution)/shard_map/ppermute | solution.py:199
  457.9 12.1 %collective-permute-start.29 = (bf16[4,192,256]{2,1,0:T(8,128)(2,1)}, bf16[4,192,256]{2,1,0:T(8,128)(2,1)}, u32[]{:S(2)}, u32[]{:S(2)}) collective-permute-start(bf16[4,192,256]{2,1,0:T(8,128)(2,1)} %get-tuple-element.232), channel_id=1, source_target_pairs={{0,16},{8,24},{16,0},{24,8},{1,17},{9,25},{17,1},{25,9},{2,18},{10... | collective-permute-start | bytes 1179656 | tf_op jit(solution)/shard_map/ppermute | solution.py:199
  460.6 19.9 %collective-permute-start.38 = (bf16[2,8,96,640]{3,2,1,0:T(8,128)(2,1)S(1)}, bf16[2,8,96,640]{3,2,1,0:T(8,128)(2,1)S(1)}, u32[]{:S(2)}, u32[]{:S(2)}) collective-permute-start(bf16[2,8,96,640]{3,2,1,0:T(8,128)(2,1)S(1)} %weight_gradient.14.refs_0_), channel_id=1, source_target_pairs={{0,8},{8,0},{16,24},{24,16},{1,9},{9,1},{17,25},{25,17},{2,10},{10... | collective-permute-start | bytes 5898248 | tf_op jit(solution)/shard_map/ppermute | solution.py:199
  470.0 4.9 collective-permute-start.44
  472.9 6.3 %collective-permute-start.30 = (bf16[128,640]{1,0:T(8,128)(2,1)S(1)}, bf16[128,640]{1,0:T(8,128)(2,1)S(1)}, u32[]{:S(2)}, u32[]{:S(2)}) collective-permute-start(bf16[128,640]{1,0:T(8,128)(2,1)S(1)} %get-tuple-element.275), channel_id=1, source_target_pairs={{0,0},{1,1},{2,2},{3,3},{8,4},{9,5},{10,6},{11,7},{4,8},{5,9},{6,1... | collective-permute-start | bytes 491528 | tf_op jit(solution)/shard_map/ppermute | solution.py:159
  475.0 34.1 %collective-permute-start.34 = (bf16[2,192,384]{2,1,0:T(8,128)(2,1)S(1)}, bf16[2,192,384]{2,1,0:T(8,128)(2,1)S(1)}, u32[]{:S(2)}, u32[]{:S(2)}) collective-permute-start(bf16[2,192,384]{2,1,0:T(8,128)(2,1)S(1)} %get-tuple-element.236), channel_id=1, source_target_pairs={{0,4},{1,5},{2,6},{3,7},{4,0},{5,1},{6,2},{7,3},{8,12},{9,13},{10,... | collective-permute-start | bytes 884744 | tf_op jit(solution)/shard_map/ppermute | solution.py:199
  478.4 30.7 %collective-permute-start.35 = (bf16[2,192,256]{2,1,0:T(8,128)(2,1)S(1)}, bf16[2,192,256]{2,1,0:T(8,128)(2,1)S(1)}, u32[]{:S(2)}, u32[]{:S(2)}) collective-permute-start(bf16[2,192,256]{2,1,0:T(8,128)(2,1)S(1)} %get-tuple-element.237), channel_id=1, source_target_pairs={{0,4},{1,5},{2,6},{3,7},{4,0},{5,1},{6,2},{7,3},{8,12},{9,13},{10,... | collective-permute-start | bytes 589832 | tf_op jit(solution)/shard_map/ppermute | solution.py:199
  478.5 15.1 %collective-permute-start.31 = (bf16[128,640]{1,0:T(8,128)(2,1)S(1)}, bf16[128,640]{1,0:T(8,128)(2,1)S(1)}, u32[]{:S(2)}, u32[]{:S(2)}) collective-permute-start(bf16[128,640]{1,0:T(8,128)(2,1)S(1)} %get-tuple-element.274), channel_id=1, source_target_pairs={{1,0},{2,1},{3,2},{0,3},{9,4},{10,5},{11,6},{8,7},{5,8},{6,9},{7,1... | collective-permute-start | bytes 491528 | tf_op jit(solution)/shard_map/ppermute | solution.py:159
  479.2 17.0 %collective-permute-start.32 = (bf16[128,640]{1,0:T(8,128)(2,1)S(1)}, bf16[128,640]{1,0:T(8,128)(2,1)S(1)}, u32[]{:S(2)}, u32[]{:S(2)}) collective-permute-start(bf16[128,640]{1,0:T(8,128)(2,1)S(1)} %get-tuple-element.273), channel_id=1, source_target_pairs={{2,0},{3,1},{0,2},{1,3},{10,4},{11,5},{8,6},{9,7},{6,8},{7,9},{4,1... | collective-permute-start | bytes 491528 | tf_op jit(solution)/shard_map/ppermute | solution.py:159
  480.5 15.8 %collective-permute-start.33 = (bf16[128,640]{1,0:T(8,128)(2,1)S(1)}, bf16[128,640]{1,0:T(8,128)(2,1)S(1)}, u32[]{:S(2)}, u32[]{:S(2)}) collective-permute-start(bf16[128,640]{1,0:T(8,128)(2,1)S(1)} %get-tuple-element.272), channel_id=1, source_target_pairs={{3,0},{0,1},{1,2},{2,3},{11,4},{8,5},{9,6},{10,7},{7,8},{4,9},{5,1... | collective-permute-start | bytes 491528 | tf_op jit(solution)/shard_map/ppermute | solution.py:159
  493.5 14.1 %collective-permute-start.39 = (bf16[8,96,640]{2,1,0:T(8,128)(2,1)S(1)}, bf16[8,96,640]{2,1,0:T(8,128)(2,1)S(1)}, u32[]{:S(2)}, u32[]{:S(2)}) collective-permute-start(bf16[8,96,640]{2,1,0:T(8,128)(2,1)S(1)} %bitcast.170), channel_id=1, source_target_pairs={{0,16},{8,24},{16,0},{24,8},{1,17},{9,25},{17,1},{25,9},{2,18},{10... | collective-permute-start | bytes 2949128 | tf_op jit(solution)/shard_map/ppermute | solution.py:199
  507.9 8.9 %collective-permute-start.40 = (bf16[4,96,640]{2,1,0:T(8,128)(2,1)S(1)}, bf16[4,96,640]{2,1,0:T(8,128)(2,1)S(1)}, u32[]{:S(2)}, u32[]{:S(2)}) collective-permute-start(bf16[4,96,640]{2,1,0:T(8,128)(2,1)S(1)} %slice.167), channel_id=1, source_target_pairs={{0,1},{1,0},{2,3},{3,2},{4,5},{5,4},{6,7},{7,6},{8,9},{9,8},{10,11... | collective-permute-start | bytes 1474568 | tf_op jit(solution)/shard_map/ppermute | solution.py:199
  509.2 27.2 %collective-permute-start.36 = (bf16[1,192,384]{2,1,0:T(8,128)(2,1)S(1)}, bf16[1,192,384]{2,1,0:T(8,128)(2,1)S(1)}, u32[]{:S(2)}, u32[]{:S(2)}) collective-permute-start(bf16[1,192,384]{2,1,0:T(8,128)(2,1)S(1)} %slice.163), channel_id=1, source_target_pairs={{0,2},{1,3},{2,0},{3,1},{4,6},{5,7},{6,4},{7,5},{8,10},{9,11},{10,... | collective-permute-start | bytes 442376 | tf_op jit(solution)/shard_map/ppermute | solution.py:199
  512.2 24.3 %collective-permute-start.37 = (bf16[1,192,256]{2,1,0:T(8,128)(2,1)S(1)}, bf16[1,192,256]{2,1,0:T(8,128)(2,1)S(1)}, u32[]{:S(2)}, u32[]{:S(2)}) collective-permute-start(bf16[1,192,256]{2,1,0:T(8,128)(2,1)S(1)} %slice.164), channel_id=1, source_target_pairs={{0,2},{1,3},{2,0},{3,1},{4,6},{5,7},{6,4},{7,5},{8,10},{9,11},{10,... | collective-permute-start | bytes 294920 | tf_op jit(solution)/shard_map/ppermute | solution.py:199
  517.0 28.6 %collective-permute-start.41 = (bf16[2,96,640]{2,1,0:T(8,128)(2,1)S(1)}, bf16[2,96,640]{2,1,0:T(8,128)(2,1)S(1)}, u32[]{:S(2)}, u32[]{:S(2)}) collective-permute-start(bf16[2,96,640]{2,1,0:T(8,128)(2,1)S(1)} %slice.169), channel_id=1, source_target_pairs={{0,4},{1,5},{2,6},{3,7},{4,0},{5,1},{6,2},{7,3},{8,12},{9,13},{10,... | collective-permute-start | bytes 737288 | tf_op jit(solution)/shard_map/ppermute | solution.py:199
  545.7 5.3 collective-permute-start.42
  (90 other events, 279.8 us)
Sparse Core Ops, SparseCore 0:
  11.5 113.1 all-gather.4
  128.2 78.8 all-gather.6
  354.2 71.7 reduce-scatter.1

commit v8 on v6

--- a/solution.py
+++ b/solution.py
@@ -388,6 +388,21 @@
                 self.pending = None
             self.advance()
         return self.result
+
+
+def round_kernel(waits, value_ref, *refs):
+    refs[waits][...] = value_ref[...].astype(BF16)
+
+
+def rounded(value, after):
+    return pl.pallas_call(
+        partial(round_kernel, len(after)),
+        in_specs=[pl.BlockSpec(memory_space=pltpu.VMEM)] + [pl.BlockSpec(memory_space=pltpu.HBM)] * len(after),
+        out_specs=pl.BlockSpec(memory_space=pltpu.VMEM),
+        out_shape=jax.ShapeDtypeStruct(value.shape, BF16),
+        compiler_params=pltpu.CompilerParams(vmem_limit_bytes=VMEM_LIMIT_PRODUCT),
+        name="round_gradient",
+    )(value, *after)
 
 
 def allowed_pairs(start, key_count, reach, lanes):
@@ -784,16 +799,11 @@
         )
     attn, ffn = [chains[0]["attn"]], chains[0]["ffn"].parts or [chains[0]["ffn"]]
     mark = grad_stream[:8]
-    mark = advance(mark, ffn)
-    mark = advance(mark, attn)
-    mark = advance(mark, ffn)
-    mark = advance(mark, attn)
-    mark = advance(mark, ffn)
-    mark, grad_stream = lax.optimization_barrier((mark, grad_stream))
-    short = to_short(grad_stream.astype(BF16), count)
-    mark = advance(mark, attn)
-    mark = advance(mark, ffn)
-    mark = advance(mark, attn)
+    for chains_now in (ffn, attn, ffn):
+        mark = advance(mark, chains_now)
+    short = to_short(rounded(grad_stream, [chain.keep for chain in ffn]), count)
+    for chains_now in (attn, ffn, attn, ffn, attn):
+        mark = advance(mark, chains_now)
     sums[0] = jnp.concatenate([chains[0]["ffn"].finish(), chains[0]["attn"].finish()], axis=1)[0]
     packed = jnp.stack([entry.astype(F32) for entry in sums])
     parts, at = [], 0

time: 510 us -> 551 us (1.080)
  starting transfers between devices: 54.3 us -> 74.3 us
  waiting for transfers between devices: 230 us -> 245 us
    ppermute x18, waiting for transfers between devices: 73.1 us -> 99.8 us  [swap(): lax.ppermute(array, axis, [(i, i ^ bit) for i in range(lax.axis_size(axis...]
    ppermute x18, starting transfers between devices: 23.3 us -> 42 us  [swap(): lax.ppermute(array, axis, [(i, i ^ bit) for i in range(lax.axis_size(axis...]
    ppermute x8, waiting for transfers between devices: 29.2 us -> 16.7 us  [to_short(): received.append(lax.ppermute(piece, ALL, route))]
    unnamed x220 -> x240, local copies, waits for them, and re-layouts: 52.8 us -> 55.6 us
  transfers between devices with their start and end apart: 45 -> 45, of which waited for: 19 -> 21; matrix products, arithmetic and copies ran while one was open for 3% -> 3% of each run, Pallas kernels for 22% -> 18%
where the time goes in v8:
time: 551 us; the launch traced here: 546 us
  waiting for transfers between devices  245 us (44%)
  Pallas kernels  130 us (24%)
  starting transfers between devices  74.3 us (13%)
  local copies, waits for them, and re-layouts  62.7 us (11%)
  other arithmetic  19.2 us (3%)
  between operations  15.4 us (3%)
    all_gather x2, waiting for transfers between devices, gather_weights(): whole = lax.all_gather(packed, ALL, axis=0, tiled=False)  111 us
    ppermute x18, waiting for transfers between devices, swap(): lax.ppermute(array, axis, [(i, i ^ bit) for i in range(lax.axis_size(axis...  99.8 us
    pallas_call x14, Pallas kernels, call(): pl.pallas_call(kernel, out_shape=tuple(outs), in_specs=vmem(len(arrays))...  89.5 us
    unnamed x240, local copies, waits for them, and re-layouts  55.6 us
    ppermute x18, starting transfers between devices, swap(): lax.ppermute(array, axis, [(i, i ^ bit) for i in range(lax.axis_size(axis...  42 us
    pallas_call x8, Pallas kernels, product(): pl.pallas_call(partial(product_kernel, len(pairs), extra is not None, got...  40.3 us
    ppermute x12, waiting for transfers between devices, to_long(): received.append(lax.ppermute(piece, ALL, chunk_route(count, k)))  17.3 us
    ppermute x8, waiting for transfers between devices, to_short(): received.append(lax.ppermute(piece, ALL, route))  16.7 us
  transfers between devices with their start and end apart: 45, of which 21 were waited for; matrix products, arithmetic and copies ran while one was open for 3% of the time, Pallas kernels for 18%

profile of v8, /device:TPU:0, one launch (start us, length us, event | category | flops | bytes accessed | tf_op | source)
XLA Modules:
  0.0 546.1 jit_solution(12377144612074433439)
XLA Ops:
  10.6 4.0 collective-permute-start
  18.2 3.7 collective-permute-done.1
  23.2 1.6 collective-permute-start.4
  24.8 2.0 collective-permute-start.5
  26.7 1.9 collective-permute-start.6
  29.4 1.8 collective-permute-done.6
  32.8 91.9 %all-gather.5.cloned.1.call-done = bf16[11776,640]{1,0:T(8,128)(2,1)} async-done(((bf16[368,640]{1,0:T(8,128)(2,1)}), bf16[11776,640]{1,0:T(8,128)(2,1)}) %all-gather.5.cloned.1.call-update) | async-done | bytes 15073296 | tf_op jit(solution)/shard_map/all_gather | solution.py:736
  126.3 2.3 key_value.2
  130.8 2.4 collective-permute-start.8
  133.9 1.6 copy-done.48
  141.1 14.7 %block_forward.2 = (bf16[512,1024]{1,0:T(8,128)(2,1)S(1)}, f32[2,1024]{1,0:T(2,128)S(1)}, f32[512,640]{1,0:T(8,128)S(1)}, f32[512,640]{1,0:T(8,128)S(1)}, bf16[5...) custom-call(bf16[512,1024]{1,0:T(8,128)(2,1)S(1)} %get-tuple-element, ...), custom_call_target="tpu_custom_call" | custom-call | flops 98566144 | bytes 260544 | tf_op jit(solution)/shard_map/block_forward/pallas_call | solution.py:108
  161.8 1.5 collective-permute-start.9
  163.4 3.3 key_value.3
  166.8 3.7 collective-permute-start.13
  172.4 1.4 query.3
  174.8 1.4 copy-done.39
  176.2 1.5 collective-permute-done.10
  177.7 8.9 %collective-permute-done.11 = bf16[128,640]{1,0:T(8,128)(2,1)S(1)} collective-permute-done((bf16[128,640]{1,0:T(8,128)(2,1)S(1)}, bf16[128,640]{1,0:T(8,128)(2,1)S(1)}, u32[]{:S(2)}, u32[]{:S(2)}) %collective-permute-start.11) | collective-permute-done | bytes 163872 | tf_op jit(solution)/shard_map/ppermute | solution.py:146
  187.7 18.8 %all-gather.7.cloned.1.call-done = bf16[6144,640]{1,0:T(8,128)(2,1)} async-done(((bf16[192,640]{1,0:T(8,128)(2,1)}), bf16[6144,640]{1,0:T(8,128)(2,1)}) %all-gather.7.cloned.1.call-update) | async-done | bytes 7864336 | tf_op jit(solution)/shard_map/all_gather | solution.py:736
  207.7 15.6 %block_forward.3 = (bf16[512,1024]{1,0:T(8,128)(2,1)S(1)}, f32[2,1024]{1,0:T(2,128)S(1)}, f32[512,640]{1,0:T(8,128)S(1)}, f32[512,640]{1,0:T(8,128)S(1)}, bf16[5...) custom-call(bf16[512,1024]{1,0:T(8,128)(2,1)S(1)} %copy-done.13, ...), custom_call_target="tpu_custom_call" | custom-call | flops 98566144 | bytes 260544 | tf_op jit(solution)/shard_map/block_forward/pallas_call | solution.py:108
  225.3 2.6 collective-permute-start.16
  228.5 14.9 %block_backward.2 = (bf16[512,640]{1,0:T(8,128)(2,1)S(1)}, bf16[512,4096]{1,0:T(8,128)(2,1)}, bf16[512,640]{1,0:T(8,128)(2,1)S(1)}, bf16[512,1024]{1,0:T(8,128)(...) custom-call(f32[512,640]{1,0:T(8,128)S(1)} %bitcast_convert_fusion.grad_ref, ...), custom_call_target="tpu_custom_call" | custom-call | flops 73400320 | bytes 270848 | tf_op jit(solution)/shard_map/block_backward/pallas_call | solution.py:108
  244.5 4.9 weight_gradient.8
  250.6 4.2 collective-permute-start.18
  254.8 6.4 %attention_backward.2 = (f32[512,1024]{1,0:T(8,128)S(1)}, bf16[512,512]{1,0:T(8,128)(2,1)S(1)}, f32[512,512]{1,0:T(8,128)S(1)}) custom-call(bf16[512,1024]{1,0:T(8,128)(2,1)S(1)} %copy-done.14, bf16[512,512]{1,0:T(8,128)(2,1)} %collective-permute-done.13.before_ref, bf16[512,512]{1,0:T(8,128)(2,1)} %get-tuple-element.132.own_ref, s32[2,1024]{1,0:T(2,128)S(1)} %bitcast.160, ...), custom_call_target="tpu_custom_call" | custom-call | flops 62914560 | bytes 106752 | tf_op jit(solution)/shard_map/attention_backward/pallas_call | solution.py:108
  261.2 1.4 copy-done.43
  263.8 8.9 %weight_gradient.9 = (bf16[1,8,192,640]{3,2,1,0:T(8,128)(2,1)S(1)}, bf16[1,8,192,640]{3,2,1,0:T(8,128)(2,1)}) custom-call(s32[5]{0:T(128)S(1)} %stack.154.numbers_ref, bf16[512,4096]{1,0:T(8,128)(2,1)} %get-tuple-element.144.refs_0_, bf16[512,2048]{1,0:T(8,128)(2,1)S(1)} %copy-done.2, bf16[512,640]{1,0:T(8,128)(2,1)S(1)} %get-tuple-element.146.refs_2_, ...), custom_call_target="tpu_custom_call" | custom-call | flops 31457280 | bytes 172032 | tf_op jit(solution)/shard_map/weight_gradient/pallas_call | solution.py:298
  274.9 3.5 input_backward.2
  280.9 1.4 copy-done.4
  285.7 2.2 weight_gradient.10
  290.1 2.6 collective-permute-done.20.refs_5_
  292.8 4.3 weight_gradient.11
  303.5 15.0 %block_backward.3 = (bf16[512,640]{1,0:T(8,128)(2,1)S(1)}, bf16[512,4096]{1,0:T(8,128)(2,1)}, bf16[512,640]{1,0:T(8,128)(2,1)S(1)}, bf16[512,1024]{1,0:T(8,128)(...) custom-call(f32[512,640]{1,0:T(8,128)S(1)} %copy-done.56, f32[512,640]{1,0:T(8,128)S(1)} %copy-done.54, ...), custom_call_target="tpu_custom_call" | custom-call | flops 73400320 | bytes 270848 | tf_op jit(solution)/shard_map/block_backward/pallas_call | solution.py:108
  320.6 5.7 %weight_gradient.12 = bf16[2,8,192,640]{3,2,1,0:T(8,128)(2,1)S(1)} custom-call(s32[5]{0:T(128)S(1)} %stack.156.numbers_ref, bf16[512,4096]{1,0:T(8,128)(2,1)} %get-tuple-element.187.refs_0_, bf16[512,2048]{1,0:T(8,128)(2,1)S(1)} %copy-done, bf16[512,640]{1,0:T(8,128)(2,1)S(1)} %copy-done.22, bf16[512,640]{1,0:T(8,128)(2,1)S(1)} %get-tuple-element.190.refs_3_), custom_call_target="tpu_custom_call" | custom-call | flops 31457280 | bytes 172032 | tf_op jit(solution)/shard_map/weight_gradient/pallas_call | solution.py:298
  326.3 8.8 %collective-permute-done.21 = bf16[8,192,640]{2,1,0:T(8,128)(2,1)} collective-permute-done((bf16[8,192,640]{2,1,0:T(8,128)(2,1)}, bf16[8,192,640]{2,1,0:T(8,128)(2,1)}, u32[]{:S(2)}, u32[]{:S(2)}) %collective-permute-start.21) | collective-permute-done | bytes 1966112 | tf_op jit(solution)/shard_map/ppermute | solution.py:199
  335.1 20.2 %collective-permute-done.22 = bf16[8,96,640]{2,1,0:T(8,128)(2,1)} collective-permute-done((bf16[8,96,640]{2,1,0:T(8,128)(2,1)}, bf16[8,96,640]{2,1,0:T(8,128)(2,1)}, u32[]{:S(2)}, u32[]{:S(2)}) %collective-permute-start.22) | collective-permute-done | bytes 983072 | tf_op jit(solution)/shard_map/ppermute | solution.py:199
  355.3 2.1 fusion
  357.4 1.4 fusion.3
  358.9 1.8 pad_maximum_fusion
  365.4 5.2 attention_backward.3
  370.6 1.4 copy-done.41
  373.0 2.0 copy-done.86
  375.0 8.8 %weight_gradient.13 = (bf16[1,8,192,384]{3,2,1,0:T(8,128)(2,1)S(1)}, bf16[1,8,192,384]{3,2,1,0:T(8,128)(2,1)}, bf16[2,4,192,256]{3,2,1,0:T(8,128)(2,1)S(1)}, bf16[2,4,192,256]{3,2,1,0:T(8,128)(2,1)}) custom-call(s32[5]{0:T(128)S(1)} %stack.156.numbers_ref, bf16[512,4096]{1,0:T(8,128)(2,1)} %get-tuple-element.187.refs_0_, bf16[512,2048]{1,0:T(8,128)(2,1)S(1)} %copy-done.1, ...), custom_call_target="tpu_custom_call" | custom-call | flops 31457280 | bytes 172032 | tf_op jit(solution)/shard_map/weight_gradient/pallas_call | solution.py:298
  385.8 1.4 collective-permute-start.26
  387.2 1.5 collective-permute-start.24
  388.7 21.0 %collective-permute-done.26 = bf16[8,192,256]{2,1,0:T(8,128)(2,1)} collective-permute-done((bf16[8,192,256]{2,1,0:T(8,128)(2,1)}, bf16[8,192,256]{2,1,0:T(8,128)(2,1)}, u32[]{:S(2)}, u32[]{:S(2)}) %collective-permute-start.26) | collective-permute-done | bytes 786464 | tf_op jit(solution)/shard_map/ppermute | solution.py:199
  409.7 3.8 collective-permute-done.25
  413.5 1.5 fusion.4
  416.0 1.7 fusion.1
  418.7 1.5 collective-permute-start.27
  422.0 3.5 input_backward.3
  430.1 2.2 weight_gradient.14
  433.4 10.6 %collective-permute-done.28 = bf16[4,192,256]{2,1,0:T(8,128)(2,1)S(1)} collective-permute-done((bf16[4,192,256]{2,1,0:T(8,128)(2,1)S(1)}, bf16[4,192,256]{2,1,0:T(8,128)(2,1)S(1)}, u32[]{:S(2)}, u32[]{:S(2)}) %collective-permute-start.28) | collective-permute-done | bytes 393248 | tf_op jit(solution)/shard_map/ppermute | solution.py:199
  446.6 3.5 collective-permute-start.33
  450.2 2.0 collective-permute-start.30
  453.4 3.3 weight_gradient.15
  456.7 14.6 %collective-permute-done.30 = bf16[128,640]{1,0:T(8,128)(2,1)S(1)} collective-permute-done((bf16[128,640]{1,0:T(8,128)(2,1)S(1)}, bf16[128,640]{1,0:T(8,128)(2,1)S(1)}, u32[]{:S(2)}, u32[]{:S(2)}) %collective-permute-start.30) | collective-permute-done | bytes 163872 | tf_op jit(solution)/shard_map/ppermute | solution.py:159
  472.1 2.1 collective-permute-done.31
  474.4 11.0 %collective-permute-done.38 = bf16[8,96,640]{2,1,0:T(8,128)(2,1)S(1)} collective-permute-done((bf16[8,96,640]{2,1,0:T(8,128)(2,1)S(1)}, bf16[8,96,640]{2,1,0:T(8,128)(2,1)S(1)}, u32[]{:S(2)}, u32[]{:S(2)}) %collective-permute-start.38) | collective-permute-done | bytes 983072 | tf_op jit(solution)/shard_map/ppermute | solution.py:199
  485.8 7.6 %collective-permute-done.34 = bf16[2,192,256]{2,1,0:T(8,128)(2,1)S(1)} collective-permute-done((bf16[2,192,256]{2,1,0:T(8,128)(2,1)S(1)}, bf16[2,192,256]{2,1,0:T(8,128)(2,1)S(1)}, u32[]{:S(2)}, u32[]{:S(2)}) %collective-permute-start.34) | collective-permute-done | bytes 196640 | tf_op jit(solution)/shard_map/ppermute | solution.py:199
  493.7 2.0 collective-permute-start.36
  496.5 23.0 %collective-permute-start.40 = (bf16[2,96,640]{2,1,0:T(8,128)(2,1)S(1)}, bf16[2,96,640]{2,1,0:T(8,128)(2,1)S(1)}, u32[]{:S(2)}, u32[]{:S(2)}) collective-permute-start(bf16[2,96,640]{2,1,0:T(8,128)(2,1)S(1)} %slice.162), channel_id=1, source_target_pairs={{0,4},{1,5},{2,6},{3,7},{4,0},{5,1},{6,2},{7,3},{8,12},{9,13},{10,... | collective-permute-start | bytes 737288 | tf_op jit(solution)/shard_map/ppermute | solution.py:199
  521.8 8.3 %collective-permute-done.40 = bf16[2,96,640]{2,1,0:T(8,128)(2,1)S(1)} collective-permute-done((bf16[2,96,640]{2,1,0:T(8,128)(2,1)S(1)}, bf16[2,96,640]{2,1,0:T(8,128)(2,1)S(1)}, u32[]{:S(2)}, u32[]{:S(2)}) %collective-permute-start.40) | collective-permute-done | bytes 245792 | tf_op jit(solution)/shard_map/ppermute | solution.py:199
  530.2 5.2 collective-permute-done.41
  (360 shorter events, 85.9 us)
Async XLA Ops:
  7.2 117.5 %all-gather.5.cloned.1.call-start = ((), (), s32[]{:S(2)}) async-start(), calls=%async_computation.2 | async-start | bytes 15544320 | tf_op jit(solution)/shard_map/all_gather | solution.py:736
  10.4 196.1 %all-gather.7.cloned.1.call-start = ((), (), s32[]{:S(2)}) async-start(), calls=%async_computation.3 | async-start | bytes 8110080 | tf_op jit(solution)/shard_map/all_gather | solution.py:736
  10.6 7.6 %collective-permute-start = (bf16[128,640]{1,0:T(8,128)(2,1)S(1)}, bf16[128,640]{1,0:T(8,128)(2,1)S(1)}, u32[]{:S(2)}, u32[]{:S(2)}) collective-permute-start(bf16[128,640]{1,0:T(8,128)(2,1)S(1)} %get-tuple-element.272), channel_id=1, source_target_pairs={{0,3},{1,0},{2,1},{3,2},{4,11},{5,8},{6,9},{7,10},{8,7},{9,4},{10,... | collective-permute-start | bytes 491528 | tf_op jit(solution)/shard_map/ppermute | solution.py:146
  14.6 7.3 %collective-permute-start.1 = (bf16[128,640]{1,0:T(8,128)(2,1)S(1)}, bf16[128,640]{1,0:T(8,128)(2,1)S(1)}, u32[]{:S(2)}, u32[]{:S(2)}) collective-permute-start(bf16[128,640]{1,0:T(8,128)(2,1)S(1)} %get-tuple-element.271), channel_id=1, source_target_pairs={{0,2},{1,3},{2,0},{3,1},{4,10},{5,11},{6,8},{7,9},{8,6},{9,7},{10,... | collective-permute-start | bytes 491528 | tf_op jit(solution)/shard_map/ppermute | solution.py:146
  15.1 7.2 %collective-permute-start.2 = (bf16[128,640]{1,0:T(8,128)(2,1)S(1)}, bf16[128,640]{1,0:T(8,128)(2,1)S(1)}, u32[]{:S(2)}, u32[]{:S(2)}) collective-permute-start(bf16[128,640]{1,0:T(8,128)(2,1)S(1)} %get-tuple-element.273), channel_id=1, source_target_pairs={{0,1},{1,2},{2,3},{3,0},{4,9},{5,10},{6,11},{7,8},{8,5},{9,6},{10,... | collective-permute-start | bytes 491528 | tf_op jit(solution)/shard_map/ppermute | solution.py:146
  15.7 6.6 %collective-permute-start.3 = (bf16[128,640]{1,0:T(8,128)(2,1)S(1)}, bf16[128,640]{1,0:T(8,128)(2,1)S(1)}, u32[]{:S(2)}, u32[]{:S(2)}) collective-permute-start(bf16[128,640]{1,0:T(8,128)(2,1)S(1)} %get-tuple-element.270), channel_id=1, source_target_pairs={{0,0},{1,1},{2,2},{3,3},{4,8},{5,9},{6,10},{7,11},{8,4},{9,5},{10,... | collective-permute-start | bytes 491528 | tf_op jit(solution)/shard_map/ppermute | solution.py:146
  22.7 498.0 %reduce-scatter.2.cloned.1.call-start = ((), (), s32[]{:S(2)}) async-start(), calls=%async_computation.1 | async-start | bytes 3317760 | tf_op jit(solution)/shard_map/reduce_scatter | solution.py:793
  23.2 6.2 %collective-permute-start.4 = (s32[128]{0:T(128)S(1)}, s32[128]{0:T(128)S(1)}, u32[]{:S(2)}, u32[]{:S(2)}) collective-permute-start(s32[128]{0:T(128)S(1)} %get-tuple-element.284), channel_id=1, source_target_pairs={{0,3},{1,0},{2,1},{3,2},{4,11},{5,8},{6,9},{7,10},{8,7},{9,4},{10,... | collective-permute-start | bytes 1544 | tf_op jit(solution)/shard_map/ppermute | solution.py:146
  24.8 4.6 collective-permute-start.5
  26.7 4.4 collective-permute-start.6
  28.7 2.5 collective-permute-start.7
  130.8 7.4 %collective-permute-start.8 = (bf16[512,512]{1,0:T(8,128)(2,1)S(1)}, bf16[512,512]{1,0:T(8,128)(2,1)S(1)}, u32[]{:S(2)}, u32[]{:S(2)}) collective-permute-start(bf16[512,512]{1,0:T(8,128)(2,1)S(1)} %get-tuple-element.125.own_ref), channel_id=1, source_target_pairs={{0,8},{1,9},{2,10},{3,11},{4,12},{5,13},{6,14},{7,15},{16,24},{17,... | collective-permute-start | bytes 1572872 | tf_op jit(solution)/shard_map/ppermute | solution.py:176
  138.2 17.6 %copy-start.10 = (bf16[512,1024]{1,0:T(8,128)(2,1)}, bf16[512,1024]{1,0:T(8,128)(2,1)S(1)}, u32[]{:S(2)}) copy-start(bf16[512,1024]{1,0:T(8,128)(2,1)S(1)} %get-tuple-element.124.q_ref) | copy-start | bytes 3145732
  141.1 19.8 %copy-start.92 = (bf16[4,128,640]{2,1,0:T(8,128)(2,1)S(1)}, bf16[4,128,640]{2,1,0:T(8,128)(2,1)}, u32[]{:S(2)}) copy-start(bf16[4,128,640]{2,1,0:T(8,128)(2,1)} %param.10) | copy-start | bytes 1966084
  161.8 14.4 %collective-permute-start.9 = (bf16[128,640]{1,0:T(8,128)(2,1)}, bf16[128,640]{1,0:T(8,128)(2,1)S(1)}, u32[]{:S(2)}, u32[]{:S(2)}) collective-permute-start(bf16[128,640]{1,0:T(8,128)(2,1)} %get-tuple-element.269), channel_id=1, source_target_pairs={{0,3},{1,0},{2,1},{3,2},{4,11},{5,8},{6,9},{7,10},{8,7},{9,4},{10,... | collective-permute-start | bytes 491528 | tf_op jit(solution)/shard_map/ppermute | solution.py:146
  163.4 8.1 %copy-start.94 = (bf16[128,640]{1,0:T(8,128)(2,1)S(1)}, bf16[128,640]{1,0:T(8,128)(2,1)}, u32[]{:S(2)}) copy-start(bf16[128,640]{1,0:T(8,128)(2,1)} %get-tuple-element.266) | copy-start | bytes 491524
  166.8 39.8 %collective-permute-start.13 = (bf16[512,512]{1,0:T(8,128)(2,1)}, bf16[512,512]{1,0:T(8,128)(2,1)}, u32[]{:S(2)}, u32[]{:S(2)}) collective-permute-start(bf16[512,512]{1,0:T(8,128)(2,1)} %get-tuple-element.132.own_ref), channel_id=1, source_target_pairs={{0,8},{1,9},{2,10},{3,11},{4,12},{5,13},{6,14},{7,15},{16,24},{17,... | collective-permute-start | bytes 1572872 | tf_op jit(solution)/shard_map/ppermute | solution.py:176
  170.4 7.3 %collective-permute-start.10 = (bf16[128,640]{1,0:T(8,128)(2,1)S(1)}, bf16[128,640]{1,0:T(8,128)(2,1)S(1)}, u32[]{:S(2)}, u32[]{:S(2)}) collective-permute-start(bf16[128,640]{1,0:T(8,128)(2,1)S(1)} %copy-done.96), channel_id=1, source_target_pairs={{0,2},{1,3},{2,0},{3,1},{4,10},{5,11},{6,8},{7,9},{8,6},{9,7},{10,... | collective-permute-start | bytes 491528 | tf_op jit(solution)/shard_map/ppermute | solution.py:146
  171.1 15.5 %collective-permute-start.11 = (bf16[128,640]{1,0:T(8,128)(2,1)S(1)}, bf16[128,640]{1,0:T(8,128)(2,1)S(1)}, u32[]{:S(2)}, u32[]{:S(2)}) collective-permute-start(bf16[128,640]{1,0:T(8,128)(2,1)S(1)} %copy-done.95), channel_id=1, source_target_pairs={{0,1},{1,2},{2,3},{3,0},{4,9},{5,10},{6,11},{7,8},{8,5},{9,6},{10,... | collective-permute-start | bytes 491528 | tf_op jit(solution)/shard_map/ppermute | solution.py:146
  171.5 15.1 %collective-permute-start.12 = (bf16[128,640]{1,0:T(8,128)(2,1)S(1)}, bf16[128,640]{1,0:T(8,128)(2,1)S(1)}, u32[]{:S(2)}, u32[]{:S(2)}) collective-permute-start(bf16[128,640]{1,0:T(8,128)(2,1)S(1)} %copy-done.94), channel_id=1, source_target_pairs={{0,0},{1,1},{2,2},{3,3},{4,8},{5,9},{6,10},{7,11},{8,4},{9,5},{10,... | collective-permute-start | bytes 491528 | tf_op jit(solution)/shard_map/ppermute | solution.py:146
  186.7 19.8 %copy-start.76 = (s32[1,2,4,256]{3,1,2,0:T(2,128)S(1)}, s32[1,2,4,256]{3,1,2,0:T(2,128)}, u32[]{:S(2)}) copy-start(s32[1,2,4,256]{3,1,2,0:T(2,128)} %copy-done.75) | copy-start | bytes 24580
  224.3 25.1 %collective-permute-start.14 = (bf16[128,640]{1,0:T(8,128)(2,1)S(1)}, bf16[128,640]{1,0:T(8,128)(2,1)S(1)}, u32[]{:S(2)}, u32[]{:S(2)}) collective-permute-start(bf16[128,640]{1,0:T(8,128)(2,1)S(1)} %get-tuple-element.265), channel_id=1, source_target_pairs={{0,0},{1,1},{2,2},{3,3},{8,4},{9,5},{10,6},{11,7},{4,8},{5,9},{6,1... | collective-permute-start | bytes 491528 | tf_op jit(solution)/shard_map/ppermute | solution.py:159
  225.1 24.3 %collective-permute-start.15 = (bf16[128,640]{1,0:T(8,128)(2,1)S(1)}, bf16[128,640]{1,0:T(8,128)(2,1)S(1)}, u32[]{:S(2)}, u32[]{:S(2)}) collective-permute-start(bf16[128,640]{1,0:T(8,128)(2,1)S(1)} %get-tuple-element.264), channel_id=1, source_target_pairs={{1,0},{2,1},{3,2},{0,3},{9,4},{10,5},{11,6},{8,7},{5,8},{6,9},{7,1... | collective-permute-start | bytes 491528 | tf_op jit(solution)/shard_map/ppermute | solution.py:159
  225.3 24.2 %collective-permute-start.16 = (bf16[128,640]{1,0:T(8,128)(2,1)S(1)}, bf16[128,640]{1,0:T(8,128)(2,1)S(1)}, u32[]{:S(2)}, u32[]{:S(2)}) collective-permute-start(bf16[128,640]{1,0:T(8,128)(2,1)S(1)} %get-tuple-element.263), channel_id=1, source_target_pairs={{2,0},{3,1},{0,2},{1,3},{10,4},{11,5},{8,6},{9,7},{6,8},{7,9},{4,1... | collective-permute-start | bytes 491528 | tf_op jit(solution)/shard_map/ppermute | solution.py:159
  227.9 21.6 %collective-permute-start.17 = (bf16[128,640]{1,0:T(8,128)(2,1)S(1)}, bf16[128,640]{1,0:T(8,128)(2,1)S(1)}, u32[]{:S(2)}, u32[]{:S(2)}) collective-permute-start(bf16[128,640]{1,0:T(8,128)(2,1)S(1)} %get-tuple-element.262), channel_id=1, source_target_pairs={{3,0},{0,1},{1,2},{2,3},{11,4},{8,5},{9,6},{10,7},{7,8},{4,9},{5,1... | collective-permute-start | bytes 491528 | tf_op jit(solution)/shard_map/ppermute | solution.py:159
  228.5 16.0 %copy-start.2 = (bf16[512,2048]{1,0:T(8,128)(2,1)S(1)}, bf16[512,2048]{1,0:T(8,128)(2,1)}, u32[]{:S(2)}) copy-start(bf16[512,2048]{1,0:T(8,128)(2,1)} %get-tuple-element.145.refs_1_) | copy-start | bytes 6291460
  250.6 13.3 %collective-permute-start.18 = (bf16[2,8,192,640]{3,2,1,0:T(8,128)(2,1)S(1)}, bf16[2,8,192,640]{3,2,1,0:T(8,128)(2,1)}, u32[]{:S(2)}, u32[]{:S(2)}) collective-permute-start(bf16[2,8,192,640]{3,2,1,0:T(8,128)(2,1)S(1)} %weight_gradient.8), channel_id=1, source_target_pairs={{0,8},{8,0},{16,24},{24,16},{1,9},{9,1},{17,25},{25,17},{2,10},{10... | collective-permute-start | bytes 11796488 | tf_op jit(solution)/shard_map/ppermute | solution.py:199
  262.5 11.6 %collective-permute-start.19 = (bf16[512,512]{1,0:T(8,128)(2,1)S(1)}, bf16[512,512]{1,0:T(8,128)(2,1)S(1)}, u32[]{:S(2)}, u32[]{:S(2)}) collective-permute-start(bf16[512,512]{1,0:T(8,128)(2,1)S(1)} %get-tuple-element.158), channel_id=1, source_target_pairs={{8,0},{9,1},{10,2},{11,3},{12,4},{13,5},{14,6},{15,7},{24,16},{25,... | collective-permute-start | bytes 1572872 | tf_op jit(solution)/shard_map/ppermute | solution.py:176
  263.8 9.0 %copy-start.40 = (f32[512,1024]{1,0:T(8,128)S(1)}, f32[512,1024]{1,0:T(8,128)}, u32[]{:S(2)}) copy-start(f32[512,1024]{1,0:T(8,128)} %copy-done.39) | copy-start | bytes 6291460
  263.8 9.0 %copy-start.44 = (f32[512,1024]{1,0:T(8,128)S(1)}, f32[512,1024]{1,0:T(8,128)}, u32[]{:S(2)}) copy-start(f32[512,1024]{1,0:T(8,128)} %copy-done.43) | copy-start | bytes 6291460
  287.9 4.8 collective-permute-start.20
  289.2 46.0 %collective-permute-start.21 = (bf16[8,192,640]{2,1,0:T(8,128)(2,1)}, bf16[8,192,640]{2,1,0:T(8,128)(2,1)}, u32[]{:S(2)}, u32[]{:S(2)}) collective-permute-start(bf16[8,192,640]{2,1,0:T(8,128)(2,1)} %bitcast.52), channel_id=1, source_target_pairs={{0,16},{8,24},{16,0},{24,8},{1,17},{9,25},{17,1},{25,9},{2,18},{10... | collective-permute-start | bytes 5898248 | tf_op jit(solution)/shard_map/ppermute | solution.py:199
  297.1 58.3 %collective-permute-start.22 = (bf16[8,96,640]{2,1,0:T(8,128)(2,1)}, bf16[8,96,640]{2,1,0:T(8,128)(2,1)}, u32[]{:S(2)}, u32[]{:S(2)}) collective-permute-start(bf16[8,96,640]{2,1,0:T(8,128)(2,1)} %bitcast.53), channel_id=1, source_target_pairs={{0,16},{8,24},{16,0},{24,8},{1,17},{9,25},{17,1},{25,9},{2,18},{10... | collective-permute-start | bytes 2949128 | tf_op jit(solution)/shard_map/ppermute | solution.py:199
  303.5 17.1 %copy-start = (bf16[512,2048]{1,0:T(8,128)(2,1)S(1)}, bf16[512,2048]{1,0:T(8,128)(2,1)}, u32[]{:S(2)}) copy-start(bf16[512,2048]{1,0:T(8,128)(2,1)} %get-tuple-element.188.refs_1_) | copy-start | bytes 6291460
  303.5 17.1 %copy-start.22 = (bf16[512,640]{1,0:T(8,128)(2,1)S(1)}, bf16[512,640]{1,0:T(8,128)(2,1)}, u32[]{:S(2)}) copy-start(bf16[512,640]{1,0:T(8,128)(2,1)} %copy-done.21) | copy-start | bytes 1966084
  320.6 34.8 %copy-start.46 = (bf16[1,8,192,640]{3,2,1,0:T(8,128)(2,1)S(1)}, bf16[1,8,192,640]{3,2,1,0:T(8,128)(2,1)}, u32[]{:S(2)}) copy-start(bf16[1,8,192,640]{3,2,1,0:T(8,128)(2,1)} %copy-done.45) | copy-start | bytes 5898244
  326.3 31.1 %copy-start.20 = (bf16[2,8,192,640]{3,2,1,0:T(8,128)(2,1)}, bf16[2,8,192,640]{3,2,1,0:T(8,128)(2,1)S(1)}, u32[]{:S(2)}) copy-start(bf16[2,8,192,640]{3,2,1,0:T(8,128)(2,1)S(1)} %weight_gradient.12) | copy-start | bytes 11796484
  360.7 12.3 %collective-permute-start.23 = (bf16[2,8,192,640]{3,2,1,0:T(8,128)(2,1)}, bf16[2,8,192,640]{3,2,1,0:T(8,128)(2,1)S(1)}, u32[]{:S(2)}, u32[]{:S(2)}) collective-permute-start(bf16[2,8,192,640]{3,2,1,0:T(8,128)(2,1)} %copy-done.20), channel_id=1, source_target_pairs={{0,8},{8,0},{16,24},{24,16},{1,9},{9,1},{17,25},{25,17},{2,10},{10... | collective-permute-start | bytes 11796488 | tf_op jit(solution)/shard_map/ppermute | solution.py:199
  365.4 9.6 %copy-start.1 = (bf16[512,2048]{1,0:T(8,128)(2,1)S(1)}, bf16[512,2048]{1,0:T(8,128)(2,1)}, u32[]{:S(2)}) copy-start(bf16[512,2048]{1,0:T(8,128)(2,1)} %get-tuple-element.188.refs_1_) | copy-start | bytes 6291460
  365.4 9.6 %copy-start.24 = (bf16[512,640]{1,0:T(8,128)(2,1)S(1)}, bf16[512,640]{1,0:T(8,128)(2,1)}, u32[]{:S(2)}) copy-start(bf16[512,640]{1,0:T(8,128)(2,1)} %copy-done.23) | copy-start | bytes 1966084
  373.0 10.8 %copy-start.82 = (bf16[512,512]{1,0:T(8,128)(2,1)}, bf16[512,512]{1,0:T(8,128)(2,1)S(1)}, u32[]{:S(2)}) copy-start(bf16[512,512]{1,0:T(8,128)(2,1)S(1)} %get-tuple-element.202) | copy-start | bytes 1572868
  384.8 28.7 %collective-permute-start.25 = (bf16[8,192,384]{2,1,0:T(8,128)(2,1)}, bf16[8,192,384]{2,1,0:T(8,128)(2,1)}, u32[]{:S(2)}, u32[]{:S(2)}) collective-permute-start(bf16[8,192,384]{2,1,0:T(8,128)(2,1)} %bitcast.57), channel_id=1, source_target_pairs={{0,16},{8,24},{16,0},{24,8},{1,17},{9,25},{17,1},{25,9},{2,18},{10... | collective-permute-start | bytes 3538952 | tf_op jit(solution)/shard_map/ppermute | solution.py:199
  385.8 23.9 %collective-permute-start.26 = (bf16[8,192,256]{2,1,0:T(8,128)(2,1)}, bf16[8,192,256]{2,1,0:T(8,128)(2,1)}, u32[]{:S(2)}, u32[]{:S(2)}) collective-permute-start(bf16[8,192,256]{2,1,0:T(8,128)(2,1)} %bitcast.58), channel_id=1, source_target_pairs={{0,1},{1,0},{2,3},{3,2},{4,5},{5,4},{6,7},{7,6},{8,9},{9,8},{10,11... | collective-permute-start | bytes 2359304 | tf_op jit(solution)/shard_map/ppermute | solution.py:199
  387.2 34.2 %collective-permute-start.24 = (bf16[512,512]{1,0:T(8,128)(2,1)S(1)}, bf16[512,512]{1,0:T(8,128)(2,1)S(1)}, u32[]{:S(2)}, u32[]{:S(2)}) collective-permute-start(bf16[512,512]{1,0:T(8,128)(2,1)S(1)} %copy-done.83), channel_id=1, source_target_pairs={{8,0},{9,1},{10,2},{11,3},{12,4},{13,5},{14,6},{15,7},{24,16},{25,... | collective-permute-start | bytes 1572872 | tf_op jit(solution)/shard_map/ppermute | solution.py:176
  418.7 25.3 %collective-permute-start.27 = (bf16[4,192,384]{2,1,0:T(8,128)(2,1)}, bf16[4,192,384]{2,1,0:T(8,128)(2,1)}, u32[]{:S(2)}, u32[]{:S(2)}) collective-permute-start(bf16[4,192,384]{2,1,0:T(8,128)(2,1)} %slice.148), channel_id=1, source_target_pairs={{0,1},{1,0},{2,3},{3,2},{4,5},{5,4},{6,7},{7,6},{8,9},{9,8},{10,11... | collective-permute-start | bytes 1769480 | tf_op jit(solution)/shard_map/ppermute | solution.py:199
  430.1 13.9 %copy-start.88 = (bf16[8,192,256]{2,1,0:T(8,128)(2,1)S(1)}, bf16[8,192,256]{2,1,0:T(8,128)(2,1)}, u32[]{:S(2)}) copy-start(bf16[8,192,256]{2,1,0:T(8,128)(2,1)} %copy-done.87) | copy-start | bytes 2359300
  432.3 11.8 %copy-start.85 = (bf16[8,192,384]{2,1,0:T(8,128)(2,1)S(1)}, bf16[8,192,384]{2,1,0:T(8,128)(2,1)}, u32[]{:S(2)}) copy-start(bf16[8,192,384]{2,1,0:T(8,128)(2,1)} %copy-done.84) | copy-start | bytes 3538948
  432.4 20.0 %collective-permute-start.37 = (bf16[2,8,96,640]{3,2,1,0:T(8,128)(2,1)S(1)}, bf16[2,8,96,640]{3,2,1,0:T(8,128)(2,1)S(1)}, u32[]{:S(2)}, u32[]{:S(2)}) collective-permute-start(bf16[2,8,96,640]{3,2,1,0:T(8,128)(2,1)S(1)} %weight_gradient.14), channel_id=1, source_target_pairs={{0,8},{8,0},{16,24},{24,16},{1,9},{9,1},{17,25},{25,17},{2,10},{10... | collective-permute-start | bytes 5898248 | tf_op jit(solution)/shard_map/ppermute | solution.py:199
  432.4 11.5 %collective-permute-start.28 = (bf16[4,192,256]{2,1,0:T(8,128)(2,1)S(1)}, bf16[4,192,256]{2,1,0:T(8,128)(2,1)S(1)}, u32[]{:S(2)}, u32[]{:S(2)}) collective-permute-start(bf16[4,192,256]{2,1,0:T(8,128)(2,1)S(1)} %copy-done.93), channel_id=1, source_target_pairs={{0,16},{8,24},{16,0},{24,8},{1,17},{9,25},{17,1},{25,9},{2,18},{10... | collective-permute-start | bytes 1179656 | tf_op jit(solution)/shard_map/ppermute | solution.py:199
  445.6 7.8 %copy-start.17 = (bf16[512,1024]{1,0:T(8,128)(2,1)S(1)}, bf16[512,1024]{1,0:T(8,128)(2,1)}, u32[]{:S(2)}) copy-start(bf16[512,1024]{1,0:T(8,128)(2,1)} %copy-done.15) | copy-start | bytes 3145732
  445.7 7.7 %copy-start.7 = (bf16[512,640]{1,0:T(8,128)(2,1)S(1)}, bf16[512,640]{1,0:T(8,128)(2,1)}, u32[]{:S(2)}) copy-start(bf16[512,640]{1,0:T(8,128)(2,1)} %copy-done.5) | copy-start | bytes 1966084
  445.7 7.7 %copy-start.27 = (bf16[512,640]{1,0:T(8,128)(2,1)S(1)}, bf16[512,640]{1,0:T(8,128)(2,1)}, u32[]{:S(2)}) copy-start(bf16[512,640]{1,0:T(8,128)(2,1)} %copy-done.25) | copy-start | bytes 1966084
  445.8 6.4 %collective-permute-start.29 = (bf16[128,640]{1,0:T(8,128)(2,1)S(1)}, bf16[128,640]{1,0:T(8,128)(2,1)S(1)}, u32[]{:S(2)}, u32[]{:S(2)}) collective-permute-start(bf16[128,640]{1,0:T(8,128)(2,1)S(1)} %get-tuple-element.261), channel_id=1, source_target_pairs={{0,0},{1,1},{2,2},{3,3},{8,4},{9,5},{10,6},{11,7},{4,8},{5,9},{6,1... | collective-permute-start | bytes 491528 | tf_op jit(solution)/shard_map/ppermute | solution.py:159
  446.6 46.8 %collective-permute-start.33 = (bf16[2,192,384]{2,1,0:T(8,128)(2,1)S(1)}, bf16[2,192,384]{2,1,0:T(8,128)(2,1)S(1)}, u32[]{:S(2)}, u32[]{:S(2)}) collective-permute-start(bf16[2,192,384]{2,1,0:T(8,128)(2,1)S(1)} %get-tuple-element.223), channel_id=1, source_target_pairs={{0,4},{1,5},{2,6},{3,7},{4,0},{5,1},{6,2},{7,3},{8,12},{9,13},{10,... | collective-permute-start | bytes 884744 | tf_op jit(solution)/shard_map/ppermute | solution.py:199
  450.1 43.3 %collective-permute-start.34 = (bf16[2,192,256]{2,1,0:T(8,128)(2,1)S(1)}, bf16[2,192,256]{2,1,0:T(8,128)(2,1)S(1)}, u32[]{:S(2)}, u32[]{:S(2)}) collective-permute-start(bf16[2,192,256]{2,1,0:T(8,128)(2,1)S(1)} %get-tuple-element.224), channel_id=1, source_target_pairs={{0,4},{1,5},{2,6},{3,7},{4,0},{5,1},{6,2},{7,3},{8,12},{9,13},{10,... | collective-permute-start | bytes 589832 | tf_op jit(solution)/shard_map/ppermute | solution.py:199
  450.2 21.1 %collective-permute-start.30 = (bf16[128,640]{1,0:T(8,128)(2,1)S(1)}, bf16[128,640]{1,0:T(8,128)(2,1)S(1)}, u32[]{:S(2)}, u32[]{:S(2)}) collective-permute-start(bf16[128,640]{1,0:T(8,128)(2,1)S(1)} %get-tuple-element.260), channel_id=1, source_target_pairs={{1,0},{2,1},{3,2},{0,3},{9,4},{10,5},{11,6},{8,7},{5,8},{6,9},{7,1... | collective-permute-start | bytes 491528 | tf_op jit(solution)/shard_map/ppermute | solution.py:159
  452.2 22.1 %collective-permute-start.31 = (bf16[128,640]{1,0:T(8,128)(2,1)S(1)}, bf16[128,640]{1,0:T(8,128)(2,1)S(1)}, u32[]{:S(2)}, u32[]{:S(2)}) collective-permute-start(bf16[128,640]{1,0:T(8,128)(2,1)S(1)} %get-tuple-element.259), channel_id=1, source_target_pairs={{2,0},{3,1},{0,2},{1,3},{10,4},{11,5},{8,6},{9,7},{6,8},{7,9},{4,1... | collective-permute-start | bytes 491528 | tf_op jit(solution)/shard_map/ppermute | solution.py:159
  452.3 21.9 %collective-permute-start.32 = (bf16[128,640]{1,0:T(8,128)(2,1)S(1)}, bf16[128,640]{1,0:T(8,128)(2,1)S(1)}, u32[]{:S(2)}, u32[]{:S(2)}) collective-permute-start(bf16[128,640]{1,0:T(8,128)(2,1)S(1)} %get-tuple-element.258), channel_id=1, source_target_pairs={{3,0},{0,1},{1,2},{2,3},{11,4},{8,5},{9,6},{10,7},{7,8},{4,9},{5,1... | collective-permute-start | bytes 491528 | tf_op jit(solution)/shard_map/ppermute | solution.py:159
  471.3 14.1 %collective-permute-start.38 = (bf16[8,96,640]{2,1,0:T(8,128)(2,1)S(1)}, bf16[8,96,640]{2,1,0:T(8,128)(2,1)S(1)}, u32[]{:S(2)}, u32[]{:S(2)}) collective-permute-start(bf16[8,96,640]{2,1,0:T(8,128)(2,1)S(1)} %bitcast.162), channel_id=1, source_target_pairs={{0,16},{8,24},{16,0},{24,8},{1,17},{9,25},{17,1},{25,9},{2,18},{10... | collective-permute-start | bytes 2949128 | tf_op jit(solution)/shard_map/ppermute | solution.py:199
  485.7 10.7 %collective-permute-start.39 = (bf16[4,96,640]{2,1,0:T(8,128)(2,1)S(1)}, bf16[4,96,640]{2,1,0:T(8,128)(2,1)S(1)}, u32[]{:S(2)}, u32[]{:S(2)}) collective-permute-start(bf16[4,96,640]{2,1,0:T(8,128)(2,1)S(1)} %slice.160), channel_id=1, source_target_pairs={{0,1},{1,0},{2,3},{3,2},{4,5},{5,4},{6,7},{7,6},{8,9},{9,8},{10,11... | collective-permute-start | bytes 1474568 | tf_op jit(solution)/shard_map/ppermute | solution.py:199
  493.6 28.1 %collective-permute-start.35 = (bf16[1,192,384]{2,1,0:T(8,128)(2,1)S(1)}, bf16[1,192,384]{2,1,0:T(8,128)(2,1)S(1)}, u32[]{:S(2)}, u32[]{:S(2)}) collective-permute-start(bf16[1,192,384]{2,1,0:T(8,128)(2,1)S(1)} %slice.156), channel_id=1, source_target_pairs={{0,2},{1,3},{2,0},{3,1},{4,6},{5,7},{6,4},{7,5},{8,10},{9,11},{10,... | collective-permute-start | bytes 442376 | tf_op jit(solution)/shard_map/ppermute | solution.py:199
  493.7 28.0 %collective-permute-start.36 = (bf16[1,192,256]{2,1,0:T(8,128)(2,1)S(1)}, bf16[1,192,256]{2,1,0:T(8,128)(2,1)S(1)}, u32[]{:S(2)}, u32[]{:S(2)}) collective-permute-start(bf16[1,192,256]{2,1,0:T(8,128)(2,1)S(1)} %slice.157), channel_id=1, source_target_pairs={{0,2},{1,3},{2,0},{3,1},{4,6},{5,7},{6,4},{7,5},{8,10},{9,11},{10,... | collective-permute-start | bytes 294920 | tf_op jit(solution)/shard_map/ppermute | solution.py:199
  496.5 33.6 %collective-permute-start.40 = (bf16[2,96,640]{2,1,0:T(8,128)(2,1)S(1)}, bf16[2,96,640]{2,1,0:T(8,128)(2,1)S(1)}, u32[]{:S(2)}, u32[]{:S(2)}) collective-permute-start(bf16[2,96,640]{2,1,0:T(8,128)(2,1)S(1)} %slice.162), channel_id=1, source_target_pairs={{0,4},{1,5},{2,6},{3,7},{4,0},{5,1},{6,2},{7,3},{8,12},{9,13},{10,... | collective-permute-start | bytes 737288 | tf_op jit(solution)/shard_map/ppermute | solution.py:199
  530.1 5.3 collective-permute-start.41
  (84 other events, 198.9 us)
Sparse Core Ops, SparseCore 0:
  11.5 113.1 all-gather.4
  128.2 78.2 all-gather.6
  387.3 101.4 reduce-scatter.1
